TPU v7x, 32 devices: a whole 2x2x4 slice. The times are simulated.
32 devices in a mesh: dp: 8 (over y, x, core), tensor: 4 (over z).
Axes of the slice: x: 2, y: 2, z: 4, core: 2. Of those that a mesh axis runs over, the one named last changes fastest.
Arguments:
- tokens: bfloat16 [24576, 1024], P('dp'), may hold values from -6 to 6
- masked_rows: int32 [24, 153], P('dp'), may hold values from 0 to 1023, as said below
- cotangent: bfloat16 [24, 153, 1024], P('dp'), may hold values from -6 to 6
- norm_gains: float32 [2, 1024], replicated, may hold values from 0.5 to 1.5
- gain_first: float32 [2, 1024], replicated
- gain_second: float32 [2, 1024], replicated, as said below
- owners: int32 [4, 32], P('tensor'), may hold values from 0 to 7, as said below
- master: float32 [4, 64, 128, 1024], P('tensor', 'dp')
- first_moment: float32 [4, 64, 128, 1024], P('tensor', 'dp')
- second_moment: float32 [4, 64, 128, 1024], P('tensor', 'dp'), as said below
Outputs:
- layer_out: bfloat16 [24576, 1024], P('dp')
- input_grad: bfloat16 [24576, 1024], P(('dp', 'tensor'))
- weight_grad: float32 [4, 64, 128, 1024], P('tensor', 'dp')
- weight_first: float32 [4, 64, 128, 1024], P('tensor', 'dp')
- weight_second: float32 [4, 64, 128, 1024], P('tensor', 'dp')
- weight_master: float32 [4, 64, 128, 1024], P('tensor', 'dp')
- weight_low: bfloat16 [4, 64, 128, 1024], P('tensor', 'dp')
- gain_grad: float32 [2, 1024], replicated
- gain_moment: float32 [2, 1024], replicated
- gain_new: float32 [2, 1024], replicated
Inputs may be any that keep to these rules, and one draw needn't show every extreme that they name: `masked_rows`: within a window the 153 row numbers are distinct. `owners`: each owner holds at most 8 tiles of one tensor index, and in every row some owner holds exactly 8. `second_moment`: Positive. `gain_second`: Positive.
All inputs are finite; a program needn't handle non-finite values.
Results may differ from a plain program's by a relative error of at most 0.014.
Values may be sent and summed in bfloat16 or wider, within the bound.
A program may use at most 320 MiB of HBM per device.

v0:
```python
import jax
import jax.numpy as jnp
from jax import lax
from jax.sharding import PartitionSpec as P

HEADS = 16
HD = 64
FF = 4096
STEP = 5


norm_eps = 1e-06
beta_one = 0.9
beta_two = 0.95
adam_eps = 1e-08
weight_rate = 0.05
gain_rate = 0.8
weight_decay = 0.1


def rotary_tables(length, head_size):
    half_size = head_size // 2
    frequency = jnp.exp(
        -jnp.log(10000.0) * (2.0 * jnp.arange(half_size, dtype=jnp.float32) / head_size)
    )
    angles = jnp.arange(length, dtype=jnp.float32)[:, None] * frequency[None, :]
    return (jnp.cos(angles), jnp.sin(angles))


def rotate(values, cosine_table, sine_table):
    front_half, back_half = jnp.split(values, 2, axis=-1)
    return jnp.concatenate(
        [
            front_half * cosine_table - back_half * sine_table,
            back_half * cosine_table + front_half * sine_table,
        ],
        axis=-1,
    )


def unrotate(values, cosine_table, sine_table):
    front_half, back_half = jnp.split(values, 2, axis=-1)
    return jnp.concatenate(
        [
            front_half * cosine_table + back_half * sine_table,
            back_half * cosine_table - front_half * sine_table,
        ],
        axis=-1,
    )


def rms_scale(values):
    return lax.rsqrt(jnp.mean(values * values, axis=-1, keepdims=True) + norm_eps)


def slot_ranks(owner_row):
    count_all = owner_row.shape[0]
    tile_order = jnp.arange(count_all, dtype=jnp.int32)
    earlier = (owner_row[:, None] == owner_row[None, :]) & (
        tile_order[None, :] < tile_order[:, None]
    )
    return jnp.sum(earlier.astype(jnp.int32), axis=1)


def unpack(weight_tiles, model_width, attn_local, ffn_local):
    flat_weights = weight_tiles.reshape(-1)
    attn_size = model_width * attn_local
    ffn_size = model_width * ffn_local
    w_query = flat_weights[0:attn_size].reshape(model_width, attn_local)
    w_key = flat_weights[attn_size : 2 * attn_size].reshape(model_width, attn_local)
    w_value = flat_weights[2 * attn_size : 3 * attn_size].reshape(model_width, attn_local)
    w_out = flat_weights[3 * attn_size : 4 * attn_size].reshape(attn_local, model_width)
    base_point = 4 * attn_size
    w_gate = flat_weights[base_point : base_point + ffn_size].reshape(model_width, ffn_local)
    w_up = flat_weights[base_point + ffn_size : base_point + 2 * ffn_size].reshape(
        model_width, ffn_local
    )
    w_down = flat_weights[base_point + 2 * ffn_size : base_point + 3 * ffn_size].reshape(
        ffn_local, model_width
    )
    return (w_query, w_key, w_value, w_out, w_gate, w_up, w_down)


def pack(matrices, tile_rows, model_width):
    return jnp.concatenate([matrix.reshape(-1) for matrix in matrices]).reshape(
        -1, tile_rows, model_width
    )


def norm_back(d_hidden, normed, row_scale, gain_row, carried):
    d_norm = d_hidden * gain_row
    inner_mean = jnp.mean(d_norm * normed, axis=-1, keepdims=True)
    return (
        carried + row_scale * (d_norm - normed * inner_mean),
        jnp.sum(d_hidden * normed, axis=0),
    )


def adam_update(grad_now, first_old, second_old, param_old, rate, decay):
    first_new = beta_one * first_old + (1.0 - beta_one) * grad_now
    second_new = beta_two * second_old + (1.0 - beta_two) * grad_now * grad_now
    first_hat = first_new / (1.0 - beta_one**STEP)
    second_hat = second_new / (1.0 - beta_two**STEP)
    param_new = param_old - rate * (
        first_hat / (jnp.sqrt(second_hat) + adam_eps) + decay * param_old
    )
    return (first_new, second_new, param_new)


def on_device(
    tokens,
    masked_rows,
    cotangent,
    norm_gains,
    gain_first,
    gain_second,
    owners,
    master,
    first_moment,
    second_moment,
):
    seq_count, mask_count = masked_rows.shape
    total_rows, model_width = tokens.shape
    window = total_rows // seq_count
    tensor_size = lax.axis_size("tensor")
    owner_count = lax.axis_size("dp")
    heads_local = HEADS // tensor_size
    attn_local = heads_local * HD
    ffn_local = FF // tensor_size
    capacity = master.shape[1]
    tile_rows = master.shape[2]
    owner_row = owners[0]
    owner_self = lax.axis_index("dp")
    slot_rank = slot_ranks(owner_row)
    slot_index = owner_row * capacity + slot_rank
    slot_match = (owner_row[None, :] == owner_self) & (
        slot_rank[None, :] == jnp.arange(capacity, dtype=jnp.int32)[:, None]
    )
    slot_used = jnp.any(slot_match, axis=1)[:, None, None]
    share_rows = total_rows // tensor_size
    share_start = lax.axis_index("tensor") * share_rows
    every_slot = lax.all_gather(master[0].astype(jnp.bfloat16), "dp", axis=0, tiled=True)
    w_query, w_key, w_value, w_out, w_gate, w_up, w_down = unpack(
        every_slot[slot_index], model_width, attn_local, ffn_local
    )
    score_scale = HD ** (-0.5)
    cosine_table, sine_table = rotary_tables(window, HD)
    cosine_full = cosine_table[None, :, None, :]
    sine_full = sine_table[None, :, None, :]
    quad_shape = (seq_count, window, heads_local, HD)
    inputs_f = tokens.astype(jnp.float32)
    scale_a = rms_scale(inputs_f)
    normed_a = inputs_f * scale_a
    hidden_a = (normed_a * norm_gains[0]).astype(jnp.bfloat16)
    proj_query = jnp.dot(hidden_a, w_query, preferred_element_type=jnp.float32).reshape(quad_shape)
    proj_key = jnp.dot(hidden_a, w_key, preferred_element_type=jnp.float32).reshape(quad_shape)
    proj_value = jnp.dot(hidden_a, w_value, preferred_element_type=jnp.float32).reshape(quad_shape)
    rot_query = rotate(proj_query, cosine_full, sine_full).astype(jnp.bfloat16)
    rot_key = rotate(proj_key, cosine_full, sine_full).astype(jnp.bfloat16)
    values_low = proj_value.astype(jnp.bfloat16)
    scores = (
        jnp.einsum("swhd,sthd->shwt", rot_query, rot_key, preferred_element_type=jnp.float32)
        * score_scale
    )
    attention = jax.nn.softmax(scores, axis=-1)
    mixed = jnp.einsum(
        "shwt,sthd->swhd",
        attention.astype(jnp.bfloat16),
        values_low,
        preferred_element_type=jnp.float32,
    )
    mixed = mixed.astype(jnp.bfloat16).reshape(total_rows, attn_local)
    attn_part = jnp.dot(mixed, w_out, preferred_element_type=jnp.float32)
    attn_branch = lax.psum(attn_part, "tensor")
    resid = inputs_f + attn_branch
    scale_f = rms_scale(resid)
    normed_f = resid * scale_f
    hidden_f = (normed_f * norm_gains[1]).astype(jnp.bfloat16)
    gate_pre = jnp.dot(hidden_f, w_gate, preferred_element_type=jnp.float32)
    up_pre = jnp.dot(hidden_f, w_up, preferred_element_type=jnp.float32)
    activated = (jax.nn.silu(gate_pre) * up_pre).astype(jnp.bfloat16)
    ffn_part = jnp.dot(activated, w_down, preferred_element_type=jnp.float32)
    ffn_branch = lax.psum(ffn_part, "tensor")
    layer_out = (resid + ffn_branch).astype(jnp.bfloat16)
    seq_pick = jnp.arange(seq_count, dtype=jnp.int32)[:, None]
    flat_rows = (masked_rows + seq_pick * window).reshape(-1)
    grad_out = cotangent.reshape(-1, model_width)
    grad_f = grad_out.astype(jnp.float32)
    act_masked = activated[flat_rows]
    gate_masked = gate_pre[flat_rows]
    up_masked = up_pre[flat_rows]
    hid_f_masked = hidden_f[flat_rows]
    g_down = jnp.einsum("rf,rd->fd", act_masked, grad_out, preferred_element_type=jnp.float32)
    d_act = jnp.einsum("rd,fd->rf", grad_out, w_down, preferred_element_type=jnp.float32)
    sigmoid_gate = jax.nn.sigmoid(gate_masked)
    d_gate = (d_act * up_masked * sigmoid_gate * (1.0 + gate_masked * (1.0 - sigmoid_gate))).astype(
        jnp.bfloat16
    )
    d_up = (d_act * gate_masked * sigmoid_gate).astype(jnp.bfloat16)
    g_gate = jnp.einsum("rd,rf->df", hid_f_masked, d_gate, preferred_element_type=jnp.float32)
    g_up = jnp.einsum("rd,rf->df", hid_f_masked, d_up, preferred_element_type=jnp.float32)
    d_hid_part = jnp.einsum("rf,df->rd", d_gate, w_gate, preferred_element_type=jnp.float32)
    d_hid_part = d_hid_part + jnp.einsum(
        "rf,df->rd", d_up, w_up, preferred_element_type=jnp.float32
    )
    d_hid_f = lax.psum(d_hid_part, "tensor")
    d_resid_masked, gain_grad_ffn = norm_back(
        d_hid_f, normed_f[flat_rows], scale_f[flat_rows], norm_gains[1], grad_f
    )
    d_resid_low = d_resid_masked.astype(jnp.bfloat16)
    g_out = jnp.einsum(
        "rh,rd->hd", mixed[flat_rows], d_resid_low, preferred_element_type=jnp.float32
    )
    d_mixed = jnp.einsum(
        "rd,hd->rh", d_resid_low, w_out, preferred_element_type=jnp.float32
    ).astype(jnp.bfloat16)
    d_mixed = d_mixed.reshape(seq_count, mask_count, heads_local, HD)
    attn_masked = attention[seq_pick, :, masked_rows]
    query_masked = rot_query[seq_pick, masked_rows]
    d_attn = jnp.einsum("sqhd,sthd->sqht", d_mixed, values_low, preferred_element_type=jnp.float32)
    d_scores = attn_masked * (d_attn - jnp.sum(d_attn * attn_masked, axis=-1, keepdims=True))
    d_scores_low = (d_scores * score_scale).astype(jnp.bfloat16)
    d_rot_query = jnp.einsum(
        "sqht,sthd->sqhd", d_scores_low, rot_key, preferred_element_type=jnp.float32
    )
    d_rot_key = jnp.einsum(
        "sqht,sqhd->sthd", d_scores_low, query_masked, preferred_element_type=jnp.float32
    )
    d_value = jnp.einsum(
        "sqht,sqhd->sthd",
        attn_masked.astype(jnp.bfloat16),
        d_mixed,
        preferred_element_type=jnp.float32,
    )
    d_value = d_value.astype(jnp.bfloat16).reshape(total_rows, attn_local)
    cosine_masked = cosine_table[masked_rows][:, :, None, :]
    sine_masked = sine_table[masked_rows][:, :, None, :]
    d_query = (
        unrotate(d_rot_query, cosine_masked, sine_masked)
        .astype(jnp.bfloat16)
        .reshape(-1, attn_local)
    )
    d_key = (
        unrotate(d_rot_key, cosine_full, sine_full)
        .astype(jnp.bfloat16)
        .reshape(total_rows, attn_local)
    )
    g_query = jnp.einsum(
        "rd,rh->dh", hidden_a[flat_rows], d_query, preferred_element_type=jnp.float32
    )
    g_key = jnp.einsum("rd,rh->dh", hidden_a, d_key, preferred_element_type=jnp.float32)
    g_value = jnp.einsum("rd,rh->dh", hidden_a, d_value, preferred_element_type=jnp.float32)
    d_hid_a = jnp.einsum("rh,dh->rd", d_key, w_key, preferred_element_type=jnp.float32)
    d_hid_a = d_hid_a + jnp.einsum(
        "rh,dh->rd", d_value, w_value, preferred_element_type=jnp.float32
    )
    d_hid_a = d_hid_a.at[flat_rows].add(
        jnp.einsum("rh,dh->rd", d_query, w_query, preferred_element_type=jnp.float32)
    )
    d_resid_full = (
        jnp.zeros((total_rows, model_width), jnp.float32).at[flat_rows].set(d_resid_masked)
    )
    d_hid_all = lax.psum(d_hid_a, "tensor")
    d_tokens, gain_grad_attn = norm_back(d_hid_all, normed_a, scale_a, norm_gains[0], d_resid_full)
    input_grad = lax.dynamic_slice_in_dim(d_tokens, share_start, share_rows, 0).astype(jnp.bfloat16)
    gain_pair = lax.psum((gain_grad_attn, gain_grad_ffn), "dp")
    gain_grad = jnp.stack(gain_pair)
    grad_tiles = pack(
        [g_query, g_key, g_value, g_out, g_gate, g_up, g_down], tile_rows, model_width
    )
    padded = (
        jnp.zeros((owner_count * capacity, tile_rows, model_width), jnp.float32)
        .at[slot_index]
        .set(grad_tiles)
    )
    reduced = lax.psum_scatter(padded, "dp", scatter_dimension=0, tiled=True)
    first_new, second_new, param_new = adam_update(
        reduced, first_moment[0], second_moment[0], master[0], weight_rate, weight_decay
    )
    weight_grad = jnp.where(slot_used, reduced, 0.0)
    weight_first = jnp.where(slot_used, first_new, 0.0)
    weight_second = jnp.where(slot_used, second_new, 0.0)
    weight_master = jnp.where(slot_used, param_new, 0.0)
    weight_low = weight_master.astype(jnp.bfloat16)
    gain_first_new, gain_moment, gain_new = adam_update(
        gain_grad, gain_first, gain_second, norm_gains, gain_rate, 0.0
    )
    return (
        layer_out,
        input_grad,
        weight_grad[None],
        weight_first[None],
        weight_second[None],
        weight_master[None],
        weight_low[None],
        gain_grad,
        gain_moment,
        gain_new,
    )


def solution(mesh):
    return jax.shard_map(
        on_device,
        mesh=mesh,
        in_specs=(
            P("dp", None),
            P("dp", None),
            P("dp", None, None),
            P(),
            P(),
            P(),
            P("tensor", None),
            P("tensor", "dp", None, None),
            P("tensor", "dp", None, None),
            P("tensor", "dp", None, None),
        ),
        out_specs=(
            P("dp", None),
            P(("dp", "tensor"), None),
            P("tensor", "dp", None, None),
            P("tensor", "dp", None, None),
            P("tensor", "dp", None, None),
            P("tensor", "dp", None, None),
            P("tensor", "dp", None, None),
            P(),
            P(),
            P(),
        ),
        check_vma=False,
    )
```

profile of v0, /device:TPU:0, one launch (start us, length us, event | category | flops | bytes accessed | tf_op | source)
XLA Modules:
  0.0 1982.1 jit_solution(2534369675866932986)
XLA Ops:
  7.2 3.8 bitcast_convert_fusion
  12.6 4.1 fusion.10
  17.3 10.2 convert_multiply_fusion
  27.4 76.4 %all-gather.2.cloned.1.call-done = bf16[64,128,1024]{2,1,0:T(8,128)(2,1)} async-done(((bf16[8,128,1024]{2,1,0:T(8,128)(2,1)}), bf16[64,128,1024]{2,1,0:T(8,128)(2,1)}) %all-gather.2.cloned.1.call-update) | async-done | bytes 16777232 | tf_op jit(solution)/shard_map/all_gather | solution.py:142
  103.8 10.9 gather_fusion
  120.0 6.5 fusion.67
  131.1 4.8 convolution_convert_fusion
  138.5 23.7 %fusion.66 = (f32[3,4,1024]{2,1,0:T(4,128)S(1)}, f32[3,4,1024,1024]{2,3,1,0:T(8,128)}) fusion(bf16[3,1024,4,32]{1,3,2,0:T(8,128)(2,1)} %get-tuple-element.49, bf16[3,1024,4,32]{1,3,2,0:T(8,128)(2,1)} %get-tuple-element.50, bf16[3,1024,4,32]{1,3,2,0:T(8,128)(2,1)} %get-tuple-element.44, bf16[3,1024,4,32]{1,3,2,0:T(8,128)(2,1)S(1)} %get-tuple-element.43), kind=kOutput, calls=%fused_computation.156 | convolution fusion | flops 1654653952 | bytes 53526528 | tf_op jit(solution)/shard_map/sub | solution.py:165
  162.3 34.4 %broadcast_divide_fusion = f32[3,4,1024,1024]{2,3,1,0:T(8,128)} fusion(f32[3,4,1024,1024]{2,3,1,0:T(8,128)} %get-tuple-element.58, f32[3,4,1024]{2,1,0:T(4,128)S(1)} %get-tuple-element.57), kind=kLoop, calls=%fused_computation.24 | loop fusion | flops 12582912 | bytes 100712448 | tf_op jit(solution)/shard_map/div | solution.py:165
  196.7 17.0 fusion.36
  215.8 6.3 fusion.69
  229.9 7.0 gather_fusion.9
  237.0 59.4 %copy.113 = f32[3,4,1024,1024]{3,1,2,0:T(4,128)} copy(f32[3,4,1024,1024]{2,3,1,0:T(8,128)} %broadcast_divide_fusion) | data formatting | bytes 100663296 | tf_op jit(solution)/shard_map/div | solution.py:165
  297.0 16.3 gather_fusion.6
  313.3 7.0 convert_element_type.115
  324.0 7.9 gather_fusion.5
  334.5 6.0 fusion.63
  340.5 308.0 %all-reduce.6.cloned.1.call-done = f32[3072,1024]{1,0:T(8,128)} async-done(((f32[3072,1024]{1,0:T(8,128)}), f32[3072,1024]{1,0:T(8,128)}) %all-reduce.6.cloned.1.call-update) | async-done | bytes 12582928 | tf_op jit(solution)/shard_map/psum | solution.py:174
  648.4 8.1 multiply_reduce_fusion.3
  660.1 14.2 multiply_convert_fusion.1
  674.3 7.0 gather_fusion.11
  681.3 12.1 fusion.70
  693.5 8.1 gather_fusion.3
  701.6 16.2 multiply_convert_fusion
  717.8 8.3 gather_fusion.2
  726.1 3.9 fusion.29
  740.5 7.5 gather_fusion.4
  748.0 5.4 copy.141
  756.4 7.1 gather_fusion.12
  769.0 12.7 fusion.71
  781.7 37.6 %all-reduce.8.cloned.1.call-done = f32[459,1024]{1,0:T(8,128)} async-done(((f32[459,1024]{1,0:T(8,128)}), f32[459,1024]{1,0:T(8,128)}) %all-reduce.8.cloned.1.call-update) | async-done | bytes 1880080 | tf_op jit(solution)/shard_map/psum | solution.py:206
  824.7 4.3 fusion.73
  829.0 19.1 convolution_bitcast_fusion.8
  848.1 19.2 convolution_bitcast_fusion.3
  872.2 6.4 fusion.74
  886.0 4.7 fusion.39
  895.2 6.4 convolution_add_fusion
  907.4 14.2 scatter_fusion
  937.8 18.2 reshape.423
  956.0 11.3 broadcast_in_dim.42
  967.3 30.4 %scatter_fusion.1 = f32[64,128,1024]{2,1,0:T(8,128)} fusion(f32[64,128,1024]{2,1,0:T(8,128)} %broadcast_in_dim.42, s32[32]{0:T(128)S(1)} %copy-done.55, f32[32,128,1024]{2,1,0:T(8,128)} %reshape.423), kind=kCustom, calls=%fused_computation.15 | custom fusion | bytes 50331776 | tf_op jit(solution)/shard_map/scatter | solution.py:274
  998.7 7.5 scatter_custom_fusion
  1006.1 748.9 %all-reduce.10.cloned.1.call-done = (f32[3072,1024]{1,0:T(8,128)}, f32[3072,1024]{1,0:T(8,128)}) async-done(((f32[3072,1024]{1,0:T(8,128)}, f32[3072,1024]{1,0:T(8,128)}), (f32[3072,1024]{1,0:T(8,128)}, f32[3072,1024]{1,0:T(8,128)})) %all-reduce.10.cloned.1.call-update) | async-done | bytes 25165840 | tf_op jit(solution)/shard_map/psum | solution.py:183
  1755.0 26.3 %multiply_reduce_fusion.1 = (f32[1024]{0:T(1024)S(1)}, f32[3072]{0:T(1024)S(1)}, f32[3072,1024]{1,0:T(8,128)}, bf16[3072,1024]{1,0:T(8,128)(2,1)}) fusion(f32[3072,1024]{1,0:T(8,128)} %get-tuple-element.17, bf16[3072,1024]{1,0:T(8,128)(2,1)} %param.10, f32[3072]{0:T(1024)S(1)} %copy-done.43, f32[1024]{0:T(1024)S(1)} %bitcast.260, ...), kind=kLoop, calls=%fused_computation.30 | loop fusion | flops 31453184 | bytes 62947328 | tf_op jit(solution)/shard_map/reduce_sum | solution.py:95
  1781.3 13.8 all-reduce
  1795.8 7.2 fusion.23
  1803.0 159.6 %reduce-scatter.2.cloned.1.call-done = f32[8,128,1024]{2,1,0:T(8,128)} async-done(((f32[64,128,1024]{2,1,0:T(8,128)}), f32[8,128,1024]{2,1,0:T(8,128)}) %reduce-scatter.2.cloned.1.call-update) | async-done | bytes 4194320 | tf_op jit(solution)/shard_map/reduce_scatter | solution.py:276
  1962.6 12.8 convert_bitcast_fusion
  (241 shorter events, 99.1 us)
Async XLA Ops:
  7.2 4.0 copy-start.56
  7.2 4.8 copy-start.47
  7.2 96.6 %all-gather.2.cloned.1.call-start = ((), (), s32[]{:S(2)}) async-start(), calls=%async_computation.1 | async-start | bytes 18874368 | tf_op jit(solution)/shard_map/all_gather | solution.py:142
  11.1 637.3 %all-reduce.6.cloned.1.call-start = ((), (), s32[]{:S(2)}) async-start(), calls=%async_computation.2 | async-start | bytes 25165824 | tf_op jit(solution)/shard_map/psum | solution.py:174
  12.6 4.7 copy-start.45
  17.2 205.0 %copy-start.25 = (f32[1024,32]{0,1:T(8,128)}, f32[1024,32]{0,1:T(8,128)S(1)}, u32[]{:S(2)}) copy-start(f32[1024,32]{0,1:T(8,128)S(1)} %get-tuple-element.55) | copy-start | bytes 393220
  17.2 205.2 %copy-start.27 = (f32[1024,32]{0,1:T(8,128)}, f32[1024,32]{0,1:T(8,128)S(1)}, u32[]{:S(2)}) copy-start(f32[1024,32]{0,1:T(8,128)S(1)} %get-tuple-element.56) | copy-start | bytes 393220
  117.3 98.5 %copy-start.14 = (bf16[2,128,1024]{2,1,0:T(8,128)(2,1)}, bf16[2,128,1024]{2,1,0:T(8,128)(2,1)S(1)}, u32[]{:S(2)}) copy-start(bf16[2,128,1024]{2,1,0:T(8,128)(2,1)S(1)} %get-tuple-element.31) | copy-start | bytes 1572868
  118.9 7.5 copy-start.10
  119.0 7.5 slice-start.3
  120.0 6.5 slice-start.4
  120.0 6.5 copy-start.39
  131.1 4.8 copy-start.23
  131.1 4.8 copy-start.24
  135.9 60.8 %copy-start = (bf16[3,1024,4,64]{1,3,2,0:T(8,128)(2,1)}, bf16[3,1024,4,64]{1,3,2,0:T(8,128)(2,1)S(1)}, u32[]{:S(2)}) copy-start(bf16[3,1024,4,64]{1,3,2,0:T(8,128)(2,1)S(1)} %convolution_convert_fusion) | copy-start | bytes 4718596
  138.5 23.8 %copy-start.20 = (bf16[3,1024,4,32]{1,3,2,0:T(8,128)(2,1)}, bf16[3,1024,4,32]{1,3,2,0:T(8,128)(2,1)S(1)}, u32[]{:S(2)}) copy-start(bf16[3,1024,4,32]{1,3,2,0:T(8,128)(2,1)S(1)} %get-tuple-element.43) | copy-start | bytes 2359300
  222.2 597.2 %all-reduce.8.cloned.1.call-start = ((), (), s32[]{:S(2)}) async-start(), calls=%async_computation.3 | async-start | bytes 3801088 | tf_op jit(solution)/shard_map/psum | solution.py:206
  229.9 7.1 copy-start.49
  313.3 7.0 copy-start.21
  313.3 7.0 copy-start.22
  340.5 385.6 %copy-start.29 = (bf16[8,128,1024]{2,1,0:T(8,128)(2,1)}, bf16[8,128,1024]{2,1,0:T(8,128)(2,1)S(1)}, u32[]{:S(2)}) copy-start(bf16[8,128,1024]{2,1,0:T(8,128)(2,1)S(1)} %get-tuple-element.28) | copy-start | bytes 6291460
  340.5 319.6 %copy-start.44 = (f32[1,1024]{1,0:T(1,128)S(1)}, f32[1,1024]{1,0:T(1,128)}, u32[]{:S(2)}) copy-start(f32[1,1024]{1,0:T(1,128)} %get-tuple-element.52) | copy-start | bytes 12292
  717.8 8.4 copy-start.17
  726.1 4.0 copy-start.32
  740.4 1014.5 %all-reduce.10.cloned.1.call-start = ((), (), s32[]{:S(2)}) async-start(), calls=%async_computation.5 | async-start | bytes 50331648 | tf_op jit(solution)/shard_map/psum | solution.py:183
  747.9 5.4 copy-start.16
  829.0 19.1 copy-start.34
  848.1 19.2 copy-start.26
  848.1 19.2 copy-start.28
  869.9 8.8 slice-start.5
  872.2 6.5 slice-start.6
  878.7 5.6 copy-start.13
  881.5 11.3 slice-start.7
  886.0 6.8 slice-start.8
  886.0 9.1 slice-start
  890.7 4.5 slice-start.1
  895.2 6.4 copy-start.19
  902.1 3.7 copy-start.3
  902.1 3.7 copy-start.37
  921.7 1040.9 %reduce-scatter.2.cloned.1.call-start = ((), (), s32[]{:S(2)}) async-start(), calls=%async_computation.4 | async-start | bytes 37748736 | tf_op jit(solution)/shard_map/reduce_scatter | solution.py:276
  921.7 6.5 copy-start.5
  928.2 3.7 copy-start.4
  931.9 3.7 copy-start.6
  956.0 11.3 copy-start.55
  998.6 756.3 %copy-start.46 = (f32[1,1024]{1,0:T(1,128)S(1)}, f32[1,1024]{1,0:T(1,128)}, u32[]{:S(2)}) copy-start(f32[1,1024]{1,0:T(1,128)} %copy-done.45) | copy-start | bytes 12292
  1755.0 40.1 %copy-start.48 = (f32[2,1024]{1,0:T(2,128)S(1)}, f32[2,1024]{1,0:T(2,128)}, u32[]{:S(2)}) copy-start(f32[2,1024]{1,0:T(2,128)} %param.13) | copy-start | bytes 24580
  1755.0 40.1 %copy-start.52 = (f32[2,1024]{1,0:T(2,128)S(1)}, f32[2,1024]{1,0:T(2,128)}, u32[]{:S(2)}) copy-start(f32[2,1024]{1,0:T(2,128)} %param.14) | copy-start | bytes 24580
  1755.0 40.2 %copy-start.53 = (f32[2,1024]{1,0:T(2,128)S(1)}, f32[2,1024]{1,0:T(2,128)}, u32[]{:S(2)}) copy-start(f32[2,1024]{1,0:T(2,128)} %param.15) | copy-start | bytes 24580
  (26 other events, 49.3 us)
Sparse Core Ops, SparseCore 0:
  11.2 92.5 all-gather.1
  222.3 426.0 all-reduce.5
  740.5 78.7 all-reduce.7
  921.8 833.1 all-reduce.9
  1758.4 204.1 reduce-scatter.1
where the time goes:
time: 1990 us; the launch traced here: 1980 us
  waiting for transfers between devices  1330 us (67%)
  local copies, waits for them, and re-layouts  283 us (14%)
  matrix products  188 us (9%)
  other arithmetic  152 us (8%)
    psum x1, waiting for transfers between devices, on_device(): ffn_branch = lax.psum(ffn_part, 'tensor')  749 us
    psum x1, waiting for transfers between devices, on_device(): attn_branch = lax.psum(attn_part, 'tensor')  308 us
    reduce_scatter x1, waiting for transfers between devices, on_device(): reduced = lax.psum_scatter(padded, 'dp', scatter_dimension=0, tiled=True)  160 us
    all_gather x1, waiting for transfers between devices, on_device(): lax.all_gather(master[0].astype(jnp.bfloat16), 'dp', axis=0, tiled=True)  76.4 us
    div x1, local copies, waits for them, and re-layouts, on_device(): attention = jax.nn.softmax(scores, axis=-1)  59.4 us
  transfers between devices with their start and end apart: 5, of which 5 were waited for; matrix products, arithmetic and copies ran while one was open for 15% of the time, Pallas kernels for 0%

commit v1 on v0

v1 whole, which is shorter than its diff:
```python
import functools

import jax
import jax.numpy as jnp
from jax import lax
from jax.experimental import pallas as pl
from jax.experimental.pallas import tpu as pltpu
from jax.sharding import PartitionSpec as P

HEADS = 16
HD = 64
FF = 4096
STEP = 5

norm_eps = 1e-06
beta_one = 0.9
beta_two = 0.95
adam_eps = 1e-08
weight_rate = 0.05
gain_rate = 0.8
weight_decay = 0.1

score_scale = HD ** (-0.5)
f32 = jnp.float32
bf16 = jnp.bfloat16
VMEM_LIMIT = 60 * 1024 * 1024
NT = (((1,), (1,)), ((), ()))
TN = (((0,), (0,)), ((), ()))


def mm(left, right):
    return jnp.dot(left, right, preferred_element_type=f32)


def mm_nt(left, right):
    return lax.dot_general(left, right, NT, preferred_element_type=f32)


def mm_tn(left, right):
    return lax.dot_general(left, right, TN, preferred_element_type=f32)


def params(**kw):
    return pltpu.CompilerParams(vmem_limit_bytes=VMEM_LIMIT, **kw)


def cost(flops, nbytes, transcendentals=0):
    return pl.CostEstimate(
        flops=int(flops), bytes_accessed=int(nbytes), transcendentals=int(transcendentals)
    )


def whole_spec(shape):
    return pl.BlockSpec(shape, lambda *_: (0,) * len(shape))


def rms_scale(values):
    return lax.rsqrt(jnp.mean(values * values, axis=-1, keepdims=True) + norm_eps)


def swap_halves(values):
    width = values.shape[1]
    lane = lax.broadcasted_iota(jnp.int32, values.shape, 1)
    return jnp.where(
        lane % HD < HD // 2,
        pltpu.roll(values, width - HD // 2, 1),
        pltpu.roll(values, HD // 2, 1),
    )


def qkv_kernel(x_ref, gains_ref, w_ref, cos_ref, sin_ref, q_ref, k_ref, v_ref):
    width = q_ref.shape[1]
    x = x_ref[...].astype(f32)
    hidden = (x * rms_scale(x) * gains_ref[0:1, :]).astype(bf16)
    cos, sin = cos_ref[...], sin_ref[...]
    q = mm(hidden, w_ref[:, 0:width])
    q_ref[...] = (q * cos + swap_halves(q) * sin).astype(bf16)
    k = mm(hidden, w_ref[:, width : 2 * width])
    k_ref[...] = (k * cos + swap_halves(k) * sin).astype(bf16)
    v_ref[...] = mm(hidden, w_ref[:, 2 * width : 3 * width]).astype(bf16)


def attend(q, k, v):
    first = lax.broadcasted_iota(jnp.int32, q.shape, 1) < HD
    first_v = lax.broadcasted_iota(jnp.int32, v.shape, 1) < HD
    zero, one = jnp.zeros((), bf16), jnp.ones((), bf16)
    outs = []
    for head in range(2):
        q_head = jnp.where(first if head == 0 else ~first, q, zero)
        v_head = jnp.where(first_v if head == 0 else ~first_v, v, one)
        s = mm_nt(q_head, k)
        s = (s - jnp.max(s, axis=-1, keepdims=True)) * score_scale
        outs.append(mm(jnp.exp(s).astype(bf16), v_head))
    value = jnp.where(first, outs[0], outs[1])
    total = pltpu.roll(jnp.where(first, outs[1], outs[0]), HD, 1)
    return (value / total).astype(bf16)


def attend_kernel(q_ref, k_ref, v_ref, o_ref):
    o_ref[...] = attend(q_ref[...], k_ref[...], v_ref[...])


def attend_masked_kernel(rows_ref, x_ref, q_ref, k_ref, v_ref, o_ref, qm_ref, xm_ref):
    window = x_ref.shape[0]
    count = rows_ref.shape[1]
    pick = (
        lax.broadcasted_iota(jnp.int32, (count, window), 1) == rows_ref[0]
    ).astype(bf16)
    xm_ref[...] = mm(pick, x_ref[...]).astype(bf16)
    qm = mm(pick, q_ref[...]).astype(bf16)
    qm_ref[...] = qm
    for pair in range(q_ref.shape[1] // 128):
        lanes = slice(pair * 128, pair * 128 + 128)
        o_ref[:, lanes] = attend(qm[:, lanes], k_ref[:, lanes], v_ref[:, lanes])


def ffn_masked_kernel(
    parts, xm_ref, cot_ref, gains_ref, wg_ref, wu_ref, wd_ref, *refs
):
    o_refs, wo_refs = refs[:parts], refs[parts : 2 * parts]
    rm_ref, dhf_ref, gg_ref, gu_ref, gd_ref, hf_ref, acc_ref = refs[2 * parts :]
    step = pl.program_id(0)

    @pl.when(step == 0)
    def _():
        r = xm_ref[...].astype(f32)
        for o_ref, wo_ref in zip(o_refs, wo_refs):
            r = r + mm(o_ref[...], wo_ref[...])
        rm_ref[...] = r
        hf_ref[...] = (r * rms_scale(r) * gains_ref[1:2, :]).astype(bf16)
        acc_ref[...] = jnp.zeros_like(acc_ref)

    hf, dy = hf_ref[...], cot_ref[...]
    wg, wu, wd = wg_ref[...], wu_ref[...], wd_ref[...]
    g, u = mm(hf, wg), mm(hf, wu)
    sig = jax.nn.sigmoid(g)
    act = (g * sig * u).astype(bf16)
    gd_ref[...] = mm_tn(act, dy).astype(bf16)
    da = mm_nt(dy, wd)
    dg = (da * u * sig * (1.0 + g * (1.0 - sig))).astype(bf16)
    du = (da * g * sig).astype(bf16)
    gg_ref[...] = mm_tn(hf, dg).astype(bf16)
    gu_ref[...] = mm_tn(hf, du).astype(bf16)
    acc_ref[...] += mm_nt(dg, wg) + mm_nt(du, wu)

    @pl.when(step == pl.num_programs(0) - 1)
    def _():
        dhf_ref[...] = acc_ref[...].astype(bf16)


def ffn_kernel(parts, place_ref, x_ref, gains_ref, wg_ref, wu_ref, wd_ref, *refs):
    o_refs, wo_refs = refs[:parts], refs[parts : 2 * parts]
    part_ref, own_ref, r_ref, hf_ref, acc_ref = refs[2 * parts :]
    step = pl.program_id(0)

    @pl.when(step == 0)
    def _():
        r = x_ref[...].astype(f32)
        for o_ref, wo_ref in zip(o_refs, wo_refs):
            r = r + mm(o_ref[...], wo_ref[...])
        r_ref[...] = r
        hf_ref[...] = (r * rms_scale(r) * gains_ref[1:2, :]).astype(bf16)
        acc_ref[...] = jnp.zeros_like(acc_ref)

    hf = hf_ref[...]
    g, u = mm(hf, wg_ref[...]), mm(hf, wu_ref[...])
    act = (g * jax.nn.sigmoid(g) * u).astype(bf16)
    acc_ref[...] += mm(act, wd_ref[...])

    @pl.when(step == pl.num_programs(0) - 1)
    def _():
        part_ref[...] = acc_ref[...].astype(bf16)
        share = own_ref.shape[0]
        mine = pl.ds(pl.multiple_of(place_ref[0] * share, share), share)
        own_ref[...] = r_ref[mine, :] + acc_ref[mine, :]


def attn_back_kernel(
    rows_ref,
    dhf_ref,
    rm_ref,
    cot_ref,
    gains_ref,
    om_ref,
    qm_ref,
    cosm_ref,
    sinm_ref,
    k_ref,
    v_ref,
    x_ref,
    cos_ref,
    sin_ref,
    wo_ref,
    w_ref,
    drm_ref,
    dha_ref,
    gw_ref,
    go_ref,
    gain_ref,
    gw_acc,
    go_acc,
    gain_acc,
    flow_ref,
):
    step = pl.program_id(0)

    @pl.when(step == 0)
    def _():
        gw_acc[...] = jnp.zeros_like(gw_acc)
        go_acc[...] = jnp.zeros_like(go_acc)
        gain_acc[...] = jnp.zeros_like(gain_acc)

    window, width = k_ref.shape
    count = rm_ref.shape[0]
    r = rm_ref[...]
    sf = rms_scale(r)
    nf = r * sf
    dhf = dhf_ref[...].astype(f32)
    dnf = dhf * gains_ref[1:2, :]
    dr = cot_ref[...].astype(f32) + sf * (
        dnf - nf * jnp.mean(dnf * nf, axis=-1, keepdims=True)
    )
    drm_ref[...] = dr
    gain_acc[1:2, :] += jnp.sum(dhf * nf, axis=0, keepdims=True)
    drb = dr.astype(bf16)
    go_acc[...] += mm_tn(om_ref[...], drb)
    dob = mm_nt(drb, wo_ref[...]).astype(bf16)

    first = lax.broadcasted_iota(jnp.int32, (count, 128), 1) < HD
    zero = jnp.zeros((), bf16)
    drq = []
    for pair in range(width // 128):
        lanes = slice(pair * 128, pair * 128 + 128)
        k, v = k_ref[:, lanes], v_ref[:, lanes]
        qm, do = qm_ref[:, lanes], dob[:, lanes]
        parts = []
        drk = dv = None
        for head in range(2):
            mine = first if head == 0 else ~first
            q_head = jnp.where(mine, qm, zero)
            do_head = jnp.where(mine, do, zero)
            s = mm_nt(k, q_head)
            s = jnp.exp((s - jnp.max(s, axis=0, keepdims=True)) * score_scale)
            att = s / jnp.sum(s, axis=0, keepdims=True)
            dpa = mm_nt(v, do_head)
            ds = att * (dpa - jnp.sum(dpa * att, axis=0, keepdims=True))
            ds = (ds * score_scale).astype(bf16)
            parts.append(mm_tn(ds, k))
            drk_head = mm(ds, q_head)
            dv_head = mm(att.astype(bf16), do_head)
            drk = drk_head if drk is None else drk + drk_head
            dv = dv_head if dv is None else dv + dv_head
        drq.append(jnp.where(first, parts[0], parts[1]))
        dk = drk * cos_ref[:, lanes] - swap_halves(drk) * sin_ref[:, lanes]
        flow_ref[:, width + pair * 128 : width + pair * 128 + 128] = dk.astype(bf16)
        flow_ref[:, 2 * width + pair * 128 : 2 * width + pair * 128 + 128] = dv.astype(
            bf16
        )
    spread = (
        lax.broadcasted_iota(jnp.int32, (window, count), 0) == rows_ref[0]
    ).astype(bf16)
    for pair in range(width // 128):
        lanes = slice(pair * 128, pair * 128 + 128)
        dq = drq[pair] * cosm_ref[:, lanes] - swap_halves(drq[pair]) * sinm_ref[:, lanes]
        flow_ref[:, lanes] = mm(spread, dq.astype(bf16)).astype(bf16)

    flow = flow_ref[...]
    x = x_ref[...].astype(f32)
    na = x * rms_scale(x)
    dha = mm_nt(flow, w_ref[...])
    gain_acc[0:1, :] += jnp.sum(dha * na, axis=0, keepdims=True)
    dha_ref[...] = dha.astype(bf16)
    gw_acc[...] += mm_tn((na * gains_ref[0:1, :]).astype(bf16), flow)

    @pl.when(step == pl.num_programs(0) - 1)
    def _():
        gw_ref[...] = gw_acc[...].astype(bf16)
        go_ref[...] = go_acc[...].astype(bf16)
        gain_ref[...] = gain_acc[...]


def input_grad_kernel(
    place_ref, rows_ref, drm_ref, gains_ref, x_ref, part_ref, up_ref, down_ref, out_ref
):
    block, count = x_ref.shape[0], drm_ref.shape[0]
    base = place_ref[0] * (pl.num_programs(0) * block) + pl.program_id(0) * block
    spread = (
        lax.broadcasted_iota(jnp.int32, (block, count), 0) + base == rows_ref[...]
    ).astype(bf16)
    dr = drm_ref[...]
    high = dr.astype(bf16)
    low = (dr - high.astype(f32)).astype(bf16)
    dr = mm(spread, high) + mm(spread, low)
    x = x_ref[...].astype(f32)
    sa = rms_scale(x)
    na = x * sa
    dha = part_ref[...].astype(f32) + up_ref[...].astype(f32) + down_ref[...].astype(f32)
    dna = dha * gains_ref[0:1, :]
    out = dr + sa * (dna - na * jnp.mean(dna * na, axis=-1, keepdims=True))
    out_ref[...] = out.astype(bf16)


def collect_kernel(slot_ref, first, slots_ref, out_ref, sems):
    count = out_ref.shape[0]

    def copy(index):
        return pltpu.make_async_copy(
            slots_ref.at[slot_ref[first + index]], out_ref.at[index], sems.at[index]
        )

    for index in range(count):
        copy(index).start()
    for index in range(count):
        copy(index).wait()


def exchange(value, axis, bit):
    size = lax.axis_size(axis)
    return lax.ppermute(value, axis, [(i, i ^ bit) for i in range(size)])


def dp_total(value):
    size = lax.axis_size("dp")
    value = value + exchange(value, "dp", 1)
    bits = []
    bit = 2
    while bit < size:
        bits.append(bit)
        bit *= 2
    core = lax.axis_index("dp") % 2
    half = value.shape[0] // 2
    mine = lax.dynamic_slice_in_dim(value, core * half, half, 0)
    cut = half // 2
    low, high = mine[:cut], mine[cut:]
    for bit_low, bit_high in zip(bits, bits[::-1]):
        low = low + exchange(low, "dp", bit_low)
        high = high + exchange(high, "dp", bit_high)
    mine = jnp.concatenate([low, high], axis=0)
    other = exchange(mine, "dp", 1)
    return jnp.where(
        core == 0,
        jnp.concatenate([mine, other], axis=0),
        jnp.concatenate([other, mine], axis=0),
    )


def around(value):
    size = lax.axis_size("tensor")
    return [value] + [
        lax.ppermute(value, "tensor", [(i, (i + k) % size) for i in range(size)])
        for k in range(1, size)
    ]


def chain_sums(value, share):
    size = lax.axis_size("tensor")
    place = lax.axis_index("tensor")
    up = down = None
    for step in range(size - 1):
        index = jnp.minimum(size - 1 - step + place, size - 1)
        send = lax.dynamic_slice_in_dim(value, index * share, share, 0)
        if up is not None:
            send = (send.astype(f32) + up.astype(f32)).astype(bf16)
        up = lax.ppermute(
            send, "tensor", [(i, i + 1) for i in range(min(step, size - 2) + 1)]
        )
        index = jnp.maximum(place - (size - 1 - step), 0)
        send = lax.dynamic_slice_in_dim(value, index * share, share, 0)
        if down is not None:
            send = (send.astype(f32) + down.astype(f32)).astype(bf16)
        down = lax.ppermute(
            send,
            "tensor",
            [(size - 1 - i, size - 2 - i) for i in range(min(step, size - 2) + 1)],
        )
    return up, down


def small_total(value):
    for axis in ("dp", "tensor"):
        bit = 1
        while bit < lax.axis_size(axis):
            value = value + exchange(value, axis, bit)
            bit *= 2
    return value


def slot_ranks(owner_row):
    count_all = owner_row.shape[0]
    tile_order = jnp.arange(count_all, dtype=jnp.int32)
    earlier = (owner_row[:, None] == owner_row[None, :]) & (
        tile_order[None, :] < tile_order[:, None]
    )
    return jnp.sum(earlier.astype(jnp.int32), axis=1)


def adam_update(grad_now, first_old, second_old, param_old, rate, decay):
    first_new = beta_one * first_old + (1.0 - beta_one) * grad_now
    second_new = beta_two * second_old + (1.0 - beta_two) * grad_now * grad_now
    first_hat = first_new / (1.0 - beta_one**STEP)
    second_hat = second_new / (1.0 - beta_two**STEP)
    param_new = param_old - rate * (
        first_hat / (jnp.sqrt(second_hat) + adam_eps) + decay * param_old
    )
    return (first_new, second_new, param_new)


def head_tables(positions, heads):
    frequency = jnp.exp(
        -jnp.log(10000.0) * (2.0 * jnp.arange(HD // 2, dtype=f32) / HD)
    )
    angles = positions.astype(f32)[..., None] * frequency
    cos, sin = jnp.cos(angles), jnp.sin(angles)
    cos = jnp.concatenate([cos, cos], axis=-1)
    sin = jnp.concatenate([-sin, sin], axis=-1)
    reps = (1,) * (cos.ndim - 1) + (heads,)
    return jnp.tile(cos, reps), jnp.tile(sin, reps)


def on_device(
    tokens,
    masked_rows,
    cotangent,
    norm_gains,
    gain_first,
    gain_second,
    owners,
    master,
    first_moment,
    second_moment,
):
    seq_count, mask_count = masked_rows.shape
    total_rows, model = tokens.shape
    window = total_rows // seq_count
    parts = lax.axis_size("tensor")
    place = lax.axis_index("tensor")
    owner_self = lax.axis_index("dp")
    heads = HEADS // parts
    width = heads * HD
    hidden = FF // parts
    capacity, tile_rows = master.shape[1:3]
    tile_size = tile_rows * model
    attn_tiles = 4 * model * width // tile_size
    ffn_tiles = 3 * model * hidden // tile_size
    count = -(-mask_count // 16) * 16
    place_ref = place.astype(jnp.int32).reshape(1)

    owner_row = owners[0]
    slot_rank = slot_ranks(owner_row)
    slot_index = owner_row * capacity + slot_rank
    slot_match = (owner_row[None, :] == owner_self) & (
        slot_rank[None, :] == jnp.arange(capacity, dtype=jnp.int32)[:, None]
    )
    slot_used = jnp.any(slot_match, axis=1)[:, None, None]
    slot_tile = jnp.argmax(slot_match, axis=1)

    low_slots = master[0].astype(bf16)
    held = (owner_row[:attn_tiles] == owner_self)[:, None, None]
    attn_mine = jnp.where(held, low_slots[slot_rank[:attn_tiles]], jnp.zeros((), bf16))
    attn_flat = dp_total(attn_mine).reshape(4, -1)
    w_qkv = jnp.concatenate(
        [attn_flat[i].reshape(model, width) for i in range(3)], axis=1
    )
    w_out = attn_flat[3].reshape(width, model)
    every_slot = lax.all_gather(low_slots, "dp", axis=0, tiled=True)
    ffn_all = pl.pallas_call(
        lambda slot_ref, slots_ref, out_ref, sems: collect_kernel(
            slot_ref, attn_tiles, slots_ref, out_ref, sems
        ),
        out_shape=jax.ShapeDtypeStruct((ffn_tiles, tile_rows, model), bf16),
        grid_spec=pltpu.PrefetchScalarGridSpec(
            num_scalar_prefetch=1,
            grid=(1,),
            in_specs=[pl.BlockSpec(memory_space=pl.ANY)],
            out_specs=pl.BlockSpec(memory_space=pl.ANY),
            scratch_shapes=[pltpu.SemaphoreType.DMA((ffn_tiles,))],
        ),
        compiler_params=params(),
        cost_estimate=cost(0, 2 * ffn_tiles * tile_size * 2),
        name="collect",
    )(slot_index, every_slot)
    ffn_flat = ffn_all.reshape(3, -1)
    w_gate = ffn_flat[0].reshape(model, hidden)
    w_up = ffn_flat[1].reshape(model, hidden)
    w_down = ffn_flat[2].reshape(hidden, model)
    w_outs = around(w_out)

    cos, sin = head_tables(jnp.arange(window), heads)
    rows = jnp.pad(masked_rows, ((0, 0), (0, count - mask_count)), constant_values=-1)
    cos_m, sin_m = head_tables(rows, heads)
    cot = jnp.pad(cotangent, ((0, 0), (0, count - mask_count), (0, 0)))
    cot = cot.reshape(seq_count * count, model)
    cos_m = cos_m.reshape(seq_count * count, width)
    sin_m = sin_m.reshape(seq_count * count, width)

    block = min(512, window)
    per_window = window // block
    row_block = pl.BlockSpec((block, model), lambda i: (i, 0))
    head_block = pl.BlockSpec((block, width), lambda i: (i, 0))
    table_block = pl.BlockSpec((block, width), lambda i: (i % per_window, 0))
    q, k, v = pl.pallas_call(
        qkv_kernel,
        out_shape=[jax.ShapeDtypeStruct((total_rows, width), bf16)] * 3,
        grid=(total_rows // block,),
        in_specs=[
            row_block,
            whole_spec((2, model)),
            whole_spec((model, 3 * width)),
            table_block,
            table_block,
        ],
        out_specs=[head_block] * 3,
        compiler_params=params(),
        cost_estimate=cost(6 * total_rows * model * width, 2 * total_rows * model * 2),
        name="qkv",
    )(tokens, norm_gains, w_qkv, cos, sin)

    win_model = pl.BlockSpec((window, model), lambda i: (i, 0))
    win_head = pl.BlockSpec((window, width), lambda i: (i, 0))
    mask_model = pl.BlockSpec((count, model), lambda i: (i, 0))
    mask_head = pl.BlockSpec((count, width), lambda i: (i, 0))
    o_m, q_m, x_m = pl.pallas_call(
        attend_masked_kernel,
        out_shape=[
            jax.ShapeDtypeStruct((seq_count * count, width), bf16),
            jax.ShapeDtypeStruct((seq_count * count, width), bf16),
            jax.ShapeDtypeStruct((seq_count * count, model), bf16),
        ],
        grid=(seq_count,),
        in_specs=[
            pl.BlockSpec((1, count, 1), lambda i: (i, 0, 0)),
            win_model,
            win_head,
            win_head,
            win_head,
        ],
        out_specs=[mask_head, mask_head, mask_model],
        compiler_params=params(),
        cost_estimate=cost(
            seq_count * count * window * (2 * model + 8 * width), 9e6, seq_count * count * window * heads
        ),
        name="attend_masked",
    )(rows[:, :, None], tokens, q, k, v)
    o_ms = around(o_m)

    q_block = min(256, window)

    def attend_window(w):
        return pl.pallas_call(
            attend_kernel,
            out_shape=jax.ShapeDtypeStruct((window, width), bf16),
            grid=(width // 128, window // q_block),
            in_specs=[
                pl.BlockSpec((q_block, 128), lambda p, i: (w * (window // q_block) + i, p)),
                pl.BlockSpec((window, 128), lambda p, i: (w, p)),
                pl.BlockSpec((window, 128), lambda p, i: (w, p)),
            ],
            out_specs=pl.BlockSpec((q_block, 128), lambda p, i: (i, p)),
            compiler_params=params(),
            cost_estimate=cost(
                16 * window * window * width, 4 * window * width * 2, window * window * heads
            ),
            name="attend",
        )(q, k, v)

    windows_o = [around(attend_window(w)) for w in range(seq_count)]

    mask_rows = seq_count * count
    cols = min(256, hidden)
    col_block = pl.BlockSpec((model, cols), lambda c: (0, c))
    down_block = pl.BlockSpec((cols, model), lambda c: (c, 0))
    r_m, dhf_part, g_gate, g_up, g_down = pl.pallas_call(
        functools.partial(ffn_masked_kernel, parts),
        out_shape=[
            jax.ShapeDtypeStruct((mask_rows, model), f32),
            jax.ShapeDtypeStruct((mask_rows, model), bf16),
            jax.ShapeDtypeStruct((model, hidden), bf16),
            jax.ShapeDtypeStruct((model, hidden), bf16),
            jax.ShapeDtypeStruct((hidden, model), bf16),
        ],
        grid=(hidden // cols,),
        in_specs=[
            whole_spec((mask_rows, model)),
            whole_spec((mask_rows, model)),
            whole_spec((2, model)),
            col_block,
            col_block,
            down_block,
        ]
        + [whole_spec((mask_rows, width))] * parts
        + [whole_spec((width, model))] * parts,
        out_specs=[
            whole_spec((mask_rows, model)),
            whole_spec((mask_rows, model)),
            col_block,
            col_block,
            down_block,
        ],
        scratch_shapes=[
            pltpu.VMEM((mask_rows, model), bf16),
            pltpu.VMEM((mask_rows, model), f32),
        ],
        compiler_params=params(),
        cost_estimate=cost(
            mask_rows * model * (18 * hidden + 2 * model), 20e6, mask_rows * hidden
        ),
        name="ffn_masked",
    )(x_m, cot, norm_gains, w_gate, w_up, w_down, *o_ms, *w_outs)

    share_m = mask_rows // parts
    dhf_mine = lax.dynamic_slice_in_dim(dhf_part, place * share_m, share_m, 0).astype(f32)
    for step in range(1, parts):
        send = lax.dynamic_slice_in_dim(
            dhf_part, lax.rem(place + step, parts) * share_m, share_m, 0
        )
        dhf_mine = dhf_mine + lax.ppermute(
            send, "tensor", [(i, (i + step) % parts) for i in range(parts)]
        ).astype(f32)
    dhf_all = around(dhf_mine.astype(bf16))
    dhf = jnp.zeros((mask_rows, model), bf16)
    for step, piece in enumerate(dhf_all):
        origin = lax.rem(place + parts - step, parts)
        dhf = lax.dynamic_update_slice_in_dim(dhf, piece, origin * share_m, 0)

    def total_tiles(tiles):
        piece = lax.psum_scatter(tiles, "dp", scatter_dimension=0, tiled=True)
        return lax.all_gather(piece, "dp", axis=0, tiled=True)

    ffn_grads = total_tiles(
        jnp.concatenate(
            [g.reshape(-1, model) for g in (g_gate, g_up, g_down)], axis=0
        )
    )

    dr_m, dha, g_qkv, g_out, gains_part = pl.pallas_call(
        attn_back_kernel,
        out_shape=[
            jax.ShapeDtypeStruct((mask_rows, model), f32),
            jax.ShapeDtypeStruct((total_rows, model), bf16),
            jax.ShapeDtypeStruct((model, 3 * width), bf16),
            jax.ShapeDtypeStruct((width, model), bf16),
            jax.ShapeDtypeStruct((2, model), f32),
        ],
        grid=(seq_count,),
        in_specs=[
            pl.BlockSpec((1, 1, count), lambda i: (i, 0, 0)),
            mask_model,
            mask_model,
            mask_model,
            whole_spec((2, model)),
            mask_head,
            mask_head,
            mask_head,
            mask_head,
            win_head,
            win_head,
            win_model,
            whole_spec((window, width)),
            whole_spec((window, width)),
            whole_spec((width, model)),
            whole_spec((model, 3 * width)),
        ],
        out_specs=[
            mask_model,
            win_model,
            whole_spec((model, 3 * width)),
            whole_spec((width, model)),
            whole_spec((2, model)),
        ],
        scratch_shapes=[
            pltpu.VMEM((model, 3 * width), f32),
            pltpu.VMEM((width, model), f32),
            pltpu.VMEM((2, model), f32),
            pltpu.VMEM((window, 3 * width), bf16),
        ],
        compiler_params=params(),
        cost_estimate=cost(
            12 * total_rows * model * width, 30e6, mask_rows * window * heads
        ),
        name="attn_back",
    )(
        rows[:, None, :],
        dhf,
        r_m,
        cot,
        norm_gains,
        o_m,
        q_m,
        cos_m,
        sin_m,
        k,
        v,
        tokens,
        cos,
        sin,
        w_out,
        w_qkv,
    )

    share_rows = total_rows // parts
    dha_up, dha_down = chain_sums(dha, share_rows)
    out_block = share_rows // 3 if share_rows % 3 == 0 else share_rows
    flat_rows = jnp.where(
        rows >= 0, rows + window * jnp.arange(seq_count, dtype=jnp.int32)[:, None], -1
    ).reshape(1, mask_rows)
    blocks = share_rows // out_block
    here = pl.BlockSpec((out_block, model), lambda i, place_ref: (i, 0))
    there = pl.BlockSpec(
        (out_block, model), lambda i, place_ref: (place_ref[0] * blocks + i, 0)
    )
    input_grad = pl.pallas_call(
        input_grad_kernel,
        out_shape=jax.ShapeDtypeStruct((share_rows, model), bf16),
        grid_spec=pltpu.PrefetchScalarGridSpec(
            num_scalar_prefetch=1,
            grid=(blocks,),
            in_specs=[
                whole_spec((1, mask_rows)),
                whole_spec((mask_rows, model)),
                whole_spec((2, model)),
                there,
                there,
                here,
                here,
            ],
            out_specs=here,
        ),
        compiler_params=params(),
        cost_estimate=cost(4 * share_rows * mask_rows * model, 10e6),
        name="input_grad",
    )(place_ref, flat_rows, dr_m, norm_gains, tokens, dha, dha_up, dha_down)

    share = window // parts
    layer_out = jnp.zeros((total_rows, model), bf16)
    for w in range(seq_count):
        part, own = pl.pallas_call(
            functools.partial(ffn_kernel, parts),
            out_shape=[
                jax.ShapeDtypeStruct((window, model), bf16),
                jax.ShapeDtypeStruct((share, model), f32),
            ],
            grid_spec=pltpu.PrefetchScalarGridSpec(
                num_scalar_prefetch=1,
                grid=(hidden // cols,),
                in_specs=[
                    pl.BlockSpec((window, model), lambda c, place_ref, w=w: (w, 0)),
                    whole_spec((2, model)),
                    pl.BlockSpec((model, cols), lambda c, place_ref: (0, c)),
                    pl.BlockSpec((model, cols), lambda c, place_ref: (0, c)),
                    pl.BlockSpec((cols, model), lambda c, place_ref: (c, 0)),
                ]
                + [whole_spec((window, width))] * parts
                + [whole_spec((width, model))] * parts,
                out_specs=[whole_spec((window, model)), whole_spec((share, model))],
                scratch_shapes=[
                    pltpu.VMEM((window, model), f32),
                    pltpu.VMEM((window, model), bf16),
                    pltpu.VMEM((window, model), f32),
                ],
            ),
            compiler_params=params(),
            cost_estimate=cost(
                window * model * (6 * hidden + 2 * model), 16e6, window * hidden
            ),
            name="ffn",
        )(place_ref, tokens, norm_gains, w_gate, w_up, w_down, *windows_o[w], *w_outs)
        up, down = chain_sums(part, share)
        piece = (own + up.astype(f32) + down.astype(f32)).astype(bf16)
        for step, got in enumerate(around(piece)):
            origin = lax.rem(place + parts - step, parts)
            layer_out = lax.dynamic_update_slice_in_dim(
                layer_out, got, w * window + origin * share, 0
            )

    even = jnp.array([[1.0], [1.0 / parts]], f32)
    gain_grad = small_total(gains_part * even)
    _, gain_moment, gain_new = adam_update(
        gain_grad, gain_first, gain_second, norm_gains, gain_rate, 0.0
    )

    attn_grads = total_tiles(
        jnp.concatenate(
            [g_qkv[:, i * width : (i + 1) * width].reshape(-1, model) for i in range(3)]
            + [g_out],
            axis=0,
        )
    )
    tiles = jnp.concatenate([attn_grads, ffn_grads], axis=0).reshape(-1, tile_rows, model)
    reduced = tiles[slot_tile].astype(f32)
    first_new, second_new, param_new = adam_update(
        reduced, first_moment[0], second_moment[0], master[0], weight_rate, weight_decay
    )
    weight_grad = jnp.where(slot_used, reduced, 0.0)
    weight_first = jnp.where(slot_used, first_new, 0.0)
    weight_second = jnp.where(slot_used, second_new, 0.0)
    weight_master = jnp.where(slot_used, param_new, 0.0)
    weight_low = weight_master.astype(bf16)
    return (
        layer_out,
        input_grad,
        weight_grad[None],
        weight_first[None],
        weight_second[None],
        weight_master[None],
        weight_low[None],
        gain_grad,
        gain_moment,
        gain_new,
    )


def solution(mesh):
    return jax.shard_map(
        on_device,
        mesh=mesh,
        in_specs=(
            P("dp", None),
            P("dp", None),
            P("dp", None, None),
            P(),
            P(),
            P(),
            P("tensor", None),
            P("tensor", "dp", None, None),
            P("tensor", "dp", None, None),
            P("tensor", "dp", None, None),
        ),
        out_specs=(
            P("dp", None),
            P(("dp", "tensor"), None),
            P("tensor", "dp", None, None),
            P("tensor", "dp", None, None),
            P("tensor", "dp", None, None),
            P("tensor", "dp", None, None),
            P("tensor", "dp", None, None),
            P(),
            P(),
            P(),
        ),
        check_vma=False,
    )
```

time: 1990 us -> 1090 us (0.55)
  waiting for transfers between devices: 1330 us -> 322 us
  Pallas kernels: 0 us -> 360 us
  starting transfers between devices: 0.21 us -> 260 us
  local copies, waits for them, and re-layouts: 283 us -> 55 us
  matrix products: 188 us -> 0 us
  other arithmetic: 152 us -> 65.6 us
    psum x3 -> x0, waiting for transfers between devices: 1090 us -> none  [the longest x1 749 us: on_device(): ffn_branch = lax.psum(ffn_part, 'tensor')]
    pallas_call x0 -> x12, Pallas kernels: none -> 360 us  [the longest x1 193 us: on_device(): pl.pallas_call(lambda slot_ref, slots_ref, out_ref, sems: collect_kernel(...]
    ppermute x0 -> x65, starting transfers between devices: none -> 260 us  [the longest x27 125 us: around(): lax.ppermute(value, 'tensor', [(i, (i + k) % size) for i in range(size)])]
    ppermute x0 -> x65, waiting for transfers between devices: none -> 207 us  [the longest x11 83.8 us: exchange(): return lax.ppermute(value, axis, [(i, i ^ bit) for i in range(size)])]
    dot_general x26 -> x0, matrix products: 164 us -> none  [the longest x1 19.2 us: on_device(): jnp.einsum('sqht,sqhd->sthd', d_scores_low, query_masked, preferred_eleme...]
    gather x19 -> x2, local copies, waits for them, and re-layouts: 90.5 us -> 6.06 us  [the longest x1 4.06 us: on_device(): reduced = tiles[slot_tile].astype(f32)]
    all_gather x1 -> x3, waiting for transfers between devices: 76.4 us -> 7.64 us  [the longest x1 7.62 us: on_device(): every_slot = lax.all_gather(low_slots, 'dp', axis=0, tiled=True)]
    div x1 -> x0, local copies, waits for them, and re-layouts: 59.4 us -> none  [on_device(): attention = jax.nn.softmax(scores, axis=-1)]
  transfers between devices with their start and end apart: 5 -> 70, of which waited for: 5 -> 26; matrix products, arithmetic and copies ran while one was open for 15% -> 7% of each run, Pallas kernels for 0% -> 28%
where the time goes in v1:
time: 1090 us; the launch traced here: 1080 us
  Pallas kernels  360 us (33%)
  waiting for transfers between devices  322 us (30%)
  starting transfers between devices  260 us (24%)
  other arithmetic  65.6 us (6%)
  local copies, waits for them, and re-layouts  55 us (5%)
  between operations  15.3 us (1%)
    pallas_call x1, Pallas kernels, on_device(): pl.pallas_call(lambda slot_ref, slots_ref, out_ref, sems: collect_kernel(...  193 us
    ppermute x27, starting transfers between devices, around(): lax.ppermute(value, 'tensor', [(i, (i + k) % size) for i in range(size)])  125 us
    reduce_scatter x2, waiting for transfers between devices, total_tiles(): piece = lax.psum_scatter(tiles, 'dp', scatter_dimension=0, tiled=True)  107 us
    ppermute x12, starting transfers between devices, chain_sums(): lax.ppermute(send, 'tensor', [(i, i + 1) for i in range(min(step, size -...  103 us
    ppermute x11, waiting for transfers between devices, exchange(): return lax.ppermute(value, axis, [(i, i ^ bit) for i in range(size)])  83.8 us
    ppermute x27, waiting for transfers between devices, around(): lax.ppermute(value, 'tensor', [(i, (i + k) % size) for i in range(size)])  74.2 us
    pallas_call x3, Pallas kernels, on_device(): pl.pallas_call(functools.partial(ffn_kernel, parts), out_shape=[jax.Shape...  48 us
    pallas_call x1, Pallas kernels, on_device(): pl.pallas_call(attn_back_kernel, out_shape=[jax.ShapeDtypeStruct((mask_ro...  36.5 us
  transfers between devices with their start and end apart: 70, of which 26 were waited for; matrix products, arithmetic and copies ran while one was open for 7% of the time, Pallas kernels for 28%

profile of v1, /device:TPU:0, one launch (start us, length us, event | category | flops | bytes accessed | tf_op | source)
XLA Modules:
  0.0 1077.8 jit_solution(11784654276230677046)
XLA Ops:
  28.1 22.3 %collective-permute-done.1 = bf16[2,128,1024]{2,1,0:T(8,128)(2,1)S(1)} collective-permute-done((bf16[2,128,1024]{2,1,0:T(8,128)(2,1)S(1)}, bf16[2,128,1024]{2,1,0:T(8,128)(2,1)S(1)}, u32[]{:S(2)}, u32[]{:S(2)}) %collective-permute-start.1) | collective-permute-done | bytes 524320 | tf_op jit(solution)/shard_map/ppermute | solution.py:319
  54.4 16.2 %collective-permute-done.4 = bf16[2,128,1024]{2,1,0:T(8,128)(2,1)S(1)} collective-permute-done((bf16[2,128,1024]{2,1,0:T(8,128)(2,1)S(1)}, bf16[2,128,1024]{2,1,0:T(8,128)(2,1)S(1)}, u32[]{:S(2)}, u32[]{:S(2)}) %collective-permute-start.4) | collective-permute-done | bytes 524320 | tf_op jit(solution)/shard_map/ppermute | solution.py:319
  81.0 12.1 %qkv.1 = (bf16[3072,256]{1,0:T(8,128)(2,1)}, bf16[3072,256]{1,0:T(8,128)(2,1)}, bf16[3072,256]{1,0:T(8,128)(2,1)}) custom-call(bf16[3072,1024]{1,0:T(8,128)(2,1)} %x_ref.13, f32[2,1024]{1,0:T(2,128)} %gains_ref.13, bf16[1024,768]{1,0:T(8,128)(2,1)} %constant_dynamic-update-slice_fusion.16.w_ref, f32[1024,256]{1,0:T(8,128)} %copy.34.cos_ref, ...), custom_call_target="tpu_custom_call" | custom-call | flops 4831838208 | bytes 12582912 | tf_op jit(solution)/shard_map/qkv/pallas_call | solution.py:501
  93.1 10.2 attend_masked.1
  112.2 7.6 all-gather.9.cloned.1.call-done
  119.9 192.7 %collect.1 = bf16[24,128,1024]{2,1,0:T(8,128)(2,1)} custom-call(s32[32]{0:T(128)} %multiply_add_fusion.slot_ref, bf16[64,128,1024]{2,1,0:T(8,128)(2,1)} %bitcast.37), custom_call_target="tpu_custom_call" | custom-call | bytes 12582912 | tf_op jit(solution)/shard_map/collect/pallas_call | solution.py:466
  316.2 5.7 fusion.13
  323.1 19.4 %ffn_masked.1 = (f32[480,1024]{1,0:T(8,128)}, bf16[480,1024]{1,0:T(8,128)(2,1)}, bf16[1024,1024]{1,0:T(8,128)(2,1)}, bf16[1024,1024]{1,0:T(8,128)(2,1)}, bf16[1024,1024]{1,0:T(8,128)(2,1)}) custom-call(bf16[480,1024]{1,0:T(8,128)(2,1)} %get-tuple-element.42.xm_ref, bf16[480,1024]{1,0:T(8,128)(2,1)} %bitcast.53, f32[2,1024]{1,0:T(2,128)} %gains_ref.13, ...), custom_call_target="tpu_custom_call" | custom-call | flops 10066329600 | bytes 20000000 | tf_op jit(solution)/shard_map/ffn_masked/pallas_call | solution.py:572
  348.5 5.8 collective-permute-done.50
  354.4 12.4 %collective-permute-done.49 = bf16[120,1024]{1,0:T(8,128)(2,1)S(1)} collective-permute-done((bf16[120,1024]{1,0:T(8,128)(2,1)S(1)}, bf16[120,1024]{1,0:T(8,128)(2,1)S(1)}, u32[]{:S(2)}, u32[]{:S(2)}) %collective-permute-start.49) | collective-permute-done | bytes 245792 | tf_op jit(solution)/shard_map/ppermute | solution.py:616
  380.2 6.9 collective-permute-done.52
  388.2 36.5 %attn_back.1 = (f32[480,1024]{1,0:T(8,128)}, bf16[3072,1024]{1,0:T(8,128)(2,1)}, bf16[1024,768]{1,0:T(8,128)(2,1)}, bf16[256,1024]{1,0:T(8,128)(2,1)}, f32[2,1024]{1,0:T(2,128)}) custom-call(s32[3,1,160]{2,1,0:T(1,128)} %broadcast_in_dim.79.rows_ref, bf16[480,1024]{1,0:T(8,128)(2,1)} %copy-done.8, f32[480,1024]{1,0:T(8,128)} %get-tuple-element.45.rm_ref, ...), custom_call_target="tpu_custom_call" | custom-call | flops 9663676416 | bytes 30000000 | tf_op jit(solution)/shard_map/attn_back/pallas_call | solution.py:635
  430.8 5.4 pad_maximum_fusion.1
  436.3 41.5 %reduce-scatter.3.cloned.1.call-done = bf16[128,1024]{1,0:T(8,128)(2,1)} async-done(((bf16[1024,1024]{1,0:T(8,128)(2,1)}), bf16[128,1024]{1,0:T(8,128)(2,1)}) %reduce-scatter.3.cloned.1.call-update) | async-done | bytes 262160 | tf_op jit(solution)/shard_map/reduce_scatter | solution.py:626
  477.9 66.0 %reduce-scatter.5.cloned.1.call-done = bf16[384,1024]{1,0:T(8,128)(2,1)} async-done(((bf16[3072,1024]{1,0:T(8,128)(2,1)}), bf16[384,1024]{1,0:T(8,128)(2,1)}) %reduce-scatter.5.cloned.1.call-update) | async-done | bytes 786448 | tf_op jit(solution)/shard_map/reduce_scatter | solution.py:626
  543.9 11.5 %attend.3.refs_0_ = bf16[1024,256]{1,0:T(8,128)(2,1)} custom-call(bf16[3072,256]{1,0:T(8,128)(2,1)} %get-tuple-element.33.q_ref, bf16[3072,256]{1,0:T(8,128)(2,1)} %get-tuple-element.34.k_ref, bf16[3072,256]{1,0:T(8,128)(2,1)} %get-tuple-element.35.v_ref), custom_call_target="tpu_custom_call" | custom-call | flops 4294967296 | bytes 2097152 | tf_op jit(solution)/shard_map/attend/pallas_call | solution.py:549
  560.8 11.4 %attend.4.refs_0_ = bf16[1024,256]{1,0:T(8,128)(2,1)} custom-call(bf16[3072,256]{1,0:T(8,128)(2,1)} %get-tuple-element.33.q_ref, bf16[3072,256]{1,0:T(8,128)(2,1)} %get-tuple-element.34.k_ref, bf16[3072,256]{1,0:T(8,128)(2,1)} %get-tuple-element.35.v_ref), custom_call_target="tpu_custom_call" | custom-call | flops 4294967296 | bytes 2097152 | tf_op jit(solution)/shard_map/attend/pallas_call | solution.py:549
  573.2 11.4 %attend.5.refs_0_ = bf16[1024,256]{1,0:T(8,128)(2,1)} custom-call(bf16[3072,256]{1,0:T(8,128)(2,1)} %get-tuple-element.33.q_ref, bf16[3072,256]{1,0:T(8,128)(2,1)} %get-tuple-element.34.k_ref, bf16[3072,256]{1,0:T(8,128)(2,1)} %get-tuple-element.35.v_ref), custom_call_target="tpu_custom_call" | custom-call | flops 4294967296 | bytes 2097152 | tf_op jit(solution)/shard_map/attend/pallas_call | solution.py:549
  587.4 7.5 collective-permute-done.7.refs_2_
  594.9 31.8 %collective-permute-start.33 = (bf16[1024,256]{1,0:T(8,128)(2,1)}, bf16[1024,256]{1,0:T(8,128)(2,1)}, u32[]{:S(2)}, u32[]{:S(2)}) collective-permute-start(bf16[1024,256]{1,0:T(8,128)(2,1)} %attend.5.refs_0_), channel_id=1, source_target_pairs={{0,1},{1,2},{2,3},{3,0},{4,5},{5,6},{6,7},{7,4},{8,9},{9,10},{10,1... | collective-permute-start | bytes 1572872 | tf_op jit(solution)/shard_map/ppermute | solution.py:350
  630.5 15.9 %ffn.3 = (bf16[1024,1024]{1,0:T(8,128)(2,1)}, f32[256,1024]{1,0:T(8,128)}) custom-call(s32[1]{0:T(128)} %bitcast.place_ref, bf16[3072,1024]{1,0:T(8,128)(2,1)} %x_ref.13, f32[2,1024]{1,0:T(2,128)} %gains_ref.13, bf16[1024,1024]{1,0:T(8,128)(2,1)} %bitcast.50, bf16[1024,1024]{1,0:T(8,128)(2,1)} %bitcast.46, bf16[1024,1024]{1,0:T(8,128)(2,1)} %bitcast.42, ...), custom_call_target="tpu_custom_call" | custom-call | flops 8589934592 | bytes 16000000 | tf_op jit(solution)/shard_map/ffn/pallas_call | solution.py:736
  649.6 11.7 %collective-permute-done.22.refs_2_ = bf16[1024,256]{1,0:T(8,128)(2,1)S(1)} collective-permute-done((bf16[1024,256]{1,0:T(8,128)(2,1)}, bf16[1024,256]{1,0:T(8,128)(2,1)S(1)}, u32[]{:S(2)}, u32[]{:S(2)}) %collective-permute-start.22) | collective-permute-done | bytes 524320 | tf_op jit(solution)/shard_map/ppermute | solution.py:350
  661.2 12.9 %collective-permute-start.12 = (bf16[256,1024]{1,0:T(8,128)(2,1)S(1)}, bf16[256,1024]{1,0:T(8,128)(2,1)S(1)}, u32[]{:S(2)}, u32[]{:S(2)}) collective-permute-start(bf16[256,1024]{1,0:T(8,128)(2,1)S(1)} %get-tuple-element.89), channel_id=1, source_target_pairs={{0,1},{4,5},{8,9},{12,13},{16,17},{20,21},{24,25},{28,29}} | collective-permute-start | bytes 1572872 | tf_op jit(solution)/shard_map/ppermute | solution.py:364
  675.6 16.1 %ffn.4 = (bf16[1024,1024]{1,0:T(8,128)(2,1)}, f32[256,1024]{1,0:T(8,128)}) custom-call(s32[1]{0:T(128)} %bitcast.place_ref, bf16[3072,1024]{1,0:T(8,128)(2,1)} %x_ref.13, f32[2,1024]{1,0:T(2,128)} %gains_ref.13, bf16[1024,1024]{1,0:T(8,128)(2,1)} %bitcast.51, bf16[1024,1024]{1,0:T(8,128)(2,1)} %bitcast.47, bf16[1024,1024]{1,0:T(8,128)(2,1)} %bitcast.43, ...), custom_call_target="tpu_custom_call" | custom-call | flops 8589934592 | bytes 16000000 | tf_op jit(solution)/shard_map/ffn/pallas_call | solution.py:736
  704.9 15.9 %ffn.5 = (bf16[1024,1024]{1,0:T(8,128)(2,1)}, f32[256,1024]{1,0:T(8,128)}) custom-call(s32[1]{0:T(128)} %bitcast.place_ref, bf16[3072,1024]{1,0:T(8,128)(2,1)} %x_ref.13, f32[2,1024]{1,0:T(2,128)} %gains_ref.13, bf16[1024,1024]{1,0:T(8,128)(2,1)} %bitcast.52, bf16[1024,1024]{1,0:T(8,128)(2,1)} %bitcast.48, bf16[1024,1024]{1,0:T(8,128)(2,1)} %bitcast.44, ...), custom_call_target="tpu_custom_call" | custom-call | flops 8589934592 | bytes 16000000 | tf_op jit(solution)/shard_map/ffn/pallas_call | solution.py:736
  724.8 4.5 collective-permute-start.25
  736.0 18.8 %collective-permute-start.36 = (bf16[256,1024]{1,0:T(8,128)(2,1)S(1)}, bf16[256,1024]{1,0:T(8,128)(2,1)S(1)}, u32[]{:S(2)}, u32[]{:S(2)}) collective-permute-start(bf16[256,1024]{1,0:T(8,128)(2,1)S(1)} %get-tuple-element.81), channel_id=1, source_target_pairs={{0,1},{4,5},{8,9},{12,13},{16,17},{20,21},{24,25},{28,29}} | collective-permute-start | bytes 1572872 | tf_op jit(solution)/shard_map/ppermute | solution.py:364
  757.4 12.4 %collective-permute-done.25 = bf16[256,1024]{1,0:T(8,128)(2,1)S(1)} collective-permute-done((bf16[256,1024]{1,0:T(8,128)(2,1)S(1)}, bf16[256,1024]{1,0:T(8,128)(2,1)S(1)}, u32[]{:S(2)}, u32[]{:S(2)}) %collective-permute-start.25) | collective-permute-done | bytes 524320 | tf_op jit(solution)/shard_map/ppermute | solution.py:364
  772.7 8.3 collective-permute-done.36
  781.9 8.9 collective-permute-done.14
  791.5 7.9 collective-permute-start.37
  803.9 7.9 collective-permute-start.18
  812.0 6.7 collective-permute-start.26
  823.4 7.2 collective-permute-start.20
  830.7 7.2 collective-permute-done.18
  842.8 12.4 %collective-permute-done.19 = bf16[256,1024]{1,0:T(8,128)(2,1)S(1)} collective-permute-done((bf16[256,1024]{1,0:T(8,128)(2,1)S(1)}, bf16[256,1024]{1,0:T(8,128)(2,1)S(1)}, u32[]{:S(2)}, u32[]{:S(2)}) %collective-permute-start.19) | collective-permute-done | bytes 524320 | tf_op jit(solution)/shard_map/ppermute | solution.py:350
  864.2 15.3 %collective-permute-start.30 = (bf16[256,1024]{1,0:T(8,128)(2,1)}, bf16[256,1024]{1,0:T(8,128)(2,1)S(1)}, u32[]{:S(2)}, u32[]{:S(2)}) collective-permute-start(bf16[256,1024]{1,0:T(8,128)(2,1)} %get-tuple-element.66), channel_id=1, source_target_pairs={{0,1},{1,2},{2,3},{3,0},{4,5},{5,6},{6,7},{7,4},{8,9},{9,10},{10,1... | collective-permute-start | bytes 1572872 | tf_op jit(solution)/shard_map/ppermute | solution.py:350
  883.3 4.6 collective-permute-start.38
  890.2 14.3 %collective-permute-done.30 = bf16[256,1024]{1,0:T(8,128)(2,1)S(1)} collective-permute-done((bf16[256,1024]{1,0:T(8,128)(2,1)}, bf16[256,1024]{1,0:T(8,128)(2,1)S(1)}, u32[]{:S(2)}, u32[]{:S(2)}) %collective-permute-start.30) | collective-permute-done | bytes 524320 | tf_op jit(solution)/shard_map/ppermute | solution.py:350
  904.5 7.6 collective-permute-start.32
  917.0 8.2 collective-permute-done.31
  925.2 39.3 %collective-permute-start.56 = (bf16[768,1024]{1,0:T(8,128)(2,1)S(1)}, bf16[768,1024]{1,0:T(8,128)(2,1)}, u32[]{:S(2)}, u32[]{:S(2)}) collective-permute-start(bf16[768,1024]{1,0:T(8,128)(2,1)S(1)} %add_convert_fusion.2), channel_id=1, source_target_pairs={{0,1},{1,2},{2,3},{4,5},{5,6},{6,7},{8,9},{9,10},{10,11},{12,13},{... | collective-permute-start | bytes 4718600 | tf_op jit(solution)/shard_map/ppermute | solution.py:364
  969.4 28.8 %collective-permute-done.63 = f32[2,1024]{1,0:T(2,128)S(1)} collective-permute-done((f32[2,1024]{1,0:T(2,128)S(1)}, f32[2,1024]{1,0:T(2,128)S(1)}, u32[]{:S(2)}, u32[]{:S(2)}) %collective-permute-start.63) | collective-permute-done | bytes 8224 | tf_op jit(solution)/shard_map/ppermute | solution.py:319
  1001.6 8.0 collective-permute-done.64
  1009.6 19.9 %collective-permute-start.44 = (bf16[256,1024]{1,0:T(8,128)(2,1)}, bf16[256,1024]{1,0:T(8,128)(2,1)}, u32[]{:S(2)}, u32[]{:S(2)}) collective-permute-start(bf16[256,1024]{1,0:T(8,128)(2,1)} %get-tuple-element.64), channel_id=1, source_target_pairs={{0,3},{1,0},{2,1},{3,2},{4,7},{5,4},{6,5},{7,6},{8,11},{9,8},{10,9... | collective-permute-start | bytes 1572872 | tf_op jit(solution)/shard_map/ppermute | solution.py:350
  1039.6 6.7 input_grad.1
  1046.3 7.7 pad_maximum_fusion
  1058.1 12.7 %fusion.12 = (bf16[1,8,128,1024]{3,2,1,0:T(8,128)(2,1)}, f32[1,8,128,1024]{3,2,1,0:T(8,128)}, f32[1,8,128,1024]{3,2,1,0:T(8,128)}, f32[1,8,128,1024]{3,2,1,0:T(8,128)}, f32[1,8,128,1024]{3,2,1,0:T(8,128)}) fusion(f32[1,8,128,1024]{3,2,1,0:T(8,128)} %param.18, f32[1,8,128,1024]{3,2,1,0:T(8,128)} %param.20, bf16[8,128,1024]{2,1,0:T(8,128)(2,1)S(1)} %gather_fusion.1, ...), kind=kLoop, calls=%fused_computation.106 | loop fusion | flops 22020096 | bytes 33554440 | tf_op jit(solution)/shard_map/convert_element_type | solution.py:797
  (273 shorter events, 180.4 us)
Async XLA Ops:
  7.2 112.7 %all-gather.9.cloned.1.call-start = ((), (), s32[]{:S(2)}) async-start(), calls=%async_computation.6 | async-start | bytes 18874368 | tf_op jit(solution)/shard_map/all_gather | solution.py:465
  11.1 466.7 %reduce-scatter.3.cloned.1.call-start = ((), (), s32[]{:S(2)}) async-start(), calls=%async_computation.2 | async-start | bytes 2359296 | tf_op jit(solution)/shard_map/reduce_scatter | solution.py:626
  103.3 209.2 %collective-permute-start.45 = (bf16[480,256]{1,0:T(8,128)(2,1)}, bf16[480,256]{1,0:T(8,128)(2,1)}, u32[]{:S(2)}, u32[]{:S(2)}) collective-permute-start(bf16[480,256]{1,0:T(8,128)(2,1)} %get-tuple-element.43.refs_0_.om_ref), channel_id=1, source_target_pairs={{0,1},{1,2},{2,3},{3,0},{4,5},{5,6},{6,7},{7,4},{8,9},{9,10},{10,1... | collective-permute-start | bytes 737288 | tf_op jit(solution)/shard_map/ppermute | solution.py:350
  104.8 217.1 %collective-permute-start.9 = (bf16[256,1024]{1,0:T(8,128)(2,1)S(1)}, bf16[256,1024]{1,0:T(8,128)(2,1)S(1)}, u32[]{:S(2)}, u32[]{:S(2)}) collective-permute-start(bf16[256,1024]{1,0:T(8,128)(2,1)S(1)} %bitcast.55), channel_id=1, source_target_pairs={{0,1},{1,2},{2,3},{3,0},{4,5},{5,6},{6,7},{7,4},{8,9},{9,10},{10,1... | collective-permute-start | bytes 1572872 | tf_op jit(solution)/shard_map/ppermute | solution.py:350
  106.3 215.7 %collective-permute-start.10 = (bf16[256,1024]{1,0:T(8,128)(2,1)S(1)}, bf16[256,1024]{1,0:T(8,128)(2,1)S(1)}, u32[]{:S(2)}, u32[]{:S(2)}) collective-permute-start(bf16[256,1024]{1,0:T(8,128)(2,1)S(1)} %bitcast.56), channel_id=1, source_target_pairs={{0,2},{1,3},{2,0},{3,1},{4,6},{5,7},{6,4},{7,5},{8,10},{9,11},{10,... | collective-permute-start | bytes 1572872 | tf_op jit(solution)/shard_map/ppermute | solution.py:350
  107.7 214.3 %collective-permute-start.11 = (bf16[256,1024]{1,0:T(8,128)(2,1)S(1)}, bf16[256,1024]{1,0:T(8,128)(2,1)}, u32[]{:S(2)}, u32[]{:S(2)}) collective-permute-start(bf16[256,1024]{1,0:T(8,128)(2,1)S(1)} %bitcast.57), channel_id=1, source_target_pairs={{0,3},{1,0},{2,1},{3,2},{4,7},{5,4},{6,5},{7,6},{8,11},{9,8},{10,9... | collective-permute-start | bytes 1572872 | tf_op jit(solution)/shard_map/ppermute | solution.py:350
  111.7 210.2 %collective-permute-start.46 = (bf16[480,256]{1,0:T(8,128)(2,1)}, bf16[480,256]{1,0:T(8,128)(2,1)S(1)}, u32[]{:S(2)}, u32[]{:S(2)}) collective-permute-start(bf16[480,256]{1,0:T(8,128)(2,1)} %get-tuple-element.43.refs_0_.om_ref), channel_id=1, source_target_pairs={{0,2},{1,3},{2,0},{3,1},{4,6},{5,7},{6,4},{7,5},{8,10},{9,11},{10,... | collective-permute-start | bytes 737288 | tf_op jit(solution)/shard_map/ppermute | solution.py:350
  430.8 113.1 %reduce-scatter.5.cloned.1.call-start = ((), (), s32[]{:S(2)}) async-start(), calls=%async_computation.4 | async-start | bytes 7077888 | tf_op jit(solution)/shard_map/reduce_scatter | solution.py:626
  436.2 610.1 %all-gather.5.cloned.1.call-start = ((), (), s32[]{:S(2)}) async-start(), calls=%async_computation.3 | async-start | bytes 2359296 | tf_op jit(solution)/shard_map/all_gather | solution.py:627
  477.8 568.5 %all-gather.7.cloned.1.call-start = ((), (), s32[]{:S(2)}) async-start(), calls=%async_computation.5 | async-start | bytes 7077888 | tf_op jit(solution)/shard_map/all_gather | solution.py:627
  555.4 29.2 %collective-permute-start.6 = (bf16[1024,256]{1,0:T(8,128)(2,1)}, bf16[1024,256]{1,0:T(8,128)(2,1)S(1)}, u32[]{:S(2)}, u32[]{:S(2)}) collective-permute-start(bf16[1024,256]{1,0:T(8,128)(2,1)} %attend.3.refs_0_), channel_id=1, source_target_pairs={{0,1},{1,2},{2,3},{3,0},{4,5},{5,6},{6,7},{7,4},{8,9},{9,10},{10,1... | collective-permute-start | bytes 1572872 | tf_op jit(solution)/shard_map/ppermute | solution.py:350
  556.9 38.0 %collective-permute-start.7 = (bf16[1024,256]{1,0:T(8,128)(2,1)}, bf16[1024,256]{1,0:T(8,128)(2,1)S(1)}, u32[]{:S(2)}, u32[]{:S(2)}) collective-permute-start(bf16[1024,256]{1,0:T(8,128)(2,1)} %attend.3.refs_0_), channel_id=1, source_target_pairs={{0,2},{1,3},{2,0},{3,1},{4,6},{5,7},{6,4},{7,5},{8,10},{9,11},{10,... | collective-permute-start | bytes 1572872 | tf_op jit(solution)/shard_map/ppermute | solution.py:350
  559.3 67.4 %collective-permute-start.8 = (bf16[1024,256]{1,0:T(8,128)(2,1)}, bf16[1024,256]{1,0:T(8,128)(2,1)S(1)}, u32[]{:S(2)}, u32[]{:S(2)}) collective-permute-start(bf16[1024,256]{1,0:T(8,128)(2,1)} %attend.3.refs_0_), channel_id=1, source_target_pairs={{0,3},{1,0},{2,1},{3,2},{4,7},{5,4},{6,5},{7,6},{8,11},{9,8},{10,9... | collective-permute-start | bytes 1572872 | tf_op jit(solution)/shard_map/ppermute | solution.py:350
  572.1 76.3 %collective-permute-start.21 = (bf16[1024,256]{1,0:T(8,128)(2,1)}, bf16[1024,256]{1,0:T(8,128)(2,1)S(1)}, u32[]{:S(2)}, u32[]{:S(2)}) collective-permute-start(bf16[1024,256]{1,0:T(8,128)(2,1)} %attend.4.refs_0_), channel_id=1, source_target_pairs={{0,1},{1,2},{2,3},{3,0},{4,5},{5,6},{6,7},{7,4},{8,9},{9,10},{10,1... | collective-permute-start | bytes 1572872 | tf_op jit(solution)/shard_map/ppermute | solution.py:350
  572.7 88.5 %collective-permute-start.22 = (bf16[1024,256]{1,0:T(8,128)(2,1)}, bf16[1024,256]{1,0:T(8,128)(2,1)S(1)}, u32[]{:S(2)}, u32[]{:S(2)}) collective-permute-start(bf16[1024,256]{1,0:T(8,128)(2,1)} %attend.4.refs_0_), channel_id=1, source_target_pairs={{0,2},{1,3},{2,0},{3,1},{4,6},{5,7},{6,4},{7,5},{8,10},{9,11},{10,... | collective-permute-start | bytes 1572872 | tf_op jit(solution)/shard_map/ppermute | solution.py:350
  584.6 89.5 %collective-permute-start.23 = (bf16[1024,256]{1,0:T(8,128)(2,1)S(1)}, bf16[1024,256]{1,0:T(8,128)(2,1)S(1)}, u32[]{:S(2)}, u32[]{:S(2)}) collective-permute-start(bf16[1024,256]{1,0:T(8,128)(2,1)S(1)} %copy-done.19), channel_id=1, source_target_pairs={{0,3},{1,0},{2,1},{3,2},{4,7},{5,4},{6,5},{7,6},{8,11},{9,8},{10,9... | collective-permute-start | bytes 1572872 | tf_op jit(solution)/shard_map/ppermute | solution.py:350
  594.9 105.0 %collective-permute-start.33 = (bf16[1024,256]{1,0:T(8,128)(2,1)}, bf16[1024,256]{1,0:T(8,128)(2,1)}, u32[]{:S(2)}, u32[]{:S(2)}) collective-permute-start(bf16[1024,256]{1,0:T(8,128)(2,1)} %attend.5.refs_0_), channel_id=1, source_target_pairs={{0,1},{1,2},{2,3},{3,0},{4,5},{5,6},{6,7},{7,4},{8,9},{9,10},{10,1... | collective-permute-start | bytes 1572872 | tf_op jit(solution)/shard_map/ppermute | solution.py:350
  626.7 74.6 %collective-permute-start.34 = (bf16[1024,256]{1,0:T(8,128)(2,1)}, bf16[1024,256]{1,0:T(8,128)(2,1)}, u32[]{:S(2)}, u32[]{:S(2)}) collective-permute-start(bf16[1024,256]{1,0:T(8,128)(2,1)} %attend.5.refs_0_), channel_id=1, source_target_pairs={{0,2},{1,3},{2,0},{3,1},{4,6},{5,7},{6,4},{7,5},{8,10},{9,11},{10,... | collective-permute-start | bytes 1572872 | tf_op jit(solution)/shard_map/ppermute | solution.py:350
  648.5 54.3 %collective-permute-start.35 = (bf16[1024,256]{1,0:T(8,128)(2,1)}, bf16[1024,256]{1,0:T(8,128)(2,1)}, u32[]{:S(2)}, u32[]{:S(2)}) collective-permute-start(bf16[1024,256]{1,0:T(8,128)(2,1)} %attend.5.refs_0_), channel_id=1, source_target_pairs={{0,3},{1,0},{2,1},{3,2},{4,7},{5,4},{6,5},{7,6},{8,11},{9,8},{10,9... | collective-permute-start | bytes 1572872 | tf_op jit(solution)/shard_map/ppermute | solution.py:350
  661.2 36.7 %collective-permute-start.12 = (bf16[256,1024]{1,0:T(8,128)(2,1)S(1)}, bf16[256,1024]{1,0:T(8,128)(2,1)S(1)}, u32[]{:S(2)}, u32[]{:S(2)}) collective-permute-start(bf16[256,1024]{1,0:T(8,128)(2,1)S(1)} %get-tuple-element.89), channel_id=1, source_target_pairs={{0,1},{4,5},{8,9},{12,13},{16,17},{20,21},{24,25},{28,29}} | collective-permute-start | bytes 1572872 | tf_op jit(solution)/shard_map/ppermute | solution.py:364
  674.2 49.4 %collective-permute-start.15 = (bf16[256,1024]{1,0:T(8,128)(2,1)}, bf16[256,1024]{1,0:T(8,128)(2,1)}, u32[]{:S(2)}, u32[]{:S(2)}) collective-permute-start(bf16[256,1024]{1,0:T(8,128)(2,1)} %get-tuple-element.90), channel_id=1, source_target_pairs={{3,2},{7,6},{11,10},{15,14},{19,18},{23,22},{27,26},{31,30}} | collective-permute-start | bytes 1572872 | tf_op jit(solution)/shard_map/ppermute | solution.py:371
  697.9 33.1 %collective-permute-start.57 = (bf16[768,1024]{1,0:T(8,128)(2,1)}, bf16[768,1024]{1,0:T(8,128)(2,1)}, u32[]{:S(2)}, u32[]{:S(2)}) collective-permute-start(bf16[768,1024]{1,0:T(8,128)(2,1)} %get-tuple-element.73), channel_id=1, source_target_pairs={{3,2},{7,6},{11,10},{15,14},{19,18},{23,22},{27,26},{31,30}} | collective-permute-start | bytes 4718600 | tf_op jit(solution)/shard_map/ppermute | solution.py:371
  701.3 54.8 %collective-permute-start.27 = (bf16[256,1024]{1,0:T(8,128)(2,1)S(1)}, bf16[256,1024]{1,0:T(8,128)(2,1)}, u32[]{:S(2)}, u32[]{:S(2)}) collective-permute-start(bf16[256,1024]{1,0:T(8,128)(2,1)S(1)} %get-tuple-element.86), channel_id=1, source_target_pairs={{3,2},{7,6},{11,10},{15,14},{19,18},{23,22},{27,26},{31,30}} | collective-permute-start | bytes 1572872 | tf_op jit(solution)/shard_map/ppermute | solution.py:371
  720.9 91.1 %collective-permute-start.54 = (bf16[768,1024]{1,0:T(8,128)(2,1)}, bf16[768,1024]{1,0:T(8,128)(2,1)S(1)}, u32[]{:S(2)}, u32[]{:S(2)}) collective-permute-start(bf16[768,1024]{1,0:T(8,128)(2,1)} %get-tuple-element.74), channel_id=1, source_target_pairs={{0,1},{4,5},{8,9},{12,13},{16,17},{20,21},{24,25},{28,29}} | collective-permute-start | bytes 4718600 | tf_op jit(solution)/shard_map/ppermute | solution.py:364
  724.8 44.9 %collective-permute-start.25 = (bf16[256,1024]{1,0:T(8,128)(2,1)S(1)}, bf16[256,1024]{1,0:T(8,128)(2,1)S(1)}, u32[]{:S(2)}, u32[]{:S(2)}) collective-permute-start(bf16[256,1024]{1,0:T(8,128)(2,1)S(1)} %add_convert_fusion.13), channel_id=1, source_target_pairs={{0,1},{1,2},{4,5},{5,6},{8,9},{9,10},{12,13},{13,14},{16,17},{17,1... | collective-permute-start | bytes 1572872 | tf_op jit(solution)/shard_map/ppermute | solution.py:364
  734.8 83.9 %collective-permute-start.58 = (bf16[768,1024]{1,0:T(8,128)(2,1)S(1)}, bf16[768,1024]{1,0:T(8,128)(2,1)S(1)}, u32[]{:S(2)}, u32[]{:S(2)}) collective-permute-start(bf16[768,1024]{1,0:T(8,128)(2,1)S(1)} %add_convert_fusion.1), channel_id=1, source_target_pairs={{3,2},{2,1},{7,6},{6,5},{11,10},{10,9},{15,14},{14,13},{19,18},{18... | collective-permute-start | bytes 4718600 | tf_op jit(solution)/shard_map/ppermute | solution.py:371
  736.0 45.0 %collective-permute-start.36 = (bf16[256,1024]{1,0:T(8,128)(2,1)S(1)}, bf16[256,1024]{1,0:T(8,128)(2,1)S(1)}, u32[]{:S(2)}, u32[]{:S(2)}) collective-permute-start(bf16[256,1024]{1,0:T(8,128)(2,1)S(1)} %get-tuple-element.81), channel_id=1, source_target_pairs={{0,1},{4,5},{8,9},{12,13},{16,17},{20,21},{24,25},{28,29}} | collective-permute-start | bytes 1572872 | tf_op jit(solution)/shard_map/ppermute | solution.py:364
  756.1 34.7 %collective-permute-start.14 = (bf16[256,1024]{1,0:T(8,128)(2,1)S(1)}, bf16[256,1024]{1,0:T(8,128)(2,1)S(1)}, u32[]{:S(2)}, u32[]{:S(2)}) collective-permute-start(bf16[256,1024]{1,0:T(8,128)(2,1)S(1)} %get-tuple-element.87), channel_id=1, source_target_pairs={{0,1},{1,2},{2,3},{4,5},{5,6},{6,7},{8,9},{9,10},{10,11},{12,13},{... | collective-permute-start | bytes 1572872 | tf_op jit(solution)/shard_map/ppermute | solution.py:364
  790.8 31.4 %collective-permute-start.39 = (bf16[256,1024]{1,0:T(8,128)(2,1)S(1)}, bf16[256,1024]{1,0:T(8,128)(2,1)S(1)}, u32[]{:S(2)}, u32[]{:S(2)}) collective-permute-start(bf16[256,1024]{1,0:T(8,128)(2,1)S(1)} %get-tuple-element.82), channel_id=1, source_target_pairs={{3,2},{7,6},{11,10},{15,14},{19,18},{23,22},{27,26},{31,30}} | collective-permute-start | bytes 1572872 | tf_op jit(solution)/shard_map/ppermute | solution.py:371
  791.5 31.9 %collective-permute-start.37 = (bf16[256,1024]{1,0:T(8,128)(2,1)S(1)}, bf16[256,1024]{1,0:T(8,128)(2,1)S(1)}, u32[]{:S(2)}, u32[]{:S(2)}) collective-permute-start(bf16[256,1024]{1,0:T(8,128)(2,1)S(1)} %add_convert_fusion.8), channel_id=1, source_target_pairs={{0,1},{1,2},{4,5},{5,6},{8,9},{9,10},{12,13},{13,14},{16,17},{17,1... | collective-permute-start | bytes 1572872 | tf_op jit(solution)/shard_map/ppermute | solution.py:364
  803.9 34.0 %collective-permute-start.18 = (bf16[256,1024]{1,0:T(8,128)(2,1)S(1)}, bf16[256,1024]{1,0:T(8,128)(2,1)S(1)}, u32[]{:S(2)}, u32[]{:S(2)}) collective-permute-start(bf16[256,1024]{1,0:T(8,128)(2,1)S(1)} %get-tuple-element.68), channel_id=1, source_target_pairs={{0,1},{1,2},{2,3},{3,0},{4,5},{5,6},{6,7},{7,4},{8,9},{9,10},{10,1... | collective-permute-start | bytes 1572872 | tf_op jit(solution)/shard_map/ppermute | solution.py:350
  812.0 50.9 %collective-permute-start.26 = (bf16[256,1024]{1,0:T(8,128)(2,1)S(1)}, bf16[256,1024]{1,0:T(8,128)(2,1)S(1)}, u32[]{:S(2)}, u32[]{:S(2)}) collective-permute-start(bf16[256,1024]{1,0:T(8,128)(2,1)S(1)} %get-tuple-element.83), channel_id=1, source_target_pairs={{0,1},{1,2},{2,3},{4,5},{5,6},{6,7},{8,9},{9,10},{10,11},{12,13},{... | collective-permute-start | bytes 1572872 | tf_op jit(solution)/shard_map/ppermute | solution.py:364
  818.7 36.5 %collective-permute-start.19 = (bf16[256,1024]{1,0:T(8,128)(2,1)S(1)}, bf16[256,1024]{1,0:T(8,128)(2,1)S(1)}, u32[]{:S(2)}, u32[]{:S(2)}) collective-permute-start(bf16[256,1024]{1,0:T(8,128)(2,1)S(1)} %get-tuple-element.68), channel_id=1, source_target_pairs={{0,2},{1,3},{2,0},{3,1},{4,6},{5,7},{6,4},{7,5},{8,10},{9,11},{10,... | collective-permute-start | bytes 1572872 | tf_op jit(solution)/shard_map/ppermute | solution.py:350
  822.1 40.8 %collective-permute-start.29 = (bf16[256,1024]{1,0:T(8,128)(2,1)S(1)}, bf16[256,1024]{1,0:T(8,128)(2,1)S(1)}, u32[]{:S(2)}, u32[]{:S(2)}) collective-permute-start(bf16[256,1024]{1,0:T(8,128)(2,1)S(1)} %add_convert_fusion.10), channel_id=1, source_target_pairs={{3,2},{2,1},{1,0},{7,6},{6,5},{5,4},{11,10},{10,9},{9,8},{15,14},{... | collective-permute-start | bytes 1572872 | tf_op jit(solution)/shard_map/ppermute | solution.py:371
  823.4 38.0 %collective-permute-start.20 = (bf16[256,1024]{1,0:T(8,128)(2,1)S(1)}, bf16[256,1024]{1,0:T(8,128)(2,1)S(1)}, u32[]{:S(2)}, u32[]{:S(2)}) collective-permute-start(bf16[256,1024]{1,0:T(8,128)(2,1)S(1)} %get-tuple-element.68), channel_id=1, source_target_pairs={{0,3},{1,0},{2,1},{3,2},{4,7},{5,4},{6,5},{7,6},{8,11},{9,8},{10,9... | collective-permute-start | bytes 1572872 | tf_op jit(solution)/shard_map/ppermute | solution.py:350
  837.9 75.0 %collective-permute-start.55 = (bf16[768,1024]{1,0:T(8,128)(2,1)}, bf16[768,1024]{1,0:T(8,128)(2,1)}, u32[]{:S(2)}, u32[]{:S(2)}) collective-permute-start(bf16[768,1024]{1,0:T(8,128)(2,1)} %get-tuple-element.72), channel_id=1, source_target_pairs={{0,1},{1,2},{4,5},{5,6},{8,9},{9,10},{12,13},{13,14},{16,17},{17,1... | collective-permute-start | bytes 4718600 | tf_op jit(solution)/shard_map/ppermute | solution.py:364
  861.4 27.3 %collective-permute-start.40 = (bf16[256,1024]{1,0:T(8,128)(2,1)}, bf16[256,1024]{1,0:T(8,128)(2,1)S(1)}, u32[]{:S(2)}, u32[]{:S(2)}) collective-permute-start(bf16[256,1024]{1,0:T(8,128)(2,1)} %get-tuple-element.80), channel_id=1, source_target_pairs={{3,2},{2,1},{7,6},{6,5},{11,10},{10,9},{15,14},{14,13},{19,18},{18... | collective-permute-start | bytes 1572872 | tf_op jit(solution)/shard_map/ppermute | solution.py:371
  864.2 40.3 %collective-permute-start.30 = (bf16[256,1024]{1,0:T(8,128)(2,1)}, bf16[256,1024]{1,0:T(8,128)(2,1)S(1)}, u32[]{:S(2)}, u32[]{:S(2)}) collective-permute-start(bf16[256,1024]{1,0:T(8,128)(2,1)} %get-tuple-element.66), channel_id=1, source_target_pairs={{0,1},{1,2},{2,3},{3,0},{4,5},{5,6},{6,7},{7,4},{8,9},{9,10},{10,1... | collective-permute-start | bytes 1572872 | tf_op jit(solution)/shard_map/ppermute | solution.py:350
  883.3 82.8 %collective-permute-start.38 = (bf16[256,1024]{1,0:T(8,128)(2,1)}, bf16[256,1024]{1,0:T(8,128)(2,1)S(1)}, u32[]{:S(2)}, u32[]{:S(2)}) collective-permute-start(bf16[256,1024]{1,0:T(8,128)(2,1)} %get-tuple-element.79), channel_id=1, source_target_pairs={{0,1},{1,2},{2,3},{4,5},{5,6},{6,7},{8,9},{9,10},{10,11},{12,13},{... | collective-permute-start | bytes 1572872 | tf_op jit(solution)/shard_map/ppermute | solution.py:364
  887.9 37.3 %collective-permute-start.31 = (bf16[256,1024]{1,0:T(8,128)(2,1)}, bf16[256,1024]{1,0:T(8,128)(2,1)S(1)}, u32[]{:S(2)}, u32[]{:S(2)}) collective-permute-start(bf16[256,1024]{1,0:T(8,128)(2,1)} %get-tuple-element.66), channel_id=1, source_target_pairs={{0,2},{1,3},{2,0},{3,1},{4,6},{5,7},{6,4},{7,5},{8,10},{9,11},{10,... | collective-permute-start | bytes 1572872 | tf_op jit(solution)/shard_map/ppermute | solution.py:350
  888.9 77.2 %collective-permute-start.41 = (bf16[256,1024]{1,0:T(8,128)(2,1)S(1)}, bf16[256,1024]{1,0:T(8,128)(2,1)S(1)}, u32[]{:S(2)}, u32[]{:S(2)}) collective-permute-start(bf16[256,1024]{1,0:T(8,128)(2,1)S(1)} %add_convert_fusion.5), channel_id=1, source_target_pairs={{3,2},{2,1},{1,0},{7,6},{6,5},{5,4},{11,10},{10,9},{9,8},{15,14},{... | collective-permute-start | bytes 1572872 | tf_op jit(solution)/shard_map/ppermute | solution.py:371
  904.5 60.8 %collective-permute-start.32 = (bf16[256,1024]{1,0:T(8,128)(2,1)}, bf16[256,1024]{1,0:T(8,128)(2,1)S(1)}, u32[]{:S(2)}, u32[]{:S(2)}) collective-permute-start(bf16[256,1024]{1,0:T(8,128)(2,1)} %get-tuple-element.66), channel_id=1, source_target_pairs={{0,3},{1,0},{2,1},{3,2},{4,7},{5,4},{6,5},{7,6},{8,11},{9,8},{10,9... | collective-permute-start | bytes 1572872 | tf_op jit(solution)/shard_map/ppermute | solution.py:350
  912.9 125.6 %collective-permute-start.59 = (bf16[768,1024]{1,0:T(8,128)(2,1)}, bf16[768,1024]{1,0:T(8,128)(2,1)S(1)}, u32[]{:S(2)}, u32[]{:S(2)}) collective-permute-start(bf16[768,1024]{1,0:T(8,128)(2,1)} %get-tuple-element.71), channel_id=1, source_target_pairs={{3,2},{2,1},{1,0},{7,6},{6,5},{5,4},{11,10},{10,9},{9,8},{15,14},{... | collective-permute-start | bytes 4718600 | tf_op jit(solution)/shard_map/ppermute | solution.py:371
  925.2 113.3 %collective-permute-start.56 = (bf16[768,1024]{1,0:T(8,128)(2,1)S(1)}, bf16[768,1024]{1,0:T(8,128)(2,1)}, u32[]{:S(2)}, u32[]{:S(2)}) collective-permute-start(bf16[768,1024]{1,0:T(8,128)(2,1)S(1)} %add_convert_fusion.2), channel_id=1, source_target_pairs={{0,1},{1,2},{2,3},{4,5},{5,6},{6,7},{8,9},{9,10},{10,11},{12,13},{... | collective-permute-start | bytes 4718600 | tf_op jit(solution)/shard_map/ppermute | solution.py:364
  965.3 32.9 %collective-permute-start.63 = (f32[2,1024]{1,0:T(2,128)S(1)}, f32[2,1024]{1,0:T(2,128)S(1)}, u32[]{:S(2)}, u32[]{:S(2)}) collective-permute-start(f32[2,1024]{1,0:T(2,128)S(1)} %add.455), channel_id=1, source_target_pairs={{0,1},{1,0},{2,3},{3,2},{4,5},{5,4},{6,7},{7,6},{8,9},{9,8},{10,11... | collective-permute-start | bytes 24584 | tf_op jit(solution)/shard_map/ppermute | solution.py:319
  967.4 63.5 %collective-permute-start.42 = (bf16[256,1024]{1,0:T(8,128)(2,1)}, bf16[256,1024]{1,0:T(8,128)(2,1)}, u32[]{:S(2)}, u32[]{:S(2)}) collective-permute-start(bf16[256,1024]{1,0:T(8,128)(2,1)} %get-tuple-element.64), channel_id=1, source_target_pairs={{0,1},{1,2},{2,3},{3,0},{4,5},{5,6},{6,7},{7,4},{8,9},{9,10},{10,1... | collective-permute-start | bytes 1572872 | tf_op jit(solution)/shard_map/ppermute | solution.py:350
  1001.4 31.4 %collective-permute-start.43 = (bf16[256,1024]{1,0:T(8,128)(2,1)}, bf16[256,1024]{1,0:T(8,128)(2,1)}, u32[]{:S(2)}, u32[]{:S(2)}) collective-permute-start(bf16[256,1024]{1,0:T(8,128)(2,1)} %get-tuple-element.64), channel_id=1, source_target_pairs={{0,2},{1,3},{2,0},{3,1},{4,6},{5,7},{6,4},{7,5},{8,10},{9,11},{10,... | collective-permute-start | bytes 1572872 | tf_op jit(solution)/shard_map/ppermute | solution.py:350
  1009.6 27.0 %collective-permute-start.44 = (bf16[256,1024]{1,0:T(8,128)(2,1)}, bf16[256,1024]{1,0:T(8,128)(2,1)}, u32[]{:S(2)}, u32[]{:S(2)}) collective-permute-start(bf16[256,1024]{1,0:T(8,128)(2,1)} %get-tuple-element.64), channel_id=1, source_target_pairs={{0,3},{1,0},{2,1},{3,2},{4,7},{5,4},{6,5},{7,6},{8,11},{9,8},{10,9... | collective-permute-start | bytes 1572872 | tf_op jit(solution)/shard_map/ppermute | solution.py:350
  (54 other events, 1317.3 us)
Sparse Core Ops, SparseCore 0:
  11.2 108.5 all-gather.8
  430.9 46.8 reduce-scatter.2
  482.1 61.7 reduce-scatter.4
  545.6 27.8 all-gather.4
  575.3 45.5 all-gather.6

commit v2 on v1

--- a/solution.py
+++ b/solution.py
@@ -54,6 +54,13 @@
     return pl.BlockSpec(shape, lambda *_: (0,) * len(shape))
 
 
+def after(kernel, inputs, count):
+    return lambda *refs: kernel(*refs[:inputs], *refs[inputs + count :])
+
+
+UNREAD = pl.BlockSpec(memory_space=pl.ANY)
+
+
 def rms_scale(values):
     return lax.rsqrt(jnp.mean(values * values, axis=-1, keepdims=True) + norm_eps)
 
@@ -68,8 +75,31 @@
     )
 
 
-def qkv_kernel(x_ref, gains_ref, w_ref, cos_ref, sin_ref, q_ref, k_ref, v_ref):
+def cast_kernel(rank_ref, held_ref, slot_ref, tile_ref, low_ref, mine_ref):
+    low_ref[...] = slot_ref[...].astype(bf16)
+    tile = tile_ref[...].astype(bf16)
+    held = held_ref[pl.program_id(0)] > 0
+    mine_ref[...] = jnp.where(held, tile, jnp.zeros((), bf16))
+
+
+def qkv_kernel(
+    x_ref, gains_ref, tiles_ref, cos_ref, sin_ref, q_ref, k_ref, v_ref, w_ref, w_wide
+):
     width = q_ref.shape[1]
+    model = x_ref.shape[1]
+    fold = model // width
+
+    @pl.when(pl.program_id(0) == 0)
+    def _():
+        for block in range(3 * width // 128):
+            part, lane = divmod(block * 128, width)
+            for piece in range(fold):
+                at = piece * width + lane
+                w_wide[block, pl.ds(piece, width, stride=fold), :] = tiles_ref[
+                    part * width : (part + 1) * width, at : at + 128
+                ].astype(f32)
+            w_ref[:, block * 128 : (block + 1) * 128] = w_wide[block].astype(bf16)
+
     x = x_ref[...].astype(f32)
     hidden = (x * rms_scale(x) * gains_ref[0:1, :]).astype(bf16)
     cos, sin = cos_ref[...], sin_ref[...]
@@ -118,8 +148,25 @@
     parts, xm_ref, cot_ref, gains_ref, wg_ref, wu_ref, wd_ref, *refs
 ):
     o_refs, wo_refs = refs[:parts], refs[parts : 2 * parts]
-    rm_ref, dhf_ref, gg_ref, gu_ref, gd_ref, hf_ref, acc_ref = refs[2 * parts :]
+    rm_ref, dhf_ref, grad_ref, hf_ref, acc_ref, wide_ref = refs[2 * parts :]
     step = pl.program_id(0)
+    width = wg_ref.shape[1]
+    cols = pl.ds(pl.multiple_of(step * width, width), width)
+    hidden, model = grad_ref.shape[1:]
+    fold = model // hidden
+
+    def put(part, grad):
+        if fold == 1:
+            grad_ref[part, :, cols] = grad.astype(bf16)
+            return
+        for block in range(width // 128):
+            wide_ref[block] = grad[:, block * 128 : (block + 1) * 128]
+            for piece in range(fold):
+                at = piece * hidden + step * width + block * 128
+                at = pl.ds(pl.multiple_of(at, 128), 128)
+                grad_ref[part, :, at] = wide_ref[
+                    block, pl.ds(piece, hidden, stride=fold), :
+                ].astype(bf16)
 
     @pl.when(step == 0)
     def _():
@@ -135,12 +182,12 @@
     g, u = mm(hf, wg), mm(hf, wu)
     sig = jax.nn.sigmoid(g)
     act = (g * sig * u).astype(bf16)
-    gd_ref[...] = mm_tn(act, dy).astype(bf16)
+    grad_ref[2, cols, :] = mm_tn(act, dy).astype(bf16)
     da = mm_nt(dy, wd)
     dg = (da * u * sig * (1.0 + g * (1.0 - sig))).astype(bf16)
     du = (da * g * sig).astype(bf16)
-    gg_ref[...] = mm_tn(hf, dg).astype(bf16)
-    gu_ref[...] = mm_tn(hf, du).astype(bf16)
+    put(0, mm_tn(hf, dg))
+    put(1, mm_tn(hf, du))
     acc_ref[...] += mm_nt(dg, wg) + mm_nt(du, wu)
 
     @pl.when(step == pl.num_programs(0) - 1)
@@ -148,9 +195,13 @@
         dhf_ref[...] = acc_ref[...].astype(bf16)
 
 
+def far_start(place, parts, share):
+    return jnp.where(place < parts // 2, share, 0)
+
+
 def ffn_kernel(parts, place_ref, x_ref, gains_ref, wg_ref, wu_ref, wd_ref, *refs):
     o_refs, wo_refs = refs[:parts], refs[parts : 2 * parts]
-    part_ref, own_ref, r_ref, hf_ref, acc_ref = refs[2 * parts :]
+    part_ref, ship_ref, own_ref, r_ref, hf_ref, acc_ref = refs[2 * parts :]
     step = pl.program_id(0)
 
     @pl.when(step == 0)
@@ -169,8 +220,10 @@
 
     @pl.when(step == pl.num_programs(0) - 1)
     def _():
+        share = own_ref.shape[0]
         part_ref[...] = acc_ref[...].astype(bf16)
-        share = own_ref.shape[0]
+        far = pl.ds(pl.multiple_of(far_start(place_ref[0], parts, share), share), ship_ref.shape[0])
+        ship_ref[...] = part_ref[far, :]
         mine = pl.ds(pl.multiple_of(place_ref[0] * share, share), share)
         own_ref[...] = r_ref[mine, :] + acc_ref[mine, :]
 
@@ -195,12 +248,12 @@
     drm_ref,
     dha_ref,
     gw_ref,
-    go_ref,
     gain_ref,
     gw_acc,
     go_acc,
     gain_acc,
     flow_ref,
+    gw_wide,
 ):
     step = pl.program_id(0)
 
@@ -269,21 +322,33 @@
     na = x * rms_scale(x)
     dha = mm_nt(flow, w_ref[...])
     gain_acc[0:1, :] += jnp.sum(dha * na, axis=0, keepdims=True)
-    dha_ref[...] = dha.astype(bf16)
+    cuts, shares, rows = dha_ref.shape[:3]
+    for piece in range(window // rows):
+        block = step * (window // rows) + piece
+        dha_ref[block % cuts, block // cuts] = dha[piece * rows : (piece + 1) * rows].astype(bf16)
     gw_acc[...] += mm_tn((na * gains_ref[0:1, :]).astype(bf16), flow)
 
     @pl.when(step == pl.num_programs(0) - 1)
     def _():
-        gw_ref[...] = gw_acc[...].astype(bf16)
-        go_ref[...] = go_acc[...].astype(bf16)
+        fold = gw_acc.shape[0] // width
+        for block in range(3 * width // 128):
+            part, lane = divmod(block * 128, width)
+            gw_wide[block] = gw_acc[:, block * 128 : (block + 1) * 128]
+            for piece in range(fold):
+                at = piece * width + lane
+                gw_ref[part * width : (part + 1) * width, at : at + 128] = gw_wide[
+                    block, pl.ds(piece, width, stride=fold), :
+                ].astype(bf16)
+        gw_ref[3 * width :, :] = go_acc[...].astype(bf16)
         gain_ref[...] = gain_acc[...]
 
 
 def input_grad_kernel(
-    place_ref, rows_ref, drm_ref, gains_ref, x_ref, part_ref, up_ref, down_ref, out_ref
+    cut, place_ref, rows_ref, drm_ref, gains_ref, x_ref, part_ref, *refs
 ):
+    out_ref = refs[-1]
     block, count = x_ref.shape[0], drm_ref.shape[0]
-    base = place_ref[0] * (pl.num_programs(0) * block) + pl.program_id(0) * block
+    base = (place_ref[0] * cut[1] + cut[0]) * block
     spread = (
         lax.broadcasted_iota(jnp.int32, (block, count), 0) + base == rows_ref[...]
     ).astype(bf16)
@@ -294,24 +359,250 @@
     x = x_ref[...].astype(f32)
     sa = rms_scale(x)
     na = x * sa
-    dha = part_ref[...].astype(f32) + up_ref[...].astype(f32) + down_ref[...].astype(f32)
+    dha = part_ref[0, 0].astype(f32)
+    for ref in refs[: cut[2]]:
+        dha = dha + ref[...].astype(f32)
     dna = dha * gains_ref[0:1, :]
     out = dr + sa * (dna - na * jnp.mean(dna * na, axis=-1, keepdims=True))
     out_ref[...] = out.astype(bf16)
 
 
-def collect_kernel(slot_ref, first, slots_ref, out_ref, sems):
-    count = out_ref.shape[0]
-
-    def copy(index):
+def input_grad_rows(dha, x, dr, gain, spread):
+    high = dr.astype(bf16)
+    low = (dr - high.astype(f32)).astype(bf16)
+    dr = mm(spread, high) + mm(spread, low)
+    sa = rms_scale(x)
+    na = x * sa
+    dna = dha * gain
+    return dr + sa * (dna - na * jnp.mean(dna * na, axis=-1, keepdims=True))
+
+
+def remote(src, dst, send, recv, place):
+    return pltpu.make_async_remote_copy(
+        src_ref=src,
+        dst_ref=dst,
+        send_sem=send,
+        recv_sem=recv,
+        device_id={"tensor": place},
+        device_id_type=pl.DeviceIdType.MESH,
+    )
+
+
+def greet_line(place):
+    barrier = pltpu.get_barrier_semaphore()
+    for k in range(1, 4):
+        pl.semaphore_signal(
+            barrier,
+            inc=1,
+            device_id={"tensor": lax.rem(place + k, 4)},
+            device_id_type=pl.DeviceIdType.MESH,
+        )
+    pl.semaphore_wait(barrier, 3)
+
+
+def rows_ref(ref, index, share, count):
+    return ref.at[pl.ds(pl.multiple_of(index * share, share), count * share), :]
+
+
+def lines_kernel(
+    cuts, windows, order, rows_in, drm_ref, gains_ref, x_ref, dha_ref, *refs
+):
+    part_refs, own_refs = refs[:windows], refs[windows : 2 * windows]
+    (
+        out_ref,
+        grad_ref,
+        ra,
+        rb,
+        rc,
+        value,
+        own,
+        piece,
+        x_rows,
+        grad,
+        a_send,
+        a_recv,
+        b_send,
+        b_recv,
+        c_send,
+        c_recv,
+        g_send,
+        g_recv,
+        v_sem,
+        o_sem,
+        x_sem,
+        l_sem,
+        i_sem,
+    ) = refs[2 * windows :]
+    place = lax.axis_index("tensor")
+    lower = place < 2
+    outer = (place == 0) | (place == 3)
+    inner = (place == 1) | (place == 2)
+    share = rc.shape[1]
+    folds = len(order)
+
+    def whole(f):
+        kind, index = order[f]
+        return part_refs[index] if kind == 0 else dha_ref.at[index]
+
+    def copy_a(f):
+        far = rows_ref(whole(f), jnp.where(lower, 1, 0), share, 3)
+        return remote(far, ra.at[f], a_send.at[f], a_recv.at[f], jnp.where(lower, 1, 2))
+
+    def copy_b(f):
+        src = rows_ref(ra.at[f], jnp.where(lower, 1, 0), share, 2)
+        return remote(src, rb.at[f], b_send.at[f], b_recv.at[f], jnp.where(lower, 2, 1))
+
+    def copy_c(f):
+        src = rows_ref(rb.at[f], jnp.where(lower, 0, 1), share, 1)
+        return remote(src, rc.at[f], c_send.at[f], c_recv.at[f], jnp.where(lower, 0, 3))
+
+    def load(f):
+        return pltpu.make_async_copy(whole(f), value.at[f], v_sem.at[f])
+
+    def load_own(w):
+        return pltpu.make_async_copy(own_refs[w], own.at[w], o_sem.at[w])
+
+    def copy_g(w, k, origin):
+        rows = pl.ds(pl.multiple_of(w * 4 * share + origin * share, share), share)
+        return remote(
+            piece.at[w],
+            out_ref.at[rows, :],
+            g_send.at[w, k - 1],
+            g_recv.at[w, k - 1],
+            lax.rem(place + k, 4),
+        )
+
+    def keep(w):
+        rows = pl.ds(pl.multiple_of(w * 4 * share + place * share, share), share)
+        return pltpu.make_async_copy(piece.at[w], out_ref.at[rows, :], l_sem.at[w])
+
+    def store(c):
         return pltpu.make_async_copy(
-            slots_ref.at[slot_ref[first + index]], out_ref.at[index], sems.at[index]
+            grad.at[c], grad_ref.at[pl.ds(c * share, share), :], i_sem.at[c]
         )
 
-    for index in range(count):
-        copy(index).start()
-    for index in range(count):
-        copy(index).wait()
+    x_load = pltpu.make_async_copy(
+        rows_ref(x_ref, place * cuts, share, cuts), x_rows, x_sem
+    )
+
+    for f in range(folds):
+        load(f).start()
+    for w in range(windows):
+        load_own(w).start()
+    x_load.start()
+    greet_line(place)
+
+    @pl.when(outer)
+    def _():
+        for f in range(2):
+            copy_a(f).start()
+
+    def add_rows(buffer, at, f, index):
+        rows = pl.ds(pl.multiple_of(at * share, share), share)
+        mine = pl.ds(pl.multiple_of(index * share, share), share)
+        total = buffer[f, rows, :].astype(f32) + value[f, mine, :].astype(f32)
+        buffer[f, rows, :] = total.astype(bf16)
+
+    def finish(f, terms):
+        kind, index = order[f]
+        if kind == 0:
+            load_own(index).wait()
+            total = own[index]
+        else:
+            mine = pl.ds(pl.multiple_of(place * share, share), share)
+            total = value[f, mine, :].astype(f32)
+        for term in terms:
+            total = total + term.astype(f32)
+        if kind == 0:
+            piece[index] = total.astype(bf16)
+            for k in range(1, 4):
+                copy_g(index, k, place).start()
+            keep(index).start()
+        else:
+            first = place * (cuts * share) + index * share
+            count = drm_ref.shape[0]
+            spread = (
+                lax.broadcasted_iota(jnp.int32, (share, count), 0) + first == rows_in[...]
+            ).astype(bf16)
+            x = x_rows[pl.ds(index * share, share), :].astype(f32)
+            grad[index] = input_grad_rows(
+                total, x, drm_ref[...], gains_ref[0:1, :], spread
+            ).astype(bf16)
+            store(index).start()
+
+    for f in range(folds):
+        load(f).wait()
+    x_load.wait()
+    for step in range(folds + 1):
+
+        @pl.when(inner)
+        def _():
+            if step < folds:
+                copy_a(step).wait_recv()
+                for n in range(2):
+                    add_rows(
+                        ra, jnp.where(lower, 1, 0) + n, step, jnp.where(lower, 2, 0) + n
+                    )
+                copy_b(step).start()
+            if step > 0:
+                f = step - 1
+                copy_b(f).wait_recv()
+                add_rows(rb, jnp.where(lower, 0, 1), f, jnp.where(lower, 0, 3))
+                copy_c(f).start()
+
+        if step > 0:
+            f = step - 1
+
+            @pl.when(outer)
+            def _():
+                copy_c(f).wait_recv()
+                finish(f, [rc[f]])
+
+            @pl.when(inner)
+            def _():
+                sel_a = pl.ds(pl.multiple_of(jnp.where(lower, 0, 2) * share, share), share)
+                sel_b = pl.ds(pl.multiple_of(jnp.where(lower, 1, 0) * share, share), share)
+                finish(f, [ra[f, sel_a, :], rb[f, sel_b, :]])
+
+        @pl.when(outer)
+        def _():
+            if step < folds:
+                copy_a(step).wait_send()
+            if step + 2 < folds:
+                copy_a(step + 2).start()
+
+    @pl.when(inner)
+    def _():
+        for f in range(folds):
+            copy_b(f).wait_send()
+            copy_c(f).wait_send()
+
+    for w in range(windows):
+        keep(w).wait()
+        for k in range(1, 4):
+            copy_g(w, k, place).wait_send()
+            copy_g(w, k, lax.rem(place + 4 - k, 4)).wait_recv()
+    for c in range(cuts):
+        store(c).wait()
+
+
+def place_kernel(place_ref, *refs):
+    out_ref = refs[-1]
+    parts = lax.axis_size("tensor")
+    share = refs[0].shape[0]
+    for step in range(parts):
+        origin = lax.rem(place_ref[0] + parts - step, parts)
+        out_ref[pl.ds(pl.multiple_of(origin * share, share), share), :] = refs[step][...]
+
+
+def copy_kernel(in_ref, out_ref):
+    out_ref[...] = in_ref[...]
+
+
+def collect_kernel(slot_ref, *refs):
+    out_ref = refs[-1]
+    for index, ref in enumerate(refs[:-1]):
+        out_ref[index] = ref[0]
 
 
 def exchange(value, axis, bit):
@@ -352,28 +643,34 @@
     ]
 
 
-def chain_sums(value, share):
-    size = lax.axis_size("tensor")
+def rows_at(value, index, share, count):
+    return lax.dynamic_slice_in_dim(value, index * share, count * share, 0)
+
+
+def line_sums(value, ship, share):
     place = lax.axis_index("tensor")
-    up = down = None
-    for step in range(size - 1):
-        index = jnp.minimum(size - 1 - step + place, size - 1)
-        send = lax.dynamic_slice_in_dim(value, index * share, share, 0)
-        if up is not None:
-            send = (send.astype(f32) + up.astype(f32)).astype(bf16)
-        up = lax.ppermute(
-            send, "tensor", [(i, i + 1) for i in range(min(step, size - 2) + 1)]
-        )
-        index = jnp.maximum(place - (size - 1 - step), 0)
-        send = lax.dynamic_slice_in_dim(value, index * share, share, 0)
-        if down is not None:
-            send = (send.astype(f32) + down.astype(f32)).astype(bf16)
-        down = lax.ppermute(
-            send,
-            "tensor",
-            [(size - 1 - i, size - 2 - i) for i in range(min(step, size - 2) + 1)],
-        )
-    return up, down
+    lower = place < 2
+    first = lax.ppermute(ship, "tensor", [(0, 1), (3, 2)])
+    send = rows_at(value, jnp.where(lower, 2, 0), share, 2).astype(f32)
+    send = send + rows_at(first, jnp.where(lower, 1, 0), share, 2).astype(f32)
+    second = lax.ppermute(send.astype(bf16), "tensor", [(1, 2), (2, 1)])
+    send = rows_at(value, jnp.where(lower, 0, 3), share, 1).astype(f32)
+    send = send + rows_at(second, jnp.where(lower, 0, 1), share, 1).astype(f32)
+    third = lax.ppermute(send.astype(bf16), "tensor", [(1, 0), (2, 3)])
+    return (
+        rows_at(first, jnp.where(lower, 0, 2), share, 1),
+        rows_at(second, jnp.where(lower, 1, 0), share, 1),
+        third,
+    )
+
+
+def other_sums(value, ship, share):
+    if lax.axis_size("tensor") == 4:
+        return line_sums(value, ship, share)
+    place = lax.axis_index("tensor")
+    total = lax.psum_scatter(value, "tensor", scatter_dimension=0, tiled=True)
+    own = rows_at(value, place, share, 1).astype(f32)
+    return (total.astype(f32) - own,)
 
 
 def small_total(value):
@@ -454,35 +751,51 @@
     slot_used = jnp.any(slot_match, axis=1)[:, None, None]
     slot_tile = jnp.argmax(slot_match, axis=1)
 
-    low_slots = master[0].astype(bf16)
-    held = (owner_row[:attn_tiles] == owner_self)[:, None, None]
-    attn_mine = jnp.where(held, low_slots[slot_rank[:attn_tiles]], jnp.zeros((), bf16))
-    attn_flat = dp_total(attn_mine).reshape(4, -1)
-    w_qkv = jnp.concatenate(
-        [attn_flat[i].reshape(model, width) for i in range(3)], axis=1
-    )
-    w_out = attn_flat[3].reshape(width, model)
-    every_slot = lax.all_gather(low_slots, "dp", axis=0, tiled=True)
-    ffn_all = pl.pallas_call(
-        lambda slot_ref, slots_ref, out_ref, sems: collect_kernel(
-            slot_ref, attn_tiles, slots_ref, out_ref, sems
-        ),
-        out_shape=jax.ShapeDtypeStruct((ffn_tiles, tile_rows, model), bf16),
+    tile_block = (1, tile_rows, model)
+    grid_size = max(capacity, attn_tiles)
+    low_slots, attn_mine = pl.pallas_call(
+        cast_kernel,
+        out_shape=[
+            jax.ShapeDtypeStruct((capacity, tile_rows, model), bf16),
+            jax.ShapeDtypeStruct((attn_tiles, tile_rows, model), bf16),
+        ],
         grid_spec=pltpu.PrefetchScalarGridSpec(
-            num_scalar_prefetch=1,
-            grid=(1,),
-            in_specs=[pl.BlockSpec(memory_space=pl.ANY)],
-            out_specs=pl.BlockSpec(memory_space=pl.ANY),
-            scratch_shapes=[pltpu.SemaphoreType.DMA((ffn_tiles,))],
+            num_scalar_prefetch=2,
+            grid=(grid_size,),
+            in_specs=[
+                pl.BlockSpec(
+                    tile_block, lambda i, rank, held: (jnp.minimum(i, capacity - 1), 0, 0)
+                ),
+                pl.BlockSpec(
+                    tile_block,
+                    lambda i, rank, held: (rank[jnp.minimum(i, attn_tiles - 1)], 0, 0),
+                ),
+            ],
+            out_specs=[
+                pl.BlockSpec(
+                    tile_block, lambda i, rank, held: (jnp.minimum(i, capacity - 1), 0, 0)
+                ),
+                pl.BlockSpec(
+                    tile_block, lambda i, rank, held: (jnp.minimum(i, attn_tiles - 1), 0, 0)
+                ),
+            ],
         ),
         compiler_params=params(),
-        cost_estimate=cost(0, 2 * ffn_tiles * tile_size * 2),
-        name="collect",
-    )(slot_index, every_slot)
-    ffn_flat = ffn_all.reshape(3, -1)
-    w_gate = ffn_flat[0].reshape(model, hidden)
-    w_up = ffn_flat[1].reshape(model, hidden)
-    w_down = ffn_flat[2].reshape(hidden, model)
+        cost_estimate=cost(0, 12 * capacity * tile_size),
+        name="cast",
+    )(
+        slot_rank,
+        jnp.pad(
+            (owner_row[:attn_tiles] == owner_self).astype(jnp.int32),
+            (0, grid_size - attn_tiles),
+            mode="edge",
+        ),
+        master[0],
+        master[0],
+    )
+    attn_flat = dp_total(attn_mine).reshape(4 * width, model)
+    w_out = attn_flat[3 * width :]
+    every_slot = lax.all_gather(low_slots, "dp", axis=0, tiled=True)
     w_outs = around(w_out)
 
     cos, sin = head_tables(jnp.arange(window), heads)
@@ -498,22 +811,24 @@
     row_block = pl.BlockSpec((block, model), lambda i: (i, 0))
     head_block = pl.BlockSpec((block, width), lambda i: (i, 0))
     table_block = pl.BlockSpec((block, width), lambda i: (i % per_window, 0))
-    q, k, v = pl.pallas_call(
+    q, k, v, w_qkv = pl.pallas_call(
         qkv_kernel,
-        out_shape=[jax.ShapeDtypeStruct((total_rows, width), bf16)] * 3,
+        out_shape=[jax.ShapeDtypeStruct((total_rows, width), bf16)] * 3
+        + [jax.ShapeDtypeStruct((model, 3 * width), bf16)],
         grid=(total_rows // block,),
         in_specs=[
             row_block,
             whole_spec((2, model)),
-            whole_spec((model, 3 * width)),
+            whole_spec((3 * width, model)),
             table_block,
             table_block,
         ],
-        out_specs=[head_block] * 3,
+        out_specs=[head_block] * 3 + [whole_spec((model, 3 * width))],
+        scratch_shapes=[pltpu.VMEM((3 * width // 128, model, 128), f32)],
         compiler_params=params(),
         cost_estimate=cost(6 * total_rows * model * width, 2 * total_rows * model * 2),
         name="qkv",
-    )(tokens, norm_gains, w_qkv, cos, sin)
+    )(tokens, norm_gains, attn_flat, cos, sin)
 
     win_model = pl.BlockSpec((window, model), lambda i: (i, 0))
     win_head = pl.BlockSpec((window, width), lambda i: (i, 0))
@@ -545,15 +860,16 @@
 
     q_block = min(256, window)
 
-    def attend_window(w):
+    def attend_window(w, before):
         return pl.pallas_call(
-            attend_kernel,
+            after(attend_kernel, 3, 1),
             out_shape=jax.ShapeDtypeStruct((window, width), bf16),
             grid=(width // 128, window // q_block),
             in_specs=[
                 pl.BlockSpec((q_block, 128), lambda p, i: (w * (window // q_block) + i, p)),
                 pl.BlockSpec((window, 128), lambda p, i: (w, p)),
                 pl.BlockSpec((window, 128), lambda p, i: (w, p)),
+                UNREAD,
             ],
             out_specs=pl.BlockSpec((q_block, 128), lambda p, i: (i, p)),
             compiler_params=params(),
@@ -561,22 +877,49 @@
                 16 * window * window * width, 4 * window * width * 2, window * window * heads
             ),
             name="attend",
-        )(q, k, v)
-
-    windows_o = [around(attend_window(w)) for w in range(seq_count)]
+        )(q, k, v, before)
+
+    early = max(seq_count - 1, 1)
+    o_own = []
+    for w in range(early):
+        o_own.append(attend_window(w, o_own[-1] if o_own else o_m))
+
+    group = 4
+    ffn_all = pl.pallas_call(
+        after(collect_kernel, 1 + group, 1),
+        out_shape=jax.ShapeDtypeStruct((ffn_tiles, tile_rows, model), bf16),
+        grid_spec=pltpu.PrefetchScalarGridSpec(
+            num_scalar_prefetch=1,
+            grid=(ffn_tiles // group,),
+            in_specs=[
+                pl.BlockSpec(
+                    tile_block,
+                    lambda i, slot, n=n: (slot[attn_tiles + i * group + n], 0, 0),
+                )
+                for n in range(group)
+            ]
+            + [UNREAD],
+            out_specs=pl.BlockSpec((group, tile_rows, model), lambda i, slot: (i, 0, 0)),
+        ),
+        compiler_params=params(),
+        cost_estimate=cost(0, 4 * ffn_tiles * tile_size),
+        name="collect",
+    )(slot_index, *[every_slot] * group, o_own[-1])
+    ffn_flat = ffn_all.reshape(3, -1)
+    w_gate = ffn_flat[0].reshape(model, hidden)
+    w_up = ffn_flat[1].reshape(model, hidden)
+    w_down = ffn_flat[2].reshape(hidden, model)
 
     mask_rows = seq_count * count
     cols = min(256, hidden)
     col_block = pl.BlockSpec((model, cols), lambda c: (0, c))
     down_block = pl.BlockSpec((cols, model), lambda c: (c, 0))
-    r_m, dhf_part, g_gate, g_up, g_down = pl.pallas_call(
+    r_m, dhf_part, ffn_grad = pl.pallas_call(
         functools.partial(ffn_masked_kernel, parts),
         out_shape=[
             jax.ShapeDtypeStruct((mask_rows, model), f32),
             jax.ShapeDtypeStruct((mask_rows, model), bf16),
-            jax.ShapeDtypeStruct((model, hidden), bf16),
-            jax.ShapeDtypeStruct((model, hidden), bf16),
-            jax.ShapeDtypeStruct((hidden, model), bf16),
+            jax.ShapeDtypeStruct((3, hidden, model), bf16),
         ],
         grid=(hidden // cols,),
         in_specs=[
@@ -592,13 +935,12 @@
         out_specs=[
             whole_spec((mask_rows, model)),
             whole_spec((mask_rows, model)),
-            col_block,
-            col_block,
-            down_block,
+            whole_spec((3, hidden, model)),
         ],
         scratch_shapes=[
             pltpu.VMEM((mask_rows, model), bf16),
             pltpu.VMEM((mask_rows, model), f32),
+            pltpu.VMEM((cols // 128, model, 128), f32),
         ],
         compiler_params=params(),
         cost_estimate=cost(
@@ -606,6 +948,10 @@
         ),
         name="ffn_masked",
     )(x_m, cot, norm_gains, w_gate, w_up, w_down, *o_ms, *w_outs)
+
+    for w in range(early, seq_count):
+        o_own.append(attend_window(w, r_m))
+    windows_o = [around(o) for o in o_own]
 
     share_m = mask_rows // parts
     dhf_mine = lax.dynamic_slice_in_dim(dhf_part, place * share_m, share_m, 0).astype(f32)
@@ -622,23 +968,92 @@
         origin = lax.rem(place + parts - step, parts)
         dhf = lax.dynamic_update_slice_in_dim(dhf, piece, origin * share_m, 0)
 
-    def total_tiles(tiles):
-        piece = lax.psum_scatter(tiles, "dp", scatter_dimension=0, tiled=True)
-        return lax.all_gather(piece, "dp", axis=0, tiled=True)
-
-    ffn_grads = total_tiles(
-        jnp.concatenate(
-            [g.reshape(-1, model) for g in (g_gate, g_up, g_down)], axis=0
+    share = window // parts
+    far = share * (parts - 1)
+    layer_out = None
+
+    def ffn_window(w, before):
+        return pl.pallas_call(
+            after(functools.partial(ffn_kernel, parts), 6 + 2 * parts, 1),
+            out_shape=[
+                jax.ShapeDtypeStruct((window, model), bf16),
+                jax.ShapeDtypeStruct((far, model), bf16),
+                jax.ShapeDtypeStruct((share, model), f32),
+            ],
+            grid_spec=pltpu.PrefetchScalarGridSpec(
+                num_scalar_prefetch=1,
+                grid=(hidden // cols,),
+                in_specs=[
+                    pl.BlockSpec((window, model), lambda c, place_ref: (w, 0)),
+                    whole_spec((2, model)),
+                    pl.BlockSpec((model, cols), lambda c, place_ref: (0, c)),
+                    pl.BlockSpec((model, cols), lambda c, place_ref: (0, c)),
+                    pl.BlockSpec((cols, model), lambda c, place_ref: (c, 0)),
+                ]
+                + [whole_spec((window, width))] * parts
+                + [whole_spec((width, model))] * parts
+                + [UNREAD],
+                out_specs=[
+                    whole_spec((window, model)),
+                    whole_spec((far, model)),
+                    whole_spec((share, model)),
+                ],
+                scratch_shapes=[
+                    pltpu.VMEM((window, model), f32),
+                    pltpu.VMEM((window, model), bf16),
+                    pltpu.VMEM((window, model), f32),
+                ],
+            ),
+            compiler_params=params(),
+            cost_estimate=cost(
+                window * model * (6 * hidden + 2 * model), 16e6, window * hidden
+            ),
+            name="ffn",
+        )(
+            place_ref,
+            tokens,
+            norm_gains,
+            w_gate,
+            w_up,
+            w_down,
+            *windows_o[w],
+            *w_outs,
+            before,
         )
-    )
-
-    dr_m, dha, g_qkv, g_out, gains_part = pl.pallas_call(
-        attn_back_kernel,
+
+    def place_window(w, part, ship, own):
+        terms = other_sums(part, ship, share)
+        total = own
+        for term in terms:
+            total = total + term.astype(f32)
+        pieces = around(total.astype(bf16))
+        return pl.pallas_call(
+            after(place_kernel, 1 + parts, 0 if layer_out is None else 1),
+            out_shape=jax.ShapeDtypeStruct((total_rows, model), bf16),
+            grid_spec=pltpu.PrefetchScalarGridSpec(
+                num_scalar_prefetch=1,
+                grid=(1,),
+                in_specs=[whole_spec((share, model))] * parts
+                + [UNREAD] * (layer_out is not None),
+                out_specs=pl.BlockSpec((window, model), lambda i, place_ref: (w, 0)),
+            ),
+            input_output_aliases={} if layer_out is None else {1 + parts: 0},
+            compiler_params=params(),
+            cost_estimate=cost(0, 4 * window * model),
+            name="place",
+        )(place_ref, *pieces, *([] if layer_out is None else [layer_out]))
+
+    parts_out = [ffn_window(0, o_own[-1])]
+
+    share_rows = total_rows // parts
+    cuts = seq_count if share_rows % (16 * seq_count) == 0 else 1
+    cut_rows = share_rows // cuts
+    dr_m, dha, attn_grad, gains_part = pl.pallas_call(
+        after(attn_back_kernel, 16, 1),
         out_shape=[
             jax.ShapeDtypeStruct((mask_rows, model), f32),
-            jax.ShapeDtypeStruct((total_rows, model), bf16),
-            jax.ShapeDtypeStruct((model, 3 * width), bf16),
-            jax.ShapeDtypeStruct((width, model), bf16),
+            jax.ShapeDtypeStruct((cuts, parts, cut_rows, model), bf16),
+            jax.ShapeDtypeStruct((4 * width, model), bf16),
             jax.ShapeDtypeStruct((2, model), f32),
         ],
         grid=(seq_count,),
@@ -659,12 +1074,12 @@
             whole_spec((window, width)),
             whole_spec((width, model)),
             whole_spec((model, 3 * width)),
+            UNREAD,
         ],
         out_specs=[
             mask_model,
-            win_model,
-            whole_spec((model, 3 * width)),
-            whole_spec((width, model)),
+            whole_spec((cuts, parts, cut_rows, model)),
+            whole_spec((4 * width, model)),
             whole_spec((2, model)),
         ],
         scratch_shapes=[
@@ -672,6 +1087,7 @@
             pltpu.VMEM((width, model), f32),
             pltpu.VMEM((2, model), f32),
             pltpu.VMEM((window, 3 * width), bf16),
+            pltpu.VMEM((3 * width // 128, model, 128), f32),
         ],
         compiler_params=params(),
         cost_estimate=cost(
@@ -695,82 +1111,106 @@
         sin,
         w_out,
         w_qkv,
-    )
-
-    share_rows = total_rows // parts
-    dha_up, dha_down = chain_sums(dha, share_rows)
-    out_block = share_rows // 3 if share_rows % 3 == 0 else share_rows
+        parts_out[0][0],
+    )
+
+    for w in range(1, seq_count):
+        parts_out.append(ffn_window(w, gains_part if w == 1 else parts_out[-1][0]))
+
     flat_rows = jnp.where(
         rows >= 0, rows + window * jnp.arange(seq_count, dtype=jnp.int32)[:, None], -1
     ).reshape(1, mask_rows)
-    blocks = share_rows // out_block
-    here = pl.BlockSpec((out_block, model), lambda i, place_ref: (i, 0))
-    there = pl.BlockSpec(
-        (out_block, model), lambda i, place_ref: (place_ref[0] * blocks + i, 0)
-    )
-    input_grad = pl.pallas_call(
-        input_grad_kernel,
-        out_shape=jax.ShapeDtypeStruct((share_rows, model), bf16),
-        grid_spec=pltpu.PrefetchScalarGridSpec(
-            num_scalar_prefetch=1,
-            grid=(blocks,),
-            in_specs=[
-                whole_spec((1, mask_rows)),
-                whole_spec((mask_rows, model)),
-                whole_spec((2, model)),
-                there,
-                there,
-                here,
-                here,
+    if parts == 4 and cut_rows == share:
+        order = [(kind, i) for i in range(seq_count) for kind in (0, 1)]
+        folds = len(order)
+        anywhere = pl.BlockSpec(memory_space=pl.ANY)
+        inside = pl.BlockSpec(memory_space=pltpu.VMEM)
+        dma = pltpu.SemaphoreType.DMA
+        layer_out, input_grad = pl.pallas_call(
+            functools.partial(lines_kernel, cuts, seq_count, order),
+            out_shape=[
+                jax.ShapeDtypeStruct((total_rows, model), bf16),
+                jax.ShapeDtypeStruct((share_rows, model), bf16),
             ],
-            out_specs=here,
-        ),
-        compiler_params=params(),
-        cost_estimate=cost(4 * share_rows * mask_rows * model, 10e6),
-        name="input_grad",
-    )(place_ref, flat_rows, dr_m, norm_gains, tokens, dha, dha_up, dha_down)
-
-    share = window // parts
-    layer_out = jnp.zeros((total_rows, model), bf16)
-    for w in range(seq_count):
-        part, own = pl.pallas_call(
-            functools.partial(ffn_kernel, parts),
-            out_shape=[
-                jax.ShapeDtypeStruct((window, model), bf16),
-                jax.ShapeDtypeStruct((share, model), f32),
+            in_specs=[inside] * 3 + [anywhere] * (2 + 2 * seq_count),
+            out_specs=[anywhere] * 2,
+            scratch_shapes=[
+                pltpu.VMEM((folds, 3 * share, model), bf16),
+                pltpu.VMEM((folds, 2 * share, model), bf16),
+                pltpu.VMEM((folds, share, model), bf16),
+                pltpu.VMEM((folds, window, model), bf16),
+                pltpu.VMEM((seq_count, share, model), f32),
+                pltpu.VMEM((seq_count, share, model), bf16),
+                pltpu.VMEM((share_rows, model), bf16),
+                pltpu.VMEM((cuts, share, model), bf16),
+                dma((folds,)),
+                dma((folds,)),
+                dma((folds,)),
+                dma((folds,)),
+                dma((folds,)),
+                dma((folds,)),
+                dma((seq_count, 3)),
+                dma((seq_count, 3)),
+                dma((folds,)),
+                dma((seq_count,)),
+                dma,
+                dma((seq_count,)),
+                dma((cuts,)),
             ],
-            grid_spec=pltpu.PrefetchScalarGridSpec(
-                num_scalar_prefetch=1,
-                grid=(hidden // cols,),
-                in_specs=[
-                    pl.BlockSpec((window, model), lambda c, place_ref, w=w: (w, 0)),
-                    whole_spec((2, model)),
-                    pl.BlockSpec((model, cols), lambda c, place_ref: (0, c)),
-                    pl.BlockSpec((model, cols), lambda c, place_ref: (0, c)),
-                    pl.BlockSpec((cols, model), lambda c, place_ref: (c, 0)),
-                ]
-                + [whole_spec((window, width))] * parts
-                + [whole_spec((width, model))] * parts,
-                out_specs=[whole_spec((window, model)), whole_spec((share, model))],
-                scratch_shapes=[
-                    pltpu.VMEM((window, model), f32),
-                    pltpu.VMEM((window, model), bf16),
-                    pltpu.VMEM((window, model), f32),
-                ],
-            ),
-            compiler_params=params(),
-            cost_estimate=cost(
-                window * model * (6 * hidden + 2 * model), 16e6, window * hidden
-            ),
-            name="ffn",
-        )(place_ref, tokens, norm_gains, w_gate, w_up, w_down, *windows_o[w], *w_outs)
-        up, down = chain_sums(part, share)
-        piece = (own + up.astype(f32) + down.astype(f32)).astype(bf16)
-        for step, got in enumerate(around(piece)):
-            origin = lax.rem(place + parts - step, parts)
-            layer_out = lax.dynamic_update_slice_in_dim(
-                layer_out, got, w * window + origin * share, 0
-            )
+            compiler_params=params(collective_id=1, has_side_effects=True),
+            cost_estimate=cost(4 * share_rows * mask_rows * model, 60e6),
+            name="lines",
+        )(
+            flat_rows,
+            dr_m,
+            norm_gains,
+            tokens,
+            dha.reshape(cuts, window, model),
+            *[outs[0] for outs in parts_out],
+            *[outs[2] for outs in parts_out],
+        )
+    else:
+        input_grad = None
+        for cut in range(cuts):
+            value = dha[cut].reshape(parts * cut_rows, model)
+            ship = rows_at(value, jnp.where(place < parts // 2, 1, 0), cut_rows, parts - 1)
+            terms = other_sums(value, ship, cut_rows)
+            before = [] if input_grad is None else [input_grad]
+            input_grad = pl.pallas_call(
+                after(
+                    functools.partial(input_grad_kernel, (cut, cuts, len(terms))),
+                    6 + len(terms),
+                    len(before),
+                ),
+                out_shape=jax.ShapeDtypeStruct((share_rows, model), bf16),
+                grid_spec=pltpu.PrefetchScalarGridSpec(
+                    num_scalar_prefetch=1,
+                    grid=(1,),
+                    in_specs=[
+                        whole_spec((1, mask_rows)),
+                        whole_spec((mask_rows, model)),
+                        whole_spec((2, model)),
+                        pl.BlockSpec(
+                            (cut_rows, model),
+                            lambda i, place_ref, cut=cut: (place_ref[0] * cuts + cut, 0),
+                        ),
+                        pl.BlockSpec(
+                            (1, 1, cut_rows, model),
+                            lambda i, place_ref, cut=cut: (cut, place_ref[0], 0, 0),
+                        ),
+                    ]
+                    + [whole_spec((cut_rows, model))] * len(terms)
+                    + [UNREAD] * len(before),
+                    out_specs=pl.BlockSpec((cut_rows, model), lambda i, place_ref, cut=cut: (cut, 0)),
+                ),
+                input_output_aliases={6 + len(terms): 0} if before else {},
+                compiler_params=params(),
+                cost_estimate=cost(4 * cut_rows * mask_rows * model, 6e6),
+                name="input_grad",
+            )(place_ref, flat_rows, dr_m, norm_gains, tokens, dha, *terms, *before)
+
+        for w, outs in enumerate(parts_out):
+            layer_out = place_window(w, *outs)
 
     even = jnp.array([[1.0], [1.0 / parts]], f32)
     gain_grad = small_total(gains_part * even)
@@ -778,13 +1218,20 @@
         gain_grad, gain_first, gain_second, norm_gains, gain_rate, 0.0
     )
 
-    attn_grads = total_tiles(
-        jnp.concatenate(
-            [g_qkv[:, i * width : (i + 1) * width].reshape(-1, model) for i in range(3)]
-            + [g_out],
-            axis=0,
-        )
-    )
+    def total_tiles(tiles, before):
+        piece = lax.psum_scatter(tiles, "dp", scatter_dimension=0, tiled=True)
+        piece = pl.pallas_call(
+            after(copy_kernel, 1, 1),
+            out_shape=jax.ShapeDtypeStruct(piece.shape, bf16),
+            in_specs=[pl.BlockSpec(memory_space=pltpu.VMEM), UNREAD],
+            out_specs=pl.BlockSpec(memory_space=pltpu.VMEM),
+            compiler_params=params(),
+            name="copy",
+        )(piece, before)
+        return lax.all_gather(piece, "dp", axis=0, tiled=True)
+
+    ffn_grads = total_tiles(ffn_grad.reshape(3 * hidden, model), parts_out[1][0])
+    attn_grads = total_tiles(attn_grad, parts_out[-1][0])
     tiles = jnp.concatenate([attn_grads, ffn_grads], axis=0).reshape(-1, tile_rows, model)
     reduced = tiles[slot_tile].astype(f32)
     first_new, second_new, param_new = adam_update(

time: 1090 us -> 826 us (0.76)
  starting transfers between devices: 260 us -> 63 us
  waiting for transfers between devices: 322 us -> 149 us
  Pallas kernels: 360 us -> 523 us
  other arithmetic: 65.6 us -> 31.7 us
  local copies, waits for them, and re-layouts: 55 us -> 34.4 us
    pallas_call x9 -> x12, Pallas kernels: 318 us -> 479 us  [the longest x1 337 us: on_device(): pl.pallas_call(functools.partial(lines_kernel, cuts, seq_count, order), o...]
    ppermute x24 -> x0, starting transfers between devices: 117 us -> none  [the longest x12 103 us: chain_sums(): lax.ppermute(send, 'tensor', [(i, i + 1) for i in range(min(step, size -...]
    reduce_scatter x2, waiting for transfers between devices: 107 us -> 0.04 us  [total_tiles(): piece = lax.psum_scatter(tiles, 'dp', scatter_dimension=0, tiled=True)]
    ppermute x27 -> x18, starting transfers between devices: 125 us -> 48.5 us  [around(): lax.ppermute(value, 'tensor', [(i, (i + k) % size) for i in range(size)])]
    ppermute x24 -> x0, waiting for transfers between devices: 30.8 us -> none  [the longest x12 30.8 us: chain_sums(): lax.ppermute(send, 'tensor', [(i, i + 1) for i in range(min(step, size -...]
    ppermute x11, waiting for transfers between devices: 83.8 us -> 55.4 us  [exchange(): return lax.ppermute(value, axis, [(i, i ^ bit) for i in range(size)])]
    ppermute x3, waiting for transfers between devices: 18.3 us -> 45 us  [on_device(): lax.ppermute(send, 'tensor', [(i, (i + step) % parts) for i in range(part...]
    ppermute x27 -> x18, waiting for transfers between devices: 74.2 us -> 47.5 us  [around(): lax.ppermute(value, 'tensor', [(i, (i + k) % size) for i in range(size)])]
  transfers between devices with their start and end apart: 70 -> 37, of which waited for: 26 -> 14; matrix products, arithmetic and copies ran while one was open for 7% -> 3% of each run, Pallas kernels for 28% -> 56%
where the time goes in v2:
time: 826 us; the launch traced here: 815 us
  Pallas kernels  523 us (63%)
  waiting for transfers between devices  149 us (18%)
  starting transfers between devices  63 us (8%)
  local copies, waits for them, and re-layouts  34.4 us (4%)
  other arithmetic  31.7 us (4%)
  between operations  14.8 us (2%)
    pallas_call x1, Pallas kernels, on_device(): pl.pallas_call(functools.partial(lines_kernel, cuts, seq_count, order), o...  337 us
    ppermute x11, waiting for transfers between devices, exchange(): return lax.ppermute(value, axis, [(i, i ^ bit) for i in range(size)])  55.4 us
    pallas_call x3, Pallas kernels, ffn_window(): pl.pallas_call(after(functools.partial(ffn_kernel, parts), 6 + 2 * parts,...  49.8 us
    ppermute x18, starting transfers between devices, around(): lax.ppermute(value, 'tensor', [(i, (i + k) % size) for i in range(size)])  48.5 us
    ppermute x18, waiting for transfers between devices, around(): lax.ppermute(value, 'tensor', [(i, (i + k) % size) for i in range(size)])  47.5 us
    ppermute x3, waiting for transfers between devices, on_device(): lax.ppermute(send, 'tensor', [(i, (i + step) % parts) for i in range(part...  45 us
    pallas_call x1, Pallas kernels, on_device(): pl.pallas_call(after(attn_back_kernel, 16, 1), out_shape=[jax.ShapeDtypeS...  38.7 us
    pallas_call x3, Pallas kernels, attend_window(): pl.pallas_call(after(attend_kernel, 3, 1), out_shape=jax.ShapeDtypeStruct...  34.1 us
  transfers between devices with their start and end apart: 37, of which 14 were waited for; matrix products, arithmetic and copies ran while one was open for 3% of the time, Pallas kernels for 56%

profile of v2, /device:TPU:0, one launch (start us, length us, event | category | flops | bytes accessed | tf_op | source)
XLA Modules:
  0.0 815.4 jit_solution(7142581489911123098)
XLA Ops:
  7.2 1.4 convert_reduce_fusion.rank_ref
  9.8 8.5 %cast.1 = (bf16[8,128,1024]{2,1,0:T(8,128)(2,1)}, bf16[8,128,1024]{2,1,0:T(8,128)(2,1)}) custom-call(s32[32]{0:T(128)} %convert_reduce_fusion.rank_ref, s32[8]{0:T(128)} %fusion.10.held_ref, f32[8,128,1024]{2,1,0:T(8,128)} %bitcast.32, f32[8,128,1024]{2,1,0:T(8,128)} %bitcast.33), custom_call_target="tpu_custom_call" | custom-call | bytes 12582912 | tf_op jit(solution)/shard_map/cast/pallas_call | solution.py:756
  18.9 4.0 collective-permute-done
  24.3 2.9 collective-permute-start.1
  27.2 1.5 collective-permute-start.3
  28.8 18.9 %collective-permute-done.1 = bf16[2,128,1024]{2,1,0:T(8,128)(2,1)S(1)} collective-permute-done((bf16[2,128,1024]{2,1,0:T(8,128)(2,1)S(1)}, bf16[2,128,1024]{2,1,0:T(8,128)(2,1)S(1)}, u32[]{:S(2)}, u32[]{:S(2)}) %collective-permute-start.1) | collective-permute-done | bytes 524320 | tf_op jit(solution)/shard_map/ppermute | solution.py:610
  47.6 2.5 collective-permute-done.3
  50.3 2.5 collective-permute-start.2
  52.8 21.8 %collective-permute-done.2 = bf16[2,128,1024]{2,1,0:T(8,128)(2,1)S(1)} collective-permute-done((bf16[2,128,1024]{2,1,0:T(8,128)(2,1)S(1)}, bf16[2,128,1024]{2,1,0:T(8,128)(2,1)S(1)}, u32[]{:S(2)}, u32[]{:S(2)}) %collective-permute-start.2) | collective-permute-done | bytes 524320 | tf_op jit(solution)/shard_map/ppermute | solution.py:610
  79.7 2.7 pad.9
  82.9 1.8 maximum_select_fusion
  84.8 3.5 collective-permute-start.11
  89.3 12.9 %qkv.1 = (bf16[3072,256]{1,0:T(8,128)(2,1)}, bf16[3072,256]{1,0:T(8,128)(2,1)}, bf16[3072,256]{1,0:T(8,128)(2,1)}, bf16[1024,768]{1,0:T(8,128)(2,1)}) custom-call(bf16[3072,1024]{1,0:T(8,128)(2,1)} %x_ref.5, f32[2,1024]{1,0:T(2,128)} %gains_ref.5, bf16[1024,1024]{1,0:T(8,128)(2,1)} %bitcast.39, f32[1024,256]{1,0:T(8,128)} %copy.34.cos_ref.refs_12_, ...), custom_call_target="tpu_custom_call" | custom-call | flops 4831838208 | bytes 12582912 | tf_op jit(solution)/shard_map/qkv/pallas_call | solution.py:814
  102.2 10.2 %attend_masked.1 = (bf16[480,256]{1,0:T(8,128)(2,1)}, bf16[480,256]{1,0:T(8,128)(2,1)}, bf16[480,1024]{1,0:T(8,128)(2,1)}) custom-call(s32[3,160,1]{2,1,0:T(8,128)} %copy.36.rows_ref, bf16[3072,1024]{1,0:T(8,128)(2,1)} %x_ref.5, bf16[3072,256]{1,0:T(8,128)(2,1)} %get-tuple-element.36.q_ref.refs_0_, ...), custom_call_target="tpu_custom_call" | custom-call | flops 2013265920 | bytes 9000000 | tf_op jit(solution)/shard_map/attend_masked/pallas_call | solution.py:837
  112.4 2.6 collective-permute-start.8
  116.1 11.3 %attend.3.refs_3_.refs_6_ = bf16[1024,256]{1,0:T(8,128)(2,1)} custom-call(bf16[3072,256]{1,0:T(8,128)(2,1)} %get-tuple-element.36.q_ref.refs_0_, bf16[3072,256]{1,0:T(8,128)(2,1)} %get-tuple-element.37.k_ref.refs_1_.refs_9_, bf16[3072,256]{1,0:T(8,128)(2,1)} %get-tuple-element.38.v_ref.refs_2_.refs_10_, ...), custom_call_target="tpu_custom_call" | custom-call | flops 4294967296 | bytes 2097152 | tf_op jit(solution)/shard_map/attend/pallas_call | solution.py:864
  127.5 11.4 %attend.4.refs_5_.refs_6_ = bf16[1024,256]{1,0:T(8,128)(2,1)} custom-call(bf16[3072,256]{1,0:T(8,128)(2,1)} %get-tuple-element.36.q_ref.refs_0_, bf16[3072,256]{1,0:T(8,128)(2,1)} %get-tuple-element.37.k_ref.refs_1_.refs_9_, bf16[3072,256]{1,0:T(8,128)(2,1)} %get-tuple-element.38.v_ref.refs_2_.refs_10_, bf16[1024,256]{1,0:T(8,128)(2,1)} %attend.3.refs_3_.refs_6_), custom_call_target="tpu_custom_call" | custom-call | flops 4294967296 | bytes 2097152 | tf_op jit(solution)/shard_map/attend/pallas_call | solution.py:864
  138.9 7.6 collect.1
  146.7 5.7 fusion.14
  152.5 2.8 collective-permute-done.6.refs_1_
  156.1 20.8 %ffn_masked.1 = (f32[480,1024]{1,0:T(8,128)}, bf16[480,1024]{1,0:T(8,128)(2,1)}, bf16[3,1024,1024]{2,1,0:T(8,128)(2,1)}) custom-call(bf16[480,1024]{1,0:T(8,128)(2,1)} %get-tuple-element.39.xm_ref, bf16[480,1024]{1,0:T(8,128)(2,1)} %bitcast.52, f32[2,1024]{1,0:T(2,128)} %gains_ref.5, bf16[1024,1024]{1,0:T(8,128)(2,1)} %bitcast.48, ...), custom_call_target="tpu_custom_call" | custom-call | flops 10066329600 | bytes 20000000 | tf_op jit(solution)/shard_map/ffn_masked/pallas_call | solution.py:917
  183.4 3.5 collective-permute-start.20
  188.8 2.4 collective-permute-start.14
  191.9 11.4 %attend.5.refs_14_.refs_6_ = bf16[1024,256]{1,0:T(8,128)(2,1)} custom-call(bf16[3072,256]{1,0:T(8,128)(2,1)} %get-tuple-element.36.q_ref.refs_0_, bf16[3072,256]{1,0:T(8,128)(2,1)} %get-tuple-element.37.k_ref.refs_1_.refs_9_, bf16[3072,256]{1,0:T(8,128)(2,1)} %get-tuple-element.38.v_ref.refs_2_.refs_10_, f32[480,1024]{1,0:T(8,128)} %get-tuple-element.43.refs_3_.refs_2_), custom_call_target="tpu_custom_call" | custom-call | flops 4294967296 | bytes 2097152 | tf_op jit(solution)/shard_map/attend/pallas_call | solution.py:864
  203.2 23.9 %collective-permute-done.14 = bf16[120,1024]{1,0:T(8,128)(2,1)S(1)} collective-permute-done((bf16[120,1024]{1,0:T(8,128)(2,1)S(1)}, bf16[120,1024]{1,0:T(8,128)(2,1)S(1)}, u32[]{:S(2)}, u32[]{:S(2)}) %collective-permute-start.14) | collective-permute-done | bytes 245792 | tf_op jit(solution)/shard_map/ppermute | solution.py:962
  227.2 21.1 %collective-permute-done.13 = bf16[120,1024]{1,0:T(8,128)(2,1)S(1)} collective-permute-done((bf16[120,1024]{1,0:T(8,128)(2,1)S(1)}, bf16[120,1024]{1,0:T(8,128)(2,1)S(1)}, u32[]{:S(2)}, u32[]{:S(2)}) %collective-permute-start.13) | collective-permute-done | bytes 245792 | tf_op jit(solution)/shard_map/ppermute | solution.py:962
  249.6 3.7 collective-permute-start.15
  254.1 16.5 %ffn.3 = (bf16[1024,1024]{1,0:T(8,128)(2,1)}, bf16[768,1024]{1,0:T(8,128)(2,1)}, f32[256,1024]{1,0:T(8,128)}) custom-call(s32[1]{0:T(128)} %bitcast.12.refs_0_, bf16[3072,1024]{1,0:T(8,128)(2,1)} %x_ref.5, f32[2,1024]{1,0:T(2,128)} %gains_ref.5, bf16[1024,1024]{1,0:T(8,128)(2,1)} %bitcast.49, bf16[1024,1024]{1,0:T(8,128)(2,1)} %bitcast.45, ...), custom_call_target="tpu_custom_call" | custom-call | flops 8589934592 | bytes 16000000 | tf_op jit(solution)/shard_map/ffn/pallas_call | solution.py:976
  271.6 38.7 %attn_back.1 = (f32[480,1024]{1,0:T(8,128)}, bf16[3,4,256,1024]{3,2,1,0:T(8,128)(2,1)}, bf16[1024,1024]{1,0:T(8,128)(2,1)}, f32[2,1024]{1,0:T(2,128)}) custom-call(s32[3,1,160]{2,1,0:T(1,128)} %broadcast_in_dim.56.refs_0_, bf16[480,1024]{1,0:T(8,128)(2,1)} %copy-done.2, f32[480,1024]{1,0:T(8,128)} %get-tuple-element.43.refs_3_.refs_2_, ...), custom_call_target="tpu_custom_call" | custom-call | flops 9663676416 | bytes 30000000 | tf_op jit(solution)/shard_map/attn_back/pallas_call | solution.py:1051
  312.2 3.3 collective-permute-start.22
  315.9 3.5 collective-permute-start.26
  319.4 9.4 %collective-permute-done.23.refs_9_ = bf16[1024,256]{1,0:T(8,128)(2,1)S(1)} collective-permute-done((bf16[1024,256]{1,0:T(8,128)(2,1)S(1)}, bf16[1024,256]{1,0:T(8,128)(2,1)S(1)}, u32[]{:S(2)}, u32[]{:S(2)}) %collective-permute-start.23) | collective-permute-done | bytes 524320 | tf_op jit(solution)/shard_map/ppermute | solution.py:641
  328.7 22.7 %collective-permute-start.24 = (bf16[1024,256]{1,0:T(8,128)(2,1)S(1)}, bf16[1024,256]{1,0:T(8,128)(2,1)S(1)}, u32[]{:S(2)}, u32[]{:S(2)}) collective-permute-start(bf16[1024,256]{1,0:T(8,128)(2,1)S(1)} %copy-done.14), channel_id=1, source_target_pairs={{0,1},{1,2},{2,3},{3,0},{4,5},{5,6},{6,7},{7,4},{8,9},{9,10},{10,1... | collective-permute-start | bytes 1572872 | tf_op jit(solution)/shard_map/ppermute | solution.py:641
  351.4 33.1 %collective-permute-done.22.refs_8_ = bf16[1024,256]{1,0:T(8,128)(2,1)S(1)} collective-permute-done((bf16[1024,256]{1,0:T(8,128)(2,1)S(1)}, bf16[1024,256]{1,0:T(8,128)(2,1)S(1)}, u32[]{:S(2)}, u32[]{:S(2)}) %collective-permute-start.22) | collective-permute-done | bytes 524320 | tf_op jit(solution)/shard_map/ppermute | solution.py:641
  385.6 16.8 %ffn.4 = (bf16[1024,1024]{1,0:T(8,128)(2,1)}, bf16[768,1024]{1,0:T(8,128)(2,1)}, f32[256,1024]{1,0:T(8,128)}) custom-call(s32[1]{0:T(128)} %bitcast.12.refs_0_, bf16[3072,1024]{1,0:T(8,128)(2,1)} %x_ref.5, f32[2,1024]{1,0:T(2,128)} %gains_ref.5, bf16[1024,1024]{1,0:T(8,128)(2,1)} %bitcast.50, bf16[1024,1024]{1,0:T(8,128)(2,1)} %bitcast.46, ...), custom_call_target="tpu_custom_call" | custom-call | flops 8589934592 | bytes 16000000 | tf_op jit(solution)/shard_map/ffn/pallas_call | solution.py:976
  402.4 2.2 collective-permute-done.25.refs_8_
  405.7 16.5 %ffn.5 = (bf16[1024,1024]{1,0:T(8,128)(2,1)}, bf16[768,1024]{1,0:T(8,128)(2,1)}, f32[256,1024]{1,0:T(8,128)}) custom-call(s32[1]{0:T(128)} %bitcast.12.refs_0_, bf16[3072,1024]{1,0:T(8,128)(2,1)} %x_ref.5, f32[2,1024]{1,0:T(2,128)} %gains_ref.5, bf16[1024,1024]{1,0:T(8,128)(2,1)} %bitcast.51, bf16[1024,1024]{1,0:T(8,128)(2,1)} %bitcast.47, ...), custom_call_target="tpu_custom_call" | custom-call | flops 8589934592 | bytes 16000000 | tf_op jit(solution)/shard_map/ffn/pallas_call | solution.py:976
  422.2 1.7 copy.47
  424.0 2.1 copy.48
  428.5 2.6 collective-permute-done.28
  431.1 1.6 collective-permute-start.29
  432.9 2.1 collective-permute-done.29
  435.6 3.0 collective-permute-done.30
  439.2 336.6 %lines.1 = (bf16[3072,1024]{1,0:T(8,128)(2,1)}, bf16[768,1024]{1,0:T(8,128)(2,1)}) custom-call(s32[1,480]{1,0:T(1,128)} %reshape.126.rows_in, f32[480,1024]{1,0:T(8,128)} %get-tuple-element.47.drm_ref, f32[2,1024]{1,0:T(2,128)} %gains_ref.5, bf16[3072,1024]{1,0:T(8,128)(2,1)} %x_ref.5, bf16[3,1024,1024]{2,1,0:T(8,128)(2,1)} %bitcast.36, ...), custom_call_target="tpu_custom_call" | custom-call | flops 1509949440 | bytes 60000000 | tf_op jit(solution)/shard_map/lines/pallas_call | solution.py:1129
  776.5 7.7 pad_maximum_fusion
  784.2 4.1 gather_fusion
  788.3 12.7 %fusion.13 = (bf16[1,8,128,1024]{3,2,1,0:T(8,128)(2,1)}, f32[1,8,128,1024]{3,2,1,0:T(8,128)}, f32[1,8,128,1024]{3,2,1,0:T(8,128)}, f32[1,8,128,1024]{3,2,1,0:T(8,128)}, f32[1,8,128,1024]{3,2,1,0:T(8,128)}) fusion(f32[1,8,128,1024]{3,2,1,0:T(8,128)} %param.18, f32[1,8,128,1024]{3,2,1,0:T(8,128)} %param.20, bf16[8,128,1024]{2,1,0:T(8,128)(2,1)S(1)} %gather_fusion, ...), kind=kLoop, calls=%fused_computation.58 | loop fusion | flops 22020096 | bytes 33554440 | tf_op jit(solution)/shard_map/convert_element_type | solution.py:1244
  800.9 6.3 copy.45
  (154 shorter events, 34.2 us)
Async XLA Ops:
  7.2 131.7 %all-gather.4.cloned.1.call-start = ((), (), s32[]{:S(2)}) async-start(), calls=%async_computation.2 | async-start | bytes 18874368 | tf_op jit(solution)/shard_map/all_gather | solution.py:798
  18.3 403.9 %reduce-scatter.3.cloned.1.call-start = ((), (), s32[]{:S(2)}) async-start(), calls=%async_computation.3 | async-start | bytes 2359296 | tf_op jit(solution)/shard_map/reduce_scatter | solution.py:1222
  18.4 4.5 collective-permute-start
  24.3 23.3 %collective-permute-start.1 = (bf16[2,128,1024]{2,1,0:T(8,128)(2,1)S(1)}, bf16[2,128,1024]{2,1,0:T(8,128)(2,1)S(1)}, u32[]{:S(2)}, u32[]{:S(2)}) collective-permute-start(bf16[2,128,1024]{2,1,0:T(8,128)(2,1)S(1)} %get-tuple-element.75), channel_id=1, source_target_pairs={{0,8},{4,12},{8,0},{12,4},{16,24},{20,28},{24,16},{28,20},{1,9},{5... | collective-permute-start | bytes 1572872 | tf_op jit(solution)/shard_map/ppermute | solution.py:610
  27.2 48.0 %copy-start.9 = (s32[3,153]{1,0:T(4,128)S(1)}, s32[3,153]{1,0:T(4,128)}, u32[]{:S(2)}) copy-start(s32[3,153]{1,0:T(4,128)} %param.12) | copy-start | bytes 5512
  27.2 22.9 %collective-permute-start.3 = (bf16[2,128,1024]{2,1,0:T(8,128)(2,1)S(1)}, bf16[2,128,1024]{2,1,0:T(8,128)(2,1)S(1)}, u32[]{:S(2)}, u32[]{:S(2)}) collective-permute-start(bf16[2,128,1024]{2,1,0:T(8,128)(2,1)S(1)} %get-tuple-element.76), channel_id=1, source_target_pairs={{0,16},{4,20},{8,24},{12,28},{16,0},{20,4},{24,8},{28,12},{1,17},{... | collective-permute-start | bytes 1572872 | tf_op jit(solution)/shard_map/ppermute | solution.py:610
  50.3 24.3 %collective-permute-start.2 = (bf16[2,128,1024]{2,1,0:T(8,128)(2,1)S(1)}, bf16[2,128,1024]{2,1,0:T(8,128)(2,1)S(1)}, u32[]{:S(2)}, u32[]{:S(2)}) collective-permute-start(bf16[2,128,1024]{2,1,0:T(8,128)(2,1)S(1)} %get-tuple-element.73), channel_id=1, source_target_pairs={{0,16},{4,20},{8,24},{12,28},{16,0},{20,4},{24,8},{28,12},{1,17},{... | collective-permute-start | bytes 1572872 | tf_op jit(solution)/shard_map/ppermute | solution.py:610
  52.8 22.0 %collective-permute-start.4 = (bf16[2,128,1024]{2,1,0:T(8,128)(2,1)S(1)}, bf16[2,128,1024]{2,1,0:T(8,128)(2,1)S(1)}, u32[]{:S(2)}, u32[]{:S(2)}) collective-permute-start(bf16[2,128,1024]{2,1,0:T(8,128)(2,1)S(1)} %get-tuple-element.74), channel_id=1, source_target_pairs={{0,8},{4,12},{8,0},{12,4},{16,24},{20,28},{24,16},{28,20},{1,9},{5... | collective-permute-start | bytes 1572872 | tf_op jit(solution)/shard_map/ppermute | solution.py:610
  75.1 7.8 collective-permute-start.5
  76.8 5.6 copy-start.10
  84.8 17.4 %copy-start.4 = (bf16[2,128,1024]{2,1,0:T(8,128)(2,1)}, bf16[2,128,1024]{2,1,0:T(8,128)(2,1)S(1)}, u32[]{:S(2)}) copy-start(bf16[2,128,1024]{2,1,0:T(8,128)(2,1)S(1)} %slice.43) | copy-start | bytes 1572868
  84.8 70.5 %collective-permute-start.11 = (bf16[256,1024]{1,0:T(8,128)(2,1)S(1)}, bf16[256,1024]{1,0:T(8,128)(2,1)S(1)}, u32[]{:S(2)}, u32[]{:S(2)}) collective-permute-start(bf16[256,1024]{1,0:T(8,128)(2,1)S(1)} %bitcast.54), channel_id=1, source_target_pairs={{0,3},{1,0},{2,1},{3,2},{4,7},{5,4},{6,5},{7,6},{8,11},{9,8},{10,9... | collective-permute-start | bytes 1572872 | tf_op jit(solution)/shard_map/ppermute | solution.py:641
  88.3 67.0 %collective-permute-start.10 = (bf16[256,1024]{1,0:T(8,128)(2,1)S(1)}, bf16[256,1024]{1,0:T(8,128)(2,1)}, u32[]{:S(2)}, u32[]{:S(2)}) collective-permute-start(bf16[256,1024]{1,0:T(8,128)(2,1)S(1)} %bitcast.55), channel_id=1, source_target_pairs={{0,2},{1,3},{2,0},{3,1},{4,6},{5,7},{6,4},{7,5},{8,10},{9,11},{10,... | collective-permute-start | bytes 1572872 | tf_op jit(solution)/shard_map/ppermute | solution.py:641
  88.3 67.0 %collective-permute-start.9 = (bf16[256,1024]{1,0:T(8,128)(2,1)S(1)}, bf16[256,1024]{1,0:T(8,128)(2,1)}, u32[]{:S(2)}, u32[]{:S(2)}) collective-permute-start(bf16[256,1024]{1,0:T(8,128)(2,1)S(1)} %bitcast.56), channel_id=1, source_target_pairs={{0,1},{1,2},{2,3},{3,0},{4,5},{5,6},{6,7},{7,4},{8,9},{9,10},{10,1... | collective-permute-start | bytes 1572872 | tf_op jit(solution)/shard_map/ppermute | solution.py:641
  112.4 34.0 %collective-permute-start.8 = (bf16[480,256]{1,0:T(8,128)(2,1)}, bf16[480,256]{1,0:T(8,128)(2,1)S(1)}, u32[]{:S(2)}, u32[]{:S(2)}) collective-permute-start(bf16[480,256]{1,0:T(8,128)(2,1)} %get-tuple-element.41.refs_3_.refs_0_.refs_5_), channel_id=1, source_target_pairs={{0,3},{1,0},{2,1},{3,2},{4,7},{5,4},{6,5},{7,6},{8,11},{9,8},{10,9... | collective-permute-start | bytes 737288 | tf_op jit(solution)/shard_map/ppermute | solution.py:641
  115.0 37.5 %collective-permute-start.7 = (bf16[480,256]{1,0:T(8,128)(2,1)}, bf16[480,256]{1,0:T(8,128)(2,1)S(1)}, u32[]{:S(2)}, u32[]{:S(2)}) collective-permute-start(bf16[480,256]{1,0:T(8,128)(2,1)} %get-tuple-element.41.refs_3_.refs_0_.refs_5_), channel_id=1, source_target_pairs={{0,2},{1,3},{2,0},{3,1},{4,6},{5,7},{6,4},{7,5},{8,10},{9,11},{10,... | collective-permute-start | bytes 737288 | tf_op jit(solution)/shard_map/ppermute | solution.py:641
  138.9 7.6 copy-start.22
  146.4 6.0 copy-start.23
  146.4 8.8 %collective-permute-start.6 = (bf16[480,256]{1,0:T(8,128)(2,1)S(1)}, bf16[480,256]{1,0:T(8,128)(2,1)S(1)}, u32[]{:S(2)}, u32[]{:S(2)}) collective-permute-start(bf16[480,256]{1,0:T(8,128)(2,1)S(1)} %copy-done.22), channel_id=1, source_target_pairs={{0,1},{1,2},{2,3},{3,0},{4,5},{5,6},{6,7},{7,4},{8,9},{9,10},{10,1... | collective-permute-start | bytes 737288 | tf_op jit(solution)/shard_map/ppermute | solution.py:641
  176.9 6.5 copy-start.13
  178.2 13.0 %collective-permute-start.12 = (bf16[120,1024]{1,0:T(8,128)(2,1)S(1)}, bf16[120,1024]{1,0:T(8,128)(2,1)S(1)}, u32[]{:S(2)}, u32[]{:S(2)}) collective-permute-start(bf16[120,1024]{1,0:T(8,128)(2,1)S(1)} %get-tuple-element.77), channel_id=1, source_target_pairs={{0,1},{1,2},{2,3},{3,0},{4,5},{5,6},{6,7},{7,4},{8,9},{9,10},{10,1... | collective-permute-start | bytes 737288 | tf_op jit(solution)/shard_map/ppermute | solution.py:962
  183.4 69.9 %collective-permute-start.20 = (bf16[1024,256]{1,0:T(8,128)(2,1)S(1)}, bf16[1024,256]{1,0:T(8,128)(2,1)S(1)}, u32[]{:S(2)}, u32[]{:S(2)}) collective-permute-start(bf16[1024,256]{1,0:T(8,128)(2,1)S(1)} %copy-done.13), channel_id=1, source_target_pairs={{0,3},{1,0},{2,1},{3,2},{4,7},{5,4},{6,5},{7,6},{8,11},{9,8},{10,9... | collective-permute-start | bytes 1572872 | tf_op jit(solution)/shard_map/ppermute | solution.py:641
  186.9 66.5 %collective-permute-start.19 = (bf16[1024,256]{1,0:T(8,128)(2,1)S(1)}, bf16[1024,256]{1,0:T(8,128)(2,1)}, u32[]{:S(2)}, u32[]{:S(2)}) collective-permute-start(bf16[1024,256]{1,0:T(8,128)(2,1)S(1)} %copy-done.13), channel_id=1, source_target_pairs={{0,2},{1,3},{2,0},{3,1},{4,6},{5,7},{6,4},{7,5},{8,10},{9,11},{10,... | collective-permute-start | bytes 1572872 | tf_op jit(solution)/shard_map/ppermute | solution.py:641
  187.4 66.1 %collective-permute-start.18 = (bf16[1024,256]{1,0:T(8,128)(2,1)S(1)}, bf16[1024,256]{1,0:T(8,128)(2,1)}, u32[]{:S(2)}, u32[]{:S(2)}) collective-permute-start(bf16[1024,256]{1,0:T(8,128)(2,1)S(1)} %copy-done.13), channel_id=1, source_target_pairs={{0,1},{1,2},{2,3},{3,0},{4,5},{5,6},{6,7},{7,4},{8,9},{9,10},{10,1... | collective-permute-start | bytes 1572872 | tf_op jit(solution)/shard_map/ppermute | solution.py:641
  188.8 38.4 %collective-permute-start.14 = (bf16[120,1024]{1,0:T(8,128)(2,1)S(1)}, bf16[120,1024]{1,0:T(8,128)(2,1)S(1)}, u32[]{:S(2)}, u32[]{:S(2)}) collective-permute-start(bf16[120,1024]{1,0:T(8,128)(2,1)S(1)} %get-tuple-element.78), channel_id=1, source_target_pairs={{0,3},{1,0},{2,1},{3,2},{4,7},{5,4},{6,5},{7,6},{8,11},{9,8},{10,9... | collective-permute-start | bytes 737288 | tf_op jit(solution)/shard_map/ppermute | solution.py:962
  191.2 57.0 %collective-permute-start.13 = (bf16[120,1024]{1,0:T(8,128)(2,1)S(1)}, bf16[120,1024]{1,0:T(8,128)(2,1)S(1)}, u32[]{:S(2)}, u32[]{:S(2)}) collective-permute-start(bf16[120,1024]{1,0:T(8,128)(2,1)S(1)} %get-tuple-element.79), channel_id=1, source_target_pairs={{0,2},{1,3},{2,0},{3,1},{4,6},{5,7},{6,4},{7,5},{8,10},{9,11},{10,... | collective-permute-start | bytes 737288 | tf_op jit(solution)/shard_map/ppermute | solution.py:962
  249.5 21.1 %collective-permute-start.16 = (bf16[120,1024]{1,0:T(8,128)(2,1)S(1)}, bf16[120,1024]{1,0:T(8,128)(2,1)S(1)}, u32[]{:S(2)}, u32[]{:S(2)}) collective-permute-start(bf16[120,1024]{1,0:T(8,128)(2,1)S(1)} %get-tuple-element.66), channel_id=1, source_target_pairs={{0,2},{1,3},{2,0},{3,1},{4,6},{5,7},{6,4},{7,5},{8,10},{9,11},{10,... | collective-permute-start | bytes 737288 | tf_op jit(solution)/shard_map/ppermute | solution.py:641
  249.6 21.0 %collective-permute-start.15 = (bf16[120,1024]{1,0:T(8,128)(2,1)S(1)}, bf16[120,1024]{1,0:T(8,128)(2,1)S(1)}, u32[]{:S(2)}, u32[]{:S(2)}) collective-permute-start(bf16[120,1024]{1,0:T(8,128)(2,1)S(1)} %get-tuple-element.66), channel_id=1, source_target_pairs={{0,1},{1,2},{2,3},{3,0},{4,5},{5,6},{6,7},{7,4},{8,9},{9,10},{10,1... | collective-permute-start | bytes 737288 | tf_op jit(solution)/shard_map/ppermute | solution.py:641
  253.3 17.4 %collective-permute-start.17 = (bf16[120,1024]{1,0:T(8,128)(2,1)S(1)}, bf16[120,1024]{1,0:T(8,128)(2,1)S(1)}, u32[]{:S(2)}, u32[]{:S(2)}) collective-permute-start(bf16[120,1024]{1,0:T(8,128)(2,1)S(1)} %get-tuple-element.66), channel_id=1, source_target_pairs={{0,3},{1,0},{2,1},{3,2},{4,7},{5,4},{6,5},{7,6},{8,11},{9,8},{10,9... | collective-permute-start | bytes 737288 | tf_op jit(solution)/shard_map/ppermute | solution.py:641
  310.4 113.6 %reduce-scatter.5.cloned.1.call-start = ((), (), s32[]{:S(2)}) async-start(), calls=%async_computation.5 | async-start | bytes 7077888 | tf_op jit(solution)/shard_map/reduce_scatter | solution.py:1222
  311.1 465.4 %all-gather.6.cloned.1.call-start = ((), (), s32[]{:S(2)}) async-start(), calls=%async_computation.4 | async-start | bytes 2359296 | tf_op jit(solution)/shard_map/all_gather | solution.py:1231
  311.4 17.3 %collective-permute-start.23 = (bf16[1024,256]{1,0:T(8,128)(2,1)S(1)}, bf16[1024,256]{1,0:T(8,128)(2,1)S(1)}, u32[]{:S(2)}, u32[]{:S(2)}) collective-permute-start(bf16[1024,256]{1,0:T(8,128)(2,1)S(1)} %copy-done.3), channel_id=1, source_target_pairs={{0,3},{1,0},{2,1},{3,2},{4,7},{5,4},{6,5},{7,6},{8,11},{9,8},{10,9... | collective-permute-start | bytes 1572872 | tf_op jit(solution)/shard_map/ppermute | solution.py:641
  312.2 72.4 %collective-permute-start.22 = (bf16[1024,256]{1,0:T(8,128)(2,1)S(1)}, bf16[1024,256]{1,0:T(8,128)(2,1)S(1)}, u32[]{:S(2)}, u32[]{:S(2)}) collective-permute-start(bf16[1024,256]{1,0:T(8,128)(2,1)S(1)} %copy-done.3), channel_id=1, source_target_pairs={{0,2},{1,3},{2,0},{3,1},{4,6},{5,7},{6,4},{7,5},{8,10},{9,11},{10,... | collective-permute-start | bytes 1572872 | tf_op jit(solution)/shard_map/ppermute | solution.py:641
  315.5 69.0 %collective-permute-start.21 = (bf16[1024,256]{1,0:T(8,128)(2,1)S(1)}, bf16[1024,256]{1,0:T(8,128)(2,1)S(1)}, u32[]{:S(2)}, u32[]{:S(2)}) collective-permute-start(bf16[1024,256]{1,0:T(8,128)(2,1)S(1)} %copy-done.3), channel_id=1, source_target_pairs={{0,1},{1,2},{2,3},{3,0},{4,5},{5,6},{6,7},{7,4},{8,9},{9,10},{10,1... | collective-permute-start | bytes 1572872 | tf_op jit(solution)/shard_map/ppermute | solution.py:641
  315.9 86.5 %collective-permute-start.26 = (bf16[1024,256]{1,0:T(8,128)(2,1)S(1)}, bf16[1024,256]{1,0:T(8,128)(2,1)S(1)}, u32[]{:S(2)}, u32[]{:S(2)}) collective-permute-start(bf16[1024,256]{1,0:T(8,128)(2,1)S(1)} %copy-done.14), channel_id=1, source_target_pairs={{0,3},{1,0},{2,1},{3,2},{4,7},{5,4},{6,5},{7,6},{8,11},{9,8},{10,9... | collective-permute-start | bytes 1572872 | tf_op jit(solution)/shard_map/ppermute | solution.py:641
  319.4 85.3 %collective-permute-start.25 = (bf16[1024,256]{1,0:T(8,128)(2,1)S(1)}, bf16[1024,256]{1,0:T(8,128)(2,1)S(1)}, u32[]{:S(2)}, u32[]{:S(2)}) collective-permute-start(bf16[1024,256]{1,0:T(8,128)(2,1)S(1)} %copy-done.14), channel_id=1, source_target_pairs={{0,2},{1,3},{2,0},{3,1},{4,6},{5,7},{6,4},{7,5},{8,10},{9,11},{10,... | collective-permute-start | bytes 1572872 | tf_op jit(solution)/shard_map/ppermute | solution.py:641
  328.7 56.7 %copy-start.19 = (bf16[1024,256]{1,0:T(8,128)(2,1)}, bf16[1024,256]{1,0:T(8,128)(2,1)S(1)}, u32[]{:S(2)}) copy-start(bf16[1024,256]{1,0:T(8,128)(2,1)S(1)} %collective-permute-done.23.refs_9_) | copy-start | bytes 1572868
  328.7 75.9 %collective-permute-start.24 = (bf16[1024,256]{1,0:T(8,128)(2,1)S(1)}, bf16[1024,256]{1,0:T(8,128)(2,1)S(1)}, u32[]{:S(2)}, u32[]{:S(2)}) collective-permute-start(bf16[1024,256]{1,0:T(8,128)(2,1)S(1)} %copy-done.14), channel_id=1, source_target_pairs={{0,1},{1,2},{2,3},{3,0},{4,5},{5,6},{6,7},{7,4},{8,9},{9,10},{10,1... | collective-permute-start | bytes 1572872 | tf_op jit(solution)/shard_map/ppermute | solution.py:641
  423.9 352.6 %all-gather.8.cloned.1.call-start = ((), (), s32[]{:S(2)}) async-start(), calls=%async_computation.6 | async-start | bytes 7077888 | tf_op jit(solution)/shard_map/all_gather | solution.py:1231
  426.2 1.2 collective-permute-start.27
  427.5 3.7 collective-permute-start.28
  431.1 3.8 collective-permute-start.29
  434.9 3.7 collective-permute-start.30
  438.6 337.2 %collective-permute-start.31 = (f32[2,1024]{1,0:T(2,128)S(1)}, f32[2,1024]{1,0:T(2,128)S(1)}, u32[]{:S(2)}, u32[]{:S(2)}) collective-permute-start(f32[2,1024]{1,0:T(2,128)S(1)} %add.181), channel_id=1, source_target_pairs={{0,2},{1,3},{2,0},{3,1},{4,6},{5,7},{6,4},{7,5},{8,10},{9,11},{10,... | collective-permute-start | bytes 24584 | tf_op jit(solution)/shard_map/ppermute | solution.py:610
  439.2 336.6 %copy-start.5 = (f32[2,1024]{1,0:T(2,128)S(1)}, f32[2,1024]{1,0:T(2,128)}, u32[]{:S(2)}) copy-start(f32[2,1024]{1,0:T(2,128)} %gains_ref.5) | copy-start | bytes 24580
  439.2 336.6 %copy-start.7 = (f32[2,1024]{1,0:T(2,128)S(1)}, f32[2,1024]{1,0:T(2,128)}, u32[]{:S(2)}) copy-start(f32[2,1024]{1,0:T(2,128)} %param.15) | copy-start | bytes 24580
  439.2 336.6 %copy-start.8 = (f32[2,1024]{1,0:T(2,128)S(1)}, f32[2,1024]{1,0:T(2,128)}, u32[]{:S(2)}) copy-start(f32[2,1024]{1,0:T(2,128)} %param.16) | copy-start | bytes 24580
  800.9 6.3 copy-start.1
  (16 other events, 36.7 us)
Sparse Core Ops, SparseCore 0:
  18.4 111.2 all-gather.3
  310.5 40.8 reduce-scatter.2
  355.7 61.7 reduce-scatter.4
  424.1 25.8 all-gather.5
  452.3 45.5 all-gather.7

commit v3 on v2

--- a/solution.py
+++ b/solution.py
@@ -195,13 +195,9 @@
         dhf_ref[...] = acc_ref[...].astype(bf16)
 
 
-def far_start(place, parts, share):
-    return jnp.where(place < parts // 2, share, 0)
-
-
 def ffn_kernel(parts, place_ref, x_ref, gains_ref, wg_ref, wu_ref, wd_ref, *refs):
     o_refs, wo_refs = refs[:parts], refs[parts : 2 * parts]
-    part_ref, ship_ref, own_ref, r_ref, hf_ref, acc_ref = refs[2 * parts :]
+    part_ref, own_ref, r_ref, hf_ref, acc_ref = refs[2 * parts :]
     step = pl.program_id(0)
 
     @pl.when(step == 0)
@@ -222,8 +218,6 @@
     def _():
         share = own_ref.shape[0]
         part_ref[...] = acc_ref[...].astype(bf16)
-        far = pl.ds(pl.multiple_of(far_start(place_ref[0], parts, share), share), ship_ref.shape[0])
-        ship_ref[...] = part_ref[far, :]
         mine = pl.ds(pl.multiple_of(place_ref[0] * share, share), share)
         own_ref[...] = r_ref[mine, :] + acc_ref[mine, :]
 
@@ -404,35 +398,462 @@
     return ref.at[pl.ds(pl.multiple_of(index * share, share), count * share), :]
 
 
-def lines_kernel(
-    cuts, windows, order, rows_in, drm_ref, gains_ref, x_ref, dha_ref, *refs
+def masked_attention_back(qm, do, k, v):
+    first = lax.broadcasted_iota(jnp.int32, qm.shape, 1) < HD
+    zero = jnp.zeros((), bf16)
+    parts = []
+    drk = dv = None
+    for head in range(2):
+        mine = first if head == 0 else ~first
+        q_head = jnp.where(mine, qm, zero)
+        do_head = jnp.where(mine, do, zero)
+        s = mm_nt(k, q_head)
+        s = jnp.exp((s - jnp.max(s, axis=0, keepdims=True)) * score_scale)
+        att = s / jnp.sum(s, axis=0, keepdims=True)
+        dpa = mm_nt(v, do_head)
+        ds = att * (dpa - jnp.sum(dpa * att, axis=0, keepdims=True))
+        ds = (ds * score_scale).astype(bf16)
+        parts.append(mm_tn(ds, k))
+        drk_head = mm(ds, q_head)
+        dv_head = mm(att.astype(bf16), do_head)
+        drk = drk_head if drk is None else drk + drk_head
+        dv = dv_head if dv is None else dv + dv_head
+    return jnp.where(first, parts[0], parts[1]), drk, dv
+
+
+def middle_kernel(
+    windows,
+    rows_in,
+    gains_ref,
+    xm_ref,
+    cot_ref,
+    qm_ref,
+    cosm_ref,
+    sinm_ref,
+    cos_ref,
+    sin_ref,
+    w_ref,
+    wg_ref,
+    wu_ref,
+    wd_ref,
+    *refs,
 ):
-    part_refs, own_refs = refs[:windows], refs[windows : 2 * windows]
+    om_refs, wo_refs, oa_refs = refs[0:4], refs[4:8], refs[8:12]
+    x_hbm, k_hbm, v_hbm, o_one, o_two = refs[12:17]
+    part_out, own_out, ra_out, dha_out, grads_out, drm_ref, gain_ref = refs[17:24]
     (
-        out_ref,
-        grad_ref,
-        ra,
-        rb,
-        rc,
-        value,
-        own,
-        piece,
-        x_rows,
-        grad,
+        r_ref,
+        hf_ref,
+        acc_ref,
+        p_ref,
+        own_ref,
+        obuf,
+        x_ref,
+        kv,
+        flow_ref,
+        gw_acc,
+        gw_wide,
+        go_acc,
+        rm_ref,
+        dpart,
+        drecv,
+        dall,
+        o_load,
+        x_sem,
+        kv_sem,
+        grad_sem,
+        p_sem,
+        dha_sem,
+        own_sem,
         a_send,
         a_recv,
-        b_send,
-        b_recv,
-        c_send,
-        c_recv,
-        g_send,
-        g_recv,
-        v_sem,
-        o_sem,
-        x_sem,
-        l_sem,
-        i_sem,
-    ) = refs[2 * windows :]
+        o_send,
+        o_recv,
+        d_send,
+        d_recv,
+        e_send,
+        e_recv,
+    ) = refs[24:]
+    place = lax.axis_index("tensor")
+    lower = place < 2
+    outer = (place == 0) | (place == 3)
+    inner = (place == 1) | (place == 2)
+    window, model = x_ref.shape
+    width = kv.shape[3]
+    hidden = wg_ref.shape[1]
+    share = own_ref.shape[0]
+    count = rm_ref.shape[0] // windows
+    masked = rm_ref.shape[0]
+    cols = 256
+    chunks = hidden // cols
+
+    def hop(g, d, up):
+        src, dst = (d - 1, d) if up else ((5 - d) % 4, 4 - d)
+        n = 0 if up else 1
+        return remote(
+            obuf.at[g, src],
+            obuf.at[g, dst],
+            o_send.at[g, d - 1, n],
+            o_recv.at[g, d - 1, n],
+            lax.rem(place + (1 if up else 3), 4),
+        )
+
+    def sends(d, up):
+        if up:
+            return (place >= d - 1) & (place <= 2)
+        return (place <= 4 - d) & (place >= 1)
+
+    def receives(d, up):
+        return place >= d if up else place <= 3 - d
+
+    def hops(g, d):
+        for up in (True, False):
+
+            @pl.when(sends(d, up))
+            def _():
+                hop(g, d, up).start()
+
+    def hops_in(g, d):
+        for up in (True, False):
+
+            @pl.when(receives(d, up))
+            def _():
+                hop(g, d, up).wait_recv()
+
+    def load_o(g):
+        return pltpu.make_async_copy((o_one, o_two)[g], obuf.at[g, 0], o_load.at[g])
+
+    def load_x(w):
+        return pltpu.make_async_copy(
+            x_hbm.at[pl.ds(w * window, window), :], x_ref, x_sem
+        )
+
+    def load_kv(w):
+        return [
+            pltpu.make_async_copy(
+                hbm.at[pl.ds(w * window, window), :], kv.at[w % 2, n], kv_sem.at[w % 2, n]
+            )
+            for n, hbm in enumerate((k_hbm, v_hbm))
+        ]
+
+    def store_p(to):
+        return pltpu.make_async_copy(p_ref, to, p_sem)
+
+    def store_own(w):
+        return pltpu.make_async_copy(own_ref, own_out.at[w], own_sem)
+
+    def copy_a(w):
+        far = rows_ref(part_out.at[w], jnp.where(lower, 1, 0), share, 3)
+        return remote(far, ra_out.at[w], a_send.at[w], a_recv.at[w], jnp.where(lower, 1, 2))
+
+    def copy_d(k):
+        to = lax.rem(place + k, 4)
+        return remote(dpart.at[to], drecv.at[k - 1], d_send.at[k - 1], d_recv.at[k - 1], to)
+
+    def copy_e(k, origin):
+        to = lax.rem(place + k, 4)
+        return remote(dall.at[origin], dall.at[origin], e_send.at[k - 1], e_recv.at[k - 1], to)
+
+    for g in range(2):
+        load_o(g).start()
+    load_x(0).start()
+    for copy in load_kv(0):
+        copy.start()
+    greet_line(place)
+    load_o(0).wait()
+    hops(0, 1)
+
+    gain_att, gain_ffn = gains_ref[0:1, :], gains_ref[1:2, :]
+    r = xm_ref[...].astype(f32)
+    for om_ref, wo_ref in zip(om_refs, wo_refs):
+        r = r + mm(om_ref[...], wo_ref[...])
+    rm_ref[...] = r
+    hf_ref[0:masked, :] = (r * rms_scale(r) * gain_ffn).astype(bf16)
+
+    def grad_copies(c):
+        side = (c % 2) * 2 * cols
+        base = 4 * width
+        at = pl.ds(c * cols, cols)
+        below = window - 2 * cols + (c % 2) * cols
+        return [
+            pltpu.make_async_copy(
+                p_ref.at[:, pl.ds(side, cols)],
+                grads_out.at[pl.ds(base, model), at],
+                grad_sem.at[c % 2, 0],
+            ),
+            pltpu.make_async_copy(
+                p_ref.at[:, pl.ds(side + cols, cols)],
+                grads_out.at[pl.ds(base + hidden, model), at],
+                grad_sem.at[c % 2, 1],
+            ),
+            pltpu.make_async_copy(
+                hf_ref.at[pl.ds(below, cols), :],
+                grads_out.at[pl.ds(base + 2 * hidden + c * cols, cols), :],
+                grad_sem.at[c % 2, 2],
+            ),
+        ]
+
+    def masked_chunk(c):
+        if c >= 2:
+            for copy in grad_copies(c - 2):
+                copy.wait()
+        at = slice(c * cols, (c + 1) * cols)
+        side = (c % 2) * 2 * cols
+        below = window - 2 * cols + (c % 2) * cols
+        hf, dy = hf_ref[0:masked, :], cot_ref[...]
+        wg, wu, wd = wg_ref[:, at], wu_ref[:, at], wd_ref[at, :]
+        g, u = mm(hf, wg), mm(hf, wu)
+        sig = jax.nn.sigmoid(g)
+        act = (g * sig * u).astype(bf16)
+        hf_ref[below : below + cols, :] = mm_tn(act, dy).astype(bf16)
+        da = mm_nt(dy, wd)
+        dg = (da * u * sig * (1.0 + g * (1.0 - sig))).astype(bf16)
+        du = (da * g * sig).astype(bf16)
+        p_ref[:, side : side + cols] = mm_tn(hf, dg).astype(bf16)
+        p_ref[:, side + cols : side + 2 * cols] = mm_tn(hf, du).astype(bf16)
+        part = mm_nt(dg, wg) + mm_nt(du, wu)
+        if c == 0:
+            acc_ref[0:masked, :] = part
+        else:
+            acc_ref[0:masked, :] += part
+        for copy in grad_copies(c):
+            copy.start()
+
+    for c in range(chunks // 2):
+        masked_chunk(c)
+    hops_in(0, 1)
+    hops(0, 2)
+    for c in range(chunks // 2, chunks):
+        masked_chunk(c)
+    block = model // 4
+    for n in range(4):
+        dpart[n] = acc_ref[0:masked, n * block : (n + 1) * block].astype(bf16)
+    for k in range(1, 4):
+        copy_d(k).start()
+    hops_in(0, 2)
+    hops(0, 3)
+    load_o(1).wait()
+    hops(1, 1)
+    for c in range(chunks - 2, chunks):
+        for copy in grad_copies(c):
+            copy.wait()
+
+    def ffn(w, o_refs, next_x):
+        half = window // 2
+
+        def first(n, carry):
+            rows = pl.ds(pl.multiple_of(n * half, half), half)
+            r = x_ref[rows, :].astype(f32)
+            for o, wo in zip(o_refs, wo_refs):
+                r = r + mm(o[rows, :], wo[...])
+            r_ref[rows, :] = r
+            hf_ref[rows, :] = (r * rms_scale(r) * gain_ffn).astype(bf16)
+            return carry
+
+        lax.fori_loop(0, 2, first, 0)
+        if next_x is not None:
+            load_x(next_x).start()
+        acc_ref[...] = jnp.zeros_like(acc_ref)
+
+        def chunk(c, carry):
+            at = pl.ds(pl.multiple_of(c * cols, cols), cols)
+            hf = hf_ref[...]
+            g, u = mm(hf, wg_ref[:, at]), mm(hf, wu_ref[:, at])
+            act = (g * jax.nn.sigmoid(g) * u).astype(bf16)
+            acc_ref[...] += mm(act, wd_ref[at, :])
+            return carry
+
+        lax.fori_loop(0, chunks, chunk, 0)
+        p_ref[...] = acc_ref[...].astype(bf16)
+        store_p(part_out.at[w]).start()
+        mine = pl.ds(pl.multiple_of(place * share, share), share)
+        own_ref[...] = r_ref[mine, :] + acc_ref[mine, :]
+        store_own(w).start()
+        store_p(part_out.at[w]).wait()
+        store_own(w).wait()
+
+    def inward(w):
+        @pl.when(outer)
+        def _():
+            copy_a(w).start()
+
+    load_x(0).wait()
+    ffn(0, oa_refs, 1)
+    inward(0)
+
+    for k in range(1, 4):
+        copy_d(k).wait_recv()
+    total = dpart[place].astype(f32)
+    for k in range(3):
+        total = total + drecv[k].astype(f32)
+    dall[place] = total.astype(bf16)
+    for k in range(1, 4):
+        copy_e(k, place).start()
+
+    hops_in(0, 3)
+    hops_in(1, 1)
+    hops(1, 2)
+    load_x(1).wait()
+    ffn(1, [obuf.at[0, n] for n in range(4)], 0)
+    inward(1)
+    hops_in(1, 2)
+    hops(1, 3)
+
+    for k in range(1, 4):
+        copy_e(k, lax.rem(place + 4 - k, 4)).wait_recv()
+    gw_acc[...] = jnp.zeros_like(gw_acc)
+    go_acc[...] = jnp.zeros_like(go_acc)
+    gain_ref[...] = jnp.zeros_like(gain_ref)
+    for w in range(windows):
+        for copy in load_kv(w):
+            copy.wait()
+        if w + 1 < windows:
+            for copy in load_kv(w + 1):
+                copy.start()
+        at = slice(w * count, (w + 1) * count)
+        r = rm_ref[at, :]
+        sf = rms_scale(r)
+        nf = r * sf
+        dhf = jnp.concatenate([dall[n, at, :] for n in range(4)], axis=1).astype(f32)
+        dnf = dhf * gain_ffn
+        dr = cot_ref[at, :].astype(f32) + sf * (
+            dnf - nf * jnp.mean(dnf * nf, axis=-1, keepdims=True)
+        )
+        drm_ref[at, :] = dr
+        gain_ref[1:2, :] += jnp.sum(dhf * nf, axis=0, keepdims=True)
+        drb = dr.astype(bf16)
+        go_acc[...] += mm_tn(om_refs[0][at, :], drb)
+        dob = mm_nt(drb, wo_refs[0][...]).astype(bf16)
+        spread = (
+            lax.broadcasted_iota(jnp.int32, (window, count), 0) == rows_in[w]
+        ).astype(bf16)
+        for pair in range(width // 128):
+            lanes = slice(pair * 128, pair * 128 + 128)
+            drq, drk, dv = masked_attention_back(
+                qm_ref[at, lanes], dob[:, lanes], kv[w % 2, 0, :, lanes], kv[w % 2, 1, :, lanes]
+            )
+            dk = drk * cos_ref[:, lanes] - swap_halves(drk) * sin_ref[:, lanes]
+            dq = drq * cosm_ref[at, lanes] - swap_halves(drq) * sinm_ref[at, lanes]
+            first = pair * 128
+            flow_ref[:, first : first + 128] = mm(spread, dq.astype(bf16)).astype(bf16)
+            flow_ref[:, width + first : width + first + 128] = dk.astype(bf16)
+            flow_ref[:, 2 * width + first : 2 * width + first + 128] = dv.astype(bf16)
+        load_x(w).wait()
+        if w > 0:
+            for copy in dha_copies(dha_out, p_ref, dha_sem, w - 1, windows, share):
+                copy.wait()
+
+        def back(n, carry):
+            rows = pl.ds(pl.multiple_of(n * share, share), share)
+            x = x_ref[rows, :].astype(f32)
+            na = x * rms_scale(x)
+            dha = mm_nt(flow_ref[rows, :], w_ref[...])
+            gain_ref[0:1, :] += jnp.sum(dha * na, axis=0, keepdims=True)
+            p_ref[rows, :] = dha.astype(bf16)
+            hf_ref[rows, :] = (na * gain_att).astype(bf16)
+            return carry
+
+        lax.fori_loop(0, window // share, back, 0)
+        for copy in dha_copies(dha_out, p_ref, dha_sem, w, windows, share):
+            copy.start()
+        if w + 1 < windows:
+            load_x(w + 1).start()
+        gw_acc[...] += mm_tn(hf_ref[...], flow_ref[...])
+
+    for copy in dha_copies(dha_out, p_ref, dha_sem, windows - 1, windows, share):
+        copy.wait()
+    fold = model // width
+    for block in range(3 * width // 128):
+        part, lane = divmod(block * 128, width)
+        gw_wide[...] = gw_acc[:, block * 128 : (block + 1) * 128]
+        for piece in range(fold):
+            at = piece * width + lane
+            p_ref[part * width : (part + 1) * width, at : at + 128] = gw_wide[
+                pl.ds(piece, width, stride=fold), :
+            ].astype(bf16)
+    p_ref[3 * width :, :] = go_acc[...].astype(bf16)
+    store = store_p(grads_out.at[pl.ds(0, 4 * width), :])
+    store.start()
+    store.wait()
+
+    hops_in(1, 3)
+    ffn(2, [obuf.at[1, n] for n in range(4)], None)
+
+    for w in range(2):
+
+        @pl.when(outer)
+        def _():
+            copy_a(w).wait_send()
+
+        @pl.when(inner)
+        def _():
+            copy_a(w).wait_recv()
+
+    for k in range(1, 4):
+        copy_d(k).wait_send()
+        copy_e(k, place).wait_send()
+    for g in range(2):
+        for d in range(1, 4):
+            for up in (True, False):
+
+                @pl.when(sends(d, up))
+                def _():
+                    hop(g, d, up).wait_send()
+
+
+def dha_copies(dha_out, p_ref, sem, w, windows, share):
+    copies = []
+    per = p_ref.shape[0] // share
+    for n in range(per):
+        block = w * per + n
+        copies.append(
+            pltpu.make_async_copy(
+                p_ref.at[pl.ds(n * share, share), :],
+                dha_out.at[block % windows, pl.ds(block // windows * share, share), :],
+                sem.at[n],
+            )
+        )
+    return copies
+
+
+def lines_kernel(
+    cuts,
+    windows,
+    order,
+    ready,
+    rows_in,
+    drm_ref,
+    gains_ref,
+    x_ref,
+    dha_ref,
+    part_ref,
+    own_in,
+    ra_in,
+    out_ref,
+    grad_ref,
+    ra,
+    rb,
+    rc,
+    value,
+    own,
+    piece,
+    x_rows,
+    grad,
+    a_send,
+    a_recv,
+    b_send,
+    b_recv,
+    c_send,
+    c_recv,
+    g_send,
+    g_recv,
+    v_sem,
+    o_sem,
+    r_sem,
+    x_sem,
+    l_sem,
+    i_sem,
+):
     place = lax.axis_index("tensor")
     lower = place < 2
     outer = (place == 0) | (place == 3)
@@ -442,7 +863,7 @@
 
     def whole(f):
         kind, index = order[f]
-        return part_refs[index] if kind == 0 else dha_ref.at[index]
+        return part_ref.at[index] if kind == 0 else dha_ref.at[index]
 
     def copy_a(f):
         far = rows_ref(whole(f), jnp.where(lower, 1, 0), share, 3)
@@ -460,17 +881,46 @@
         return pltpu.make_async_copy(whole(f), value.at[f], v_sem.at[f])
 
     def load_own(w):
-        return pltpu.make_async_copy(own_refs[w], own.at[w], o_sem.at[w])
-
-    def copy_g(w, k, origin):
+        return pltpu.make_async_copy(own_in.at[w], own.at[w], o_sem.at[w])
+
+    def load_ra(f):
+        return pltpu.make_async_copy(ra_in.at[order[f][1]], ra.at[f], r_sem.at[f])
+
+    def hop(w, d, up, origin):
         rows = pl.ds(pl.multiple_of(w * 4 * share + origin * share, share), share)
+        n = 0 if up else 1
         return remote(
-            piece.at[w],
+            piece.at[w] if d == 1 else out_ref.at[rows, :],
             out_ref.at[rows, :],
-            g_send.at[w, k - 1],
-            g_recv.at[w, k - 1],
-            lax.rem(place + k, 4),
+            g_send.at[w, d - 1, n],
+            g_recv.at[w, d - 1, n],
+            lax.rem(place + (1 if up else 3), 4),
         )
+
+    def sends(d, up):
+        if up:
+            return (place >= d - 1) & (place <= 2)
+        return (place <= 4 - d) & (place >= 1)
+
+    def receives(d, up):
+        return place >= d if up else place <= 3 - d
+
+    def source(d, up):
+        return jnp.clip(place - (d - 1) if up else place + (d - 1), 0, 3)
+
+    def hops(w, d):
+        for up in (True, False):
+
+            @pl.when(sends(d, up))
+            def _():
+                hop(w, d, up, source(d, up)).start()
+
+    def hops_in(w, d):
+        for up in (True, False):
+
+            @pl.when(receives(d, up))
+            def _():
+                hop(w, d, up, source(d + 1, up)).wait_recv()
 
     def keep(w):
         rows = pl.ds(pl.multiple_of(w * 4 * share + place * share, share), share)
@@ -491,11 +941,17 @@
         load_own(w).start()
     x_load.start()
     greet_line(place)
+    sent = list(range(ready, folds))
 
     @pl.when(outer)
     def _():
-        for f in range(2):
+        for f in sent[:2]:
             copy_a(f).start()
+
+    @pl.when(inner)
+    def _():
+        for f in range(ready):
+            load_ra(f).start()
 
     def add_rows(buffer, at, f, index):
         rows = pl.ds(pl.multiple_of(at * share, share), share)
@@ -506,7 +962,6 @@
     def finish(f, terms):
         kind, index = order[f]
         if kind == 0:
-            load_own(index).wait()
             total = own[index]
         else:
             mine = pl.ds(pl.multiple_of(place * share, share), share)
@@ -515,9 +970,6 @@
             total = total + term.astype(f32)
         if kind == 0:
             piece[index] = total.astype(bf16)
-            for k in range(1, 4):
-                copy_g(index, k, place).start()
-            keep(index).start()
         else:
             first = place * (cuts * share) + index * share
             count = drm_ref.shape[0]
@@ -532,44 +984,71 @@
 
     for f in range(folds):
         load(f).wait()
+    for w in range(windows):
+        load_own(w).wait()
     x_load.wait()
+    moving = {}
     for step in range(folds + 1):
-
-        @pl.when(inner)
-        def _():
-            if step < folds:
-                copy_a(step).wait_recv()
+        if step < folds:
+
+            @pl.when(inner)
+            def _():
+                if step < ready:
+                    load_ra(step).wait()
+                else:
+                    copy_a(step).wait_recv()
                 for n in range(2):
                     add_rows(
                         ra, jnp.where(lower, 1, 0) + n, step, jnp.where(lower, 2, 0) + n
                     )
                 copy_b(step).start()
-            if step > 0:
-                f = step - 1
+
+        if step > 0:
+            f = step - 1
+
+            @pl.when(inner)
+            def _():
                 copy_b(f).wait_recv()
                 add_rows(rb, jnp.where(lower, 0, 1), f, jnp.where(lower, 0, 3))
                 copy_c(f).start()
-
-        if step > 0:
-            f = step - 1
+                sel_a = pl.ds(pl.multiple_of(jnp.where(lower, 0, 2) * share, share), share)
+                sel_b = pl.ds(pl.multiple_of(jnp.where(lower, 1, 0) * share, share), share)
+                finish(f, [ra[f, sel_a, :], rb[f, sel_b, :]])
 
             @pl.when(outer)
             def _():
                 copy_c(f).wait_recv()
                 finish(f, [rc[f]])
 
-            @pl.when(inner)
+            for w in list(moving):
+                hops_in(w, moving[w])
+                if moving[w] == 3:
+                    del moving[w]
+                else:
+                    moving[w] += 1
+                    hops(w, moving[w])
+            kind, index = order[f]
+            if kind == 0:
+                hops(index, 1)
+                keep(index).start()
+                moving[index] = 1
+
+        if ready <= step < folds:
+
+            @pl.when(outer)
             def _():
-                sel_a = pl.ds(pl.multiple_of(jnp.where(lower, 0, 2) * share, share), share)
-                sel_b = pl.ds(pl.multiple_of(jnp.where(lower, 1, 0) * share, share), share)
-                finish(f, [ra[f, sel_a, :], rb[f, sel_b, :]])
-
-        @pl.when(outer)
-        def _():
-            if step < folds:
                 copy_a(step).wait_send()
-            if step + 2 < folds:
-                copy_a(step + 2).start()
+                if step + 2 < folds:
+                    copy_a(step + 2).start()
+
+    while moving:
+        for w in list(moving):
+            hops_in(w, moving[w])
+            if moving[w] == 3:
+                del moving[w]
+            else:
+                moving[w] += 1
+                hops(w, moving[w])
 
     @pl.when(inner)
     def _():
@@ -579,9 +1058,13 @@
 
     for w in range(windows):
         keep(w).wait()
-        for k in range(1, 4):
-            copy_g(w, k, place).wait_send()
-            copy_g(w, k, lax.rem(place + 4 - k, 4)).wait_recv()
+        for d in range(1, 4):
+            for up in (True, False):
+
+                @pl.when(sends(d, up))
+                def _():
+                    hop(w, d, up, source(d, up)).wait_send()
+
     for c in range(cuts):
         store(c).wait()
 
@@ -593,6 +1076,15 @@
     for step in range(parts):
         origin = lax.rem(place_ref[0] + parts - step, parts)
         out_ref[pl.ds(pl.multiple_of(origin * share, share), share), :] = refs[step][...]
+
+
+def spread_kernel(tile_ref, used_ref, *refs):
+    out_ref = refs[-1]
+    step = pl.program_id(0)
+    per = len(refs) - 1
+    for n in range(per):
+        used = used_ref[step * per + n] > 0
+        out_ref[n] = jnp.where(used, refs[n][0], jnp.zeros((), bf16))
 
 
 def copy_kernel(in_ref, out_ref):
@@ -647,26 +1139,7 @@
     return lax.dynamic_slice_in_dim(value, index * share, count * share, 0)
 
 
-def line_sums(value, ship, share):
-    place = lax.axis_index("tensor")
-    lower = place < 2
-    first = lax.ppermute(ship, "tensor", [(0, 1), (3, 2)])
-    send = rows_at(value, jnp.where(lower, 2, 0), share, 2).astype(f32)
-    send = send + rows_at(first, jnp.where(lower, 1, 0), share, 2).astype(f32)
-    second = lax.ppermute(send.astype(bf16), "tensor", [(1, 2), (2, 1)])
-    send = rows_at(value, jnp.where(lower, 0, 3), share, 1).astype(f32)
-    send = send + rows_at(second, jnp.where(lower, 0, 1), share, 1).astype(f32)
-    third = lax.ppermute(send.astype(bf16), "tensor", [(1, 0), (2, 3)])
-    return (
-        rows_at(first, jnp.where(lower, 0, 2), share, 1),
-        rows_at(second, jnp.where(lower, 1, 0), share, 1),
-        third,
-    )
-
-
-def other_sums(value, ship, share):
-    if lax.axis_size("tensor") == 4:
-        return line_sums(value, ship, share)
+def other_sums(value, share):
     place = lax.axis_index("tensor")
     total = lax.psum_scatter(value, "tensor", scatter_dimension=0, tiled=True)
     own = rows_at(value, place, share, 1).astype(f32)
@@ -879,7 +1352,11 @@
             name="attend",
         )(q, k, v, before)
 
-    early = max(seq_count - 1, 1)
+    mask_rows = seq_count * count
+    share = window // parts
+    share_rows = total_rows // parts
+    lines = parts == 4 and seq_count == 3 and hidden == model and mask_rows <= window // 2
+    early = seq_count if lines else max(seq_count - 1, 1)
     o_own = []
     for w in range(early):
         o_own.append(attend_window(w, o_own[-1] if o_own else o_m))
@@ -910,229 +1387,125 @@
     w_up = ffn_flat[1].reshape(model, hidden)
     w_down = ffn_flat[2].reshape(hidden, model)
 
-    mask_rows = seq_count * count
-    cols = min(256, hidden)
-    col_block = pl.BlockSpec((model, cols), lambda c: (0, c))
-    down_block = pl.BlockSpec((cols, model), lambda c: (c, 0))
-    r_m, dhf_part, ffn_grad = pl.pallas_call(
-        functools.partial(ffn_masked_kernel, parts),
-        out_shape=[
-            jax.ShapeDtypeStruct((mask_rows, model), f32),
-            jax.ShapeDtypeStruct((mask_rows, model), bf16),
-            jax.ShapeDtypeStruct((3, hidden, model), bf16),
-        ],
-        grid=(hidden // cols,),
-        in_specs=[
-            whole_spec((mask_rows, model)),
-            whole_spec((mask_rows, model)),
-            whole_spec((2, model)),
-            col_block,
-            col_block,
-            down_block,
-        ]
-        + [whole_spec((mask_rows, width))] * parts
-        + [whole_spec((width, model))] * parts,
-        out_specs=[
-            whole_spec((mask_rows, model)),
-            whole_spec((mask_rows, model)),
-            whole_spec((3, hidden, model)),
-        ],
-        scratch_shapes=[
-            pltpu.VMEM((mask_rows, model), bf16),
-            pltpu.VMEM((mask_rows, model), f32),
-            pltpu.VMEM((cols // 128, model, 128), f32),
-        ],
-        compiler_params=params(),
-        cost_estimate=cost(
-            mask_rows * model * (18 * hidden + 2 * model), 20e6, mask_rows * hidden
-        ),
-        name="ffn_masked",
-    )(x_m, cot, norm_gains, w_gate, w_up, w_down, *o_ms, *w_outs)
-
-    for w in range(early, seq_count):
-        o_own.append(attend_window(w, r_m))
-    windows_o = [around(o) for o in o_own]
-
-    share_m = mask_rows // parts
-    dhf_mine = lax.dynamic_slice_in_dim(dhf_part, place * share_m, share_m, 0).astype(f32)
-    for step in range(1, parts):
-        send = lax.dynamic_slice_in_dim(
-            dhf_part, lax.rem(place + step, parts) * share_m, share_m, 0
-        )
-        dhf_mine = dhf_mine + lax.ppermute(
-            send, "tensor", [(i, (i + step) % parts) for i in range(parts)]
-        ).astype(f32)
-    dhf_all = around(dhf_mine.astype(bf16))
-    dhf = jnp.zeros((mask_rows, model), bf16)
-    for step, piece in enumerate(dhf_all):
-        origin = lax.rem(place + parts - step, parts)
-        dhf = lax.dynamic_update_slice_in_dim(dhf, piece, origin * share_m, 0)
-
-    share = window // parts
-    far = share * (parts - 1)
-    layer_out = None
-
-    def ffn_window(w, before):
-        return pl.pallas_call(
-            after(functools.partial(ffn_kernel, parts), 6 + 2 * parts, 1),
+    flat_rows = jnp.where(
+        rows >= 0, rows + window * jnp.arange(seq_count, dtype=jnp.int32)[:, None], -1
+    ).reshape(1, mask_rows)
+    if lines:
+        anywhere = pl.BlockSpec(memory_space=pl.ANY)
+        inside = pl.BlockSpec(memory_space=pltpu.VMEM)
+        dma = pltpu.SemaphoreType.DMA
+        grad_rows = 4 * width + 3 * hidden
+        part, own, first_sums, dha, grads, dr_m, gains_part = pl.pallas_call(
+            functools.partial(middle_kernel, seq_count),
             out_shape=[
-                jax.ShapeDtypeStruct((window, model), bf16),
-                jax.ShapeDtypeStruct((far, model), bf16),
-                jax.ShapeDtypeStruct((share, model), f32),
+                jax.ShapeDtypeStruct((seq_count, window, model), bf16),
+                jax.ShapeDtypeStruct((seq_count, share, model), f32),
+                jax.ShapeDtypeStruct((2, 3 * share, model), bf16),
+                jax.ShapeDtypeStruct((seq_count, window, model), bf16),
+                jax.ShapeDtypeStruct((grad_rows, model), bf16),
+                jax.ShapeDtypeStruct((mask_rows, model), f32),
+                jax.ShapeDtypeStruct((2, model), f32),
             ],
-            grid_spec=pltpu.PrefetchScalarGridSpec(
-                num_scalar_prefetch=1,
-                grid=(hidden // cols,),
-                in_specs=[
-                    pl.BlockSpec((window, model), lambda c, place_ref: (w, 0)),
-                    whole_spec((2, model)),
-                    pl.BlockSpec((model, cols), lambda c, place_ref: (0, c)),
-                    pl.BlockSpec((model, cols), lambda c, place_ref: (0, c)),
-                    pl.BlockSpec((cols, model), lambda c, place_ref: (c, 0)),
-                ]
-                + [whole_spec((window, width))] * parts
-                + [whole_spec((width, model))] * parts
-                + [UNREAD],
-                out_specs=[
-                    whole_spec((window, model)),
-                    whole_spec((far, model)),
-                    whole_spec((share, model)),
-                ],
-                scratch_shapes=[
-                    pltpu.VMEM((window, model), f32),
-                    pltpu.VMEM((window, model), bf16),
-                    pltpu.VMEM((window, model), f32),
-                ],
-            ),
-            compiler_params=params(),
-            cost_estimate=cost(
-                window * model * (6 * hidden + 2 * model), 16e6, window * hidden
-            ),
-            name="ffn",
+            in_specs=[inside] * (13 + 3 * parts) + [anywhere] * 5,
+            out_specs=[anywhere] * 5 + [inside] * 2,
+            scratch_shapes=[
+                pltpu.VMEM((window, model), f32),
+                pltpu.VMEM((window, model), bf16),
+                pltpu.VMEM((window, model), f32),
+                pltpu.VMEM((window, model), bf16),
+                pltpu.VMEM((share, model), f32),
+                pltpu.VMEM((2, 4, window, width), bf16),
+                pltpu.VMEM((window, model), bf16),
+                pltpu.VMEM((2, 2, window, width), bf16),
+                pltpu.VMEM((window, 3 * width), bf16),
+                pltpu.VMEM((model, 3 * width), f32),
+                pltpu.VMEM((model, 128), f32),
+                pltpu.VMEM((width, model), f32),
+                pltpu.VMEM((mask_rows, model), f32),
+                pltpu.VMEM((4, mask_rows, model // 4), bf16),
+                pltpu.VMEM((3, mask_rows, model // 4), bf16),
+                pltpu.VMEM((4, mask_rows, model // 4), bf16),
+                dma((2,)),
+                dma,
+                dma((2, 2)),
+                dma((2, 3)),
+                dma,
+                dma((window // share,)),
+                dma,
+                dma((2,)),
+                dma((2,)),
+                dma((2, 3, 2)),
+                dma((2, 3, 2)),
+                dma((3,)),
+                dma((3,)),
+                dma((3,)),
+                dma((3,)),
+            ],
+            compiler_params=params(collective_id=1, has_side_effects=True),
+            cost_estimate=cost(1e11, 100e6),
+            name="middle",
         )(
-            place_ref,
-            tokens,
+            rows[:, None, :],
             norm_gains,
+            x_m,
+            cot,
+            q_m,
+            cos_m,
+            sin_m,
+            cos,
+            sin,
+            w_qkv,
             w_gate,
             w_up,
             w_down,
-            *windows_o[w],
+            *o_ms,
             *w_outs,
-            before,
+            *around(o_own[0]),
+            tokens,
+            k,
+            v,
+            o_own[1],
+            o_own[2],
         )
 
-    def place_window(w, part, ship, own):
-        terms = other_sums(part, ship, share)
-        total = own
-        for term in terms:
-            total = total + term.astype(f32)
-        pieces = around(total.astype(bf16))
-        return pl.pallas_call(
-            after(place_kernel, 1 + parts, 0 if layer_out is None else 1),
-            out_shape=jax.ShapeDtypeStruct((total_rows, model), bf16),
+        slots = lax.axis_size("dp") * capacity
+        slot_hit = slot_index[None, :] == jnp.arange(slots, dtype=jnp.int32)[:, None]
+        group = 4
+        in_slots = pl.pallas_call(
+            spread_kernel,
+            out_shape=jax.ShapeDtypeStruct((slots, tile_rows, model), bf16),
             grid_spec=pltpu.PrefetchScalarGridSpec(
-                num_scalar_prefetch=1,
-                grid=(1,),
-                in_specs=[whole_spec((share, model))] * parts
-                + [UNREAD] * (layer_out is not None),
-                out_specs=pl.BlockSpec((window, model), lambda i, place_ref: (w, 0)),
+                num_scalar_prefetch=2,
+                grid=(slots // group,),
+                in_specs=[
+                    pl.BlockSpec(
+                        tile_block, lambda i, tile, used, n=n: (tile[i * group + n], 0, 0)
+                    )
+                    for n in range(group)
+                ],
+                out_specs=pl.BlockSpec(
+                    (group, tile_rows, model), lambda i, tile, used: (i, 0, 0)
+                ),
             ),
-            input_output_aliases={} if layer_out is None else {1 + parts: 0},
             compiler_params=params(),
-            cost_estimate=cost(0, 4 * window * model),
-            name="place",
-        )(place_ref, *pieces, *([] if layer_out is None else [layer_out]))
-
-    parts_out = [ffn_window(0, o_own[-1])]
-
-    share_rows = total_rows // parts
-    cuts = seq_count if share_rows % (16 * seq_count) == 0 else 1
-    cut_rows = share_rows // cuts
-    dr_m, dha, attn_grad, gains_part = pl.pallas_call(
-        after(attn_back_kernel, 16, 1),
-        out_shape=[
-            jax.ShapeDtypeStruct((mask_rows, model), f32),
-            jax.ShapeDtypeStruct((cuts, parts, cut_rows, model), bf16),
-            jax.ShapeDtypeStruct((4 * width, model), bf16),
-            jax.ShapeDtypeStruct((2, model), f32),
-        ],
-        grid=(seq_count,),
-        in_specs=[
-            pl.BlockSpec((1, 1, count), lambda i: (i, 0, 0)),
-            mask_model,
-            mask_model,
-            mask_model,
-            whole_spec((2, model)),
-            mask_head,
-            mask_head,
-            mask_head,
-            mask_head,
-            win_head,
-            win_head,
-            win_model,
-            whole_spec((window, width)),
-            whole_spec((window, width)),
-            whole_spec((width, model)),
-            whole_spec((model, 3 * width)),
-            UNREAD,
-        ],
-        out_specs=[
-            mask_model,
-            whole_spec((cuts, parts, cut_rows, model)),
-            whole_spec((4 * width, model)),
-            whole_spec((2, model)),
-        ],
-        scratch_shapes=[
-            pltpu.VMEM((model, 3 * width), f32),
-            pltpu.VMEM((width, model), f32),
-            pltpu.VMEM((2, model), f32),
-            pltpu.VMEM((window, 3 * width), bf16),
-            pltpu.VMEM((3 * width // 128, model, 128), f32),
-        ],
-        compiler_params=params(),
-        cost_estimate=cost(
-            12 * total_rows * model * width, 30e6, mask_rows * window * heads
-        ),
-        name="attn_back",
-    )(
-        rows[:, None, :],
-        dhf,
-        r_m,
-        cot,
-        norm_gains,
-        o_m,
-        q_m,
-        cos_m,
-        sin_m,
-        k,
-        v,
-        tokens,
-        cos,
-        sin,
-        w_out,
-        w_qkv,
-        parts_out[0][0],
-    )
-
-    for w in range(1, seq_count):
-        parts_out.append(ffn_window(w, gains_part if w == 1 else parts_out[-1][0]))
-
-    flat_rows = jnp.where(
-        rows >= 0, rows + window * jnp.arange(seq_count, dtype=jnp.int32)[:, None], -1
-    ).reshape(1, mask_rows)
-    if parts == 4 and cut_rows == share:
-        order = [(kind, i) for i in range(seq_count) for kind in (0, 1)]
+            cost_estimate=cost(0, 24 * capacity * tile_size),
+            name="spread",
+        )(
+            jnp.argmax(slot_hit, axis=1).astype(jnp.int32),
+            jnp.any(slot_hit, axis=1).astype(jnp.int32),
+            *[grads.reshape(-1, tile_rows, model)] * group,
+        )
+        reduced = lax.psum_scatter(in_slots, "dp", scatter_dimension=0, tiled=True).astype(f32)
+
+        order = [(0, 0), (0, 1), (1, 0), (0, 2), (1, 1), (1, 2)]
         folds = len(order)
-        anywhere = pl.BlockSpec(memory_space=pl.ANY)
-        inside = pl.BlockSpec(memory_space=pltpu.VMEM)
-        dma = pltpu.SemaphoreType.DMA
         layer_out, input_grad = pl.pallas_call(
-            functools.partial(lines_kernel, cuts, seq_count, order),
+            after(functools.partial(lines_kernel, seq_count, seq_count, order, 2), 8, 1),
             out_shape=[
                 jax.ShapeDtypeStruct((total_rows, model), bf16),
                 jax.ShapeDtypeStruct((share_rows, model), bf16),
             ],
-            in_specs=[inside] * 3 + [anywhere] * (2 + 2 * seq_count),
+            in_specs=[inside] * 3 + [anywhere] * 6,
             out_specs=[anywhere] * 2,
             scratch_shapes=[
                 pltpu.VMEM((folds, 3 * share, model), bf16),
@@ -1142,22 +1515,23 @@
                 pltpu.VMEM((seq_count, share, model), f32),
                 pltpu.VMEM((seq_count, share, model), bf16),
                 pltpu.VMEM((share_rows, model), bf16),
-                pltpu.VMEM((cuts, share, model), bf16),
+                pltpu.VMEM((seq_count, share, model), bf16),
                 dma((folds,)),
                 dma((folds,)),
                 dma((folds,)),
                 dma((folds,)),
                 dma((folds,)),
                 dma((folds,)),
-                dma((seq_count, 3)),
-                dma((seq_count, 3)),
+                dma((seq_count, 3, 2)),
+                dma((seq_count, 3, 2)),
                 dma((folds,)),
                 dma((seq_count,)),
+                dma((2,)),
                 dma,
                 dma((seq_count,)),
-                dma((cuts,)),
+                dma((seq_count,)),
             ],
-            compiler_params=params(collective_id=1, has_side_effects=True),
+            compiler_params=params(collective_id=2, has_side_effects=True),
             cost_estimate=cost(4 * share_rows * mask_rows * model, 60e6),
             name="lines",
         )(
@@ -1165,16 +1539,218 @@
             dr_m,
             norm_gains,
             tokens,
-            dha.reshape(cuts, window, model),
-            *[outs[0] for outs in parts_out],
-            *[outs[2] for outs in parts_out],
+            dha,
+            part,
+            own,
+            first_sums,
+            in_slots,
         )
     else:
+        cols = min(256, hidden)
+        col_block = pl.BlockSpec((model, cols), lambda c: (0, c))
+        down_block = pl.BlockSpec((cols, model), lambda c: (c, 0))
+        r_m, dhf_part, ffn_grad = pl.pallas_call(
+            functools.partial(ffn_masked_kernel, parts),
+            out_shape=[
+                jax.ShapeDtypeStruct((mask_rows, model), f32),
+                jax.ShapeDtypeStruct((mask_rows, model), bf16),
+                jax.ShapeDtypeStruct((3, hidden, model), bf16),
+            ],
+            grid=(hidden // cols,),
+            in_specs=[
+                whole_spec((mask_rows, model)),
+                whole_spec((mask_rows, model)),
+                whole_spec((2, model)),
+                col_block,
+                col_block,
+                down_block,
+            ]
+            + [whole_spec((mask_rows, width))] * parts
+            + [whole_spec((width, model))] * parts,
+            out_specs=[
+                whole_spec((mask_rows, model)),
+                whole_spec((mask_rows, model)),
+                whole_spec((3, hidden, model)),
+            ],
+            scratch_shapes=[
+                pltpu.VMEM((mask_rows, model), bf16),
+                pltpu.VMEM((mask_rows, model), f32),
+                pltpu.VMEM((cols // 128, model, 128), f32),
+            ],
+            compiler_params=params(),
+            cost_estimate=cost(
+                mask_rows * model * (18 * hidden + 2 * model), 20e6, mask_rows * hidden
+            ),
+            name="ffn_masked",
+        )(x_m, cot, norm_gains, w_gate, w_up, w_down, *o_ms, *w_outs)
+
+        for w in range(early, seq_count):
+            o_own.append(attend_window(w, r_m))
+        windows_o = [around(o) for o in o_own]
+
+        share_m = mask_rows // parts
+        dhf_mine = lax.dynamic_slice_in_dim(dhf_part, place * share_m, share_m, 0).astype(f32)
+        for step in range(1, parts):
+            send = lax.dynamic_slice_in_dim(
+                dhf_part, lax.rem(place + step, parts) * share_m, share_m, 0
+            )
+            dhf_mine = dhf_mine + lax.ppermute(
+                send, "tensor", [(i, (i + step) % parts) for i in range(parts)]
+            ).astype(f32)
+        dhf_all = around(dhf_mine.astype(bf16))
+        dhf = jnp.zeros((mask_rows, model), bf16)
+        for step, piece in enumerate(dhf_all):
+            origin = lax.rem(place + parts - step, parts)
+            dhf = lax.dynamic_update_slice_in_dim(dhf, piece, origin * share_m, 0)
+
+        layer_out = None
+
+        def ffn_window(w, before):
+            return pl.pallas_call(
+                after(functools.partial(ffn_kernel, parts), 6 + 2 * parts, 1),
+                out_shape=[
+                    jax.ShapeDtypeStruct((window, model), bf16),
+                    jax.ShapeDtypeStruct((share, model), f32),
+                ],
+                grid_spec=pltpu.PrefetchScalarGridSpec(
+                    num_scalar_prefetch=1,
+                    grid=(hidden // cols,),
+                    in_specs=[
+                        pl.BlockSpec((window, model), lambda c, place_ref: (w, 0)),
+                        whole_spec((2, model)),
+                        pl.BlockSpec((model, cols), lambda c, place_ref: (0, c)),
+                        pl.BlockSpec((model, cols), lambda c, place_ref: (0, c)),
+                        pl.BlockSpec((cols, model), lambda c, place_ref: (c, 0)),
+                    ]
+                    + [whole_spec((window, width))] * parts
+                    + [whole_spec((width, model))] * parts
+                    + [UNREAD],
+                    out_specs=[
+                        whole_spec((window, model)),
+                        whole_spec((share, model)),
+                    ],
+                    scratch_shapes=[
+                        pltpu.VMEM((window, model), f32),
+                        pltpu.VMEM((window, model), bf16),
+                        pltpu.VMEM((window, model), f32),
+                    ],
+                ),
+                compiler_params=params(),
+                cost_estimate=cost(
+                    window * model * (6 * hidden + 2 * model), 16e6, window * hidden
+                ),
+                name="ffn",
+            )(
+                place_ref,
+                tokens,
+                norm_gains,
+                w_gate,
+                w_up,
+                w_down,
+                *windows_o[w],
+                *w_outs,
+                before,
+            )
+
+        def place_window(w, part, own):
+            terms = other_sums(part, share)
+            total = own
+            for term in terms:
+                total = total + term.astype(f32)
+            pieces = around(total.astype(bf16))
+            return pl.pallas_call(
+                after(place_kernel, 1 + parts, 0 if layer_out is None else 1),
+                out_shape=jax.ShapeDtypeStruct((total_rows, model), bf16),
+                grid_spec=pltpu.PrefetchScalarGridSpec(
+                    num_scalar_prefetch=1,
+                    grid=(1,),
+                    in_specs=[whole_spec((share, model))] * parts
+                    + [UNREAD] * (layer_out is not None),
+                    out_specs=pl.BlockSpec((window, model), lambda i, place_ref: (w, 0)),
+                ),
+                input_output_aliases={} if layer_out is None else {1 + parts: 0},
+                compiler_params=params(),
+                cost_estimate=cost(0, 4 * window * model),
+                name="place",
+            )(place_ref, *pieces, *([] if layer_out is None else [layer_out]))
+
+        parts_out = [ffn_window(0, o_own[-1])]
+
+        cuts = seq_count if share_rows % (16 * seq_count) == 0 else 1
+        cut_rows = share_rows // cuts
+        dr_m, dha, attn_grad, gains_part = pl.pallas_call(
+            after(attn_back_kernel, 16, 1),
+            out_shape=[
+                jax.ShapeDtypeStruct((mask_rows, model), f32),
+                jax.ShapeDtypeStruct((cuts, parts, cut_rows, model), bf16),
+                jax.ShapeDtypeStruct((4 * width, model), bf16),
+                jax.ShapeDtypeStruct((2, model), f32),
+            ],
+            grid=(seq_count,),
+            in_specs=[
+                pl.BlockSpec((1, 1, count), lambda i: (i, 0, 0)),
+                mask_model,
+                mask_model,
+                mask_model,
+                whole_spec((2, model)),
+                mask_head,
+                mask_head,
+                mask_head,
+                mask_head,
+                win_head,
+                win_head,
+                win_model,
+                whole_spec((window, width)),
+                whole_spec((window, width)),
+                whole_spec((width, model)),
+                whole_spec((model, 3 * width)),
+                UNREAD,
+            ],
+            out_specs=[
+                mask_model,
+                whole_spec((cuts, parts, cut_rows, model)),
+                whole_spec((4 * width, model)),
+                whole_spec((2, model)),
+            ],
+            scratch_shapes=[
+                pltpu.VMEM((model, 3 * width), f32),
+                pltpu.VMEM((width, model), f32),
+                pltpu.VMEM((2, model), f32),
+                pltpu.VMEM((window, 3 * width), bf16),
+                pltpu.VMEM((3 * width // 128, model, 128), f32),
+            ],
+            compiler_params=params(),
+            cost_estimate=cost(
+                12 * total_rows * model * width, 30e6, mask_rows * window * heads
+            ),
+            name="attn_back",
+        )(
+            rows[:, None, :],
+            dhf,
+            r_m,
+            cot,
+            norm_gains,
+            o_m,
+            q_m,
+            cos_m,
+            sin_m,
+            k,
+            v,
+            tokens,
+            cos,
+            sin,
+            w_out,
+            w_qkv,
+            parts_out[0][0],
+        )
+
+        for w in range(1, seq_count):
+            parts_out.append(ffn_window(w, gains_part if w == 1 else parts_out[-1][0]))
+
         input_grad = None
         for cut in range(cuts):
             value = dha[cut].reshape(parts * cut_rows, model)
-            ship = rows_at(value, jnp.where(place < parts // 2, 1, 0), cut_rows, parts - 1)
-            terms = other_sums(value, ship, cut_rows)
+            terms = other_sums(value, cut_rows)
             before = [] if input_grad is None else [input_grad]
             input_grad = pl.pallas_call(
                 after(
@@ -1212,28 +1788,29 @@
         for w, outs in enumerate(parts_out):
             layer_out = place_window(w, *outs)
 
+        def total_tiles(tiles, before):
+            piece = lax.psum_scatter(tiles, "dp", scatter_dimension=0, tiled=True)
+            piece = pl.pallas_call(
+                after(copy_kernel, 1, 1),
+                out_shape=jax.ShapeDtypeStruct(piece.shape, bf16),
+                in_specs=[pl.BlockSpec(memory_space=pltpu.VMEM), UNREAD],
+                out_specs=pl.BlockSpec(memory_space=pltpu.VMEM),
+                compiler_params=params(),
+                name="copy",
+            )(piece, before)
+            return lax.all_gather(piece, "dp", axis=0, tiled=True)
+
+        ffn_grads = total_tiles(ffn_grad.reshape(3 * hidden, model), parts_out[1][0])
+        attn_grads = total_tiles(attn_grad, parts_out[-1][0])
+        tiles = jnp.concatenate([attn_grads, ffn_grads], axis=0).reshape(-1, tile_rows, model)
+        reduced = tiles[slot_tile].astype(f32)
+
     even = jnp.array([[1.0], [1.0 / parts]], f32)
     gain_grad = small_total(gains_part * even)
     _, gain_moment, gain_new = adam_update(
         gain_grad, gain_first, gain_second, norm_gains, gain_rate, 0.0
     )
 
-    def total_tiles(tiles, before):
-        piece = lax.psum_scatter(tiles, "dp", scatter_dimension=0, tiled=True)
-        piece = pl.pallas_call(
-            after(copy_kernel, 1, 1),
-            out_shape=jax.ShapeDtypeStruct(piece.shape, bf16),
-            in_specs=[pl.BlockSpec(memory_space=pltpu.VMEM), UNREAD],
-            out_specs=pl.BlockSpec(memory_space=pltpu.VMEM),
-            compiler_params=params(),
-            name="copy",
-        )(piece, before)
-        return lax.all_gather(piece, "dp", axis=0, tiled=True)
-
-    ffn_grads = total_tiles(ffn_grad.reshape(3 * hidden, model), parts_out[1][0])
-    attn_grads = total_tiles(attn_grad, parts_out[-1][0])
-    tiles = jnp.concatenate([attn_grads, ffn_grads], axis=0).reshape(-1, tile_rows, model)
-    reduced = tiles[slot_tile].astype(f32)
     first_new, second_new, param_new = adam_update(
         reduced, first_moment[0], second_moment[0], master[0], weight_rate, weight_decay
     )

time: 826 us -> 676 us (0.82)
  waiting for transfers between devices: 149 us -> 67.7 us
  Pallas kernels: 523 us -> 474 us
  local copies, waits for them, and re-layouts: 34.4 us -> 24.8 us
    pallas_call x8 -> x3, Pallas kernels: 450 us -> 401 us  [the longest x1 225 us: on_device(): pl.pallas_call(after(functools.partial(lines_kernel, seq_count, seq_count...]
    ppermute x3 -> x0, waiting for transfers between devices: 45 us -> none  [on_device(): lax.ppermute(send, 'tensor', [(i, (i + step) % parts) for i in range(part...]
    ppermute x18 -> x9, waiting for transfers between devices: 47.5 us -> 18.6 us  [around(): lax.ppermute(value, 'tensor', [(i, (i + k) % size) for i in range(size)])]
    broadcast_in_dim x0 -> x1, other arithmetic: none -> 12.9 us  [on_device(): weight_low[None]]
    convert_element_type x1, other arithmetic: 12.7 us -> 0.57 us  [on_device(): jnp.any(slot_hit, axis=1).astype(jnp.int32)]
    ppermute x11, starting transfers between devices: 10.9 us -> 21.1 us  [exchange(): return lax.ppermute(value, axis, [(i, i ^ bit) for i in range(size)])]
    ppermute x18 -> x9, starting transfers between devices: 48.5 us -> 40.4 us  [around(): lax.ppermute(value, 'tensor', [(i, (i + k) % size) for i in range(size)])]
  transfers between devices with their start and end apart: 37 -> 22, of which waited for: 14 -> 11; matrix products, arithmetic and copies ran while one was open for 3% -> 4% of each run, Pallas kernels for 56% -> 43%
where the time goes in v3:
time: 676 us; the launch traced here: 667 us
  Pallas kernels  474 us (70%)
  waiting for transfers between devices  67.7 us (10%)
  starting transfers between devices  61.5 us (9%)
  local copies, waits for them, and re-layouts  24.8 us (4%)
  other arithmetic  24.4 us (4%)
  between operations  14.6 us (2%)
    pallas_call x1, Pallas kernels, on_device(): pl.pallas_call(after(functools.partial(lines_kernel, seq_count, seq_count...  225 us
    pallas_call x1, Pallas kernels, on_device(): pl.pallas_call(functools.partial(middle_kernel, seq_count), out_shape=[ja...  160 us
    ppermute x11, waiting for transfers between devices, exchange(): return lax.ppermute(value, axis, [(i, i ^ bit) for i in range(size)])  49 us
    ppermute x9, starting transfers between devices, around(): lax.ppermute(value, 'tensor', [(i, (i + k) % size) for i in range(size)])  40.4 us
    pallas_call x3, Pallas kernels, attend_window(): pl.pallas_call(after(attend_kernel, 3, 1), out_shape=jax.ShapeDtypeStruct...  34.3 us
    ppermute x11, starting transfers between devices, exchange(): return lax.ppermute(value, axis, [(i, i ^ bit) for i in range(size)])  21.1 us
    ppermute x9, waiting for transfers between devices, around(): lax.ppermute(value, 'tensor', [(i, (i + k) % size) for i in range(size)])  18.6 us
    pallas_call x1, Pallas kernels, on_device(): pl.pallas_call(spread_kernel, out_shape=jax.ShapeDtypeStruct((slots, tile...  15.7 us
  transfers between devices with their start and end apart: 22, of which 11 were waited for; matrix products, arithmetic and copies ran while one was open for 4% of the time, Pallas kernels for 43%

profile of v3, /device:TPU:0, one launch (start us, length us, event | category | flops | bytes accessed | tf_op | source)
XLA Modules:
  0.0 666.8 jit_solution(6521752318378670138)
XLA Ops:
  7.2 1.4 convert_reduce_fusion.rank_ref
  8.7 1.2 fusion.10.held_ref
  9.8 8.2 %cast.1 = (bf16[8,128,1024]{2,1,0:T(8,128)(2,1)}, bf16[8,128,1024]{2,1,0:T(8,128)(2,1)}) custom-call(s32[32]{0:T(128)} %convert_reduce_fusion.rank_ref, s32[8]{0:T(128)} %fusion.10.held_ref, f32[8,128,1024]{2,1,0:T(8,128)} %bitcast.57, f32[8,128,1024]{2,1,0:T(8,128)} %bitcast.58), custom_call_target="tpu_custom_call" | custom-call | bytes 12582912 | tf_op jit(solution)/shard_map/cast/pallas_call | solution.py:1229
  18.6 4.0 collective-permute-done
  22.6 1.3 dynamic-slice_add_fusion
  24.1 2.9 collective-permute-start.1
  27.0 1.5 collective-permute-start.3
  29.2 18.0 %collective-permute-done.1 = bf16[2,128,1024]{2,1,0:T(8,128)(2,1)S(1)} collective-permute-done((bf16[2,128,1024]{2,1,0:T(8,128)(2,1)S(1)}, bf16[2,128,1024]{2,1,0:T(8,128)(2,1)S(1)}, u32[]{:S(2)}, u32[]{:S(2)}) %collective-permute-start.1) | collective-permute-done | bytes 524320 | tf_op jit(solution)/shard_map/ppermute | solution.py:1102
  47.2 2.5 collective-permute-done.3
  49.9 2.5 collective-permute-start.2
  53.0 0.9 copy.34.rows_ref
  54.6 1.3 copy.32.cos_ref
  56.0 1.3 copy.33.sin_ref
  57.3 15.6 %collective-permute-done.4 = bf16[2,128,1024]{2,1,0:T(8,128)(2,1)S(1)} collective-permute-done((bf16[2,128,1024]{2,1,0:T(8,128)(2,1)S(1)}, bf16[2,128,1024]{2,1,0:T(8,128)(2,1)S(1)}, u32[]{:S(2)}, u32[]{:S(2)}) %collective-permute-start.4) | collective-permute-done | bytes 524320 | tf_op jit(solution)/shard_map/ppermute | solution.py:1102
  73.1 1.3 collective-permute-done.2
  74.8 0.9 fusion.3
  76.1 1.4 tile.39.cosm_ref
  77.7 1.4 tile.41.sinm_ref
  79.7 2.7 pad.9
  83.6 1.8 maximum_select_fusion
  85.5 1.5 collective-permute-start.9
  86.9 12.8 %qkv.1 = (bf16[3072,256]{1,0:T(8,128)(2,1)}, bf16[3072,256]{1,0:T(8,128)(2,1)}, bf16[3072,256]{1,0:T(8,128)(2,1)}, bf16[1024,768]{1,0:T(8,128)(2,1)}) custom-call(bf16[3072,1024]{1,0:T(8,128)(2,1)} %refs_3_.1, f32[2,1024]{1,0:T(2,128)} %refs_2_.1, bf16[1024,1024]{1,0:T(8,128)(2,1)} %bitcast.62, f32[1024,256]{1,0:T(8,128)} %copy.32.cos_ref, ...), custom_call_target="tpu_custom_call" | custom-call | flops 4831838208 | bytes 12582912 | tf_op jit(solution)/shard_map/qkv/pallas_call | solution.py:1287
  99.7 10.2 %attend_masked.1 = (bf16[480,256]{1,0:T(8,128)(2,1)}, bf16[480,256]{1,0:T(8,128)(2,1)}, bf16[480,1024]{1,0:T(8,128)(2,1)}) custom-call(s32[3,160,1]{2,1,0:T(8,128)} %copy.34.rows_ref, bf16[3072,1024]{1,0:T(8,128)(2,1)} %refs_3_.1, bf16[3072,256]{1,0:T(8,128)(2,1)} %get-tuple-element.30.q_ref.refs_0_, ...), custom_call_target="tpu_custom_call" | custom-call | flops 2013265920 | bytes 9000000 | tf_op jit(solution)/shard_map/attend_masked/pallas_call | solution.py:1310
  109.9 11.4 %attend.3.refs_3_.refs_8_ = bf16[1024,256]{1,0:T(8,128)(2,1)} custom-call(bf16[3072,256]{1,0:T(8,128)(2,1)} %get-tuple-element.30.q_ref.refs_0_, bf16[3072,256]{1,0:T(8,128)(2,1)} %get-tuple-element.31.k_ref.refs_1_.refs_13_, bf16[3072,256]{1,0:T(8,128)(2,1)} %get-tuple-element.32.v_ref.refs_2_.refs_14_, bf16[480,256]{1,0:T(8,128)(2,1)} %get-tuple-element.37.refs_3_.refs_0_), custom_call_target="tpu_custom_call" | custom-call | flops 4294967296 | bytes 2097152 | tf_op jit(solution)/shard_map/attend/pallas_call | solution.py:1337
  121.3 1.5 collective-permute-start.6
  122.8 2.4 collective-permute-start.7
  125.2 2.2 collective-permute-start.8
  127.6 11.4 %attend.4.refs_3_.refs_15_ = bf16[1024,256]{1,0:T(8,128)(2,1)} custom-call(bf16[3072,256]{1,0:T(8,128)(2,1)} %get-tuple-element.30.q_ref.refs_0_, bf16[3072,256]{1,0:T(8,128)(2,1)} %get-tuple-element.31.k_ref.refs_1_.refs_13_, bf16[3072,256]{1,0:T(8,128)(2,1)} %get-tuple-element.32.v_ref.refs_2_.refs_14_, bf16[1024,256]{1,0:T(8,128)(2,1)} %attend.3.refs_3_.refs_8_), custom_call_target="tpu_custom_call" | custom-call | flops 4294967296 | bytes 2097152 | tf_op jit(solution)/shard_map/attend/pallas_call | solution.py:1337
  138.9 2.5 collective-permute-start.11
  141.4 1.0 collective-permute-done.7.refs_2_
  142.5 26.7 %collective-permute-start.12 = (bf16[1024,256]{1,0:T(8,128)(2,1)S(1)}, bf16[1024,256]{1,0:T(8,128)(2,1)S(1)}, u32[]{:S(2)}, u32[]{:S(2)}) collective-permute-start(bf16[1024,256]{1,0:T(8,128)(2,1)S(1)} %copy-done.13), channel_id=1, source_target_pairs={{0,1},{1,2},{2,3},{3,0},{4,5},{5,6},{6,7},{7,4},{8,9},{9,10},{10,1... | collective-permute-start | bytes 1572872 | tf_op jit(solution)/shard_map/ppermute | solution.py:1133
  169.2 3.4 collective-permute-start.13
  172.6 11.5 %attend.5.refs_5_.refs_16_ = bf16[1024,256]{1,0:T(8,128)(2,1)} custom-call(bf16[3072,256]{1,0:T(8,128)(2,1)} %get-tuple-element.30.q_ref.refs_0_, bf16[3072,256]{1,0:T(8,128)(2,1)} %get-tuple-element.31.k_ref.refs_1_.refs_13_, bf16[3072,256]{1,0:T(8,128)(2,1)} %get-tuple-element.32.v_ref.refs_2_.refs_14_, bf16[1024,256]{1,0:T(8,128)(2,1)} %attend.4.refs_3_.refs_15_), custom_call_target="tpu_custom_call" | custom-call | flops 4294967296 | bytes 2097152 | tf_op jit(solution)/shard_map/attend/pallas_call | solution.py:1337
  184.1 7.4 %collect.1 = bf16[24,128,1024]{2,1,0:T(8,128)(2,1)} custom-call(s32[32]{0:T(128)} %multiply_add_fusion.refs_0_, bf16[64,128,1024]{2,1,0:T(8,128)(2,1)} %all-gather.2.cloned.1.call-done.refs_1_.refs_2_.refs_3_.refs_4_, bf16[64,128,1024]{2,1,0:T(8,128)(2,1)} %all-gather.2.cloned.1.call-done.refs_1_.refs_2_.refs_3_.refs_4_, ...), custom_call_target="tpu_custom_call" | custom-call | bytes 12582912 | tf_op jit(solution)/shard_map/collect/pallas_call | solution.py:1365
  191.6 5.7 fusion.14
  197.4 17.5 %collective-permute-done.13.refs_10_ = bf16[1024,256]{1,0:T(8,128)(2,1)} collective-permute-done((bf16[1024,256]{1,0:T(8,128)(2,1)S(1)}, bf16[1024,256]{1,0:T(8,128)(2,1)}, u32[]{:S(2)}, u32[]{:S(2)}) %collective-permute-start.13) | collective-permute-done | bytes 524320 | tf_op jit(solution)/shard_map/ppermute | solution.py:1133
  214.9 160.0 %middle.1 = (bf16[3,1024,1024]{2,1,0:T(8,128)(2,1)}, f32[3,256,1024]{2,1,0:T(8,128)}, bf16[2,768,1024]{2,1,0:T(8,128)(2,1)}, bf16[3,1024,1024]{2,1,0:T(8,128)(2,...) custom-call(s32[3,1,160]{2,1,0:T(1,128)} %broadcast_in_dim.62.rows_in, f32[2,1024]{1,0:T(2,128)} %refs_2_.1, ...), custom_call_target="tpu_custom_call" | custom-call | flops 99999997952 | bytes 100000000 | tf_op jit(solution)/shard_map/middle/pallas_call | solution.py:1398
  375.0 15.7 %spread.1.refs_8_ = bf16[64,128,1024]{2,1,0:T(8,128)(2,1)} custom-call(s32[64]{0:T(128)} %get-tuple-element.43.tile_ref, s32[64]{0:T(128)} %convert_element_type.40.used_ref, bf16[32,128,1024]{2,1,0:T(8,128)(2,1)} %bitcast.53, bf16[32,128,1024]{2,1,0:T(8,128)(2,1)} %bitcast.54, bf16[32,128,1024]{2,1,0:T(8,128)(2,1)} %bitcast.55, bf16[32,128,1024]{2,1,0:T(8,128)(2,1)} %bitcast.56), custom_call_target="tpu_custom_call" | custom-call | bytes 25165824 | tf_op jit(solution)/shard_map/spread/pallas_call | solution.py:1474
  391.4 1.2 collective-permute-done.15
  393.0 3.3 collective-permute-done.16
  396.3 1.3 collective-permute-start.17
  397.6 2.4 collective-permute-done.17
  400.0 4.8 collective-permute-start.18
  406.4 7.0 %collective-permute-start.19 = (f32[2,1024]{1,0:T(2,128)S(1)}, f32[2,1024]{1,0:T(2,128)S(1)}, u32[]{:S(2)}, u32[]{:S(2)}) collective-permute-start(f32[2,1024]{1,0:T(2,128)S(1)} %add.105), channel_id=1, source_target_pairs={{0,2},{1,3},{2,0},{3,1},{4,6},{5,7},{6,4},{7,5},{8,10},{9,11},{10,... | collective-permute-start | bytes 24584 | tf_op jit(solution)/shard_map/ppermute | solution.py:1102
  413.5 225.2 %lines.1 = (bf16[3072,1024]{1,0:T(8,128)(2,1)}, bf16[768,1024]{1,0:T(8,128)(2,1)}) custom-call(s32[1,480]{1,0:T(1,128)} %reshape.91.refs_0_, f32[480,1024]{1,0:T(8,128)} %get-tuple-element.38.refs_1_, f32[2,1024]{1,0:T(2,128)} %refs_2_.1, bf16[3072,1024]{1,0:T(8,128)(2,1)} %refs_3_.1, bf16[3,1024,1024]{2,1,0:T(8,128)(2,1)} %get-tuple-element.39.refs_4_, ...), custom_call_target="tpu_custom_call" | custom-call | flops 1509949440 | bytes 60000000 | tf_op jit(solution)/shard_map/lines/pallas_call | solution.py:1502
  639.3 12.9 %convert_bitcast_fusion = (bf16[1,8,128,1024]{3,2,1,0:T(8,128)(2,1)}, f32[8,128,1024]{2,1,0:T(8,128)}, f32[1,8,128,1024]{3,2,1,0:T(8,128)}, f32[1,8,128,1024]{3,2,1,0:T(8,128)}, f32[1,8,128,1024]{3,2,1,0:T(8,128)}) fusion(f32[1,8,128,1024]{3,2,1,0:T(8,128)} %param.20, bf16[8,128,1024]{2,1,0:T(8,128)(2,1)} %reduce-scatter.2.cloned.1.call-done, ...), kind=kLoop, calls=%fused_computation.11 | loop fusion | flops 22020096 | bytes 33554440 | tf_op jit(solution)/shard_map/broadcast_in_dim | solution.py:1829
  652.3 6.3 copy.39
  658.6 1.1 copy.40
  (99 shorter events, 9.7 us)
Async XLA Ops:
  7.2 177.0 %all-gather.2.cloned.1.call-start = ((), (), s32[]{:S(2)}) async-start(), calls=%async_computation.1 | async-start | bytes 18874368 | tf_op jit(solution)/shard_map/all_gather | solution.py:1271
  18.0 10.5 %copy-start.8 = (s32[3,153]{1,0:T(4,128)S(1)}, s32[3,153]{1,0:T(4,128)}, u32[]{:S(2)}) copy-start(s32[3,153]{1,0:T(4,128)} %param.12) | copy-start | bytes 5512
  18.1 621.2 %reduce-scatter.2.cloned.1.call-start = ((), (), s32[]{:S(2)}) async-start(), calls=%async_computation.2 | async-start | bytes 18874368 | tf_op jit(solution)/shard_map/reduce_scatter | solution.py:1498
  18.1 4.5 collective-permute-start
  24.1 23.1 %collective-permute-start.1 = (bf16[2,128,1024]{2,1,0:T(8,128)(2,1)S(1)}, bf16[2,128,1024]{2,1,0:T(8,128)(2,1)S(1)}, u32[]{:S(2)}, u32[]{:S(2)}) collective-permute-start(bf16[2,128,1024]{2,1,0:T(8,128)(2,1)S(1)} %get-tuple-element.61), channel_id=1, source_target_pairs={{0,8},{4,12},{8,0},{12,4},{16,24},{20,28},{24,16},{28,20},{1,9},{5... | collective-permute-start | bytes 1572872 | tf_op jit(solution)/shard_map/ppermute | solution.py:1102
  27.0 22.7 %collective-permute-start.3 = (bf16[2,128,1024]{2,1,0:T(8,128)(2,1)S(1)}, bf16[2,128,1024]{2,1,0:T(8,128)(2,1)S(1)}, u32[]{:S(2)}, u32[]{:S(2)}) collective-permute-start(bf16[2,128,1024]{2,1,0:T(8,128)(2,1)S(1)} %get-tuple-element.62), channel_id=1, source_target_pairs={{0,16},{4,20},{8,24},{12,28},{16,0},{20,4},{24,8},{28,12},{1,17},{... | collective-permute-start | bytes 1572872 | tf_op jit(solution)/shard_map/ppermute | solution.py:1102
  49.8 23.2 %collective-permute-start.4 = (bf16[2,128,1024]{2,1,0:T(8,128)(2,1)S(1)}, bf16[2,128,1024]{2,1,0:T(8,128)(2,1)S(1)}, u32[]{:S(2)}, u32[]{:S(2)}) collective-permute-start(bf16[2,128,1024]{2,1,0:T(8,128)(2,1)S(1)} %get-tuple-element.60), channel_id=1, source_target_pairs={{0,8},{4,12},{8,0},{12,4},{16,24},{20,28},{24,16},{28,20},{1,9},{5... | collective-permute-start | bytes 1572872 | tf_op jit(solution)/shard_map/ppermute | solution.py:1102
  49.9 24.5 %collective-permute-start.2 = (bf16[2,128,1024]{2,1,0:T(8,128)(2,1)S(1)}, bf16[2,128,1024]{2,1,0:T(8,128)(2,1)S(1)}, u32[]{:S(2)}, u32[]{:S(2)}) collective-permute-start(bf16[2,128,1024]{2,1,0:T(8,128)(2,1)S(1)} %get-tuple-element.59), channel_id=1, source_target_pairs={{0,16},{4,20},{8,24},{12,28},{16,0},{20,4},{24,8},{28,12},{1,17},{... | collective-permute-start | bytes 1572872 | tf_op jit(solution)/shard_map/ppermute | solution.py:1102
  74.7 4.3 copy-start.10
  74.7 4.3 copy-start.20
  74.7 8.9 %collective-permute-start.5 = (bf16[4,128,1024]{2,1,0:T(8,128)(2,1)S(1)}, bf16[4,128,1024]{2,1,0:T(8,128)(2,1)}, u32[]{:S(2)}, u32[]{:S(2)}) collective-permute-start(bf16[4,128,1024]{2,1,0:T(8,128)(2,1)S(1)} %pad_maximum_fusion), channel_id=1, source_target_pairs={{0,4},{4,0},{8,12},{12,8},{16,20},{20,16},{24,28},{28,24},{1,5},{5... | collective-permute-start | bytes 3145736 | tf_op jit(solution)/shard_map/ppermute | solution.py:1102
  85.4 1.5 copy-start
  85.5 53.5 %copy-start.2 = (bf16[2,128,1024]{2,1,0:T(8,128)(2,1)}, bf16[2,128,1024]{2,1,0:T(8,128)(2,1)S(1)}, u32[]{:S(2)}) copy-start(bf16[2,128,1024]{2,1,0:T(8,128)(2,1)S(1)} %slice.41) | copy-start | bytes 1572868
  85.5 87.1 %collective-permute-start.9 = (bf16[256,1024]{1,0:T(8,128)(2,1)S(1)}, bf16[256,1024]{1,0:T(8,128)(2,1)S(1)}, u32[]{:S(2)}, u32[]{:S(2)}) collective-permute-start(bf16[256,1024]{1,0:T(8,128)(2,1)S(1)} %bitcast.67), channel_id=1, source_target_pairs={{0,1},{1,2},{2,3},{3,0},{4,5},{5,6},{6,7},{7,4},{8,9},{9,10},{10,1... | collective-permute-start | bytes 1572872 | tf_op jit(solution)/shard_map/ppermute | solution.py:1133
  109.9 11.4 %copy-start.17 = (bf16[480,256]{1,0:T(8,128)(2,1)S(1)}, bf16[480,256]{1,0:T(8,128)(2,1)}, u32[]{:S(2)}) copy-start(bf16[480,256]{1,0:T(8,128)(2,1)} %get-tuple-element.37.refs_3_.refs_0_) | copy-start | bytes 737284
  121.3 21.2 %copy-start.13 = (bf16[1024,256]{1,0:T(8,128)(2,1)S(1)}, bf16[1024,256]{1,0:T(8,128)(2,1)}, u32[]{:S(2)}) copy-start(bf16[1024,256]{1,0:T(8,128)(2,1)} %attend.3.refs_3_.refs_8_) | copy-start | bytes 1572868
  121.3 17.7 %collective-permute-start.6 = (bf16[480,256]{1,0:T(8,128)(2,1)S(1)}, bf16[480,256]{1,0:T(8,128)(2,1)S(1)}, u32[]{:S(2)}, u32[]{:S(2)}) collective-permute-start(bf16[480,256]{1,0:T(8,128)(2,1)S(1)} %copy-done.17), channel_id=1, source_target_pairs={{0,1},{1,2},{2,3},{3,0},{4,5},{5,6},{6,7},{7,4},{8,9},{9,10},{10,1... | collective-permute-start | bytes 737288 | tf_op jit(solution)/shard_map/ppermute | solution.py:1133
  122.8 19.7 %collective-permute-start.7 = (bf16[480,256]{1,0:T(8,128)(2,1)S(1)}, bf16[480,256]{1,0:T(8,128)(2,1)S(1)}, u32[]{:S(2)}, u32[]{:S(2)}) collective-permute-start(bf16[480,256]{1,0:T(8,128)(2,1)S(1)} %copy-done.17), channel_id=1, source_target_pairs={{0,2},{1,3},{2,0},{3,1},{4,6},{5,7},{6,4},{7,5},{8,10},{9,11},{10,... | collective-permute-start | bytes 737288 | tf_op jit(solution)/shard_map/ppermute | solution.py:1133
  125.2 44.0 %collective-permute-start.8 = (bf16[480,256]{1,0:T(8,128)(2,1)S(1)}, bf16[480,256]{1,0:T(8,128)(2,1)}, u32[]{:S(2)}, u32[]{:S(2)}) collective-permute-start(bf16[480,256]{1,0:T(8,128)(2,1)S(1)} %copy-done.17), channel_id=1, source_target_pairs={{0,3},{1,0},{2,1},{3,2},{4,7},{5,4},{6,5},{7,6},{8,11},{9,8},{10,9... | collective-permute-start | bytes 737288 | tf_op jit(solution)/shard_map/ppermute | solution.py:1133
  127.4 69.9 %collective-permute-start.10 = (bf16[256,1024]{1,0:T(8,128)(2,1)S(1)}, bf16[256,1024]{1,0:T(8,128)(2,1)S(1)}, u32[]{:S(2)}, u32[]{:S(2)}) collective-permute-start(bf16[256,1024]{1,0:T(8,128)(2,1)S(1)} %bitcast.68), channel_id=1, source_target_pairs={{0,2},{1,3},{2,0},{3,1},{4,6},{5,7},{6,4},{7,5},{8,10},{9,11},{10,... | collective-permute-start | bytes 1572872 | tf_op jit(solution)/shard_map/ppermute | solution.py:1133
  138.9 33.7 %copy-start.18 = (bf16[480,256]{1,0:T(8,128)(2,1)}, bf16[480,256]{1,0:T(8,128)(2,1)S(1)}, u32[]{:S(2)}) copy-start(bf16[480,256]{1,0:T(8,128)(2,1)S(1)} %collective-permute-done.6.refs_1_) | copy-start | bytes 737284
  138.9 58.4 %collective-permute-start.11 = (bf16[256,1024]{1,0:T(8,128)(2,1)S(1)}, bf16[256,1024]{1,0:T(8,128)(2,1)S(1)}, u32[]{:S(2)}, u32[]{:S(2)}) collective-permute-start(bf16[256,1024]{1,0:T(8,128)(2,1)S(1)} %bitcast.69), channel_id=1, source_target_pairs={{0,3},{1,0},{2,1},{3,2},{4,7},{5,4},{6,5},{7,6},{8,11},{9,8},{10,9... | collective-permute-start | bytes 1572872 | tf_op jit(solution)/shard_map/ppermute | solution.py:1133
  142.5 30.1 %copy-start.19 = (bf16[480,256]{1,0:T(8,128)(2,1)}, bf16[480,256]{1,0:T(8,128)(2,1)S(1)}, u32[]{:S(2)}) copy-start(bf16[480,256]{1,0:T(8,128)(2,1)S(1)} %collective-permute-done.7.refs_2_) | copy-start | bytes 737284
  142.5 54.9 %collective-permute-start.12 = (bf16[1024,256]{1,0:T(8,128)(2,1)S(1)}, bf16[1024,256]{1,0:T(8,128)(2,1)S(1)}, u32[]{:S(2)}, u32[]{:S(2)}) collective-permute-start(bf16[1024,256]{1,0:T(8,128)(2,1)S(1)} %copy-done.13), channel_id=1, source_target_pairs={{0,1},{1,2},{2,3},{3,0},{4,5},{5,6},{6,7},{7,4},{8,9},{9,10},{10,1... | collective-permute-start | bytes 1572872 | tf_op jit(solution)/shard_map/ppermute | solution.py:1133
  169.2 45.7 %collective-permute-start.13 = (bf16[1024,256]{1,0:T(8,128)(2,1)S(1)}, bf16[1024,256]{1,0:T(8,128)(2,1)}, u32[]{:S(2)}, u32[]{:S(2)}) collective-permute-start(bf16[1024,256]{1,0:T(8,128)(2,1)S(1)} %copy-done.13), channel_id=1, source_target_pairs={{0,2},{1,3},{2,0},{3,1},{4,6},{5,7},{6,4},{7,5},{8,10},{9,11},{10,... | collective-permute-start | bytes 1572872 | tf_op jit(solution)/shard_map/ppermute | solution.py:1133
  172.6 11.6 %copy-start.12 = (bf16[256,1024]{1,0:T(8,128)(2,1)}, bf16[256,1024]{1,0:T(8,128)(2,1)S(1)}, u32[]{:S(2)}) copy-start(bf16[256,1024]{1,0:T(8,128)(2,1)S(1)} %collective-permute-done.9.refs_5_) | copy-start | bytes 1572868
  172.6 42.3 %collective-permute-start.14 = (bf16[1024,256]{1,0:T(8,128)(2,1)S(1)}, bf16[1024,256]{1,0:T(8,128)(2,1)}, u32[]{:S(2)}, u32[]{:S(2)}) collective-permute-start(bf16[1024,256]{1,0:T(8,128)(2,1)S(1)} %copy-done.13), channel_id=1, source_target_pairs={{0,3},{1,0},{2,1},{3,2},{4,7},{5,4},{6,5},{7,6},{8,11},{9,8},{10,9... | collective-permute-start | bytes 1572872 | tf_op jit(solution)/shard_map/ppermute | solution.py:1133
  197.3 17.6 %copy-start.14 = (bf16[256,1024]{1,0:T(8,128)(2,1)}, bf16[256,1024]{1,0:T(8,128)(2,1)S(1)}, u32[]{:S(2)}) copy-start(bf16[256,1024]{1,0:T(8,128)(2,1)S(1)} %collective-permute-done.10.refs_6_) | copy-start | bytes 1572868
  197.3 17.6 %copy-start.15 = (bf16[256,1024]{1,0:T(8,128)(2,1)}, bf16[256,1024]{1,0:T(8,128)(2,1)S(1)}, u32[]{:S(2)}) copy-start(bf16[256,1024]{1,0:T(8,128)(2,1)S(1)} %collective-permute-done.11.refs_7_) | copy-start | bytes 1572868
  197.3 17.6 %copy-start.16 = (bf16[1024,256]{1,0:T(8,128)(2,1)}, bf16[1024,256]{1,0:T(8,128)(2,1)S(1)}, u32[]{:S(2)}) copy-start(bf16[1024,256]{1,0:T(8,128)(2,1)S(1)} %collective-permute-done.12.refs_9_) | copy-start | bytes 1572868
  390.7 0.7 copy-start.4
  390.7 0.7 copy-start.9
  390.7 7.0 %copy-start.21 = (s32[1,32]{1,0:T(1,128)S(1)}, s32[1,32]{1,0:T(1,128)}, u32[]{:S(2)}) copy-start(s32[1,32]{1,0:T(1,128)} %param.17) | copy-start | bytes 388
  390.7 14.1 %copy-start.11 = (s32[32]{0:T(128)S(1)}, s32[32]{0:T(128)}, u32[]{:S(2)}) copy-start(s32[32]{0:T(128)} %convert_reduce_fusion.rank_ref) | copy-start | bytes 388
  390.7 14.2 %copy-start.5 = (s32[3,160]{1,0:T(4,128)S(1)}, s32[3,160]{1,0:T(4,128)}, u32[]{:S(2)}) copy-start(s32[3,160]{1,0:T(4,128)} %get-tuple-element.70) | copy-start | bytes 5764
  391.4 1.2 collective-permute-start.15
  392.7 3.7 collective-permute-start.16
  396.3 3.7 collective-permute-start.17
  400.0 6.4 collective-permute-start.18
  406.4 232.2 %collective-permute-start.19 = (f32[2,1024]{1,0:T(2,128)S(1)}, f32[2,1024]{1,0:T(2,128)S(1)}, u32[]{:S(2)}, u32[]{:S(2)}) collective-permute-start(f32[2,1024]{1,0:T(2,128)S(1)} %add.105), channel_id=1, source_target_pairs={{0,2},{1,3},{2,0},{3,1},{4,6},{5,7},{6,4},{7,5},{8,10},{9,11},{10,... | collective-permute-start | bytes 24584 | tf_op jit(solution)/shard_map/ppermute | solution.py:1102
  413.5 225.2 %copy-start.3 = (f32[2,1024]{1,0:T(2,128)S(1)}, f32[2,1024]{1,0:T(2,128)}, u32[]{:S(2)}) copy-start(f32[2,1024]{1,0:T(2,128)} %refs_2_.1) | copy-start | bytes 24580
  413.5 225.2 %copy-start.6 = (f32[2,1024]{1,0:T(2,128)S(1)}, f32[2,1024]{1,0:T(2,128)}, u32[]{:S(2)}) copy-start(f32[2,1024]{1,0:T(2,128)} %param.15) | copy-start | bytes 24580
  413.5 225.2 %copy-start.7 = (f32[2,1024]{1,0:T(2,128)S(1)}, f32[2,1024]{1,0:T(2,128)}, u32[]{:S(2)}) copy-start(f32[2,1024]{1,0:T(2,128)} %param.16) | copy-start | bytes 24580
  652.3 6.3 copy-start.1
Sparse Core Ops, SparseCore 0:
  18.2 111.0 all-gather.1
  390.8 124.0 reduce-scatter.1

commit v4 on v3

--- a/solution.py
+++ b/solution.py
@@ -2,6 +2,7 @@
 
 import jax
 import jax.numpy as jnp
+import numpy as np
 from jax import lax
 from jax.experimental import pallas as pl
 from jax.experimental.pallas import tpu as pltpu
@@ -382,8 +383,15 @@
     )
 
 
-def greet_line(place):
+def greet_line(place, others=()):
     barrier = pltpu.get_barrier_semaphore()
+    for axis, other in others:
+        pl.semaphore_signal(
+            barrier,
+            inc=1,
+            device_id={axis: other},
+            device_id_type=pl.DeviceIdType.MESH,
+        )
     for k in range(1, 4):
         pl.semaphore_signal(
             barrier,
@@ -391,11 +399,358 @@
             device_id={"tensor": lax.rem(place + k, 4)},
             device_id_type=pl.DeviceIdType.MESH,
         )
-    pl.semaphore_wait(barrier, 3)
+    pl.semaphore_wait(barrier, 3 + len(others))
+
+
+def sends(place, d, up):
+    if up:
+        return (place >= d - 1) & (place <= 2)
+    return (place <= 4 - d) & (place >= 1)
+
+
+def receives(place, d, up):
+    return place >= d if up else place <= 3 - d
+
+
+def each_way(place, d, rule, act):
+    for up in (True, False):
+
+        @pl.when(rule(place, d, up))
+        def _():
+            act(up)
 
 
 def rows_ref(ref, index, share, count):
     return ref.at[pl.ds(pl.multiple_of(index * share, share), count * share), :]
+
+
+def weights_kernel(
+    rank_ref,
+    held_ref,
+    master_ref,
+    low_ref,
+    out_ref,
+    mine,
+    got,
+    work,
+    trade,
+    h_send,
+    h_recv,
+    t_send,
+    t_recv,
+    f_send,
+    f_recv,
+    f_keep,
+):
+    me = lax.axis_index("dp")
+    core = lax.rem(me, 2)
+    tiles = mine.shape[0]
+    half = tiles // 2
+
+    def pair(bit):
+        return me + bit - 2 * bit * lax.rem(me // bit, 2)
+
+    def to(src, dst, send, recv, bit):
+        return pltpu.make_async_remote_copy(
+            src_ref=src,
+            dst_ref=dst,
+            send_sem=send,
+            recv_sem=recv,
+            device_id={"dp": pair(bit)},
+            device_id_type=pl.DeviceIdType.MESH,
+        )
+
+    def share(first):
+        return pl.ds(first * half, half)
+
+    swap = to(mine.at[share(1 - core)], got, h_send, h_recv, 1)
+
+    def move(stage, t):
+        bit = (2, 4)[(stage + t // (half // 2)) % 2]
+        return to(
+            work.at[stage, t],
+            trade.at[stage, t],
+            t_send.at[stage, t],
+            t_recv.at[stage, t],
+            bit,
+        )
+
+    def final(t):
+        return to(work.at[2, t], out_ref.at[core * half + t], f_send.at[t], f_recv.at[t], 1)
+
+    def final_in(t):
+        at = out_ref.at[(1 - core) * half + t]
+        return to(at, at, f_send.at[t], f_recv.at[t], 1)
+
+    def keep(t):
+        return pltpu.make_async_copy(
+            work.at[2, t], out_ref.at[core * half + t], f_keep.at[t]
+        )
+
+    barrier = pltpu.get_barrier_semaphore()
+    for bit in (1, 2, 4):
+        pl.semaphore_signal(
+            barrier, inc=1, device_id={"dp": pair(bit)}, device_id_type=pl.DeviceIdType.MESH
+        )
+    for t in range(tiles):
+        tile = master_ref[rank_ref[t]].astype(bf16)
+        mine[t] = jnp.where(held_ref[t] > 0, tile, jnp.zeros((), bf16))
+    pl.semaphore_wait(barrier, 3)
+    swap.start()
+    for n in range(low_ref.shape[0]):
+        low_ref[n] = master_ref[n].astype(bf16)
+    swap.wait_recv()
+    turns = [t + n for t in range(half // 2) for n in (0, half // 2)]
+    for t in turns:
+        work[0, t] = mine[core * half + t] + got[t]
+        move(0, t).start()
+    for stage in (1, 2):
+        for t in turns:
+            move(stage - 1, t).wait_recv()
+            work[stage, t] = work[stage - 1, t] + trade[stage - 1, t]
+            if stage == 1:
+                move(1, t).start()
+            else:
+                final(t).start()
+                keep(t).start()
+    for t in range(half):
+        final_in(t).wait_recv()
+    swap.wait_send()
+    for t in range(half):
+        keep(t).wait()
+        final(t).wait_send()
+        for stage in range(2):
+            move(stage, t).wait_send()
+
+
+def attend_all_kernel(
+    windows,
+    rows_in,
+    gains_ref,
+    tiles_ref,
+    cos_ref,
+    sin_ref,
+    x_hbm,
+    tiles_hbm,
+    om_out,
+    oa_out,
+    ob_out,
+    oc_out,
+    wo_out,
+    qm_ref,
+    xm_ref,
+    cosm_ref,
+    sinm_ref,
+    k_ref,
+    v_ref,
+    w_ref,
+    q_ref,
+    w_wide,
+    om_own,
+    o_own,
+    x_ref,
+    x_sem,
+    own_sem,
+    keep_sem,
+    m_send,
+    m_recv,
+    o_send,
+    o_recv,
+    w_send,
+    w_recv,
+    c_send,
+    c_recv,
+):
+    place = lax.axis_index("tensor")
+    window = x_ref.shape[1]
+    width = q_ref.shape[1]
+    count = rows_in.shape[1]
+    q_block = 256
+
+    def load_x(w):
+        return pltpu.make_async_copy(
+            x_hbm.at[pl.ds(w * window, window), :], x_ref.at[w % 2], x_sem.at[w % 2]
+        )
+
+    def hop(kind, d, up):
+        own, out, send, recv = (
+            (om_own, om_out, m_send, m_recv) if kind == 0 else (o_own.at[0], oa_out, o_send, o_recv)
+        )
+        src, dst = (d - 1, d) if up else ((5 - d) % 4, 4 - d)
+        n = 0 if up else 1
+        return remote(
+            own if d == 1 else out.at[src],
+            out.at[dst],
+            send.at[d - 1, n],
+            recv.at[d - 1, n],
+            lax.rem(place + (1 if up else 3), 4),
+        )
+
+    me = lax.axis_index("dp")
+    core = lax.rem(me, 2)
+    half = width // 2
+
+    def half_of(ref, first):
+        return ref.at[pl.ds(pl.multiple_of(first + core * half, half), half), :]
+
+    def hop_w(d, up):
+        src, dst = (d - 1, d) if up else ((5 - d) % 4, 4 - d)
+        n = 0 if up else 1
+        return remote(
+            half_of(tiles_hbm, 3 * width) if d == 1 else half_of(wo_out.at[src - 1], 0),
+            half_of(wo_out.at[dst - 1], 0),
+            w_send.at[d - 1, n],
+            w_recv.at[d - 1, n],
+            lax.rem(place + (1 if up else 3), 4),
+        )
+
+    sibling = me + 1 - 2 * core
+
+    def copy_w(n):
+        return pltpu.make_async_remote_copy(
+            src_ref=half_of(wo_out.at[n], 0),
+            dst_ref=half_of(wo_out.at[n], 0),
+            send_sem=c_send.at[n],
+            recv_sem=c_recv.at[n],
+            device_id={"dp": sibling},
+            device_id_type=pl.DeviceIdType.MESH,
+        )
+
+    def copy_w_in(n):
+        rows = pl.ds(pl.multiple_of((1 - core) * half, half), half)
+        return pltpu.make_async_remote_copy(
+            src_ref=wo_out.at[n].at[rows, :],
+            dst_ref=wo_out.at[n].at[rows, :],
+            send_sem=c_send.at[n],
+            recv_sem=c_recv.at[n],
+            device_id={"dp": sibling},
+            device_id_type=pl.DeviceIdType.MESH,
+        )
+
+    def any_hop(kind, d, up):
+        return hop_w(d, up) if kind == 2 else hop(kind, d, up)
+
+    def hops(kind, d):
+        each_way(place, d, sends, lambda up: any_hop(kind, d, up).start())
+
+    def hops_in(kind, d):
+        each_way(place, d, receives, lambda up: any_hop(kind, d, up).wait_recv())
+
+    def store(w):
+        to = (oa_out.at[0], ob_out, oc_out)[w]
+        return pltpu.make_async_copy(o_own.at[w], to, own_sem.at[w])
+
+    def attend_rows(w, first, last):
+        for pair in range(width // 128):
+            lanes = slice(pair * 128, pair * 128 + 128)
+            keys = slice(w * window, (w + 1) * window)
+
+            def block(i, carry):
+                rows = pl.ds(pl.multiple_of(w * window + i * q_block, q_block), q_block)
+                into = pl.ds(pl.multiple_of(i * q_block, q_block), q_block)
+                o_own[w, into, lanes] = attend(
+                    q_ref[rows, lanes], k_ref[keys, lanes], v_ref[keys, lanes]
+                )
+                return carry
+
+            lax.fori_loop(first, last, block, 0)
+
+    def picked(pick, table):
+        high = table.astype(bf16)
+        low = (table - high.astype(f32)).astype(bf16)
+        return mm(pick, high) + mm(pick, low)
+
+    def project(w):
+        rows = window // 2
+
+        def block(n, carry):
+            here = pl.ds(pl.multiple_of(n * rows, rows), rows)
+            at = pl.ds(pl.multiple_of(w * window + n * rows, rows), rows)
+            x = x_ref[w % 2, here, :].astype(f32)
+            hidden = (x * rms_scale(x) * gains_ref[0:1, :]).astype(bf16)
+            cos, sin = cos_ref[here, :], sin_ref[here, :]
+            q = mm(hidden, w_ref[:, 0:width])
+            q_ref[at, :] = (q * cos + swap_halves(q) * sin).astype(bf16)
+            k = mm(hidden, w_ref[:, width : 2 * width])
+            k_ref[at, :] = (k * cos + swap_halves(k) * sin).astype(bf16)
+            v_ref[at, :] = mm(hidden, w_ref[:, 2 * width : 3 * width]).astype(bf16)
+            return carry
+
+        load_x(w).wait()
+        lax.fori_loop(0, 2, block, 0)
+        at = slice(w * count, (w + 1) * count)
+        pick = (
+            lax.broadcasted_iota(jnp.int32, (count, window), 1) == rows_in[w]
+        ).astype(bf16)
+        xm_ref[at, :] = mm(pick, x_ref[w % 2]).astype(bf16)
+        if w + 2 < windows:
+            load_x(w + 2).start()
+        cosm_ref[at, :] = picked(pick, cos_ref[...])
+        sinm_ref[at, :] = picked(pick, sin_ref[...])
+        qm_ref[at, :] = mm(pick, q_ref[w * window : (w + 1) * window, :]).astype(bf16)
+
+    for w in range(2):
+        load_x(w).start()
+    greet_line(place, [("dp", sibling)])
+    blocks = window // q_block
+    hops(2, 1)
+    fold = tiles_ref.shape[1] // width
+    for block in range(3 * width // 128):
+        part, lane = divmod(block * 128, width)
+        for piece in range(fold):
+            at = piece * width + lane
+            w_wide[block, pl.ds(piece, width, stride=fold), :] = tiles_ref[
+                part * width : (part + 1) * width, at : at + 128
+            ].astype(f32)
+        w_ref[:, block * 128 : (block + 1) * 128] = w_wide[block].astype(bf16)
+    project(0)
+    hops_in(2, 1)
+    hops(2, 2)
+    attend_rows(0, 0, blocks)
+    hops(1, 1)
+    store(0).start()
+    hops_in(2, 2)
+    hops(2, 3)
+    project(1)
+    project(2)
+    hops_in(1, 1)
+    hops(1, 2)
+    for w in range(windows):
+        keys = slice(w * window, (w + 1) * window)
+        at = slice(w * count, (w + 1) * count)
+        for pair in range(width // 128):
+            lanes = slice(pair * 128, pair * 128 + 128)
+            om_own[at, lanes] = attend(
+                qm_ref[at, lanes], k_ref[keys, lanes], v_ref[keys, lanes]
+            )
+    hops(0, 1)
+    keep = pltpu.make_async_copy(om_own, om_out.at[0], keep_sem)
+    keep.start()
+    attend_rows(1, 0, blocks // 2)
+    hops_in(0, 1)
+    hops(0, 2)
+    attend_rows(1, blocks // 2, blocks)
+    store(1).start()
+    hops_in(0, 2)
+    hops(0, 3)
+    hops_in(1, 2)
+    hops(1, 3)
+    attend_rows(2, 0, blocks)
+    store(2).start()
+    hops_in(2, 3)
+    for n in range(3):
+        copy_w(n).start()
+    keep.wait()
+    for w in range(windows):
+        store(w).wait()
+    for kind in range(2):
+        hops_in(kind, 3)
+    for kind in range(3):
+        for d in range(1, 4):
+            each_way(place, d, sends, lambda up: any_hop(kind, d, up).wait_send())
+    for n in range(3):
+        copy_w(n).wait_send()
+        copy_w_in(n).wait_recv()
 
 
 def masked_attention_back(qm, do, k, v):
@@ -433,14 +788,18 @@
     cos_ref,
     sin_ref,
     w_ref,
-    wg_ref,
-    wu_ref,
-    wd_ref,
+    ffn_ref,
+    om_ref,
+    oa_ref,
+    wo_ref,
+    wo_far,
     *refs,
 ):
-    om_refs, wo_refs, oa_refs = refs[0:4], refs[4:8], refs[8:12]
-    x_hbm, k_hbm, v_hbm, o_one, o_two = refs[12:17]
-    part_out, own_out, ra_out, dha_out, grads_out, drm_ref, gain_ref = refs[17:24]
+    wg_ref, wu_ref, wd_ref = (ffn_ref.at[n] for n in range(3))
+    om_refs, oa_refs = ([ref.at[n] for n in range(4)] for ref in (om_ref, oa_ref))
+    wo_refs = [wo_ref] + [wo_far.at[n] for n in range(3)]
+    x_hbm, k_hbm, v_hbm, o_one, o_two = refs[0:5]
+    part_out, own_out, ra_out, rb_out, dha_out, grads_out, drm_ref, gain_ref = refs[5:13]
     (
         r_ref,
         hf_ref,
@@ -458,6 +817,10 @@
         dpart,
         drecv,
         dall,
+        bsum,
+        b_load,
+        b_send,
+        b_recv,
         o_load,
         x_sem,
         kv_sem,
@@ -473,14 +836,14 @@
         d_recv,
         e_send,
         e_recv,
-    ) = refs[24:]
+    ) = refs[13:]
     place = lax.axis_index("tensor")
     lower = place < 2
     outer = (place == 0) | (place == 3)
     inner = (place == 1) | (place == 2)
     window, model = x_ref.shape
     width = kv.shape[3]
-    hidden = wg_ref.shape[1]
+    hidden = ffn_ref.shape[2]
     share = own_ref.shape[0]
     count = rm_ref.shape[0] // windows
     masked = rm_ref.shape[0]
@@ -498,27 +861,11 @@
             lax.rem(place + (1 if up else 3), 4),
         )
 
-    def sends(d, up):
-        if up:
-            return (place >= d - 1) & (place <= 2)
-        return (place <= 4 - d) & (place >= 1)
-
-    def receives(d, up):
-        return place >= d if up else place <= 3 - d
-
     def hops(g, d):
-        for up in (True, False):
-
-            @pl.when(sends(d, up))
-            def _():
-                hop(g, d, up).start()
+        each_way(place, d, sends, lambda up: hop(g, d, up).start())
 
     def hops_in(g, d):
-        for up in (True, False):
-
-            @pl.when(receives(d, up))
-            def _():
-                hop(g, d, up).wait_recv()
+        each_way(place, d, receives, lambda up: hop(g, d, up).wait_recv())
 
     def load_o(g):
         return pltpu.make_async_copy((o_one, o_two)[g], obuf.at[g, 0], o_load.at[g])
@@ -562,13 +909,7 @@
     greet_line(place)
     load_o(0).wait()
     hops(0, 1)
-
     gain_att, gain_ffn = gains_ref[0:1, :], gains_ref[1:2, :]
-    r = xm_ref[...].astype(f32)
-    for om_ref, wo_ref in zip(om_refs, wo_refs):
-        r = r + mm(om_ref[...], wo_ref[...])
-    rm_ref[...] = r
-    hf_ref[0:masked, :] = (r * rms_scale(r) * gain_ffn).astype(bf16)
 
     def grad_copies(c):
         side = (c % 2) * 2 * cols
@@ -619,6 +960,65 @@
         for copy in grad_copies(c):
             copy.start()
 
+    def ffn(w, o_refs, next_x, between=None):
+        half = window // 2
+
+        def first(n, carry):
+            rows = pl.ds(pl.multiple_of(n * half, half), half)
+            r = x_ref[rows, :].astype(f32)
+            for o, wo in zip(o_refs, wo_refs):
+                r = r + mm(o[rows, :], wo[...])
+            r_ref[rows, :] = r
+            hf_ref[rows, :] = (r * rms_scale(r) * gain_ffn).astype(bf16)
+            return carry
+
+        lax.fori_loop(0, 2, first, 0)
+        if next_x is not None:
+            load_x(next_x).start()
+        acc_ref[...] = jnp.zeros_like(acc_ref)
+
+        def chunk(c, carry):
+            at = pl.ds(pl.multiple_of(c * cols, cols), cols)
+            hf = hf_ref[...]
+            g, u = mm(hf, wg_ref[:, at]), mm(hf, wu_ref[:, at])
+            act = (g * jax.nn.sigmoid(g) * u).astype(bf16)
+            acc_ref[...] += mm(act, wd_ref[at, :])
+            return carry
+
+        if between is None:
+            lax.fori_loop(0, chunks, chunk, 0)
+        else:
+            lax.fori_loop(0, chunks - 1, chunk, 0)
+            between()
+            lax.fori_loop(chunks - 1, chunks, chunk, 0)
+        p_ref[...] = acc_ref[...].astype(bf16)
+        store_p(part_out.at[w]).start()
+        mine = pl.ds(pl.multiple_of(place * share, share), share)
+        own_ref[...] = r_ref[mine, :] + acc_ref[mine, :]
+        store_own(w).start()
+        store_p(part_out.at[w]).wait()
+        store_own(w).wait()
+
+    def inward(w):
+        @pl.when(outer)
+        def _():
+            copy_a(w).start()
+
+    def sum_dhf():
+        for k in range(1, 4):
+            copy_d(k).wait_recv()
+        total = dpart[place].astype(f32)
+        for k in range(3):
+            total = total + drecv[k].astype(f32)
+        dall[place] = total.astype(bf16)
+        for k in range(1, 4):
+            copy_e(k, place).start()
+
+    r = xm_ref[...].astype(f32)
+    for om, wo in zip(om_refs, wo_refs):
+        r = r + mm(om[...], wo[...])
+    rm_ref[...] = r
+    hf_ref[0:masked, :] = (r * rms_scale(r) * gain_ffn).astype(bf16)
     for c in range(chunks // 2):
         masked_chunk(c)
     hops_in(0, 1)
@@ -632,79 +1032,61 @@
         copy_d(k).start()
     hops_in(0, 2)
     hops(0, 3)
-    load_o(1).wait()
-    hops(1, 1)
     for c in range(chunks - 2, chunks):
         for copy in grad_copies(c):
             copy.wait()
 
-    def ffn(w, o_refs, next_x):
-        half = window // 2
-
-        def first(n, carry):
-            rows = pl.ds(pl.multiple_of(n * half, half), half)
-            r = x_ref[rows, :].astype(f32)
-            for o, wo in zip(o_refs, wo_refs):
-                r = r + mm(o[rows, :], wo[...])
-            r_ref[rows, :] = r
-            hf_ref[rows, :] = (r * rms_scale(r) * gain_ffn).astype(bf16)
-            return carry
-
-        lax.fori_loop(0, 2, first, 0)
-        if next_x is not None:
-            load_x(next_x).start()
-        acc_ref[...] = jnp.zeros_like(acc_ref)
-
-        def chunk(c, carry):
-            at = pl.ds(pl.multiple_of(c * cols, cols), cols)
-            hf = hf_ref[...]
-            g, u = mm(hf, wg_ref[:, at]), mm(hf, wu_ref[:, at])
-            act = (g * jax.nn.sigmoid(g) * u).astype(bf16)
-            acc_ref[...] += mm(act, wd_ref[at, :])
-            return carry
-
-        lax.fori_loop(0, chunks, chunk, 0)
-        p_ref[...] = acc_ref[...].astype(bf16)
-        store_p(part_out.at[w]).start()
-        mine = pl.ds(pl.multiple_of(place * share, share), share)
-        own_ref[...] = r_ref[mine, :] + acc_ref[mine, :]
-        store_own(w).start()
-        store_p(part_out.at[w]).wait()
-        store_own(w).wait()
-
-    def inward(w):
-        @pl.when(outer)
-        def _():
-            copy_a(w).start()
-
+    load_o(1).wait()
     load_x(0).wait()
     ffn(0, oa_refs, 1)
     inward(0)
-
-    for k in range(1, 4):
-        copy_d(k).wait_recv()
-    total = dpart[place].astype(f32)
-    for k in range(3):
-        total = total + drecv[k].astype(f32)
-    dall[place] = total.astype(bf16)
-    for k in range(1, 4):
-        copy_e(k, place).start()
-
     hops_in(0, 3)
-    hops_in(1, 1)
-    hops(1, 2)
+    hops(1, 1)
     load_x(1).wait()
-    ffn(1, [obuf.at[0, n] for n in range(4)], 0)
+
+    def meanwhile():
+        sum_dhf()
+        hops_in(1, 1)
+        hops(1, 2)
+
+    ffn(1, [obuf.at[0, n] for n in range(4)], 2, meanwhile)
     inward(1)
     hops_in(1, 2)
     hops(1, 3)
+    hops_in(1, 3)
+    load_x(2).wait()
+    ffn(2, [obuf.at[1, n] for n in range(4)], 0)
+    inward(2)
+
+    def copy_b(w):
+        return remote(
+            bsum.at[w], rb_out.at[w], b_send.at[w], b_recv.at[w], jnp.where(lower, 2, 1)
+        )
+
+    def exchange_rows(w):
+        @pl.when(inner)
+        def _():
+            copy_a(w).wait_recv()
+            rows = rows_ref(ra_out.at[w], jnp.where(lower, 1, 0), share, 2)
+            mine = rows_ref(part_out.at[w], jnp.where(lower, 2, 0), share, 2)
+            got = pltpu.make_async_copy(rows, bsum.at[w], b_load.at[0])
+            add = pltpu.make_async_copy(mine, hf_ref.at[pl.ds(0, 2 * share), :], b_load.at[1])
+            got.start()
+            add.start()
+            got.wait()
+            add.wait()
+            total = bsum[w].astype(f32) + hf_ref[0 : 2 * share, :].astype(f32)
+            bsum[w] = total.astype(bf16)
+            copy_b(w).start()
+
+    exchange_rows(0)
 
     for k in range(1, 4):
         copy_e(k, lax.rem(place + 4 - k, 4)).wait_recv()
     gw_acc[...] = jnp.zeros_like(gw_acc)
     go_acc[...] = jnp.zeros_like(go_acc)
     gain_ref[...] = jnp.zeros_like(gain_ref)
-    for w in range(windows):
+    def back_window(w, next_x):
         for copy in load_kv(w):
             copy.wait()
         if w + 1 < windows:
@@ -739,9 +1121,6 @@
             flow_ref[:, width + first : width + first + 128] = dk.astype(bf16)
             flow_ref[:, 2 * width + first : 2 * width + first + 128] = dv.astype(bf16)
         load_x(w).wait()
-        if w > 0:
-            for copy in dha_copies(dha_out, p_ref, dha_sem, w - 1, windows, share):
-                copy.wait()
 
         def back(n, carry):
             rows = pl.ds(pl.multiple_of(n * share, share), share)
@@ -756,12 +1135,21 @@
         lax.fori_loop(0, window // share, back, 0)
         for copy in dha_copies(dha_out, p_ref, dha_sem, w, windows, share):
             copy.start()
-        if w + 1 < windows:
-            load_x(w + 1).start()
+        if next_x is not None:
+            load_x(next_x).start()
         gw_acc[...] += mm_tn(hf_ref[...], flow_ref[...])
 
-    for copy in dha_copies(dha_out, p_ref, dha_sem, windows - 1, windows, share):
-        copy.wait()
+    def dha_stored(w):
+        for copy in dha_copies(dha_out, p_ref, dha_sem, w, windows, share):
+            copy.wait()
+
+    back_window(0, 1)
+    dha_stored(0)
+    back_window(1, 2)
+    dha_stored(1)
+    exchange_rows(1)
+    back_window(2, None)
+    dha_stored(2)
     fold = model // width
     for block in range(3 * width // 128):
         part, lane = divmod(block * 128, width)
@@ -776,29 +1164,25 @@
     store.start()
     store.wait()
 
-    hops_in(1, 3)
-    ffn(2, [obuf.at[1, n] for n in range(4)], None)
-
-    for w in range(2):
+    for w in range(windows):
 
         @pl.when(outer)
         def _():
             copy_a(w).wait_send()
 
-        @pl.when(inner)
-        def _():
-            copy_a(w).wait_recv()
+    @pl.when(inner)
+    def _():
+        copy_a(2).wait_recv()
+        for w in range(2):
+            copy_b(w).wait_send()
+            copy_b(w).wait_recv()
 
     for k in range(1, 4):
         copy_d(k).wait_send()
         copy_e(k, place).wait_send()
     for g in range(2):
         for d in range(1, 4):
-            for up in (True, False):
-
-                @pl.when(sends(d, up))
-                def _():
-                    hop(g, d, up).wait_send()
+            each_way(place, d, sends, lambda up: hop(g, d, up).wait_send())
 
 
 def dha_copies(dha_out, p_ref, sem, w, windows, share):
@@ -821,6 +1205,7 @@
     windows,
     order,
     ready,
+    traded,
     rows_in,
     drm_ref,
     gains_ref,
@@ -829,8 +1214,11 @@
     part_ref,
     own_in,
     ra_in,
+    rb_in,
+    gain_in,
     out_ref,
     grad_ref,
+    gain_ref,
     ra,
     rb,
     rc,
@@ -839,6 +1227,10 @@
     piece,
     x_rows,
     grad,
+    gain_sum,
+    gain_got,
+    s_send,
+    s_recv,
     a_send,
     a_recv,
     b_send,
@@ -850,6 +1242,7 @@
     v_sem,
     o_sem,
     r_sem,
+    t_sem,
     x_sem,
     l_sem,
     i_sem,
@@ -886,6 +1279,9 @@
     def load_ra(f):
         return pltpu.make_async_copy(ra_in.at[order[f][1]], ra.at[f], r_sem.at[f])
 
+    def load_rb(f):
+        return pltpu.make_async_copy(rb_in.at[order[f][1]], rb.at[f], t_sem.at[f])
+
     def hop(w, d, up, origin):
         rows = pl.ds(pl.multiple_of(w * 4 * share + origin * share, share), share)
         n = 0 if up else 1
@@ -897,30 +1293,16 @@
             lax.rem(place + (1 if up else 3), 4),
         )
 
-    def sends(d, up):
-        if up:
-            return (place >= d - 1) & (place <= 2)
-        return (place <= 4 - d) & (place >= 1)
-
-    def receives(d, up):
-        return place >= d if up else place <= 3 - d
-
     def source(d, up):
         return jnp.clip(place - (d - 1) if up else place + (d - 1), 0, 3)
 
     def hops(w, d):
-        for up in (True, False):
-
-            @pl.when(sends(d, up))
-            def _():
-                hop(w, d, up, source(d, up)).start()
+        each_way(place, d, sends, lambda up: hop(w, d, up, source(d, up)).start())
 
     def hops_in(w, d):
-        for up in (True, False):
-
-            @pl.when(receives(d, up))
-            def _():
-                hop(w, d, up, source(d + 1, up)).wait_recv()
+        each_way(
+            place, d, receives, lambda up: hop(w, d, up, source(d + 1, up)).wait_recv()
+        )
 
     def keep(w):
         rows = pl.ds(pl.multiple_of(w * 4 * share + place * share, share), share)
@@ -940,7 +1322,35 @@
     for w in range(windows):
         load_own(w).start()
     x_load.start()
-    greet_line(place)
+
+    pairs = []
+    for axis in ("dp", "tensor"):
+        index, bit = lax.axis_index(axis), 1
+        while bit < lax.axis_size(axis):
+            pairs.append((axis, index + bit - 2 * bit * lax.rem(index // bit, 2)))
+            bit *= 2
+
+    def copy_s(t):
+        axis, other = pairs[t]
+        return pltpu.make_async_remote_copy(
+            src_ref=gain_sum.at[t],
+            dst_ref=gain_got.at[t],
+            send_sem=s_send.at[t],
+            recv_sem=s_recv.at[t],
+            device_id={axis: other},
+            device_id_type=pl.DeviceIdType.MESH,
+        )
+
+    def next_pair(t):
+        if t > 0:
+            copy_s(t - 1).wait_recv()
+            gain_sum[t] = gain_sum[t - 1] + gain_got[t - 1]
+        if t < len(pairs):
+            copy_s(t).start()
+
+    greet_line(place, [pair for pair in pairs if pair[0] == "dp"])
+    gain_sum[0] = jnp.zeros(gain_sum.shape[1:], f32)
+    gain_sum[0, 0:2, :] = gain_in[...]
     sent = list(range(ready, folds))
 
     @pl.when(outer)
@@ -952,6 +1362,8 @@
     def _():
         for f in range(ready):
             load_ra(f).start()
+        for f in range(traded):
+            load_rb(f).start()
 
     def add_rows(buffer, at, f, index):
         rows = pl.ds(pl.multiple_of(at * share, share), share)
@@ -988,7 +1400,11 @@
         load_own(w).wait()
     x_load.wait()
     moving = {}
+    turn = 0
     for step in range(folds + 1):
+        if turn <= len(pairs):
+            next_pair(turn)
+            turn += 1
         if step < folds:
 
             @pl.when(inner)
@@ -997,18 +1413,25 @@
                     load_ra(step).wait()
                 else:
                     copy_a(step).wait_recv()
-                for n in range(2):
-                    add_rows(
-                        ra, jnp.where(lower, 1, 0) + n, step, jnp.where(lower, 2, 0) + n
-                    )
-                copy_b(step).start()
+                if step >= traded:
+                    for n in range(2):
+                        add_rows(
+                            ra,
+                            jnp.where(lower, 1, 0) + n,
+                            step,
+                            jnp.where(lower, 2, 0) + n,
+                        )
+                    copy_b(step).start()
 
         if step > 0:
             f = step - 1
 
             @pl.when(inner)
             def _():
-                copy_b(f).wait_recv()
+                if f < traded:
+                    load_rb(f).wait()
+                else:
+                    copy_b(f).wait_recv()
                 add_rows(rb, jnp.where(lower, 0, 1), f, jnp.where(lower, 0, 3))
                 copy_c(f).start()
                 sel_a = pl.ds(pl.multiple_of(jnp.where(lower, 0, 2) * share, share), share)
@@ -1041,6 +1464,12 @@
                 if step + 2 < folds:
                     copy_a(step + 2).start()
 
+    while turn <= len(pairs):
+        next_pair(turn)
+        turn += 1
+    gain_ref[...] = gain_sum[len(pairs), 0:2, :]
+    for t in range(len(pairs)):
+        copy_s(t).wait_send()
     while moving:
         for w in list(moving):
             hops_in(w, moving[w])
@@ -1053,17 +1482,16 @@
     @pl.when(inner)
     def _():
         for f in range(folds):
-            copy_b(f).wait_send()
+            if f >= traded:
+                copy_b(f).wait_send()
             copy_c(f).wait_send()
 
     for w in range(windows):
         keep(w).wait()
         for d in range(1, 4):
-            for up in (True, False):
-
-                @pl.when(sends(d, up))
-                def _():
-                    hop(w, d, up, source(d, up)).wait_send()
+            each_way(
+                place, d, sends, lambda up: hop(w, d, up, source(d, up)).wait_send()
+            )
 
     for c in range(cuts):
         store(c).wait()
@@ -1084,7 +1512,14 @@
     per = len(refs) - 1
     for n in range(per):
         used = used_ref[step * per + n] > 0
-        out_ref[n] = jnp.where(used, refs[n][0], jnp.zeros((), bf16))
+
+        @pl.when(used)
+        def _():
+            out_ref[n] = refs[n][0]
+
+        @pl.when(jnp.logical_not(used))
+        def _():
+            out_ref[n] = jnp.zeros(out_ref.shape[1:], bf16)
 
 
 def copy_kernel(in_ref, out_ref):
@@ -1175,16 +1610,17 @@
     return (first_new, second_new, param_new)
 
 
-def head_tables(positions, heads):
-    frequency = jnp.exp(
-        -jnp.log(10000.0) * (2.0 * jnp.arange(HD // 2, dtype=f32) / HD)
+def head_tables(positions, heads, lib):
+    frequency = lib.exp(
+        -lib.log(lib.float32(10000.0))
+        * (2.0 * lib.arange(HD // 2, dtype=lib.float32) / HD).astype(lib.float32)
     )
-    angles = positions.astype(f32)[..., None] * frequency
-    cos, sin = jnp.cos(angles), jnp.sin(angles)
-    cos = jnp.concatenate([cos, cos], axis=-1)
-    sin = jnp.concatenate([-sin, sin], axis=-1)
+    angles = positions.astype(lib.float32)[..., None] * frequency
+    cos, sin = lib.cos(angles), lib.sin(angles)
+    cos = lib.concatenate([cos, cos], axis=-1)
+    sin = lib.concatenate([-sin, sin], axis=-1)
     reps = (1,) * (cos.ndim - 1) + (heads,)
-    return jnp.tile(cos, reps), jnp.tile(sin, reps)
+    return lib.tile(cos, reps), lib.tile(sin, reps)
 
 
 def on_device(
@@ -1224,142 +1660,237 @@
     slot_used = jnp.any(slot_match, axis=1)[:, None, None]
     slot_tile = jnp.argmax(slot_match, axis=1)
 
+    mask_rows = seq_count * count
+    share = window // parts
+    share_rows = total_rows // parts
+    dp_size = lax.axis_size("dp")
+    lines = dp_size == 8 and attn_tiles == 8 and parts == 4 and seq_count == 3 and hidden == model and mask_rows <= window // 2
+    anywhere = pl.BlockSpec(memory_space=pl.ANY)
+    inside = pl.BlockSpec(memory_space=pltpu.VMEM)
+    dma = pltpu.SemaphoreType.DMA
+
     tile_block = (1, tile_rows, model)
-    grid_size = max(capacity, attn_tiles)
-    low_slots, attn_mine = pl.pallas_call(
-        cast_kernel,
-        out_shape=[
-            jax.ShapeDtypeStruct((capacity, tile_rows, model), bf16),
-            jax.ShapeDtypeStruct((attn_tiles, tile_rows, model), bf16),
-        ],
-        grid_spec=pltpu.PrefetchScalarGridSpec(
-            num_scalar_prefetch=2,
-            grid=(grid_size,),
-            in_specs=[
-                pl.BlockSpec(
-                    tile_block, lambda i, rank, held: (jnp.minimum(i, capacity - 1), 0, 0)
-                ),
-                pl.BlockSpec(
-                    tile_block,
-                    lambda i, rank, held: (rank[jnp.minimum(i, attn_tiles - 1)], 0, 0),
-                ),
+    if lines:
+        small = pl.BlockSpec(memory_space=pltpu.SMEM)
+        half_tiles = attn_tiles // 2
+        low_slots, attn_sums = pl.pallas_call(
+            weights_kernel,
+            out_shape=[
+                jax.ShapeDtypeStruct((capacity, tile_rows, model), bf16),
+                jax.ShapeDtypeStruct((attn_tiles, tile_rows, model), bf16),
             ],
-            out_specs=[
-                pl.BlockSpec(
-                    tile_block, lambda i, rank, held: (jnp.minimum(i, capacity - 1), 0, 0)
-                ),
-                pl.BlockSpec(
-                    tile_block, lambda i, rank, held: (jnp.minimum(i, attn_tiles - 1), 0, 0)
-                ),
+            in_specs=[small, small, inside],
+            out_specs=[inside, anywhere],
+            scratch_shapes=[
+                pltpu.VMEM((attn_tiles, tile_rows, model), bf16),
+                pltpu.VMEM((half_tiles, tile_rows, model), bf16),
+                pltpu.VMEM((3, half_tiles, tile_rows, model), bf16),
+                pltpu.VMEM((2, half_tiles, tile_rows, model), bf16),
+                dma,
+                dma,
+                dma((2, half_tiles)),
+                dma((2, half_tiles)),
+                dma((half_tiles,)),
+                dma((half_tiles,)),
+                dma((half_tiles,)),
             ],
-        ),
-        compiler_params=params(),
-        cost_estimate=cost(0, 12 * capacity * tile_size),
-        name="cast",
-    )(
-        slot_rank,
-        jnp.pad(
+            compiler_params=params(collective_id=4, has_side_effects=True),
+            cost_estimate=cost(0, 12e6),
+            name="weights",
+        )(
+            slot_rank[:attn_tiles],
             (owner_row[:attn_tiles] == owner_self).astype(jnp.int32),
-            (0, grid_size - attn_tiles),
-            mode="edge",
-        ),
-        master[0],
-        master[0],
-    )
-    attn_flat = dp_total(attn_mine).reshape(4 * width, model)
+            master[0],
+        )
+        attn_flat = attn_sums.reshape(4 * width, model)
+    else:
+        grid_size = max(capacity, attn_tiles)
+        low_slots, attn_mine = pl.pallas_call(
+            cast_kernel,
+            out_shape=[
+                jax.ShapeDtypeStruct((capacity, tile_rows, model), bf16),
+                jax.ShapeDtypeStruct((attn_tiles, tile_rows, model), bf16),
+            ],
+            grid_spec=pltpu.PrefetchScalarGridSpec(
+                num_scalar_prefetch=2,
+                grid=(grid_size,),
+                in_specs=[
+                    pl.BlockSpec(
+                        tile_block, lambda i, rank, held: (jnp.minimum(i, capacity - 1), 0, 0)
+                    ),
+                    pl.BlockSpec(
+                        tile_block,
+                        lambda i, rank, held: (rank[jnp.minimum(i, attn_tiles - 1)], 0, 0),
+                    ),
+                ],
+                out_specs=[
+                    pl.BlockSpec(
+                        tile_block, lambda i, rank, held: (jnp.minimum(i, capacity - 1), 0, 0)
+                    ),
+                    pl.BlockSpec(
+                        tile_block, lambda i, rank, held: (jnp.minimum(i, attn_tiles - 1), 0, 0)
+                    ),
+                ],
+            ),
+            compiler_params=params(),
+            cost_estimate=cost(0, 12 * capacity * tile_size),
+            name="cast",
+        )(
+            slot_rank,
+            jnp.pad(
+                (owner_row[:attn_tiles] == owner_self).astype(jnp.int32),
+                (0, grid_size - attn_tiles),
+                mode="edge",
+            ),
+            master[0],
+            master[0],
+        )
+        attn_flat = dp_total(attn_mine).reshape(4 * width, model)
     w_out = attn_flat[3 * width :]
     every_slot = lax.all_gather(low_slots, "dp", axis=0, tiled=True)
-    w_outs = around(w_out)
-
-    cos, sin = head_tables(jnp.arange(window), heads)
+
+    cos, sin = map(jnp.asarray, head_tables(np.arange(window), heads, np))
     rows = jnp.pad(masked_rows, ((0, 0), (0, count - mask_count)), constant_values=-1)
-    cos_m, sin_m = head_tables(rows, heads)
     cot = jnp.pad(cotangent, ((0, 0), (0, count - mask_count), (0, 0)))
     cot = cot.reshape(seq_count * count, model)
-    cos_m = cos_m.reshape(seq_count * count, width)
-    sin_m = sin_m.reshape(seq_count * count, width)
-
-    block = min(512, window)
-    per_window = window // block
-    row_block = pl.BlockSpec((block, model), lambda i: (i, 0))
-    head_block = pl.BlockSpec((block, width), lambda i: (i, 0))
-    table_block = pl.BlockSpec((block, width), lambda i: (i % per_window, 0))
-    q, k, v, w_qkv = pl.pallas_call(
-        qkv_kernel,
-        out_shape=[jax.ShapeDtypeStruct((total_rows, width), bf16)] * 3
-        + [jax.ShapeDtypeStruct((model, 3 * width), bf16)],
-        grid=(total_rows // block,),
-        in_specs=[
-            row_block,
-            whole_spec((2, model)),
-            whole_spec((3 * width, model)),
-            table_block,
-            table_block,
-        ],
-        out_specs=[head_block] * 3 + [whole_spec((model, 3 * width))],
-        scratch_shapes=[pltpu.VMEM((3 * width // 128, model, 128), f32)],
-        compiler_params=params(),
-        cost_estimate=cost(6 * total_rows * model * width, 2 * total_rows * model * 2),
-        name="qkv",
-    )(tokens, norm_gains, attn_flat, cos, sin)
 
     win_model = pl.BlockSpec((window, model), lambda i: (i, 0))
     win_head = pl.BlockSpec((window, width), lambda i: (i, 0))
     mask_model = pl.BlockSpec((count, model), lambda i: (i, 0))
     mask_head = pl.BlockSpec((count, width), lambda i: (i, 0))
-    o_m, q_m, x_m = pl.pallas_call(
-        attend_masked_kernel,
-        out_shape=[
-            jax.ShapeDtypeStruct((seq_count * count, width), bf16),
-            jax.ShapeDtypeStruct((seq_count * count, width), bf16),
-            jax.ShapeDtypeStruct((seq_count * count, model), bf16),
-        ],
-        grid=(seq_count,),
-        in_specs=[
-            pl.BlockSpec((1, count, 1), lambda i: (i, 0, 0)),
-            win_model,
-            win_head,
-            win_head,
-            win_head,
-        ],
-        out_specs=[mask_head, mask_head, mask_model],
-        compiler_params=params(),
-        cost_estimate=cost(
-            seq_count * count * window * (2 * model + 8 * width), 9e6, seq_count * count * window * heads
-        ),
-        name="attend_masked",
-    )(rows[:, :, None], tokens, q, k, v)
-    o_ms = around(o_m)
-
-    q_block = min(256, window)
-
-    def attend_window(w, before):
-        return pl.pallas_call(
-            after(attend_kernel, 3, 1),
-            out_shape=jax.ShapeDtypeStruct((window, width), bf16),
-            grid=(width // 128, window // q_block),
+    if lines:
+        (
+            o_m,
+            o_first,
+            o_second,
+            o_third,
+            w_far,
+            q_m,
+            x_m,
+            cos_m,
+            sin_m,
+            k,
+            v,
+            w_qkv,
+        ) = pl.pallas_call(
+            functools.partial(attend_all_kernel, seq_count),
+            out_shape=[
+                jax.ShapeDtypeStruct((4, mask_rows, width), bf16),
+                jax.ShapeDtypeStruct((4, window, width), bf16),
+                jax.ShapeDtypeStruct((window, width), bf16),
+                jax.ShapeDtypeStruct((window, width), bf16),
+                jax.ShapeDtypeStruct((3, width, model), bf16),
+                jax.ShapeDtypeStruct((mask_rows, width), bf16),
+                jax.ShapeDtypeStruct((mask_rows, model), bf16),
+                jax.ShapeDtypeStruct((mask_rows, width), f32),
+                jax.ShapeDtypeStruct((mask_rows, width), f32),
+                jax.ShapeDtypeStruct((total_rows, width), bf16),
+                jax.ShapeDtypeStruct((total_rows, width), bf16),
+                jax.ShapeDtypeStruct((model, 3 * width), bf16),
+            ],
+            in_specs=[inside] * 5 + [anywhere] * 2,
+            out_specs=[anywhere] * 5 + [inside] * 7,
+            scratch_shapes=[
+                pltpu.VMEM((total_rows, width), bf16),
+                pltpu.VMEM((3 * width // 128, model, 128), f32),
+                pltpu.VMEM((mask_rows, width), bf16),
+                pltpu.VMEM((seq_count, window, width), bf16),
+                pltpu.VMEM((2, window, model), bf16),
+                dma((2,)),
+                dma((seq_count,)),
+                dma,
+                dma((3, 2)),
+                dma((3, 2)),
+                dma((3, 2)),
+                dma((3, 2)),
+                dma((3, 2)),
+                dma((3, 2)),
+                dma((3,)),
+                dma((3,)),
+            ],
+            compiler_params=params(collective_id=3, has_side_effects=True),
+            cost_estimate=cost(4e10, 20e6),
+            name="attend_all",
+        )(rows[:, :, None], norm_gains, attn_flat, cos, sin, tokens, attn_flat)
+        before_tiles = o_third
+    else:
+        block = min(512, window)
+        per_window = window // block
+        row_block = pl.BlockSpec((block, model), lambda i: (i, 0))
+        head_block = pl.BlockSpec((block, width), lambda i: (i, 0))
+        table_block = pl.BlockSpec((block, width), lambda i: (i % per_window, 0))
+        q, k, v, w_qkv = pl.pallas_call(
+            qkv_kernel,
+            out_shape=[jax.ShapeDtypeStruct((total_rows, width), bf16)] * 3
+            + [jax.ShapeDtypeStruct((model, 3 * width), bf16)],
+            grid=(total_rows // block,),
             in_specs=[
-                pl.BlockSpec((q_block, 128), lambda p, i: (w * (window // q_block) + i, p)),
-                pl.BlockSpec((window, 128), lambda p, i: (w, p)),
-                pl.BlockSpec((window, 128), lambda p, i: (w, p)),
-                UNREAD,
+                row_block,
+                whole_spec((2, model)),
+                whole_spec((3 * width, model)),
+                table_block,
+                table_block,
             ],
-            out_specs=pl.BlockSpec((q_block, 128), lambda p, i: (i, p)),
+            out_specs=[head_block] * 3 + [whole_spec((model, 3 * width))],
+            scratch_shapes=[pltpu.VMEM((3 * width // 128, model, 128), f32)],
+            compiler_params=params(),
+            cost_estimate=cost(6 * total_rows * model * width, 2 * total_rows * model * 2),
+            name="qkv",
+        )(tokens, norm_gains, attn_flat, cos, sin)
+
+        o_m, q_m, x_m = pl.pallas_call(
+            attend_masked_kernel,
+            out_shape=[
+                jax.ShapeDtypeStruct((seq_count * count, width), bf16),
+                jax.ShapeDtypeStruct((seq_count * count, width), bf16),
+                jax.ShapeDtypeStruct((seq_count * count, model), bf16),
+            ],
+            grid=(seq_count,),
+            in_specs=[
+                pl.BlockSpec((1, count, 1), lambda i: (i, 0, 0)),
+                win_model,
+                win_head,
+                win_head,
+                win_head,
+            ],
+            out_specs=[mask_head, mask_head, mask_model],
             compiler_params=params(),
             cost_estimate=cost(
-                16 * window * window * width, 4 * window * width * 2, window * window * heads
+                seq_count * count * window * (2 * model + 8 * width), 9e6, seq_count * count * window * heads
             ),
-            name="attend",
-        )(q, k, v, before)
-
-    mask_rows = seq_count * count
-    share = window // parts
-    share_rows = total_rows // parts
-    lines = parts == 4 and seq_count == 3 and hidden == model and mask_rows <= window // 2
-    early = seq_count if lines else max(seq_count - 1, 1)
-    o_own = []
-    for w in range(early):
-        o_own.append(attend_window(w, o_own[-1] if o_own else o_m))
+            name="attend_masked",
+        )(rows[:, :, None], tokens, q, k, v)
+        o_ms = around(o_m)
+
+        q_block = min(256, window)
+
+        def attend_window(w, before):
+            return pl.pallas_call(
+                after(attend_kernel, 3, 1),
+                out_shape=jax.ShapeDtypeStruct((window, width), bf16),
+                grid=(width // 128, window // q_block),
+                in_specs=[
+                    pl.BlockSpec((q_block, 128), lambda p, i: (w * (window // q_block) + i, p)),
+                    pl.BlockSpec((window, 128), lambda p, i: (w, p)),
+                    pl.BlockSpec((window, 128), lambda p, i: (w, p)),
+                    UNREAD,
+                ],
+                out_specs=pl.BlockSpec((q_block, 128), lambda p, i: (i, p)),
+                compiler_params=params(),
+                cost_estimate=cost(
+                    16 * window * window * width, 4 * window * width * 2, window * window * heads
+                ),
+                name="attend",
+            )(q, k, v, before)
+
+        early = max(seq_count - 1, 1)
+        o_own = []
+        for w in range(early):
+            o_own.append(attend_window(w, o_own[-1] if o_own else o_m))
+        before_tiles = o_own[-1]
+        cos_m, sin_m = (
+            table.reshape(mask_rows, width) for table in head_tables(rows, heads, jnp)
+        )
 
     group = 4
     ffn_all = pl.pallas_call(
@@ -1381,33 +1912,27 @@
         compiler_params=params(),
         cost_estimate=cost(0, 4 * ffn_tiles * tile_size),
         name="collect",
-    )(slot_index, *[every_slot] * group, o_own[-1])
-    ffn_flat = ffn_all.reshape(3, -1)
-    w_gate = ffn_flat[0].reshape(model, hidden)
-    w_up = ffn_flat[1].reshape(model, hidden)
-    w_down = ffn_flat[2].reshape(hidden, model)
-
+    )(slot_index, *[every_slot] * group, before_tiles)
+    even = jnp.array([[1.0], [1.0 / parts]], f32)
     flat_rows = jnp.where(
         rows >= 0, rows + window * jnp.arange(seq_count, dtype=jnp.int32)[:, None], -1
     ).reshape(1, mask_rows)
     if lines:
-        anywhere = pl.BlockSpec(memory_space=pl.ANY)
-        inside = pl.BlockSpec(memory_space=pltpu.VMEM)
-        dma = pltpu.SemaphoreType.DMA
         grad_rows = 4 * width + 3 * hidden
-        part, own, first_sums, dha, grads, dr_m, gains_part = pl.pallas_call(
+        part, own, first_sums, second_sums, dha, grads, dr_m, gains_part = pl.pallas_call(
             functools.partial(middle_kernel, seq_count),
             out_shape=[
                 jax.ShapeDtypeStruct((seq_count, window, model), bf16),
                 jax.ShapeDtypeStruct((seq_count, share, model), f32),
-                jax.ShapeDtypeStruct((2, 3 * share, model), bf16),
+                jax.ShapeDtypeStruct((seq_count, 3 * share, model), bf16),
+                jax.ShapeDtypeStruct((2, 2 * share, model), bf16),
                 jax.ShapeDtypeStruct((seq_count, window, model), bf16),
                 jax.ShapeDtypeStruct((grad_rows, model), bf16),
                 jax.ShapeDtypeStruct((mask_rows, model), f32),
                 jax.ShapeDtypeStruct((2, model), f32),
             ],
-            in_specs=[inside] * (13 + 3 * parts) + [anywhere] * 5,
-            out_specs=[anywhere] * 5 + [inside] * 2,
+            in_specs=[inside] * 15 + [anywhere] * 5,
+            out_specs=[anywhere] * 6 + [inside] * 2,
             scratch_shapes=[
                 pltpu.VMEM((window, model), f32),
                 pltpu.VMEM((window, model), bf16),
@@ -1425,6 +1950,10 @@
                 pltpu.VMEM((4, mask_rows, model // 4), bf16),
                 pltpu.VMEM((3, mask_rows, model // 4), bf16),
                 pltpu.VMEM((4, mask_rows, model // 4), bf16),
+                pltpu.VMEM((2, 2 * share, model), bf16),
+                dma((2,)),
+                dma((2,)),
+                dma((2,)),
                 dma((2,)),
                 dma,
                 dma((2, 2)),
@@ -1432,8 +1961,8 @@
                 dma,
                 dma((window // share,)),
                 dma,
-                dma((2,)),
-                dma((2,)),
+                dma((seq_count,)),
+                dma((seq_count,)),
                 dma((2, 3, 2)),
                 dma((2, 3, 2)),
                 dma((3,)),
@@ -1455,22 +1984,27 @@
             cos,
             sin,
             w_qkv,
-            w_gate,
-            w_up,
-            w_down,
-            *o_ms,
-            *w_outs,
-            *around(o_own[0]),
+            ffn_all.reshape(3, model, hidden),
+            o_m,
+            o_first,
+            w_out,
+            w_far,
             tokens,
             k,
             v,
-            o_own[1],
-            o_own[2],
-        )
-
+            o_second,
+            o_third,
+        )
+
+        group = 8
         slots = lax.axis_size("dp") * capacity
         slot_hit = slot_index[None, :] == jnp.arange(slots, dtype=jnp.int32)[:, None]
-        group = 4
+        used = jnp.any(slot_hit, axis=1).astype(jnp.int32)
+        tile_count = slot_index.shape[0]
+        held_at = jnp.arange(slots, dtype=jnp.int32) // group * tile_count
+        held_at = held_at + jnp.argmax(slot_hit, axis=1).astype(jnp.int32)
+        held_at = jnp.where(used > 0, held_at, 0).reshape(-1, group)
+        from_tile = lax.rem(lax.cummax(held_at, axis=0), tile_count).reshape(-1)
         in_slots = pl.pallas_call(
             spread_kernel,
             out_shape=jax.ShapeDtypeStruct((slots, tile_rows, model), bf16),
@@ -1491,22 +2025,24 @@
             cost_estimate=cost(0, 24 * capacity * tile_size),
             name="spread",
         )(
-            jnp.argmax(slot_hit, axis=1).astype(jnp.int32),
-            jnp.any(slot_hit, axis=1).astype(jnp.int32),
+            from_tile,
+            used,
             *[grads.reshape(-1, tile_rows, model)] * group,
         )
         reduced = lax.psum_scatter(in_slots, "dp", scatter_dimension=0, tiled=True).astype(f32)
 
-        order = [(0, 0), (0, 1), (1, 0), (0, 2), (1, 1), (1, 2)]
+        order = [(kind, i) for kind in (0, 1) for i in range(seq_count)]
         folds = len(order)
-        layer_out, input_grad = pl.pallas_call(
-            after(functools.partial(lines_kernel, seq_count, seq_count, order, 2), 8, 1),
+        pair_count = (lax.axis_size("dp") * parts).bit_length() - 1
+        layer_out, input_grad, gain_grad = pl.pallas_call(
+            after(functools.partial(lines_kernel, seq_count, seq_count, order, seq_count, 2), 10, 1),
             out_shape=[
                 jax.ShapeDtypeStruct((total_rows, model), bf16),
                 jax.ShapeDtypeStruct((share_rows, model), bf16),
+                jax.ShapeDtypeStruct((2, model), f32),
             ],
-            in_specs=[inside] * 3 + [anywhere] * 6,
-            out_specs=[anywhere] * 2,
+            in_specs=[inside] * 3 + [anywhere] * 6 + [inside, anywhere],
+            out_specs=[anywhere] * 2 + [inside],
             scratch_shapes=[
                 pltpu.VMEM((folds, 3 * share, model), bf16),
                 pltpu.VMEM((folds, 2 * share, model), bf16),
@@ -1516,6 +2052,10 @@
                 pltpu.VMEM((seq_count, share, model), bf16),
                 pltpu.VMEM((share_rows, model), bf16),
                 pltpu.VMEM((seq_count, share, model), bf16),
+                pltpu.VMEM((pair_count + 1, 8, model), f32),
+                pltpu.VMEM((pair_count, 8, model), f32),
+                dma((pair_count,)),
+                dma((pair_count,)),
                 dma((folds,)),
                 dma((folds,)),
                 dma((folds,)),
@@ -1525,6 +2065,7 @@
                 dma((seq_count, 3, 2)),
                 dma((seq_count, 3, 2)),
                 dma((folds,)),
+                dma((seq_count,)),
                 dma((seq_count,)),
                 dma((2,)),
                 dma,
@@ -1543,9 +2084,16 @@
             part,
             own,
             first_sums,
+            second_sums,
+            gains_part * even,
             in_slots,
         )
     else:
+        w_outs = around(w_out)
+        ffn_flat = ffn_all.reshape(3, -1)
+        w_gate = ffn_flat[0].reshape(model, hidden)
+        w_up = ffn_flat[1].reshape(model, hidden)
+        w_down = ffn_flat[2].reshape(hidden, model)
         cols = min(256, hidden)
         col_block = pl.BlockSpec((model, cols), lambda c: (0, c))
         down_block = pl.BlockSpec((cols, model), lambda c: (c, 0))
@@ -1788,6 +2336,8 @@
         for w, outs in enumerate(parts_out):
             layer_out = place_window(w, *outs)
 
+        gain_grad = small_total(gains_part * even)
+
         def total_tiles(tiles, before):
             piece = lax.psum_scatter(tiles, "dp", scatter_dimension=0, tiled=True)
             piece = pl.pallas_call(
@@ -1805,8 +2355,6 @@
         tiles = jnp.concatenate([attn_grads, ffn_grads], axis=0).reshape(-1, tile_rows, model)
         reduced = tiles[slot_tile].astype(f32)
 
-    even = jnp.array([[1.0], [1.0 / parts]], f32)
-    gain_grad = small_total(gains_part * even)
     _, gain_moment, gain_new = adam_update(
         gain_grad, gain_first, gain_second, norm_gains, gain_rate, 0.0
     )

time: 676 us -> 600 us (0.89)
  waiting for transfers between devices: 67.7 us -> 0.06 us
  Pallas kernels: 474 us -> 541 us
  starting transfers between devices: 61.5 us -> 0.08 us
  local copies, waits for them, and re-layouts: 24.8 us -> 13.9 us
    ppermute x20 -> x0, waiting for transfers between devices: 67.6 us -> none  [the longest x11 49 us: exchange(): return lax.ppermute(value, axis, [(i, i ^ bit) for i in range(size)])]
    ppermute x20 -> x0, starting transfers between devices: 61.4 us -> none  [the longest x9 40.4 us: around(): lax.ppermute(value, 'tensor', [(i, (i + k) % size) for i in range(size)])]
    pallas_call x6 -> x2, Pallas kernels: 65.4 us -> 120 us  [the longest x1 84 us: on_device(): pl.pallas_call(functools.partial(attend_all_kernel, seq_count), out_shape...]
    pallas_call x1, Pallas kernels: 160 us -> 182 us  [on_device(): pl.pallas_call(functools.partial(middle_kernel, seq_count), out_shape=[ja...]
  transfers between devices with their start and end apart: 22 -> 2, of which waited for: 11 -> 0; matrix products, arithmetic and copies ran while one was open for 4% -> 2% of each run, Pallas kernels for 43% -> 52%
where the time goes in v4:
time: 600 us; the launch traced here: 590 us
  Pallas kernels  541 us (90%)
  other arithmetic  20.6 us (3%)
  between operations  14.4 us (2%)
  local copies, waits for them, and re-layouts  13.9 us (2%)
    pallas_call x1, Pallas kernels, on_device(): pl.pallas_call(after(functools.partial(lines_kernel, seq_count, seq_count...  221 us
    pallas_call x1, Pallas kernels, on_device(): pl.pallas_call(functools.partial(middle_kernel, seq_count), out_shape=[ja...  182 us
    pallas_call x1, Pallas kernels, on_device(): pl.pallas_call(functools.partial(attend_all_kernel, seq_count), out_shape...  84 us
    pallas_call x1, Pallas kernels, on_device(): pl.pallas_call(weights_kernel, out_shape=[jax.ShapeDtypeStruct((capacity,...  35.5 us
    broadcast_in_dim x1, other arithmetic, on_device(): weight_low[None]  12.9 us
  transfers between devices with their start and end apart: 2, of which 0 were waited for; matrix products, arithmetic and copies ran while one was open for 2% of the time, Pallas kernels for 52%

profile of v4, /device:TPU:0, one launch (start us, length us, event | category | flops | bytes accessed | tf_op | source)
XLA Modules:
  0.0 590.2 jit_solution(3617087819624116286)
XLA Ops:
  7.2 0.0 copy-start.12
  7.2 0.0 copy-start.8
  7.2 0.0 copy-start.1
  7.2 0.0 all-gather.2.cloned.1.call-start
  7.3 1.4 convert_reduce_fusion
  8.7 1.2 fusion.10.held_ref
  9.9 35.5 %weights.1 = (bf16[8,128,1024]{2,1,0:T(8,128)(2,1)}, bf16[8,128,1024]{2,1,0:T(8,128)(2,1)}) custom-call(s32[8]{0:T(128)} %bitcast.61, s32[8]{0:T(128)} %fusion.10.held_ref, f32[8,128,1024]{2,1,0:T(8,128)} %bitcast.54), custom_call_target="tpu_custom_call" | custom-call | bytes 12000000 | tf_op jit(solution)/shard_map/weights/pallas_call | solution.py:1676
  45.4 0.0 all-gather.2.cloned.1.call-update
  45.4 0.0 reduce-scatter.2.cloned.1.call-start
  45.5 0.0 copy-done.8
  45.5 0.7 pad_bitcast_fusion
  46.1 0.6 broadcast_in_dim.60.rows_in
  46.7 0.9 copy.25.rows_in
  47.6 1.9 slice.15
  49.5 0.0 copy-done.12
  49.5 0.0 copy-done.9
  49.5 0.1 fusion.3
  49.6 0.5 convert_element_type.22.used_ref
  50.1 0.6 iota_reduce_fusion
  50.7 0.1 reshape.63
  50.8 0.1 reduce_window_max.13
  50.9 0.0 copy-done.1
  50.9 1.0 pad.9
  51.9 0.5 compare_select_fusion.tile_ref
  52.4 0.5 multiply_add_fusion.refs_0_
  53.0 84.0 %attend_all.1 = (bf16[4,480,256]{2,1,0:T(8,128)(2,1)}, bf16[4,1024,256]{2,1,0:T(8,128)(2,1)}, bf16[1024,256]{1,0:T(8,128)(2,1)}, bf16[1024,256]{1,0:T(8,128)(2,1...) custom-call(s32[3,160,1]{2,1,0:T(8,128)} %copy.25.rows_in, ...), custom_call_target="tpu_custom_call" | custom-call | flops 40000000000 | bytes 20000000 | tf_op jit(solution)/shard_map/attend_all/pallas_call | solution.py:1775
  137.0 0.0 all-gather.2.cloned.1.call-done.refs_1_.refs_2_.refs_3_.refs_4_
  137.0 7.6 %collect.1 = bf16[24,128,1024]{2,1,0:T(8,128)(2,1)} custom-call(s32[32]{0:T(128)} %multiply_add_fusion.refs_0_, bf16[64,128,1024]{2,1,0:T(8,128)(2,1)} %all-gather.2.cloned.1.call-done.refs_1_.refs_2_.refs_3_.refs_4_, bf16[64,128,1024]{2,1,0:T(8,128)(2,1)} %all-gather.2.cloned.1.call-done.refs_1_.refs_2_.refs_3_.refs_4_, ...), custom_call_target="tpu_custom_call" | custom-call | bytes 12582912 | tf_op jit(solution)/shard_map/collect/pallas_call | solution.py:1896
  144.6 181.8 %middle.1 = (bf16[3,1024,1024]{2,1,0:T(8,128)(2,1)}, f32[3,256,1024]{2,1,0:T(8,128)}, bf16[3,768,1024]{2,1,0:T(8,128)(2,1)}, bf16[2,512,1024]{2,1,0:T(8,128)(2,1...) custom-call(s32[3,1,160]{2,1,0:T(1,128)} %broadcast_in_dim.60.rows_in,, ...), custom_call_target="tpu_custom_call" | custom-call | flops 99999997952 | bytes 100000000 | tf_op jit(solution)/shard_map/middle/pallas_call | solution.py:1922
  326.4 11.3 %spread.1.refs_10_ = bf16[64,128,1024]{2,1,0:T(8,128)(2,1)} custom-call(s32[64]{0:T(128)} %compare_select_fusion.tile_ref, s32[64]{0:T(128)} %convert_element_type.22.used_ref, bf16[32,128,1024]{2,1,0:T(8,128)(2,1)} %bitcast.46, bf16[32,128,1024]{2,1,0:T(8,128)(2,1)} %bitcast.47, bf16[32,128,1024]{2,1,0:T(8,128)(2,1)} %bitcast.48, ...), custom_call_target="tpu_custom_call" | custom-call | bytes 25165824 | tf_op jit(solution)/shard_map/spread/pallas_call | solution.py:2008
  337.7 0.0 copy-start.10
  337.7 0.0 copy-start.11
  337.7 0.0 reduce-scatter.2.cloned.1.call-update
  337.7 0.6 copy-done.4
  338.4 0.7 reshape.59.refs_0_
  339.0 0.0 copy-done.13
  339.0 0.0 copy-done.10
  339.0 0.1 fusion.7
  339.2 0.7 broadcast_multiply_fusion.refs_9_
  339.8 220.9 %lines.1 = (bf16[3072,1024]{1,0:T(8,128)(2,1)}, bf16[768,1024]{1,0:T(8,128)(2,1)}, f32[2,1024]{1,0:T(2,128)}) custom-call(s32[1,480]{1,0:T(1,128)} %reshape.59.refs_0_, f32[480,1024]{1,0:T(8,128)} %get-tuple-element.50.refs_1_, f32[2,1024]{1,0:T(2,128)} %refs_2_.1, bf16[3072,1024]{1,0:T(8,128)(2,1)} %refs_3_.1, ...), custom_call_target="tpu_custom_call" | custom-call | flops 1509949440 | bytes 60000000 | tf_op jit(solution)/shard_map/lines/pallas_call | solution.py:2037
  560.8 0.0 copy-done.3
  560.8 0.0 copy-done.6
  560.8 0.0 copy-done.7
  560.8 1.3 multiply_subtract_fusion
  562.2 12.9 %convert_bitcast_fusion = (bf16[1,8,128,1024]{3,2,1,0:T(8,128)(2,1)}, f32[8,128,1024]{2,1,0:T(8,128)}, f32[1,8,128,1024]{3,2,1,0:T(8,128)}, f32[1,8,128,1024]{3,2,1,0:T(8,128)}, f32[1,8,128,1024]{3,2,1,0:T(8,128)}) fusion(f32[1,8,128,1024]{3,2,1,0:T(8,128)} %param.22, bf16[8,128,1024]{2,1,0:T(8,128)(2,1)} %reduce-scatter.2.cloned.1.call-done, ...), kind=kLoop, calls=%fused_computation.10 | loop fusion | flops 22020096 | bytes 33554440 | tf_op jit(solution)/shard_map/broadcast_in_dim | solution.py:2377
  575.1 6.3 %copy.29 = bf16[3072,1024]{1,0:T(8,128)(2,1)} copy(bf16[3072,1024]{1,0:T(8,128)(2,1)} %get-tuple-element.82) | data formatting | bytes 12582912
  581.4 1.1 copy.30
  582.6 0.6 copy.31
  (19 shorter events, 0.1 us)
Async XLA Ops:
  7.2 42.3 %copy-start.12 = (s32[1,32]{1,0:T(1,128)S(1)}, s32[1,32]{1,0:T(1,128)}, u32[]{:S(2)}) copy-start(s32[1,32]{1,0:T(1,128)} %param.19) | copy-start | bytes 388
  7.2 38.3 %copy-start.8 = (s32[3,153]{1,0:T(4,128)S(1)}, s32[3,153]{1,0:T(4,128)}, u32[]{:S(2)}) copy-start(s32[3,153]{1,0:T(4,128)} %param.14) | copy-start | bytes 5512
  7.2 43.7 %copy-start.1 = (bf16[3,153,1024]{2,1,0:T(8,128)(2,1)S(1)}, bf16[3,153,1024]{2,1,0:T(8,128)(2,1)}, u32[]{:S(2)}) copy-start(bf16[3,153,1024]{2,1,0:T(8,128)(2,1)} %param.15) | copy-start | bytes 2820100
  7.2 129.8 %all-gather.2.cloned.1.call-start = ((), (), s32[]{:S(2)}) async-start(), calls=%async_computation.1 | async-start | bytes 18874368 | tf_op jit(solution)/shard_map/all_gather | solution.py:1750
  8.7 40.8 %copy-start.9 = (s32[32]{0:T(128)S(1)}, s32[32]{0:T(128)}, u32[]{:S(2)}) copy-start(s32[32]{0:T(128)} %convert_reduce_fusion) | copy-start | bytes 388
  45.4 516.8 %reduce-scatter.2.cloned.1.call-start = ((), (), s32[]{:S(2)}) async-start(), calls=%async_computation.2 | async-start | bytes 18874368 | tf_op jit(solution)/shard_map/reduce_scatter | solution.py:2032
  337.7 0.7 copy-start.4
  337.7 1.3 copy-start.13
  337.7 1.3 copy-start.10
  337.7 1.5 copy-start.5
  337.7 1.5 copy-start.11
  339.8 221.0 %copy-start.3 = (f32[2,1024]{1,0:T(2,128)S(1)}, f32[2,1024]{1,0:T(2,128)}, u32[]{:S(2)}) copy-start(f32[2,1024]{1,0:T(2,128)} %refs_2_.1) | copy-start | bytes 24580
  339.8 221.0 %copy-start.6 = (f32[2,1024]{1,0:T(2,128)S(1)}, f32[2,1024]{1,0:T(2,128)}, u32[]{:S(2)}) copy-start(f32[2,1024]{1,0:T(2,128)} %param.17) | copy-start | bytes 24580
  339.8 221.0 %copy-start.7 = (f32[2,1024]{1,0:T(2,128)S(1)}, f32[2,1024]{1,0:T(2,128)}, u32[]{:S(2)}) copy-start(f32[2,1024]{1,0:T(2,128)} %param.18) | copy-start | bytes 24580
  575.1 6.3 %copy-start = (bf16[768,1024]{1,0:T(8,128)(2,1)S(1)}, bf16[768,1024]{1,0:T(8,128)(2,1)}, u32[]{:S(2)}) copy-start(bf16[768,1024]{1,0:T(8,128)(2,1)} %get-tuple-element.83) | copy-start | bytes 4718596
  575.1 7.5 %copy-start.2 = (f32[2,1024]{1,0:T(2,128)S(1)}, f32[2,1024]{1,0:T(2,128)}, u32[]{:S(2)}) copy-start(f32[2,1024]{1,0:T(2,128)} %get-tuple-element.89) | copy-start | bytes 24580
Sparse Core Ops, SparseCore 0:
  45.5 90.1 all-gather.1
  337.9 116.9 reduce-scatter.1

commit v5 on v4

--- a/solution.py
+++ b/solution.py
@@ -1039,24 +1039,20 @@
     load_o(1).wait()
     load_x(0).wait()
     ffn(0, oa_refs, 1)
-    inward(0)
     hops_in(0, 3)
     hops(1, 1)
     load_x(1).wait()
 
     def meanwhile():
         sum_dhf()
-        hops_in(1, 1)
-        hops(1, 2)
-
-    ffn(1, [obuf.at[0, n] for n in range(4)], 2, meanwhile)
+        inward(0)
+
+    ffn(1, [obuf.at[0, n] for n in range(4)], 0, meanwhile)
     inward(1)
+    hops_in(1, 1)
+    hops(1, 2)
     hops_in(1, 2)
     hops(1, 3)
-    hops_in(1, 3)
-    load_x(2).wait()
-    ffn(2, [obuf.at[1, n] for n in range(4)], 0)
-    inward(2)
 
     def copy_b(w):
         return remote(
@@ -1078,8 +1074,6 @@
             total = bsum[w].astype(f32) + hf_ref[0 : 2 * share, :].astype(f32)
             bsum[w] = total.astype(bf16)
             copy_b(w).start()
-
-    exchange_rows(0)
 
     for k in range(1, 4):
         copy_e(k, lax.rem(place + 4 - k, 4)).wait_recv()
@@ -1147,9 +1141,11 @@
     dha_stored(0)
     back_window(1, 2)
     dha_stored(1)
-    exchange_rows(1)
+    exchange_rows(0)
     back_window(2, None)
     dha_stored(2)
+    hops_in(1, 3)
+    ffn(2, [obuf.at[1, n] for n in range(4)], None)
     fold = model // width
     for block in range(3 * width // 128):
         part, lane = divmod(block * 128, width)
@@ -1164,18 +1160,16 @@
     store.start()
     store.wait()
 
-    for w in range(windows):
-
-        @pl.when(outer)
-        def _():
+    @pl.when(outer)
+    def _():
+        for w in range(2):
             copy_a(w).wait_send()
 
     @pl.when(inner)
     def _():
-        copy_a(2).wait_recv()
-        for w in range(2):
-            copy_b(w).wait_send()
-            copy_b(w).wait_recv()
+        copy_a(1).wait_recv()
+        copy_b(0).wait_send()
+        copy_b(0).wait_recv()
 
     for k in range(1, 4):
         copy_d(k).wait_send()
@@ -1253,22 +1247,39 @@
     inner = (place == 1) | (place == 2)
     share = rc.shape[1]
     folds = len(order)
+    next_in = jnp.where(lower, 1, 2)
+    inner_far = 3 - place
+    outer_near = jnp.where(lower, 0, 3)
+    outer_far = 3 - outer_near
+
+    def block(ref, index):
+        return rows_ref(ref, index, share, 1)
 
     def whole(f):
         kind, index = order[f]
         return part_ref.at[index] if kind == 0 else dha_ref.at[index]
 
-    def copy_a(f):
-        far = rows_ref(whole(f), jnp.where(lower, 1, 0), share, 3)
-        return remote(far, ra.at[f], a_send.at[f], a_recv.at[f], jnp.where(lower, 1, 2))
-
-    def copy_b(f):
-        src = rows_ref(ra.at[f], jnp.where(lower, 1, 0), share, 2)
-        return remote(src, rb.at[f], b_send.at[f], b_recv.at[f], jnp.where(lower, 2, 1))
+    def copy_a(f, i):
+        return remote(
+            block(whole(f), jnp.where(lower, 3 - i, i)),
+            block(ra.at[f], jnp.where(lower, 2 - i, i)),
+            a_send.at[f, i],
+            a_recv.at[f, i],
+            next_in,
+        )
+
+    def copy_b(f, i):
+        return remote(
+            block(ra.at[f], jnp.where(lower, 2 - i, i)),
+            block(rb.at[f], jnp.where(lower, 1 - i, i)),
+            b_send.at[f, i],
+            b_recv.at[f, i],
+            jnp.where(lower, 2, 1),
+        )
 
     def copy_c(f):
-        src = rows_ref(rb.at[f], jnp.where(lower, 0, 1), share, 1)
-        return remote(src, rc.at[f], c_send.at[f], c_recv.at[f], jnp.where(lower, 0, 3))
+        src = block(rb.at[f], jnp.where(lower, 0, 1))
+        return remote(src, rc.at[f], c_send.at[f], c_recv.at[f], outer_near)
 
     def load(f):
         return pltpu.make_async_copy(whole(f), value.at[f], v_sem.at[f])
@@ -1282,31 +1293,34 @@
     def load_rb(f):
         return pltpu.make_async_copy(rb_in.at[order[f][1]], rb.at[f], t_sem.at[f])
 
-    def hop(w, d, up, origin):
-        rows = pl.ds(pl.multiple_of(w * 4 * share + origin * share, share), share)
-        n = 0 if up else 1
+    def rows_of(w, origin):
+        return pl.ds(pl.multiple_of((w * 4 + origin) * share, share), share)
+
+    def pass_on(w, origin, way, n, target):
+        rows = rows_of(w, origin)
         return remote(
-            piece.at[w] if d == 1 else out_ref.at[rows, :],
+            piece.at[w] if way < 2 else out_ref.at[rows, :],
             out_ref.at[rows, :],
-            g_send.at[w, d - 1, n],
-            g_recv.at[w, d - 1, n],
-            lax.rem(place + (1 if up else 3), 4),
-        )
-
-    def source(d, up):
-        return jnp.clip(place - (d - 1) if up else place + (d - 1), 0, 3)
-
-    def hops(w, d):
-        each_way(place, d, sends, lambda up: hop(w, d, up, source(d, up)).start())
-
-    def hops_in(w, d):
-        each_way(
-            place, d, receives, lambda up: hop(w, d, up, source(d + 1, up)).wait_recv()
+            g_send.at[w, way],
+            g_recv.at[w, n],
+            target,
+        )
+
+    def got(w, n):
+        origin = (
+            jnp.where(outer, next_in, inner_far),
+            jnp.where(outer, 3 - next_in, outer_near),
+            jnp.where(outer, 3 - place, outer_far),
+        )[n]
+        rows = rows_of(w, origin)
+        return remote(
+            out_ref.at[rows, :], out_ref.at[rows, :], g_send.at[w, 0], g_recv.at[w, n], inner_far
         )
 
     def keep(w):
-        rows = pl.ds(pl.multiple_of(w * 4 * share + place * share, share), share)
-        return pltpu.make_async_copy(piece.at[w], out_ref.at[rows, :], l_sem.at[w])
+        return pltpu.make_async_copy(
+            piece.at[w], out_ref.at[rows_of(w, place), :], l_sem.at[w]
+        )
 
     def store(c):
         return pltpu.make_async_copy(
@@ -1317,10 +1331,11 @@
         rows_ref(x_ref, place * cuts, share, cuts), x_rows, x_sem
     )
 
-    for f in range(folds):
+    for w in range(windows):
+        load(w).start()
+        load_own(w).start()
+    for f in range(windows, folds):
         load(f).start()
-    for w in range(windows):
-        load_own(w).start()
     x_load.start()
 
     pairs = []
@@ -1348,40 +1363,24 @@
         if t < len(pairs):
             copy_s(t).start()
 
-    greet_line(place, [pair for pair in pairs if pair[0] == "dp"])
     gain_sum[0] = jnp.zeros(gain_sum.shape[1:], f32)
     gain_sum[0, 0:2, :] = gain_in[...]
-    sent = list(range(ready, folds))
-
-    @pl.when(outer)
-    def _():
-        for f in sent[:2]:
-            copy_a(f).start()
-
-    @pl.when(inner)
-    def _():
-        for f in range(ready):
-            load_ra(f).start()
-        for f in range(traded):
-            load_rb(f).start()
-
-    def add_rows(buffer, at, f, index):
-        rows = pl.ds(pl.multiple_of(at * share, share), share)
-        mine = pl.ds(pl.multiple_of(index * share, share), share)
-        total = buffer[f, rows, :].astype(f32) + value[f, mine, :].astype(f32)
-        buffer[f, rows, :] = total.astype(bf16)
+
+    def rows_at_(index):
+        return pl.ds(pl.multiple_of(index * share, share), share)
 
     def finish(f, terms):
         kind, index = order[f]
         if kind == 0:
+            load_own(index).wait()
             total = own[index]
         else:
-            mine = pl.ds(pl.multiple_of(place * share, share), share)
-            total = value[f, mine, :].astype(f32)
+            total = value[f, rows_at_(place), :].astype(f32)
         for term in terms:
             total = total + term.astype(f32)
         if kind == 0:
             piece[index] = total.astype(bf16)
+            keep(index).start()
         else:
             first = place * (cuts * share) + index * share
             count = drm_ref.shape[0]
@@ -1394,105 +1393,156 @@
             ).astype(bf16)
             store(index).start()
 
-    for f in range(folds):
-        load(f).wait()
-    for w in range(windows):
-        load_own(w).wait()
-    x_load.wait()
-    moving = {}
-    turn = 0
-    for step in range(folds + 1):
-        if turn <= len(pairs):
-            next_pair(turn)
-            turn += 1
-        if step < folds:
-
-            @pl.when(inner)
-            def _():
-                if step < ready:
-                    load_ra(step).wait()
-                else:
-                    copy_a(step).wait_recv()
-                if step >= traded:
-                    for n in range(2):
-                        add_rows(
-                            ra,
-                            jnp.where(lower, 1, 0) + n,
-                            step,
-                            jnp.where(lower, 2, 0) + n,
-                        )
-                    copy_b(step).start()
-
-        if step > 0:
-            f = step - 1
-
-            @pl.when(inner)
-            def _():
-                if f < traded:
-                    load_rb(f).wait()
-                else:
-                    copy_b(f).wait_recv()
-                add_rows(rb, jnp.where(lower, 0, 1), f, jnp.where(lower, 0, 3))
-                copy_c(f).start()
-                sel_a = pl.ds(pl.multiple_of(jnp.where(lower, 0, 2) * share, share), share)
-                sel_b = pl.ds(pl.multiple_of(jnp.where(lower, 1, 0) * share, share), share)
-                finish(f, [ra[f, sel_a, :], rb[f, sel_b, :]])
-
-            @pl.when(outer)
-            def _():
-                copy_c(f).wait_recv()
-                finish(f, [rc[f]])
-
-            for w in list(moving):
-                hops_in(w, moving[w])
-                if moving[w] == 3:
-                    del moving[w]
-                else:
-                    moving[w] += 1
-                    hops(w, moving[w])
-            kind, index = order[f]
-            if kind == 0:
-                hops(index, 1)
-                keep(index).start()
-                moving[index] = 1
-
-        if ready <= step < folds:
-
-            @pl.when(outer)
-            def _():
-                copy_a(step).wait_send()
-                if step + 2 < folds:
-                    copy_a(step + 2).start()
-
-    while turn <= len(pairs):
-        next_pair(turn)
-        turn += 1
+    greet_line(place, [pair for pair in pairs if pair[0] == "dp"])
+
+    @pl.when(outer)
+    def _():
+        chunks = [(f, i) for f in range(ready, folds) for i in range(3)]
+
+        def step(n):
+            copy_a(*chunks[n]).wait_send()
+            if n + 2 < len(chunks):
+                copy_a(*chunks[n + 2]).start()
+
+        def total(f):
+            copy_c(f).wait_recv()
+            if order[f][0] == 1:
+                load(f).wait()
+            finish(f, [rc[f]])
+            if order[f][0] == 0:
+                pass_on(f, place, 0, 1, next_in).start()
+
+        for n in range(2):
+            copy_a(*chunks[n]).start()
+        next_pair(0)
+        total(0)
+        step(0)
+        step(1)
+        next_pair(1)
+        total(1)
+        step(2)
+        step(3)
+        step(4)
+        next_pair(2)
+        total(2)
+        next_pair(3)
+        step(5)
+        step(6)
+        x_load.wait()
+        total(3)
+        next_pair(4)
+        for n in range(7, 12):
+            step(n)
+        total(4)
+        next_pair(5)
+        total(5)
+        for w in range(windows):
+            load(w).wait()
+            pass_on(w, place, 0, 1, next_in).wait_send()
+            for n in range(3):
+                got(w, n).wait_recv()
+
+    @pl.when(inner)
+    def _():
+        for f in range(ready):
+            load_ra(f).start()
+        for f in range(traded):
+            load_rb(f).start()
+
+        def give_b(f):
+            load(f).wait()
+            if f < ready:
+                load_ra(f).wait()
+            for i in range(2):
+                if f >= ready:
+                    copy_a(f, i).wait_recv()
+                to = rows_at_(jnp.where(lower, 2 - i, i))
+                mine = value[f, rows_at_(jnp.where(lower, 3 - i, i)), :]
+                ra[f, to, :] = (ra[f, to, :].astype(f32) + mine.astype(f32)).astype(bf16)
+                copy_b(f, i).start()
+
+        def total(f):
+            if f < traded:
+                load(f).wait()
+                load_ra(f).wait()
+                load_rb(f).wait()
+            else:
+                came(f, 0)
+            to = rows_at_(jnp.where(lower, 0, 1))
+            mine = value[f, rows_at_(outer_near), :]
+            rb[f, to, :] = (rb[f, to, :].astype(f32) + mine.astype(f32)).astype(bf16)
+            copy_c(f).start()
+            if f >= traded:
+                came(f, 1)
+            if f >= ready:
+                copy_a(f, 2).wait_recv()
+            near = rows_at_(jnp.where(lower, 0, 2))
+            other = rows_at_(jnp.where(lower, 1, 0))
+            finish(f, [ra[f, near, :], rb[f, other, :]])
+            if order[f][0] == 0:
+                pass_on(f, place, 0, 0, inner_far).start()
+                pass_on(f, place, 1, 0, outer_near).start()
+
+        def came(f, i):
+            to = block(rb.at[f], jnp.where(lower, i, 1 - i))
+            remote(to, to, b_send.at[f, i], b_recv.at[f, i], inner_far).wait_recv()
+
+        def from_far_inner(w):
+            got(w, 0).wait_recv()
+            pass_on(w, inner_far, 2, 1, outer_near).start()
+
+        def from_outer(w):
+            got(w, 1).wait_recv()
+            pass_on(w, outer_near, 3, 2, inner_far).start()
+
+        def from_far_outer(w):
+            got(w, 2).wait_recv()
+            pass_on(w, outer_far, 4, 2, outer_near).start()
+
+        next_pair(0)
+        total(0)
+        give_b(1)
+        next_pair(1)
+        from_far_inner(0)
+        total(1)
+        next_pair(2)
+        give_b(2)
+        from_outer(0)
+        from_far_inner(1)
+        total(2)
+        next_pair(3)
+        from_far_outer(0)
+        from_outer(1)
+        give_b(3)
+        from_far_inner(2)
+        from_far_outer(1)
+        x_load.wait()
+        total(3)
+        next_pair(4)
+        from_outer(2)
+        give_b(4)
+        from_far_outer(2)
+        total(4)
+        give_b(5)
+        total(5)
+        next_pair(5)
+        for f in range(folds):
+            copy_c(f).wait_send()
+            for i in range(2):
+                if f >= traded:
+                    copy_b(f, i).wait_send()
+        for w in range(windows):
+            pass_on(w, place, 0, 0, inner_far).wait_send()
+            pass_on(w, place, 1, 0, outer_near).wait_send()
+            pass_on(w, inner_far, 2, 1, outer_near).wait_send()
+            pass_on(w, outer_near, 3, 2, inner_far).wait_send()
+            pass_on(w, outer_far, 4, 2, outer_near).wait_send()
+
     gain_ref[...] = gain_sum[len(pairs), 0:2, :]
     for t in range(len(pairs)):
         copy_s(t).wait_send()
-    while moving:
-        for w in list(moving):
-            hops_in(w, moving[w])
-            if moving[w] == 3:
-                del moving[w]
-            else:
-                moving[w] += 1
-                hops(w, moving[w])
-
-    @pl.when(inner)
-    def _():
-        for f in range(folds):
-            if f >= traded:
-                copy_b(f).wait_send()
-            copy_c(f).wait_send()
-
     for w in range(windows):
         keep(w).wait()
-        for d in range(1, 4):
-            each_way(
-                place, d, sends, lambda up: hop(w, d, up, source(d, up)).wait_send()
-            )
-
     for c in range(cuts):
         store(c).wait()
 
@@ -1924,8 +1974,8 @@
             out_shape=[
                 jax.ShapeDtypeStruct((seq_count, window, model), bf16),
                 jax.ShapeDtypeStruct((seq_count, share, model), f32),
-                jax.ShapeDtypeStruct((seq_count, 3 * share, model), bf16),
-                jax.ShapeDtypeStruct((2, 2 * share, model), bf16),
+                jax.ShapeDtypeStruct((2, 3 * share, model), bf16),
+                jax.ShapeDtypeStruct((1, 2 * share, model), bf16),
                 jax.ShapeDtypeStruct((seq_count, window, model), bf16),
                 jax.ShapeDtypeStruct((grad_rows, model), bf16),
                 jax.ShapeDtypeStruct((mask_rows, model), f32),
@@ -1950,10 +2000,10 @@
                 pltpu.VMEM((4, mask_rows, model // 4), bf16),
                 pltpu.VMEM((3, mask_rows, model // 4), bf16),
                 pltpu.VMEM((4, mask_rows, model // 4), bf16),
-                pltpu.VMEM((2, 2 * share, model), bf16),
+                pltpu.VMEM((1, 2 * share, model), bf16),
                 dma((2,)),
-                dma((2,)),
-                dma((2,)),
+                dma((1,)),
+                dma((1,)),
                 dma((2,)),
                 dma,
                 dma((2, 2)),
@@ -1961,8 +2011,8 @@
                 dma,
                 dma((window // share,)),
                 dma,
-                dma((seq_count,)),
-                dma((seq_count,)),
+                dma((2,)),
+                dma((2,)),
                 dma((2, 3, 2)),
                 dma((2, 3, 2)),
                 dma((3,)),
@@ -2035,7 +2085,7 @@
         folds = len(order)
         pair_count = (lax.axis_size("dp") * parts).bit_length() - 1
         layer_out, input_grad, gain_grad = pl.pallas_call(
-            after(functools.partial(lines_kernel, seq_count, seq_count, order, seq_count, 2), 10, 1),
+            after(functools.partial(lines_kernel, seq_count, seq_count, order, 2, 1), 10, 1),
             out_shape=[
                 jax.ShapeDtypeStruct((total_rows, model), bf16),
                 jax.ShapeDtypeStruct((share_rows, model), bf16),
@@ -2056,18 +2106,18 @@
                 pltpu.VMEM((pair_count, 8, model), f32),
                 dma((pair_count,)),
                 dma((pair_count,)),
+                dma((folds, 3)),
+                dma((folds, 3)),
+                dma((folds, 2)),
+                dma((folds, 2)),
                 dma((folds,)),
                 dma((folds,)),
-                dma((folds,)),
-                dma((folds,)),
-                dma((folds,)),
-                dma((folds,)),
-                dma((seq_count, 3, 2)),
-                dma((seq_count, 3, 2)),
+                dma((seq_count, 5)),
+                dma((seq_count, 3)),
                 dma((folds,)),
                 dma((seq_count,)),
-                dma((seq_count,)),
                 dma((2,)),
+                dma((1,)),
                 dma,
                 dma((seq_count,)),
                 dma((seq_count,)),

time: 600 us -> 553 us (0.922)
  Pallas kernels: 541 us -> 497 us
    pallas_call x1, Pallas kernels: 182 us -> 158 us  [on_device(): pl.pallas_call(functools.partial(middle_kernel, seq_count), out_shape=[ja...]
    pallas_call x1, Pallas kernels: 221 us -> 201 us  [on_device(): pl.pallas_call(after(functools.partial(lines_kernel, seq_count, seq_count...]
where the time goes in v5:
time: 553 us; the launch traced here: 546 us
  Pallas kernels  497 us (90%)
  other arithmetic  20.6 us (4%)
  between operations  14.5 us (3%)
  local copies, waits for them, and re-layouts  13.9 us (3%)
    pallas_call x1, Pallas kernels, on_device(): pl.pallas_call(after(functools.partial(lines_kernel, seq_count, seq_count...  201 us
    pallas_call x1, Pallas kernels, on_device(): pl.pallas_call(functools.partial(middle_kernel, seq_count), out_shape=[ja...  158 us
    pallas_call x1, Pallas kernels, on_device(): pl.pallas_call(functools.partial(attend_all_kernel, seq_count), out_shape...  84.1 us
    pallas_call x1, Pallas kernels, on_device(): pl.pallas_call(weights_kernel, out_shape=[jax.ShapeDtypeStruct((capacity,...  35.5 us
    broadcast_in_dim x1, other arithmetic, on_device(): weight_low[None]  12.9 us
    pallas_call x1, Pallas kernels, on_device(): pl.pallas_call(spread_kernel, out_shape=jax.ShapeDtypeStruct((slots, tile...  11.3 us
  transfers between devices with their start and end apart: 2, of which 0 were waited for; matrix products, arithmetic and copies ran while one was open for 2% of the time, Pallas kernels for 52%

profile of v5, /device:TPU:0, one launch (start us, length us, event | category | flops | bytes accessed | tf_op | source)
XLA Modules:
  0.0 546.0 jit_solution(15420525538025364216)
XLA Ops:
  7.2 0.0 copy-start.12
  7.2 0.0 copy-start.8
  7.2 0.0 copy-start.1
  7.2 0.0 all-gather.2.cloned.1.call-start
  7.3 1.4 convert_reduce_fusion
  8.7 1.2 fusion.10.held_ref
  9.9 35.5 %weights.1 = (bf16[8,128,1024]{2,1,0:T(8,128)(2,1)}, bf16[8,128,1024]{2,1,0:T(8,128)(2,1)}) custom-call(s32[8]{0:T(128)} %bitcast.61, s32[8]{0:T(128)} %fusion.10.held_ref, f32[8,128,1024]{2,1,0:T(8,128)} %bitcast.54), custom_call_target="tpu_custom_call" | custom-call | bytes 12000000 | tf_op jit(solution)/shard_map/weights/pallas_call | solution.py:1726
  45.4 0.0 all-gather.2.cloned.1.call-update
  45.4 0.0 reduce-scatter.2.cloned.1.call-start
  45.5 0.0 copy-done.8
  45.5 0.7 pad_bitcast_fusion
  46.1 0.6 broadcast_in_dim.60.rows_in
  46.7 0.9 copy.25.rows_in
  47.6 1.9 slice.15
  49.5 0.0 copy-done.12
  49.5 0.0 copy-done.9
  49.5 0.1 fusion.3
  49.6 0.5 convert_element_type.22.used_ref
  50.1 0.6 iota_reduce_fusion
  50.7 0.1 reshape.63
  50.8 0.1 reduce_window_max.13
  50.9 0.0 copy-done.1
  50.9 1.0 pad.9
  51.9 0.5 compare_select_fusion.tile_ref
  52.4 0.5 multiply_add_fusion.refs_0_
  53.0 84.1 %attend_all.1 = (bf16[4,480,256]{2,1,0:T(8,128)(2,1)}, bf16[4,1024,256]{2,1,0:T(8,128)(2,1)}, bf16[1024,256]{1,0:T(8,128)(2,1)}, bf16[1024,256]{1,0:T(8,128)(2,1...) custom-call(s32[3,160,1]{2,1,0:T(8,128)} %copy.25.rows_in, ...), custom_call_target="tpu_custom_call" | custom-call | flops 40000000000 | bytes 20000000 | tf_op jit(solution)/shard_map/attend_all/pallas_call | solution.py:1825
  137.0 0.0 all-gather.2.cloned.1.call-done.refs_1_.refs_2_.refs_3_.refs_4_
  137.0 7.8 %collect.1 = bf16[24,128,1024]{2,1,0:T(8,128)(2,1)} custom-call(s32[32]{0:T(128)} %multiply_add_fusion.refs_0_, bf16[64,128,1024]{2,1,0:T(8,128)(2,1)} %all-gather.2.cloned.1.call-done.refs_1_.refs_2_.refs_3_.refs_4_, bf16[64,128,1024]{2,1,0:T(8,128)(2,1)} %all-gather.2.cloned.1.call-done.refs_1_.refs_2_.refs_3_.refs_4_, ...), custom_call_target="tpu_custom_call" | custom-call | bytes 12582912 | tf_op jit(solution)/shard_map/collect/pallas_call | solution.py:1946
  144.9 157.6 %middle.1 = (bf16[3,1024,1024]{2,1,0:T(8,128)(2,1)}, f32[3,256,1024]{2,1,0:T(8,128)}, bf16[2,768,1024]{2,1,0:T(8,128)(2,1)}, bf16[1,512,1024]{2,1,0:T(8,128)(2,1...) custom-call(s32[3,1,160]{2,1,0:T(1,128)} %broadcast_in_dim.60.rows_in,, ...), custom_call_target="tpu_custom_call" | custom-call | flops 99999997952 | bytes 100000000 | tf_op jit(solution)/shard_map/middle/pallas_call | solution.py:1972
  302.4 11.3 %spread.1.refs_10_ = bf16[64,128,1024]{2,1,0:T(8,128)(2,1)} custom-call(s32[64]{0:T(128)} %compare_select_fusion.tile_ref, s32[64]{0:T(128)} %convert_element_type.22.used_ref, bf16[32,128,1024]{2,1,0:T(8,128)(2,1)} %bitcast.46, bf16[32,128,1024]{2,1,0:T(8,128)(2,1)} %bitcast.47, bf16[32,128,1024]{2,1,0:T(8,128)(2,1)} %bitcast.48, ...), custom_call_target="tpu_custom_call" | custom-call | bytes 25165824 | tf_op jit(solution)/shard_map/spread/pallas_call | solution.py:2058
  313.7 0.0 copy-start.10
  313.7 0.0 copy-start.5
  313.8 0.0 copy-start.11
  313.8 0.0 reduce-scatter.2.cloned.1.call-update
  313.8 0.6 copy-done.4
  314.4 0.7 reshape.59.refs_0_
  315.1 0.0 copy-done.13
  315.1 0.0 copy-done.10
  315.1 0.1 fusion.7
  315.2 0.0 copy-done.5
  315.2 0.7 broadcast_multiply_fusion.refs_9_
  315.9 200.6 %lines.1 = (bf16[3072,1024]{1,0:T(8,128)(2,1)}, bf16[768,1024]{1,0:T(8,128)(2,1)}, f32[2,1024]{1,0:T(2,128)}) custom-call(s32[1,480]{1,0:T(1,128)} %reshape.59.refs_0_, f32[480,1024]{1,0:T(8,128)} %get-tuple-element.50.refs_1_, f32[2,1024]{1,0:T(2,128)} %refs_2_.1, bf16[3072,1024]{1,0:T(8,128)(2,1)} %refs_3_.1, ...), custom_call_target="tpu_custom_call" | custom-call | flops 1509949440 | bytes 60000000 | tf_op jit(solution)/shard_map/lines/pallas_call | solution.py:2087
  516.6 1.3 multiply_subtract_fusion
  517.9 12.9 %convert_bitcast_fusion = (bf16[1,8,128,1024]{3,2,1,0:T(8,128)(2,1)}, f32[8,128,1024]{2,1,0:T(8,128)}, f32[1,8,128,1024]{3,2,1,0:T(8,128)}, f32[1,8,128,1024]{3,2,1,0:T(8,128)}, f32[1,8,128,1024]{3,2,1,0:T(8,128)}) fusion(f32[1,8,128,1024]{3,2,1,0:T(8,128)} %param.22, bf16[8,128,1024]{2,1,0:T(8,128)(2,1)} %reduce-scatter.2.cloned.1.call-done, ...), kind=kLoop, calls=%fused_computation.10 | loop fusion | flops 22020096 | bytes 33554440 | tf_op jit(solution)/shard_map/broadcast_in_dim | solution.py:2427
  530.9 6.3 %copy.29 = bf16[3072,1024]{1,0:T(8,128)(2,1)} copy(bf16[3072,1024]{1,0:T(8,128)(2,1)} %get-tuple-element.82) | data formatting | bytes 12582912
  537.2 1.1 copy.30
  538.3 0.0 copy-done.2
  538.3 0.6 copy.31
  (19 shorter events, 0.1 us)
Async XLA Ops:
  7.2 42.3 %copy-start.12 = (s32[1,32]{1,0:T(1,128)S(1)}, s32[1,32]{1,0:T(1,128)}, u32[]{:S(2)}) copy-start(s32[1,32]{1,0:T(1,128)} %param.19) | copy-start | bytes 388
  7.2 38.3 %copy-start.8 = (s32[3,153]{1,0:T(4,128)S(1)}, s32[3,153]{1,0:T(4,128)}, u32[]{:S(2)}) copy-start(s32[3,153]{1,0:T(4,128)} %param.14) | copy-start | bytes 5512
  7.2 43.7 %copy-start.1 = (bf16[3,153,1024]{2,1,0:T(8,128)(2,1)S(1)}, bf16[3,153,1024]{2,1,0:T(8,128)(2,1)}, u32[]{:S(2)}) copy-start(bf16[3,153,1024]{2,1,0:T(8,128)(2,1)} %param.15) | copy-start | bytes 2820100
  7.2 129.8 %all-gather.2.cloned.1.call-start = ((), (), s32[]{:S(2)}) async-start(), calls=%async_computation.1 | async-start | bytes 18874368 | tf_op jit(solution)/shard_map/all_gather | solution.py:1800
  8.7 40.8 %copy-start.9 = (s32[32]{0:T(128)S(1)}, s32[32]{0:T(128)}, u32[]{:S(2)}) copy-start(s32[32]{0:T(128)} %convert_reduce_fusion) | copy-start | bytes 388
  45.4 472.5 %reduce-scatter.2.cloned.1.call-start = ((), (), s32[]{:S(2)}) async-start(), calls=%async_computation.2 | async-start | bytes 18874368 | tf_op jit(solution)/shard_map/reduce_scatter | solution.py:2082
  313.7 0.7 copy-start.4
  313.7 1.3 copy-start.13
  313.7 1.3 copy-start.10
  313.7 1.5 copy-start.5
  313.8 1.5 copy-start.11
  315.9 200.7 %copy-start.3 = (f32[2,1024]{1,0:T(2,128)S(1)}, f32[2,1024]{1,0:T(2,128)}, u32[]{:S(2)}) copy-start(f32[2,1024]{1,0:T(2,128)} %refs_2_.1) | copy-start | bytes 24580
  315.9 200.7 %copy-start.6 = (f32[2,1024]{1,0:T(2,128)S(1)}, f32[2,1024]{1,0:T(2,128)}, u32[]{:S(2)}) copy-start(f32[2,1024]{1,0:T(2,128)} %param.17) | copy-start | bytes 24580
  315.9 200.7 %copy-start.7 = (f32[2,1024]{1,0:T(2,128)S(1)}, f32[2,1024]{1,0:T(2,128)}, u32[]{:S(2)}) copy-start(f32[2,1024]{1,0:T(2,128)} %param.18) | copy-start | bytes 24580
  530.8 6.3 %copy-start = (bf16[768,1024]{1,0:T(8,128)(2,1)S(1)}, bf16[768,1024]{1,0:T(8,128)(2,1)}, u32[]{:S(2)}) copy-start(bf16[768,1024]{1,0:T(8,128)(2,1)} %get-tuple-element.83) | copy-start | bytes 4718596
  530.8 7.5 %copy-start.2 = (f32[2,1024]{1,0:T(2,128)S(1)}, f32[2,1024]{1,0:T(2,128)}, u32[]{:S(2)}) copy-start(f32[2,1024]{1,0:T(2,128)} %get-tuple-element.89) | copy-start | bytes 24580
Sparse Core Ops, SparseCore 0:
  45.5 90.1 all-gather.1
  313.9 116.3 reduce-scatter.1

commit v6 on v5

--- a/solution.py
+++ b/solution.py
@@ -889,9 +889,14 @@
     def store_own(w):
         return pltpu.make_async_copy(own_ref, own_out.at[w], own_sem)
 
-    def copy_a(w):
-        far = rows_ref(part_out.at[w], jnp.where(lower, 1, 0), share, 3)
-        return remote(far, ra_out.at[w], a_send.at[w], a_recv.at[w], jnp.where(lower, 1, 2))
+    def copy_a(w, i):
+        return remote(
+            rows_ref(part_out.at[w], jnp.where(lower, 3 - i, i), share, 1),
+            rows_ref(ra_out.at[w], jnp.where(lower, 2 - i, i), share, 1),
+            a_send.at[w, i],
+            a_recv.at[w, i],
+            jnp.where(lower, 1, 2),
+        )
 
     def copy_d(k):
         to = lax.rem(place + k, 4)
@@ -999,10 +1004,11 @@
         store_p(part_out.at[w]).wait()
         store_own(w).wait()
 
-    def inward(w):
+    def inward(w, blocks):
         @pl.when(outer)
         def _():
-            copy_a(w).start()
+            for i in blocks:
+                copy_a(w, i).start()
 
     def sum_dhf():
         for k in range(1, 4):
@@ -1039,16 +1045,17 @@
     load_o(1).wait()
     load_x(0).wait()
     ffn(0, oa_refs, 1)
+    inward(0, (0,))
     hops_in(0, 3)
     hops(1, 1)
     load_x(1).wait()
 
     def meanwhile():
         sum_dhf()
-        inward(0)
+        inward(0, (1, 2))
 
     ffn(1, [obuf.at[0, n] for n in range(4)], 0, meanwhile)
-    inward(1)
+    inward(1, (0, 1, 2))
     hops_in(1, 1)
     hops(1, 2)
     hops_in(1, 2)
@@ -1062,7 +1069,8 @@
     def exchange_rows(w):
         @pl.when(inner)
         def _():
-            copy_a(w).wait_recv()
+            for i in range(3):
+                copy_a(w, i).wait_recv()
             rows = rows_ref(ra_out.at[w], jnp.where(lower, 1, 0), share, 2)
             mine = rows_ref(part_out.at[w], jnp.where(lower, 2, 0), share, 2)
             got = pltpu.make_async_copy(rows, bsum.at[w], b_load.at[0])
@@ -1163,11 +1171,13 @@
     @pl.when(outer)
     def _():
         for w in range(2):
-            copy_a(w).wait_send()
+            for i in range(3):
+                copy_a(w, i).wait_send()
 
     @pl.when(inner)
     def _():
-        copy_a(1).wait_recv()
+        for i in range(3):
+            copy_a(1, i).wait_recv()
         copy_b(0).wait_send()
         copy_b(0).wait_recv()
 
@@ -2011,8 +2021,8 @@
                 dma,
                 dma((window // share,)),
                 dma,
-                dma((2,)),
-                dma((2,)),
+                dma((2, 3)),
+                dma((2, 3)),
                 dma((2, 3, 2)),
                 dma((2, 3, 2)),
                 dma((3,)),

time: 553 us -> 547 us (0.989)
  Pallas kernels: 497 us -> 490 us
    pallas_call x1, Pallas kernels: 158 us -> 151 us  [on_device(): pl.pallas_call(functools.partial(middle_kernel, seq_count), out_shape=[ja...]
  transfers between devices with their start and end apart: 2 -> 2, of which waited for: 0 -> 0; matrix products, arithmetic and copies ran while one was open for 2% -> 2% of each run, Pallas kernels for 52% -> 53%
where the time goes in v6:
time: 547 us; the launch traced here: 539 us
  Pallas kernels  490 us (90%)
  other arithmetic  20.6 us (4%)
  between operations  14.5 us (3%)
  local copies, waits for them, and re-layouts  13.9 us (3%)
    pallas_call x1, Pallas kernels, on_device(): pl.pallas_call(after(functools.partial(lines_kernel, seq_count, seq_count...  199 us
    pallas_call x1, Pallas kernels, on_device(): pl.pallas_call(functools.partial(middle_kernel, seq_count), out_shape=[ja...  151 us
    pallas_call x1, Pallas kernels, on_device(): pl.pallas_call(functools.partial(attend_all_kernel, seq_count), out_shape...  84.1 us
    pallas_call x1, Pallas kernels, on_device(): pl.pallas_call(weights_kernel, out_shape=[jax.ShapeDtypeStruct((capacity,...  35.5 us
    broadcast_in_dim x1, other arithmetic, on_device(): weight_low[None]  12.9 us
    pallas_call x1, Pallas kernels, on_device(): pl.pallas_call(spread_kernel, out_shape=jax.ShapeDtypeStruct((slots, tile...  12.4 us
  transfers between devices with their start and end apart: 2, of which 0 were waited for; matrix products, arithmetic and copies ran while one was open for 2% of the time, Pallas kernels for 53%

profile of v6, /device:TPU:0, one launch (start us, length us, event | category | flops | bytes accessed | tf_op | source)
XLA Modules:
  0.0 538.8 jit_solution(11588226489913996451)
XLA Ops:
  7.2 0.0 copy-start.12
  7.2 0.0 copy-start.8
  7.2 0.0 copy-start.1
  7.2 0.0 all-gather.2.cloned.1.call-start
  7.3 1.4 convert_reduce_fusion
  8.7 1.2 fusion.10.held_ref
  9.9 35.5 %weights.1 = (bf16[8,128,1024]{2,1,0:T(8,128)(2,1)}, bf16[8,128,1024]{2,1,0:T(8,128)(2,1)}) custom-call(s32[8]{0:T(128)} %bitcast.61, s32[8]{0:T(128)} %fusion.10.held_ref, f32[8,128,1024]{2,1,0:T(8,128)} %bitcast.54), custom_call_target="tpu_custom_call" | custom-call | bytes 12000000 | tf_op jit(solution)/shard_map/weights/pallas_call | solution.py:1736
  45.4 0.0 all-gather.2.cloned.1.call-update
  45.4 0.0 reduce-scatter.2.cloned.1.call-start
  45.5 0.0 copy-done.8
  45.5 0.7 pad_bitcast_fusion
  46.1 0.6 broadcast_in_dim.60.rows_in
  46.7 0.9 copy.25.rows_in
  47.6 1.9 slice.15
  49.5 0.0 copy-done.12
  49.5 0.0 copy-done.9
  49.5 0.1 fusion.3
  49.6 0.5 convert_element_type.22.used_ref
  50.1 0.6 iota_reduce_fusion
  50.7 0.1 reshape.63
  50.8 0.1 reduce_window_max.13
  50.9 0.0 copy-done.1
  50.9 1.0 pad.9
  51.9 0.5 compare_select_fusion.tile_ref
  52.4 0.5 multiply_add_fusion.refs_0_
  53.0 84.1 %attend_all.1 = (bf16[4,480,256]{2,1,0:T(8,128)(2,1)}, bf16[4,1024,256]{2,1,0:T(8,128)(2,1)}, bf16[1024,256]{1,0:T(8,128)(2,1)}, bf16[1024,256]{1,0:T(8,128)(2,1...) custom-call(s32[3,160,1]{2,1,0:T(8,128)} %copy.25.rows_in, ...), custom_call_target="tpu_custom_call" | custom-call | flops 40000000000 | bytes 20000000 | tf_op jit(solution)/shard_map/attend_all/pallas_call | solution.py:1835
  137.0 0.0 all-gather.2.cloned.1.call-done.refs_1_.refs_2_.refs_3_.refs_4_
  137.0 7.8 %collect.1 = bf16[24,128,1024]{2,1,0:T(8,128)(2,1)} custom-call(s32[32]{0:T(128)} %multiply_add_fusion.refs_0_, bf16[64,128,1024]{2,1,0:T(8,128)(2,1)} %all-gather.2.cloned.1.call-done.refs_1_.refs_2_.refs_3_.refs_4_, bf16[64,128,1024]{2,1,0:T(8,128)(2,1)} %all-gather.2.cloned.1.call-done.refs_1_.refs_2_.refs_3_.refs_4_, ...), custom_call_target="tpu_custom_call" | custom-call | bytes 12582912 | tf_op jit(solution)/shard_map/collect/pallas_call | solution.py:1956
  144.9 150.6 %middle.1 = (bf16[3,1024,1024]{2,1,0:T(8,128)(2,1)}, f32[3,256,1024]{2,1,0:T(8,128)}, bf16[2,768,1024]{2,1,0:T(8,128)(2,1)}, bf16[1,512,1024]{2,1,0:T(8,128)(2,1...) custom-call(s32[3,1,160]{2,1,0:T(1,128)} %broadcast_in_dim.60.rows_in,, ...), custom_call_target="tpu_custom_call" | custom-call | flops 99999997952 | bytes 100000000 | tf_op jit(solution)/shard_map/middle/pallas_call | solution.py:1982
  295.4 12.4 %spread.1.refs_10_ = bf16[64,128,1024]{2,1,0:T(8,128)(2,1)} custom-call(s32[64]{0:T(128)} %compare_select_fusion.tile_ref, s32[64]{0:T(128)} %convert_element_type.22.used_ref, bf16[32,128,1024]{2,1,0:T(8,128)(2,1)} %bitcast.46, bf16[32,128,1024]{2,1,0:T(8,128)(2,1)} %bitcast.47, bf16[32,128,1024]{2,1,0:T(8,128)(2,1)} %bitcast.48, ...), custom_call_target="tpu_custom_call" | custom-call | bytes 25165824 | tf_op jit(solution)/shard_map/spread/pallas_call | solution.py:2068
  307.8 0.0 copy-start.10
  307.8 0.0 copy-start.5
  307.8 0.0 copy-start.11
  307.9 0.0 reduce-scatter.2.cloned.1.call-update
  307.9 0.6 copy-done.4
  308.5 0.7 reshape.59.refs_0_
  309.2 0.0 copy-done.13
  309.2 0.0 copy-done.10
  309.2 0.1 fusion.7
  309.3 0.0 copy-done.5
  309.3 0.7 broadcast_multiply_fusion.refs_9_
  310.0 199.3 %lines.1 = (bf16[3072,1024]{1,0:T(8,128)(2,1)}, bf16[768,1024]{1,0:T(8,128)(2,1)}, f32[2,1024]{1,0:T(2,128)}) custom-call(s32[1,480]{1,0:T(1,128)} %reshape.59.refs_0_, f32[480,1024]{1,0:T(8,128)} %get-tuple-element.50.refs_1_, f32[2,1024]{1,0:T(2,128)} %refs_2_.1, bf16[3072,1024]{1,0:T(8,128)(2,1)} %refs_3_.1, ...), custom_call_target="tpu_custom_call" | custom-call | flops 1509949440 | bytes 60000000 | tf_op jit(solution)/shard_map/lines/pallas_call | solution.py:2097
  509.3 1.3 multiply_subtract_fusion
  510.7 12.9 %convert_bitcast_fusion = (bf16[1,8,128,1024]{3,2,1,0:T(8,128)(2,1)}, f32[8,128,1024]{2,1,0:T(8,128)}, f32[1,8,128,1024]{3,2,1,0:T(8,128)}, f32[1,8,128,1024]{3,2,1,0:T(8,128)}, f32[1,8,128,1024]{3,2,1,0:T(8,128)}) fusion(f32[1,8,128,1024]{3,2,1,0:T(8,128)} %param.22, bf16[8,128,1024]{2,1,0:T(8,128)(2,1)} %reduce-scatter.2.cloned.1.call-done, ...), kind=kLoop, calls=%fused_computation.10 | loop fusion | flops 22020096 | bytes 33554440 | tf_op jit(solution)/shard_map/broadcast_in_dim | solution.py:2437
  523.6 6.3 %copy.29 = bf16[3072,1024]{1,0:T(8,128)(2,1)} copy(bf16[3072,1024]{1,0:T(8,128)(2,1)} %get-tuple-element.82) | data formatting | bytes 12582912
  529.9 1.1 copy.30
  531.1 0.0 copy-done.2
  531.1 0.6 copy.31
  (19 shorter events, 0.1 us)
Async XLA Ops:
  7.2 42.3 %copy-start.12 = (s32[1,32]{1,0:T(1,128)S(1)}, s32[1,32]{1,0:T(1,128)}, u32[]{:S(2)}) copy-start(s32[1,32]{1,0:T(1,128)} %param.19) | copy-start | bytes 388
  7.2 38.3 %copy-start.8 = (s32[3,153]{1,0:T(4,128)S(1)}, s32[3,153]{1,0:T(4,128)}, u32[]{:S(2)}) copy-start(s32[3,153]{1,0:T(4,128)} %param.14) | copy-start | bytes 5512
  7.2 43.7 %copy-start.1 = (bf16[3,153,1024]{2,1,0:T(8,128)(2,1)S(1)}, bf16[3,153,1024]{2,1,0:T(8,128)(2,1)}, u32[]{:S(2)}) copy-start(bf16[3,153,1024]{2,1,0:T(8,128)(2,1)} %param.15) | copy-start | bytes 2820100
  7.2 129.8 %all-gather.2.cloned.1.call-start = ((), (), s32[]{:S(2)}) async-start(), calls=%async_computation.1 | async-start | bytes 18874368 | tf_op jit(solution)/shard_map/all_gather | solution.py:1810
  8.7 40.8 %copy-start.9 = (s32[32]{0:T(128)S(1)}, s32[32]{0:T(128)}, u32[]{:S(2)}) copy-start(s32[32]{0:T(128)} %convert_reduce_fusion) | copy-start | bytes 388
  45.4 465.3 %reduce-scatter.2.cloned.1.call-start = ((), (), s32[]{:S(2)}) async-start(), calls=%async_computation.2 | async-start | bytes 18874368 | tf_op jit(solution)/shard_map/reduce_scatter | solution.py:2092
  307.8 0.7 copy-start.4
  307.8 1.3 copy-start.13
  307.8 1.3 copy-start.10
  307.8 1.5 copy-start.5
  307.8 1.5 copy-start.11
  310.0 199.3 %copy-start.3 = (f32[2,1024]{1,0:T(2,128)S(1)}, f32[2,1024]{1,0:T(2,128)}, u32[]{:S(2)}) copy-start(f32[2,1024]{1,0:T(2,128)} %refs_2_.1) | copy-start | bytes 24580
  310.0 199.3 %copy-start.6 = (f32[2,1024]{1,0:T(2,128)S(1)}, f32[2,1024]{1,0:T(2,128)}, u32[]{:S(2)}) copy-start(f32[2,1024]{1,0:T(2,128)} %param.17) | copy-start | bytes 24580
  310.0 199.4 %copy-start.7 = (f32[2,1024]{1,0:T(2,128)S(1)}, f32[2,1024]{1,0:T(2,128)}, u32[]{:S(2)}) copy-start(f32[2,1024]{1,0:T(2,128)} %param.18) | copy-start | bytes 24580
  523.6 6.3 %copy-start = (bf16[768,1024]{1,0:T(8,128)(2,1)S(1)}, bf16[768,1024]{1,0:T(8,128)(2,1)}, u32[]{:S(2)}) copy-start(bf16[768,1024]{1,0:T(8,128)(2,1)} %get-tuple-element.83) | copy-start | bytes 4718596
  523.6 7.5 %copy-start.2 = (f32[2,1024]{1,0:T(2,128)S(1)}, f32[2,1024]{1,0:T(2,128)}, u32[]{:S(2)}) copy-start(f32[2,1024]{1,0:T(2,128)} %get-tuple-element.89) | copy-start | bytes 24580
Sparse Core Ops, SparseCore 0:
  45.5 90.1 all-gather.1
  308.0 116.6 reduce-scatter.1

commit v7 on v6

--- a/solution.py
+++ b/solution.py
@@ -1522,9 +1522,9 @@
         total(2)
         next_pair(3)
         from_far_outer(0)
+        from_far_inner(2)
+        give_b(3)
         from_outer(1)
-        give_b(3)
-        from_far_inner(2)
         from_far_outer(1)
         x_load.wait()
         total(3)

time: 547 us -> 547 us (level)
  no operation moved by 1% of the time
where the time goes in v7:
time: 547 us; the launch traced here: 540 us
  Pallas kernels  491 us (90%)
  other arithmetic  20.6 us (4%)
  between operations  14.5 us (3%)
  local copies, waits for them, and re-layouts  13.9 us (3%)
    pallas_call x1, Pallas kernels, on_device(): pl.pallas_call(after(functools.partial(lines_kernel, seq_count, seq_count...  200 us
    pallas_call x1, Pallas kernels, on_device(): pl.pallas_call(functools.partial(middle_kernel, seq_count), out_shape=[ja...  151 us
    pallas_call x1, Pallas kernels, on_device(): pl.pallas_call(functools.partial(attend_all_kernel, seq_count), out_shape...  84.1 us
    pallas_call x1, Pallas kernels, on_device(): pl.pallas_call(weights_kernel, out_shape=[jax.ShapeDtypeStruct((capacity,...  35.5 us
    broadcast_in_dim x1, other arithmetic, on_device(): weight_low[None]  12.9 us
    pallas_call x1, Pallas kernels, on_device(): pl.pallas_call(spread_kernel, out_shape=jax.ShapeDtypeStruct((slots, tile...  12.9 us
  transfers between devices with their start and end apart: 2, of which 0 were waited for; matrix products, arithmetic and copies ran while one was open for 2% of the time, Pallas kernels for 53%

profile of v7, /device:TPU:0, one launch (start us, length us, event | category | flops | bytes accessed | tf_op | source)
XLA Modules:
  0.0 540.1 jit_solution(1841869471388427863)
XLA Ops:
  7.2 0.0 copy-start.12
  7.2 0.0 copy-start.8
  7.2 0.0 copy-start.1
  7.2 0.0 all-gather.2.cloned.1.call-start
  7.3 1.4 convert_reduce_fusion
  8.7 1.2 fusion.10.held_ref
  9.9 35.5 %weights.1 = (bf16[8,128,1024]{2,1,0:T(8,128)(2,1)}, bf16[8,128,1024]{2,1,0:T(8,128)(2,1)}) custom-call(s32[8]{0:T(128)} %bitcast.61, s32[8]{0:T(128)} %fusion.10.held_ref, f32[8,128,1024]{2,1,0:T(8,128)} %bitcast.54), custom_call_target="tpu_custom_call" | custom-call | bytes 12000000 | tf_op jit(solution)/shard_map/weights/pallas_call | solution.py:1736
  45.4 0.0 all-gather.2.cloned.1.call-update
  45.4 0.0 reduce-scatter.2.cloned.1.call-start
  45.5 0.0 copy-done.8
  45.5 0.7 pad_bitcast_fusion
  46.1 0.6 broadcast_in_dim.60.rows_in
  46.7 0.9 copy.25.rows_in
  47.6 1.9 slice.15
  49.5 0.0 copy-done.12
  49.5 0.0 copy-done.9
  49.5 0.1 fusion.3
  49.6 0.5 convert_element_type.22.used_ref
  50.1 0.6 iota_reduce_fusion
  50.7 0.1 reshape.63
  50.8 0.1 reduce_window_max.13
  50.9 0.0 copy-done.1
  50.9 1.0 pad.9
  51.9 0.5 compare_select_fusion.tile_ref
  52.4 0.5 multiply_add_fusion.refs_0_
  53.0 84.1 %attend_all.1 = (bf16[4,480,256]{2,1,0:T(8,128)(2,1)}, bf16[4,1024,256]{2,1,0:T(8,128)(2,1)}, bf16[1024,256]{1,0:T(8,128)(2,1)}, bf16[1024,256]{1,0:T(8,128)(2,1...) custom-call(s32[3,160,1]{2,1,0:T(8,128)} %copy.25.rows_in, ...), custom_call_target="tpu_custom_call" | custom-call | flops 40000000000 | bytes 20000000 | tf_op jit(solution)/shard_map/attend_all/pallas_call | solution.py:1835
  137.0 0.0 all-gather.2.cloned.1.call-done.refs_1_.refs_2_.refs_3_.refs_4_
  137.0 7.8 %collect.1 = bf16[24,128,1024]{2,1,0:T(8,128)(2,1)} custom-call(s32[32]{0:T(128)} %multiply_add_fusion.refs_0_, bf16[64,128,1024]{2,1,0:T(8,128)(2,1)} %all-gather.2.cloned.1.call-done.refs_1_.refs_2_.refs_3_.refs_4_, bf16[64,128,1024]{2,1,0:T(8,128)(2,1)} %all-gather.2.cloned.1.call-done.refs_1_.refs_2_.refs_3_.refs_4_, ...), custom_call_target="tpu_custom_call" | custom-call | bytes 12582912 | tf_op jit(solution)/shard_map/collect/pallas_call | solution.py:1956
  144.9 150.6 %middle.1 = (bf16[3,1024,1024]{2,1,0:T(8,128)(2,1)}, f32[3,256,1024]{2,1,0:T(8,128)}, bf16[2,768,1024]{2,1,0:T(8,128)(2,1)}, bf16[1,512,1024]{2,1,0:T(8,128)(2,1...) custom-call(s32[3,1,160]{2,1,0:T(1,128)} %broadcast_in_dim.60.rows_in,, ...), custom_call_target="tpu_custom_call" | custom-call | flops 99999997952 | bytes 100000000 | tf_op jit(solution)/shard_map/middle/pallas_call | solution.py:1982
  295.4 12.9 %spread.1.refs_10_ = bf16[64,128,1024]{2,1,0:T(8,128)(2,1)} custom-call(s32[64]{0:T(128)} %compare_select_fusion.tile_ref, s32[64]{0:T(128)} %convert_element_type.22.used_ref, bf16[32,128,1024]{2,1,0:T(8,128)(2,1)} %bitcast.46, bf16[32,128,1024]{2,1,0:T(8,128)(2,1)} %bitcast.47, bf16[32,128,1024]{2,1,0:T(8,128)(2,1)} %bitcast.48, ...), custom_call_target="tpu_custom_call" | custom-call | bytes 25165824 | tf_op jit(solution)/shard_map/spread/pallas_call | solution.py:2068
  308.4 0.0 copy-start.10
  308.4 0.0 copy-start.5
  308.4 0.0 copy-start.11
  308.4 0.0 reduce-scatter.2.cloned.1.call-update
  308.4 0.6 copy-done.4
  309.1 0.7 reshape.59.refs_0_
  309.7 0.0 copy-done.13
  309.7 0.0 copy-done.10
  309.7 0.1 fusion.7
  309.8 0.0 copy-done.5
  309.9 0.7 broadcast_multiply_fusion.refs_9_
  310.5 200.1 %lines.1 = (bf16[3072,1024]{1,0:T(8,128)(2,1)}, bf16[768,1024]{1,0:T(8,128)(2,1)}, f32[2,1024]{1,0:T(2,128)}) custom-call(s32[1,480]{1,0:T(1,128)} %reshape.59.refs_0_, f32[480,1024]{1,0:T(8,128)} %get-tuple-element.50.refs_1_, f32[2,1024]{1,0:T(2,128)} %refs_2_.1, bf16[3072,1024]{1,0:T(8,128)(2,1)} %refs_3_.1, ...), custom_call_target="tpu_custom_call" | custom-call | flops 1509949440 | bytes 60000000 | tf_op jit(solution)/shard_map/lines/pallas_call | solution.py:2097
  510.7 1.3 multiply_subtract_fusion
  512.0 12.9 %convert_bitcast_fusion = (bf16[1,8,128,1024]{3,2,1,0:T(8,128)(2,1)}, f32[8,128,1024]{2,1,0:T(8,128)}, f32[1,8,128,1024]{3,2,1,0:T(8,128)}, f32[1,8,128,1024]{3,2,1,0:T(8,128)}, f32[1,8,128,1024]{3,2,1,0:T(8,128)}) fusion(f32[1,8,128,1024]{3,2,1,0:T(8,128)} %param.22, bf16[8,128,1024]{2,1,0:T(8,128)(2,1)} %reduce-scatter.2.cloned.1.call-done, ...), kind=kLoop, calls=%fused_computation.10 | loop fusion | flops 22020096 | bytes 33554440 | tf_op jit(solution)/shard_map/broadcast_in_dim | solution.py:2437
  525.0 6.3 %copy.29 = bf16[3072,1024]{1,0:T(8,128)(2,1)} copy(bf16[3072,1024]{1,0:T(8,128)(2,1)} %get-tuple-element.82) | data formatting | bytes 12582912
  531.3 0.0 copy-done
  531.3 1.1 copy.30
  532.5 0.6 copy.31
  (19 shorter events, 0.1 us)
Async XLA Ops:
  7.2 42.3 %copy-start.12 = (s32[1,32]{1,0:T(1,128)S(1)}, s32[1,32]{1,0:T(1,128)}, u32[]{:S(2)}) copy-start(s32[1,32]{1,0:T(1,128)} %param.19) | copy-start | bytes 388
  7.2 38.3 %copy-start.8 = (s32[3,153]{1,0:T(4,128)S(1)}, s32[3,153]{1,0:T(4,128)}, u32[]{:S(2)}) copy-start(s32[3,153]{1,0:T(4,128)} %param.14) | copy-start | bytes 5512
  7.2 43.7 %copy-start.1 = (bf16[3,153,1024]{2,1,0:T(8,128)(2,1)S(1)}, bf16[3,153,1024]{2,1,0:T(8,128)(2,1)}, u32[]{:S(2)}) copy-start(bf16[3,153,1024]{2,1,0:T(8,128)(2,1)} %param.15) | copy-start | bytes 2820100
  7.2 129.8 %all-gather.2.cloned.1.call-start = ((), (), s32[]{:S(2)}) async-start(), calls=%async_computation.1 | async-start | bytes 18874368 | tf_op jit(solution)/shard_map/all_gather | solution.py:1810
  8.7 40.8 %copy-start.9 = (s32[32]{0:T(128)S(1)}, s32[32]{0:T(128)}, u32[]{:S(2)}) copy-start(s32[32]{0:T(128)} %convert_reduce_fusion) | copy-start | bytes 388
  45.4 466.6 %reduce-scatter.2.cloned.1.call-start = ((), (), s32[]{:S(2)}) async-start(), calls=%async_computation.2 | async-start | bytes 18874368 | tf_op jit(solution)/shard_map/reduce_scatter | solution.py:2092
  308.4 0.7 copy-start.4
  308.4 1.3 copy-start.13
  308.4 1.3 copy-start.10
  308.4 1.5 copy-start.5
  308.4 1.5 copy-start.11
  310.5 200.2 %copy-start.3 = (f32[2,1024]{1,0:T(2,128)S(1)}, f32[2,1024]{1,0:T(2,128)}, u32[]{:S(2)}) copy-start(f32[2,1024]{1,0:T(2,128)} %refs_2_.1) | copy-start | bytes 24580
  310.5 200.2 %copy-start.6 = (f32[2,1024]{1,0:T(2,128)S(1)}, f32[2,1024]{1,0:T(2,128)}, u32[]{:S(2)}) copy-start(f32[2,1024]{1,0:T(2,128)} %param.17) | copy-start | bytes 24580
  310.5 200.2 %copy-start.7 = (f32[2,1024]{1,0:T(2,128)S(1)}, f32[2,1024]{1,0:T(2,128)}, u32[]{:S(2)}) copy-start(f32[2,1024]{1,0:T(2,128)} %param.18) | copy-start | bytes 24580
  525.0 6.3 %copy-start = (bf16[768,1024]{1,0:T(8,128)(2,1)S(1)}, bf16[768,1024]{1,0:T(8,128)(2,1)}, u32[]{:S(2)}) copy-start(bf16[768,1024]{1,0:T(8,128)(2,1)} %get-tuple-element.83) | copy-start | bytes 4718596
  525.0 7.5 %copy-start.2 = (f32[2,1024]{1,0:T(2,128)S(1)}, f32[2,1024]{1,0:T(2,128)}, u32[]{:S(2)}) copy-start(f32[2,1024]{1,0:T(2,128)} %get-tuple-element.89) | copy-start | bytes 24580
Sparse Core Ops, SparseCore 0:
  45.5 90.1 all-gather.1
  308.6 117.4 reduce-scatter.1
